TPU v7x, 32 devices: a whole 2x2x4 slice. The times are simulated.
32 devices in a mesh: dp: 8 (over z, core), fsdp: 4 (over y, x).
Axes of the slice: x: 2, y: 2, z: 4, core: 2. Of those that a mesh axis runs over, the one named last changes fastest.
Arguments:
- tokens: bfloat16 [8, 2624, 1536], P('dp', 'fsdp'), may hold values from -6 to 6
- cotangent: bfloat16 [8, 2624, 1536], P('dp', 'fsdp'), may hold values from -6 to 6
- text_states: bfloat16 [8, 2, 256, 4096], P('dp', None, 'fsdp'), may hold values from -6 to 6
- conditioning: bfloat16 [8, 2, 1024], P('dp'), may hold values from -6 to 6
- image_sizes: int32 [8, 2, 2], P('dp'), may hold values from 6 to 96, as said below
- ada_weight: bfloat16 [1024, 6144], P('fsdp'), may hold values from -0.1875 to 0.1875
- ada_bias: float32 [6144], replicated, may hold values from -3 to 3
- qkv_weight: bfloat16 [1536, 4608], P('fsdp'), may hold values from -0.15625 to 0.15625
- out_weight: bfloat16 [1536, 1536], P('fsdp'), may hold values from -0.15625 to 0.15625
- text_weight: bfloat16 [4096, 3072], P('fsdp'), may hold values from -0.09375 to 0.09375
- gate_up_weight: bfloat16 [1536, 8192], P('fsdp'), may hold values from -0.15625 to 0.15625
- down_weight: bfloat16 [4096, 1536], P('fsdp'), may hold values from -0.09375 to 0.09375
- norm_gains: float32 [7, 1536], replicated, may hold values from 0.1 to 1.9
- norm_shifts: float32 [2, 1536], replicated, may hold values from -3 to 3
- text_gain: float32 [4096], replicated, may hold values from 0.1 to 1.9
- head_gate: float32 [24], replicated, may hold values from 0.2 to 0.8
Outputs:
- block_out: bfloat16 [8, 2624, 1536], P('dp', 'fsdp')
- tokens_grad: bfloat16 [8, 2624, 1536], P('dp', 'fsdp')
- text_grad: bfloat16 [8, 2, 256, 4096], P('dp', None, 'fsdp')
- ada_weight_grad: float32 [1024, 6144], P(('dp', 'fsdp'))
- qkv_weight_grad: float32 [1536, 4608], P(('dp', 'fsdp'))
- out_weight_grad: float32 [1536, 1536], P(('dp', 'fsdp'))
- text_weight_grad: float32 [4096, 3072], P(('dp', 'fsdp'))
- gate_up_weight_grad: float32 [1536, 8192], P(('dp', 'fsdp'))
- down_weight_grad: float32 [4096, 1536], P(('dp', 'fsdp'))
- ada_bias_grad: float32 [6144], replicated
- norm_gains_grad: float32 [7, 1536], replicated
- norm_shifts_grad: float32 [2, 1536], replicated
- text_gain_grad: float32 [4096], replicated
- head_gate_grad: float32 [24], replicated
Inputs may be any that keep to these rules, and one draw needn't show every extreme that they name: `image_sizes`: in every group image 0 has 16 * 12**2 patches and image 1 has 12**2; an image is square or has rows and columns in the ratio 1:4 or 4:1.
All inputs are finite; a program needn't handle non-finite values.
Results may differ from a plain program's by a relative error of at most 0.023.
Values may be sent and summed in bfloat16 or wider, within the bound.
A program may use at most 512 MiB of HBM per device.

v0:
```python
import jax
import jax.numpy as jnp
from jax import lax
from jax.sharding import PartitionSpec as P

EPS = 1e-05
HIGHEST_PRECISION = lax.Precision.HIGHEST
MASKED = -1e30


def low_product(left, right):
    return jnp.dot(left, right, preferred_element_type=jnp.float32)


def times_transposed(left, right):
    return lax.dot_general(
        left, right, (((1,), (1,)), ((), ())), preferred_element_type=jnp.float32
    )


def outer_sum(left, right):
    return lax.dot_general(
        left, right, (((0,), (0,)), ((), ())), preferred_element_type=jnp.float32
    )


def exact_product(left, right):
    return jnp.dot(left, right, precision=HIGHEST_PRECISION, preferred_element_type=jnp.float32)


def exact_outer(left, right):
    return lax.dot_general(
        left,
        right,
        (((0,), (0,)), ((), ())),
        precision=HIGHEST_PRECISION,
        preferred_element_type=jnp.float32,
    )


def dp_major(value, wide, narrow):
    rows = value.shape[0] // (wide * narrow)
    return (
        value.reshape(wide, narrow, rows, value.shape[1]).transpose(1, 0, 2, 3).reshape(value.shape)
    )


def rms_norm(value, gain):
    return value * lax.rsqrt(jnp.mean(value * value, axis=-1, keepdims=True) + EPS) * gain


def layer_norm(value, weight, shift):
    centred = value - jnp.mean(value, axis=-1, keepdims=True)
    return (
        centred * lax.rsqrt(jnp.mean(centred * centred, axis=-1, keepdims=True) + EPS) * weight
        + shift
    )


def modulated_norm(value, gain, shift):
    return rms_norm(value, gain) * (1.0 + shift)


def residual_branch(base, value, gain, gate_value):
    return base + jnp.tanh(gate_value) * rms_norm(value, gain)


def key_norm(value, weight):
    return layer_norm(value, weight, 0.0)


def token_layout(image_sizes, first_token, token_count, image_count):
    patch_rows = image_sizes[:, 0]
    patch_cols = image_sizes[:, 1]
    image_tokens = patch_rows * (patch_cols + 1)
    image_ends = jnp.cumsum(image_tokens)
    image_starts = image_ends - image_tokens
    position = first_token + jnp.arange(token_count, dtype=jnp.int32)
    member_of = (position[:, None] >= image_starts[None, :]) & (
        position[:, None] < image_ends[None, :]
    )
    member_int = member_of.astype(jnp.int32)
    in_image = jnp.sum(member_int, axis=1)
    slot_ids = jnp.arange(image_count, dtype=jnp.int32)
    image_index = jnp.sum(member_int * slot_ids[None, :], axis=1) + image_count * (1 - in_image)
    offset_in = position - jnp.sum(member_int * image_starts[None, :], axis=1)
    line_width = jnp.sum(member_int * (patch_cols + 1)[None, :], axis=1) + (1 - in_image)
    token_row = offset_in // line_width * in_image
    token_col = offset_in % line_width * in_image
    return (member_of.astype(jnp.float32), image_index, token_row, token_col)


def rope_tables(token_row, token_col, head_dim):
    quarter = head_dim // 4
    frequency = 10000.0 ** (-jnp.arange(quarter, dtype=jnp.float32) / quarter)
    angles = jnp.concatenate(
        [
            token_row.astype(jnp.float32)[:, None] * frequency[None, :],
            token_col.astype(jnp.float32)[:, None] * frequency[None, :],
        ],
        axis=1,
    )
    return (jnp.cos(angles), jnp.sin(angles))


def rotate(value, cosine, sine_table):
    paired = value.reshape(value.shape[0], value.shape[1], value.shape[2] // 2, 2)
    real_part = paired[..., 0]
    imag_part = paired[..., 1]
    cos_b = cosine[:, None, :]
    sin_b = sine_table[:, None, :]
    turned = jnp.stack(
        [real_part * cos_b - imag_part * sin_b, real_part * sin_b + imag_part * cos_b], axis=-1
    )
    return turned.reshape(value.shape)


def head_forward(queries, key_block, value_block, allowed, score_scale):
    scores = jnp.where(allowed, times_transposed(queries, key_block) * score_scale, MASKED)
    maximum = jnp.max(scores, axis=1, keepdims=True)
    exponent = jnp.exp(scores - maximum)
    row_total = jnp.sum(exponent, axis=1, keepdims=True)
    attn_probs = (exponent / row_total).astype(jnp.bfloat16)
    return (low_product(attn_probs, value_block), maximum + jnp.log(row_total))


def head_backward(queries, key_block, value_block, allowed, log_total, grad_out, score_scale):
    scores = jnp.where(allowed, times_transposed(queries, key_block) * score_scale, MASKED)
    attn_probs = jnp.exp(scores - log_total)
    probs_low = attn_probs.astype(jnp.bfloat16)
    grad_probs = times_transposed(grad_out, value_block)
    grad_scores = (
        attn_probs * (grad_probs - jnp.sum(attn_probs * grad_probs, axis=1, keepdims=True))
    ).astype(jnp.bfloat16)
    grad_queries = low_product(grad_scores, key_block) * score_scale
    grad_keys = outer_sum(grad_scores, queries) * score_scale
    grad_values = outer_sum(probs_low, grad_out)
    return (grad_queries, grad_keys, grad_values)


def shards(
    tokens,
    cotangent,
    text_states,
    conditioning,
    image_sizes,
    ada_weight,
    ada_bias,
    qkv_weight,
    out_weight,
    text_weight,
    gate_up_weight,
    down_weight,
    norm_gains,
    norm_shifts,
    text_gain,
    head_gate,
):
    model_width = tokens.shape[2]
    head_count = head_gate.shape[0]
    head_dim = model_width // head_count
    image_count = text_states.shape[1]
    caption_local = text_states.shape[2]
    caption_width = text_states.shape[3]
    local_tok = tokens.shape[1]
    wide = lax.axis_size("dp")
    narrow = lax.axis_size("fsdp")
    group_tok = local_tok * narrow
    caption_full = caption_local * narrow
    first_token = lax.axis_index("fsdp") * local_tok
    score_scale = head_dim ** (-0.5)
    text_total = image_count * caption_full
    gathered = (
        lax.all_gather(ada_weight, "fsdp", axis=0, tiled=True),
        lax.all_gather(qkv_weight, "fsdp", axis=0, tiled=True),
        lax.all_gather(out_weight, "fsdp", axis=0, tiled=True),
        lax.all_gather(text_weight, "fsdp", axis=0, tiled=True),
        lax.all_gather(gate_up_weight, "fsdp", axis=0, tiled=True),
        lax.all_gather(down_weight, "fsdp", axis=0, tiled=True),
    )
    full_ada, full_qkv, full_out, full_text, full_gate_up, full_down = gathered
    group_sizes = image_sizes[0]
    onehot, image_index, token_row, token_col = token_layout(
        group_sizes, first_token, local_tok, image_count
    )
    key_image = token_layout(group_sizes, 0, group_tok, image_count)[1]
    token_in = tokens[0].astype(jnp.float32)
    cond_low = jax.nn.silu(conditioning[0].astype(jnp.float32)).astype(jnp.bfloat16)
    modulation = low_product(cond_low, full_ada) + ada_bias
    per_token = exact_product(onehot, modulation)
    scale_attend = per_token[:, :model_width]
    gate_attend = per_token[:, model_width : 2 * model_width]
    scale_feed = per_token[:, 2 * model_width : 3 * model_width]
    gate_feed = per_token[:, 3 * model_width :]
    normed, pull_normed = jax.vjp(modulated_norm, token_in, norm_gains[0], scale_attend)
    normed_low = normed.astype(jnp.bfloat16)
    projected = low_product(normed_low, full_qkv)
    cosine, sine_table = rope_tables(token_row, token_col, head_dim)

    def rotated(value, weight, shift):
        return rotate(
            layer_norm(value, weight, shift).reshape(local_tok, head_count, head_dim),
            cosine,
            sine_table,
        )

    queries, pull_queries = jax.vjp(
        rotated, projected[:, :model_width], norm_gains[2], norm_shifts[0]
    )
    key_rows, pull_keys = jax.vjp(
        rotated, projected[:, model_width : 2 * model_width], norm_gains[3], norm_shifts[1]
    )
    queries_low = queries.astype(jnp.bfloat16)
    keys_low = key_rows.astype(jnp.bfloat16).reshape(local_tok, model_width)
    values_low = projected[:, 2 * model_width :].astype(jnp.bfloat16)
    group_keys, group_values = (
        lax.all_gather(keys_low, "fsdp", axis=0, tiled=True),
        lax.all_gather(values_low, "fsdp", axis=0, tiled=True),
    )
    text_in = text_states[0].astype(jnp.float32)
    text_normed, pull_text = jax.vjp(rms_norm, text_in, text_gain)
    text_low = text_normed.astype(jnp.bfloat16).reshape(image_count * caption_local, caption_width)
    text_projected = low_product(text_low, full_text)
    text_keys, pull_text_keys = jax.vjp(key_norm, text_projected[:, :model_width], norm_gains[4])
    text_pair = (
        text_keys.astype(jnp.bfloat16).reshape(image_count, caption_local, model_width),
        text_projected[:, model_width:]
        .astype(jnp.bfloat16)
        .reshape(image_count, caption_local, model_width),
    )
    group_text_keys, group_text_values = (
        lax.all_gather(text_pair[0], "fsdp", axis=1, tiled=True),
        lax.all_gather(text_pair[1], "fsdp", axis=1, tiled=True),
    )

    def heads_first(value, count):
        return value.reshape(count, head_count, head_dim).transpose(1, 0, 2)

    def heads_last(value, count):
        return value.transpose(1, 0, 2).reshape(count, model_width)

    query_heads = queries_low.transpose(1, 0, 2)
    key_heads = heads_first(group_keys, group_tok)
    value_heads = heads_first(group_values, group_tok)
    text_key_heads = heads_first(group_text_keys.reshape(text_total, model_width), text_total)
    text_value_heads = heads_first(group_text_values.reshape(text_total, model_width), text_total)
    same_image = image_index[:, None] == key_image[None, :]
    text_image = jnp.arange(text_total, dtype=jnp.int32) // caption_full
    linked = (image_index[:, None] == text_image[None, :]) | (image_index[:, None] == image_count)

    def run_forward(key_block, value_block, allowed):
        return lax.map(
            lambda packed: head_forward(packed[0], packed[1], packed[2], allowed, score_scale),
            (query_heads, key_block, value_block),
        )

    self_out, self_total = run_forward(key_heads, value_heads, same_image)
    cross_out, cross_total = run_forward(text_key_heads, text_value_heads, linked)
    gate_tanh = jnp.tanh(head_gate)
    mixed = heads_last(self_out + gate_tanh[:, None, None] * cross_out, local_tok)
    mixed_low = mixed.astype(jnp.bfloat16)
    branch = low_product(mixed_low, full_out)
    hidden, pull_attend = jax.vjp(residual_branch, token_in, branch, norm_gains[1], gate_attend)
    normed_feed, pull_feed_in = jax.vjp(modulated_norm, hidden, norm_gains[5], scale_feed)
    normed_feed_low = normed_feed.astype(jnp.bfloat16)
    gate_up = low_product(normed_feed_low, full_gate_up)
    hidden_units = gate_up.shape[1] // 2

    def swiglu(value):
        return jax.nn.silu(value[:, :hidden_units]) * value[:, hidden_units:]

    activated, pull_swiglu = jax.vjp(swiglu, gate_up)
    activated_low = activated.astype(jnp.bfloat16)
    down_out = low_product(activated_low, full_down)
    result, pull_result = jax.vjp(residual_branch, hidden, down_out, norm_gains[6], gate_feed)
    back_weights = (
        lax.all_gather(ada_weight, "fsdp", axis=0, tiled=True),
        lax.all_gather(qkv_weight, "fsdp", axis=0, tiled=True),
        lax.all_gather(out_weight, "fsdp", axis=0, tiled=True),
        lax.all_gather(text_weight, "fsdp", axis=0, tiled=True),
        lax.all_gather(gate_up_weight, "fsdp", axis=0, tiled=True),
        lax.all_gather(down_weight, "fsdp", axis=0, tiled=True),
    )
    back_qkv = back_weights[1]
    back_out = back_weights[2]
    back_text = back_weights[3]
    back_gate_up = back_weights[4]
    back_down = back_weights[5]
    grad_result = cotangent[0].astype(jnp.float32)
    grad_hidden, grad_down, grad_gain_six, grad_gate_feed = pull_result(grad_result)
    grad_down_low = grad_down.astype(jnp.bfloat16)
    grad_down_weight = outer_sum(activated_low, grad_down_low)
    grad_activated = times_transposed(grad_down_low, back_down)
    (grad_gate_up,) = pull_swiglu(grad_activated)
    grad_gate_up_low = grad_gate_up.astype(jnp.bfloat16)
    grad_gate_up_weight = outer_sum(normed_feed_low, grad_gate_up_low)
    grad_normed_feed = times_transposed(grad_gate_up_low, back_gate_up)
    grad_hidden_in, grad_gain_five, grad_scale_feed = pull_feed_in(grad_normed_feed)
    grad_hidden = grad_hidden + grad_hidden_in
    feed_narrow = (
        lax.psum_scatter(
            dp_major(grad_gate_up_weight, wide, narrow).astype(jnp.bfloat16),
            "fsdp",
            scatter_dimension=0,
            tiled=True,
        ).astype(jnp.float32),
        lax.psum_scatter(
            dp_major(grad_down_weight, wide, narrow).astype(jnp.bfloat16),
            "fsdp",
            scatter_dimension=0,
            tiled=True,
        ).astype(jnp.float32),
    )
    feed_parts = (
        lax.psum_scatter(
            feed_narrow[0].astype(jnp.bfloat16), "dp", scatter_dimension=0, tiled=True
        ).astype(jnp.float32),
        lax.psum_scatter(
            feed_narrow[1].astype(jnp.bfloat16), "dp", scatter_dimension=0, tiled=True
        ).astype(jnp.float32),
    )
    grad_tokens, grad_branch, grad_gain_one, grad_gate_attend = pull_attend(grad_hidden)
    grad_branch_low = grad_branch.astype(jnp.bfloat16)
    grad_out_weight = outer_sum(mixed_low, grad_branch_low)
    grad_mixed = (
        times_transposed(grad_branch_low, back_out)
        .reshape(local_tok, head_count, head_dim)
        .transpose(1, 0, 2)
    )
    grad_self_low = grad_mixed.astype(jnp.bfloat16)
    grad_cross_low = (gate_tanh[:, None, None] * grad_mixed).astype(jnp.bfloat16)
    grad_head_gate = jnp.sum(grad_mixed * cross_out, axis=(1, 2)) * (1.0 - gate_tanh * gate_tanh)

    def run_backward(key_block, value_block, allowed, log_total, grad_out):
        return lax.map(
            lambda packed: head_backward(
                packed[0], packed[1], packed[2], allowed, packed[3], packed[4], score_scale
            ),
            (query_heads, key_block, value_block, log_total, grad_out),
        )

    self_query_grad, self_key_grad, self_value_grad = run_backward(
        key_heads, value_heads, same_image, self_total, grad_self_low
    )
    cross_query_grad, cross_key_grad, cross_value_grad = run_backward(
        text_key_heads, text_value_heads, linked, cross_total, grad_cross_low
    )
    grad_key_rows, grad_value_rows = (
        lax.psum_scatter(
            heads_last(self_key_grad, group_tok).astype(jnp.bfloat16),
            "fsdp",
            scatter_dimension=0,
            tiled=True,
        ).astype(jnp.float32),
        lax.psum_scatter(
            heads_last(self_value_grad, group_tok).astype(jnp.bfloat16),
            "fsdp",
            scatter_dimension=0,
            tiled=True,
        ).astype(jnp.float32),
    )
    text_key_grad = heads_last(cross_key_grad, text_total).reshape(
        image_count, caption_full, model_width
    )
    text_value_grad = heads_last(cross_value_grad, text_total).reshape(
        image_count, caption_full, model_width
    )
    grad_text_keys, grad_text_values = (
        lax.psum_scatter(
            text_key_grad.astype(jnp.bfloat16), "fsdp", scatter_dimension=1, tiled=True
        ).astype(jnp.float32),
        lax.psum_scatter(
            text_value_grad.astype(jnp.bfloat16), "fsdp", scatter_dimension=1, tiled=True
        ).astype(jnp.float32),
    )
    grad_query_pre, grad_gain_two, grad_shift_zero = pull_queries(
        (self_query_grad + cross_query_grad).transpose(1, 0, 2)
    )
    grad_key_pre, grad_gain_three, grad_shift_one = pull_keys(
        grad_key_rows.reshape(local_tok, head_count, head_dim)
    )
    grad_projected_low = jnp.concatenate(
        [grad_query_pre, grad_key_pre, grad_value_rows], axis=1
    ).astype(jnp.bfloat16)
    grad_qkv_weight = outer_sum(normed_low, grad_projected_low)
    grad_normed = times_transposed(grad_projected_low, back_qkv)
    grad_tokens_in, grad_gain_zero, grad_scale_attend = pull_normed(grad_normed)
    grad_tokens = grad_tokens + grad_tokens_in
    grad_text_key_pre, grad_gain_four = pull_text_keys(
        grad_text_keys.reshape(image_count * caption_local, model_width)
    )
    grad_text_projected = jnp.concatenate(
        [grad_text_key_pre, grad_text_values.reshape(image_count * caption_local, model_width)],
        axis=1,
    ).astype(jnp.bfloat16)
    grad_text_weight = outer_sum(text_low, grad_text_projected)
    grad_text_normed = times_transposed(grad_text_projected, back_text).reshape(
        image_count, caption_local, caption_width
    )
    grad_text_in, grad_text_gain = pull_text(grad_text_normed)
    grad_per_token = jnp.concatenate(
        [grad_scale_attend, grad_gate_attend, grad_scale_feed, grad_gate_feed], axis=1
    )
    grad_modulation = exact_outer(onehot, grad_per_token)
    grad_ada_bias = jnp.sum(grad_modulation, axis=0)
    grad_ada_weight = exact_outer(cond_low.astype(jnp.float32), grad_modulation)
    ada_part = lax.psum_scatter(grad_ada_weight, ("dp", "fsdp"), scatter_dimension=0, tiled=True)
    attend_narrow = (
        lax.psum_scatter(
            dp_major(grad_qkv_weight, wide, narrow).astype(jnp.bfloat16),
            "fsdp",
            scatter_dimension=0,
            tiled=True,
        ).astype(jnp.float32),
        lax.psum_scatter(
            dp_major(grad_out_weight, wide, narrow).astype(jnp.bfloat16),
            "fsdp",
            scatter_dimension=0,
            tiled=True,
        ).astype(jnp.float32),
        lax.psum_scatter(
            dp_major(grad_text_weight, wide, narrow).astype(jnp.bfloat16),
            "fsdp",
            scatter_dimension=0,
            tiled=True,
        ).astype(jnp.float32),
    )
    attend_parts = (
        lax.psum_scatter(
            attend_narrow[0].astype(jnp.bfloat16), "dp", scatter_dimension=0, tiled=True
        ).astype(jnp.float32),
        lax.psum_scatter(
            attend_narrow[1].astype(jnp.bfloat16), "dp", scatter_dimension=0, tiled=True
        ).astype(jnp.float32),
        lax.psum_scatter(
            attend_narrow[2].astype(jnp.bfloat16), "dp", scatter_dimension=0, tiled=True
        ).astype(jnp.float32),
    )
    grad_gains = jnp.stack(
        [
            grad_gain_zero,
            grad_gain_one,
            grad_gain_two,
            grad_gain_three,
            grad_gain_four,
            grad_gain_five,
            grad_gain_six,
        ]
    )
    grad_shifts = jnp.stack([grad_shift_zero, grad_shift_one])
    small_parts = lax.psum(
        (grad_gains, grad_shifts, grad_text_gain, grad_ada_bias, grad_head_gate), ("dp", "fsdp")
    )
    return (
        result.astype(jnp.bfloat16)[None],
        grad_tokens.astype(jnp.bfloat16)[None],
        grad_text_in.astype(jnp.bfloat16)[None],
        ada_part,
        attend_parts[0],
        attend_parts[1],
        attend_parts[2],
        feed_parts[0],
        feed_parts[1],
        small_parts[3],
        small_parts[0],
        small_parts[1],
        small_parts[2],
        small_parts[4],
    )


def solution(mesh):
    placed = (
        P("dp", "fsdp", None),
        P("dp", "fsdp", None),
        P("dp", None, "fsdp", None),
        P("dp", None, None),
        P("dp", None, None),
        P("fsdp", None),
        P(),
        P("fsdp", None),
        P("fsdp", None),
        P("fsdp", None),
        P("fsdp", None),
        P("fsdp", None),
        P(),
        P(),
        P(),
        P(),
    )
    return jax.shard_map(
        shards,
        mesh=mesh,
        in_specs=placed,
        out_specs=(
            P("dp", "fsdp", None),
            P("dp", "fsdp", None),
            P("dp", None, "fsdp", None),
            P(("dp", "fsdp"), None),
            P(("dp", "fsdp"), None),
            P(("dp", "fsdp"), None),
            P(("dp", "fsdp"), None),
            P(("dp", "fsdp"), None),
            P(("dp", "fsdp"), None),
            P(),
            P(),
            P(),
            P(),
            P(),
        ),
        check_vma=False,
    )
```

profile of v0, /device:TPU:0, one launch (start us, length us, event | category | flops | bytes accessed | tf_op | source)
XLA Modules:
  0.0 3543.2 jit_solution(3431875302075425536)
XLA Ops:
  11.9 123.2 %all-gather.11.cloned.1.call-done = bf16[1024,6144]{1,0:T(8,128)(2,1)} async-done(((bf16[256,6144]{1,0:T(8,128)(2,1)}), bf16[1024,6144]{1,0:T(8,128)(2,1)}) %all-gather.11.cloned.1.call-update) | async-done | bytes 12582928 | tf_op jit(solution)/shard_map/all_gather | solution.py:174
  156.8 115.8 %all-gather.13.cloned.1.call-done = bf16[1536,4608]{1,0:T(8,128)(2,1)} async-done(((bf16[384,4608]{1,0:T(8,128)(2,1)}), bf16[1536,4608]{1,0:T(8,128)(2,1)}) %all-gather.13.cloned.1.call-update) | async-done | bytes 14155792 | tf_op jit(solution)/shard_map/all_gather | solution.py:175
  321.5 16.2 subtract_convert_fusion
  355.2 147.0 %all-gather.19.cloned.1.call-done = bf16[4096,3072]{1,0:T(8,128)(2,1)} async-done(((bf16[1024,3072]{1,0:T(8,128)(2,1)}), bf16[4096,3072]{1,0:T(8,128)(2,1)}) %all-gather.19.cloned.1.call-update) | async-done | bytes 25165840 | tf_op jit(solution)/shard_map/all_gather | solution.py:177
  531.9 57.5 %all-gather.15.cloned.1.call-done = bf16[2624,1536]{1,0:T(8,128)(2,1)} async-done(((bf16[656,1536]{1,0:T(8,128)(2,1)}), bf16[2624,1536]{1,0:T(8,128)(2,1)}) %all-gather.15.cloned.1.call-update) | async-done | bytes 8060944 | tf_op jit(solution)/shard_map/all_gather | solution.py:217
  600.5 16.5 copy.125
  617.1 58.9 %all-gather.17.cloned.1.call-done = bf16[2624,1536]{1,0:T(8,128)(2,1)} async-done(((bf16[656,1536]{1,0:T(8,128)(2,1)}), bf16[2624,1536]{1,0:T(8,128)(2,1)}) %all-gather.17.cloned.1.call-update) | async-done | bytes 8060944 | tf_op jit(solution)/shard_map/all_gather | solution.py:218
  687.1 16.6 copy.126
  706.3 172.8 %while.56 = (s32[]{:T(128)}, f32[24,656,64]{1,2,0:T(8,128)}, f32[24,656,1]{1,2,0:T(1,128)S(1)}, bf16[24,656,64]{2,1,0:T(8,128)(2,1)}, bf16[24,2624,64]{2,1,0:T(8...) while((s32[]{:T(128)}, f32[24,656,64]{1,2,0:T(8,128)}, ...), condition=%wide.region_15.16_spmd.clone, body=%wide.region_12.15_spmd.clone.sunk | while | flops 456155520 | bytes 22407584 | solution.py:252
  901.7 97.6 %while.57 = (s32[]{:T(128)}, f32[24,656,64]{1,2,0:T(8,128)}, f32[24,656,1]{1,2,0:T(1,128)S(1)}, bf16[24,656,64]{2,1,0:T(8,128)(2,1)}, bf16[24,512,64]{2,1,0:T(8,...) while((s32[]{:T(128)}, f32[24,656,64]{1,2,0:T(8,128)}, ...), condition=%wide.region_22.23_spmd.clone, body=%wide.region_19.22_spmd.clone.sunk | while | flops 89341296 | bytes 4692793 | solution.py:252
  1031.3 25.5 fusion.178
  1067.9 87.6 %all-gather.29.cloned.1.call-done = bf16[4096,1536]{1,0:T(8,128)(2,1)} async-done(((bf16[1024,1536]{1,0:T(8,128)(2,1)}), bf16[4096,1536]{1,0:T(8,128)(2,1)}) %all-gather.29.cloned.1.call-update) | async-done | bytes 12582928 | tf_op jit(solution)/shard_map/all_gather | solution.py:179
  1179.7 24.5 fusion.128
  1204.2 31.6 multiply_reduce_fusion.4
  1262.8 541.7 %while.58 = (s32[]{:T(128)}, f32[24,656,64]{1,2,0:T(8,128)}, bf16[24,2624,64]{1,2,0:T(8,128)(2,1)}, bf16[24,2624,64]{1,2,0:T(8,128)(2,1)}, bf16[24,656,64]{2,1,0...) while((s32[]{:T(128)}, f32[24,656,64]{1,2,0:T(8,128)}, ...), condition=%wide.region_31.32_spmd.clone, body=%wide.region_29.31_spmd.clone.sunk | while | flops 1119082880 | bytes 55960312 | solution.py:335
  1836.6 204.9 %while.59 = (s32[]{:T(128)}, f32[24,656,64]{1,2,0:T(8,128)}, bf16[24,512,64]{1,2,0:T(8,128)(2,1)}, bf16[24,512,64]{1,2,0:T(8,128)(2,1)}, bf16[24,656,64]{2,1,0:T...) while((s32[]{:T(128)}, f32[24,656,64]{1,2,0:T(8,128)}, ...), condition=%wide.region_34.35_spmd.clone, body=%wide.region_32.34_spmd.clone.sunk | while | flops 218726768 | bytes 11484305 | solution.py:335
  2103.1 14.6 multiply_add_fusion.5
  2174.8 16.6 convolution_convert_fusion.1
  2203.9 30.5 convolution_convert_fusion
  2234.3 21.0 copy.152
  2274.2 21.0 copy.151
  2297.0 136.6 %reduce-scatter.26.cloned.1.call-done = bf16[384,4608]{1,0:T(8,128)(2,1)} async-done(((bf16[1536,4608]{1,0:T(8,128)(2,1)}), bf16[384,4608]{1,0:T(8,128)(2,1)}) %reduce-scatter.26.cloned.1.call-update) | async-done | bytes 3538960 | tf_op jit(solution)/shard_map/reduce_scatter | solution.py:409
  2433.6 224.8 %reduce-scatter.38.cloned.1.call-done = bf16[384,8192]{1,0:T(8,128)(2,1)} async-done(((bf16[1536,8192]{1,0:T(8,128)(2,1)}), bf16[384,8192]{1,0:T(8,128)(2,1)}) %reduce-scatter.38.cloned.1.call-update) | async-done | bytes 6291472 | tf_op jit(solution)/shard_map/reduce_scatter | solution.py:301
  2658.6 225.1 %reduce-scatter.34.cloned.1.call-done = bf16[1024,3072]{1,0:T(8,128)(2,1)} async-done(((bf16[4096,3072]{1,0:T(8,128)(2,1)}), bf16[1024,3072]{1,0:T(8,128)(2,1)}) %reduce-scatter.34.cloned.1.call-update) | async-done | bytes 6291472 | tf_op jit(solution)/shard_map/reduce_scatter | solution.py:421
  2884.5 14.9 multiply_reduce_fusion.18
  2901.9 18.2 fusion.109
  2934.2 13.5 fusion.164
  2962.0 42.9 %reduce-scatter.28.cloned.1.call-done = bf16[48,4608]{1,0:T(8,128)(2,1)} async-done(((bf16[384,4608]{1,0:T(8,128)(2,1)}), bf16[48,4608]{1,0:T(8,128)(2,1)}) %reduce-scatter.28.cloned.1.call-update) | async-done | bytes 442384 | tf_op jit(solution)/shard_map/reduce_scatter | solution.py:429
  3006.9 68.8 %reduce-scatter.40.cloned.1.call-done = bf16[48,8192]{1,0:T(8,128)(2,1)} async-done(((bf16[384,8192]{1,0:T(8,128)(2,1)}), bf16[48,8192]{1,0:T(8,128)(2,1)}) %reduce-scatter.40.cloned.1.call-update) | async-done | bytes 786448 | tf_op jit(solution)/shard_map/reduce_scatter | solution.py:315
  3078.0 68.1 %reduce-scatter.36.cloned.1.call-done = bf16[128,3072]{1,0:T(8,128)(2,1)} async-done(((bf16[1024,3072]{1,0:T(8,128)(2,1)}), bf16[128,3072]{1,0:T(8,128)(2,1)}) %reduce-scatter.36.cloned.1.call-update) | async-done | bytes 786448 | tf_op jit(solution)/shard_map/reduce_scatter | solution.py:435
  3148.5 127.0 %all-reduce.9.cloned.1.call-done = (f32[6144]{0:T(1024)}, f32[7,1536]{1,0:T(8,128)}, f32[2,1536]{1,0:T(2,128)}, f32[4096]{0:T(1024)}, f32[24]{0:T(128)}) async-done(((f32[6144]{0:T(1024)}, f32[7,1536]{1,0:T(8,128)}, f32[2,1536]{1,0:T(2,128)}, f32[4096]{0:T(1024)}, f32[24]{0:T(128)}), (f32[6144]{0:T(1024)}, f32[7,1536]{1,0:T(8,128)}, f32[2,1536]{1,0:T(2,128)}, f32[4096]{0:T(1024)}, ...) | async-done | bytes 96368 | tf_op jit(solution)/shard_map/psum | solution.py:451
  3275.6 254.4 %reduce-scatter.24.cloned.1.call-done = f32[32,6144]{1,0:T(8,128)} async-done(((f32[1024,6144]{1,0:T(8,128)}), f32[32,6144]{1,0:T(8,128)}) %reduce-scatter.24.cloned.1.call-update) | async-done | bytes 786448 | tf_op jit(solution)/shard_map/reduce_scatter | solution.py:407
  (1020 shorter events, 1506.4 us)
Async XLA Ops:
  7.2 127.9 %all-gather.11.cloned.1.call-start = ((), (), s32[]{:S(2)}) async-start(), calls=%async_computation.15 | async-start | bytes 15728640 | tf_op jit(solution)/shard_map/all_gather | solution.py:174
  7.9 264.7 %all-gather.13.cloned.1.call-start = ((), (), s32[]{:S(2)}) async-start(), calls=%async_computation.16 | async-start | bytes 17694720 | tf_op jit(solution)/shard_map/all_gather | solution.py:175
  8.7 493.5 %all-gather.19.cloned.1.call-start = ((), (), s32[]{:S(2)}) async-start(), calls=%async_computation.19 | async-start | bytes 31457280 | tf_op jit(solution)/shard_map/all_gather | solution.py:177
  9.5 579.9 %all-gather.15.cloned.1.call-start = ((), (), s32[]{:S(2)}) async-start(), calls=%async_computation.17 | async-start | bytes 10076160 | tf_op jit(solution)/shard_map/all_gather | solution.py:217
  10.7 310.8 %copy-start.30 = (f32[656,32]{0,1:T(8,128)}, f32[656,32]{0,1:T(8,128)S(1)}, u32[]{:S(2)}) copy-start(f32[656,32]{0,1:T(8,128)S(1)} %get-tuple-element.598) | copy-start | bytes 251908
  10.7 310.8 %copy-start.32 = (f32[656,32]{0,1:T(8,128)}, f32[656,32]{0,1:T(8,128)S(1)}, u32[]{:S(2)}) copy-start(f32[656,32]{0,1:T(8,128)S(1)} %get-tuple-element.599) | copy-start | bytes 251908
  11.4 276.9 %copy-start.44 = (f32[1536]{0:T(1024)}, f32[1536]{0:T(1024)S(1)}, u32[]{:S(2)}) copy-start(f32[1536]{0:T(1024)S(1)} %get-tuple-element.449) | copy-start | bytes 18436
  11.4 276.9 %copy-start.46 = (f32[1536]{0:T(1024)}, f32[1536]{0:T(1024)S(1)}, u32[]{:S(2)}) copy-start(f32[1536]{0:T(1024)S(1)} %get-tuple-element.450) | copy-start | bytes 18436
  11.4 501.2 %copy-start.42 = (f32[1536]{0:T(1024)}, f32[1536]{0:T(1024)S(1)}, u32[]{:S(2)}) copy-start(f32[1536]{0:T(1024)S(1)} %get-tuple-element.448) | copy-start | bytes 18436
  350.4 325.6 %all-gather.17.cloned.1.call-start = ((), (), s32[]{:S(2)}) async-start(), calls=%async_computation.18 | async-start | bytes 10076160 | tf_op jit(solution)/shard_map/all_gather | solution.py:218
  354.2 525.0 %all-gather.21.cloned.1.call-start = ((), (), s32[]{:S(2)}) async-start(), calls=%async_computation.20 | async-start | bytes 1966080 | tf_op jit(solution)/shard_map/all_gather | solution.py:232
  514.0 374.9 %all-gather.23.cloned.1.call-start = ((), (), s32[]{:S(2)}) async-start(), calls=%async_computation.21 | async-start | bytes 1966080 | tf_op jit(solution)/shard_map/all_gather | solution.py:233
  515.2 489.5 %all-gather.25.cloned.1.call-start = ((), (), s32[]{:S(2)}) async-start(), calls=%async_computation.22 | async-start | bytes 5898240 | tf_op jit(solution)/shard_map/all_gather | solution.py:176
  516.0 515.3 %all-gather.27.cloned.1.call-start = ((), (), s32[]{:S(2)}) async-start(), calls=%async_computation.23 | async-start | bytes 31457280 | tf_op jit(solution)/shard_map/all_gather | solution.py:178
  516.8 638.7 %all-gather.29.cloned.1.call-start = ((), (), s32[]{:S(2)}) async-start(), calls=%async_computation.24 | async-start | bytes 15728640 | tf_op jit(solution)/shard_map/all_gather | solution.py:179
  517.4 1579.0 %reduce-scatter.46.cloned.1.call-start = ((), (), s32[]{:S(2)}) async-start(), calls=%async_computation.39 | async-start | bytes 10076160
  517.8 482.2 %copy-start.99 = (f32[24]{0:T(128)}, f32[24]{0:T(128)S(1)}, u32[]{:S(2)}) copy-start(f32[24]{0:T(128)S(1)} %tanh.10) | copy-start | bytes 292
  1816.1 357.9 %reduce-scatter.18.cloned.1.call-start = ((), (), s32[]{:S(2)}) async-start(), calls=%async_computation.25 | async-start | bytes 10076160 | tf_op jit(solution)/shard_map/reduce_scatter | solution.py:355
  1833.8 424.1 %reduce-scatter.20.cloned.1.call-start = ((), (), s32[]{:S(2)}) async-start(), calls=%async_computation.26 | async-start | bytes 1966080 | tf_op jit(solution)/shard_map/reduce_scatter | solution.py:369
  2047.7 213.3 %reduce-scatter.22.cloned.1.call-start = ((), (), s32[]{:S(2)}) async-start(), calls=%async_computation.27 | async-start | bytes 1966080 | tf_op jit(solution)/shard_map/reduce_scatter | solution.py:372
  2053.6 241.7 %reduce-scatter.30.cloned.1.call-start = ((), (), s32[]{:S(2)}) async-start(), calls=%async_computation.31 | async-start | bytes 5898240 | tf_op jit(solution)/shard_map/reduce_scatter | solution.py:415
  2062.5 234.4 %reduce-scatter.42.cloned.1.call-start = ((), (), s32[]{:S(2)}) async-start(), calls=%async_computation.37 | async-start | bytes 15728640 | tf_op jit(solution)/shard_map/reduce_scatter | solution.py:307
  2082.7 350.9 %reduce-scatter.26.cloned.1.call-start = ((), (), s32[]{:S(2)}) async-start(), calls=%async_computation.29 | async-start | bytes 17694720 | tf_op jit(solution)/shard_map/reduce_scatter | solution.py:409
  2202.3 456.2 %reduce-scatter.38.cloned.1.call-start = ((), (), s32[]{:S(2)}) async-start(), calls=%async_computation.35 | async-start | bytes 31457280 | tf_op jit(solution)/shard_map/reduce_scatter | solution.py:301
  2255.4 628.3 %reduce-scatter.34.cloned.1.call-start = ((), (), s32[]{:S(2)}) async-start(), calls=%async_computation.33 | async-start | bytes 31457280 | tf_op jit(solution)/shard_map/reduce_scatter | solution.py:421
  2295.2 656.7 %reduce-scatter.32.cloned.1.call-start = ((), (), s32[]{:S(2)}) async-start(), calls=%async_computation.32 | async-start | bytes 1327104 | tf_op jit(solution)/shard_map/reduce_scatter | solution.py:432
  2295.8 664.2 %reduce-scatter.44.cloned.1.call-start = ((), (), s32[]{:S(2)}) async-start(), calls=%async_computation.38 | async-start | bytes 3538944 | tf_op jit(solution)/shard_map/reduce_scatter | solution.py:318
  2297.0 707.9 %reduce-scatter.28.cloned.1.call-start = ((), (), s32[]{:S(2)}) async-start(), calls=%async_computation.30 | async-start | bytes 3981312 | tf_op jit(solution)/shard_map/reduce_scatter | solution.py:429
  2433.6 642.0 %reduce-scatter.40.cloned.1.call-start = ((), (), s32[]{:S(2)}) async-start(), calls=%async_computation.36 | async-start | bytes 7077888 | tf_op jit(solution)/shard_map/reduce_scatter | solution.py:315
  2658.5 487.6 %reduce-scatter.36.cloned.1.call-start = ((), (), s32[]{:S(2)}) async-start(), calls=%async_computation.34 | async-start | bytes 7077888 | tf_op jit(solution)/shard_map/reduce_scatter | solution.py:435
  2883.7 391.8 %all-reduce.9.cloned.1.call-start = ((), (), s32[]{:S(2)}) async-start(), calls=%async_computation.40 | async-start | bytes 205824 | tf_op jit(solution)/shard_map/psum | solution.py:451
  2933.9 596.1 %reduce-scatter.24.cloned.1.call-start = ((), (), s32[]{:S(2)}) async-start(), calls=%async_computation.28 | async-start | bytes 25952256 | tf_op jit(solution)/shard_map/reduce_scatter | solution.py:407
  (106 other events, 3333.5 us)
Sparse Core Ops, SparseCore 0:
  9.9 125.2 all-gather.10
  136.9 135.5 all-gather.12
  274.5 227.7 all-gather.18
  504.5 84.8 all-gather.14
  591.1 84.8 all-gather.16
  678.3 30.9 all-gather.20
  711.7 30.9 all-gather.22
  744.6 57.0 all-gather.24
  803.5 227.7 all-gather.26
  1033.0 122.5 all-gather.28
  1816.3 83.6 reduce-scatter.45
  1903.0 83.7 reduce-scatter.17
  2047.8 31.0 reduce-scatter.19
  2082.3 30.9 reduce-scatter.21
  2116.1 57.0 reduce-scatter.29
  2176.2 120.7 reduce-scatter.41
  2299.9 133.6 reduce-scatter.25
  2436.5 221.8 reduce-scatter.37
  2661.8 221.8 reduce-scatter.33
  2885.8 32.7 reduce-scatter.31
  2921.0 38.5 reduce-scatter.43
  2961.9 42.9 reduce-scatter.27
  3007.3 68.3 reduce-scatter.39
  3077.9 68.1 reduce-scatter.35
  3154.2 121.3 all-reduce.8
  3283.5 246.3 reduce-scatter.23
where the time goes:
time: 3570 us; the launch traced here: 3540 us
  waiting for transfers between devices  1750 us (49%)
  matrix products  1130 us (32%)
  local copies, waits for them, and re-layouts  336 us (9%)
  other arithmetic  301 us (8%)
    dot_general x149, matrix products, times_transposed(): lax.dot_general(left, right, (((1,), (1,)), ((), ())), preferred_element_...  468 us
    dot_general x102, matrix products, low_product(): return jnp.dot(left, right, preferred_element_type=jnp.float32)  324 us
    dot_general x101, matrix products, outer_sum(): lax.dot_general(left, right, (((0,), (0,)), ((), ())), preferred_element_...  309 us
    reduce_scatter x1, waiting for transfers between devices, shards(): lax.psum_scatter(grad_ada_weight, ('dp', 'fsdp'), scatter_dimension=0, ti...  254 us
    reduce_scatter x1, waiting for transfers between devices, shards(): lax.psum_scatter(dp_major(grad_text_weight, wide, narrow).astype(jnp.bflo...  225 us
    reduce_scatter x1, waiting for transfers between devices, shards(): lax.psum_scatter(dp_major(grad_gate_up_weight, wide, narrow).astype(jnp.b...  225 us
    all_gather x1, waiting for transfers between devices, shards(): lax.all_gather(text_weight, 'fsdp', axis=0, tiled=True)  147 us
    reduce_scatter x1, waiting for transfers between devices, shards(): lax.psum_scatter(dp_major(grad_qkv_weight, wide, narrow).astype(jnp.bfloa...  137 us
  transfers between devices with their start and end apart: 26, of which 16 were waited for; matrix products, arithmetic and copies ran while one was open for 31% of the time, Pallas kernels for 0%

commit v1 on v0

v1 whole, which is shorter than its diff:
```python
import functools

import jax
import jax.numpy as jnp
from jax import lax
from jax.experimental import pallas as pl
from jax.experimental.pallas import tpu as pltpu
from jax.sharding import Mesh
from jax.sharding import PartitionSpec as P

EPS = 1e-05
HIGHEST_PRECISION = lax.Precision.HIGHEST
MASKED = -1e30
LOG2E = 1.4426950408889634
FIRST_PATCHES = 16 * 12**2
FIRST_MOST = FIRST_PATCHES + 96
QBLOCK = 256
BF16 = jnp.bfloat16
F32 = jnp.float32
VMEM_LIMIT = 60 * 1024 * 1024


def round_up(value, step):
    return -(-value // step) * step


def low_product(left, right):
    return jnp.dot(left, right, preferred_element_type=F32)


def times_transposed(left, right):
    return lax.dot_general(left, right, (((1,), (1,)), ((), ())), preferred_element_type=F32)


def outer_sum(left, right):
    return lax.dot_general(left, right, (((0,), (0,)), ((), ())), preferred_element_type=F32)


def exact_outer(left, right):
    return lax.dot_general(
        left, right, (((0,), (0,)), ((), ())), precision=HIGHEST_PRECISION, preferred_element_type=F32
    )


def exact_transposed(left, right):
    return lax.dot_general(
        left, right, (((1,), (1,)), ((), ())), precision=HIGHEST_PRECISION, preferred_element_type=F32
    )


def row_mean(value):
    return jnp.mean(value, axis=-1, keepdims=True)


def inverse_rms(value):
    return lax.rsqrt(row_mean(value * value) + EPS)


def norm_pull(grad, unit, inverse):
    return (grad - unit * row_mean(grad * unit)) * inverse


def token_layout(image_sizes, position, image_count):
    start = jnp.int32(0)
    image_index = jnp.full(position.shape, image_count, jnp.int32)
    token_row = jnp.zeros(position.shape, jnp.int32)
    token_col = jnp.zeros(position.shape, jnp.int32)
    for i in range(image_count):
        width = image_sizes[i, 1] + 1
        end = start + image_sizes[i, 0] * width
        inside = (position >= start) & (position < end)
        offset = position - start
        image_index = jnp.where(inside, i, image_index)
        token_row = jnp.where(inside, offset // width, token_row)
        token_col = jnp.where(inside, offset % width, token_col)
        start = end
    return image_index, token_row, token_col


def rope_tables(token_row, token_col, head_dim):
    quarter = head_dim // 4
    pair = (jnp.arange(128, dtype=jnp.int32) % head_dim) // 2
    frequency = 10000.0 ** (-(pair % quarter).astype(F32) / quarter)
    place = jnp.where(
        (pair < quarter)[None, :], token_row.astype(F32)[:, None], token_col.astype(F32)[:, None]
    )
    angles = place * frequency[None, :]
    even = (jnp.arange(128, dtype=jnp.int32) % 2 == 0)[None, :]
    return jnp.cos(angles), jnp.where(even, -jnp.sin(angles), jnp.sin(angles))


def swap_pairs(value):
    width = value.shape[1]
    even = lax.broadcasted_iota(jnp.int32, value.shape, 1) % 2 == 0
    return jnp.where(even, pltpu.roll(value, width - 1, 1), pltpu.roll(value, 1, 1))


def wide_table(table, width):
    return jnp.concatenate([table] * (width // table.shape[1]), axis=1)


def pack_columns(columns):
    rows = columns[0].shape[0]
    lane = lax.broadcasted_iota(jnp.int32, (rows, 128), 1)
    packed = jnp.zeros((rows, 128), F32)
    for i, column in enumerate(columns):
        packed = jnp.where(lane == i, column, packed)
    return jnp.transpose(packed)[:8, :]


def as_columns(rows_list):
    width = rows_list[0].shape[1]
    stacked = jnp.concatenate(
        rows_list + [jnp.zeros((128 - len(rows_list), width), F32)], axis=0
    )
    return jnp.transpose(stacked)


def real_lanes(shape, part):
    return lax.broadcasted_iota(jnp.int32, shape, 1) < part


def own_stats(value, part):
    mean = jnp.sum(value, axis=1, keepdims=True) * (1.0 / part)
    centred = value - mean
    if value.shape[1] != part:
        centred = jnp.where(real_lanes(value.shape, part), centred, 0.0)
    return mean, jnp.sum(centred * centred, axis=1, keepdims=True)


def joined_stats(stats_ref, part, slot):
    narrow = stats_ref.shape[0]
    means = [stats_ref[i, 2 * slot : 2 * slot + 1, :] for i in range(narrow)]
    squares = [stats_ref[i, 2 * slot + 1 : 2 * slot + 2, :] for i in range(narrow)]
    mean = functools.reduce(jnp.add, means) * (1.0 / narrow)
    square = functools.reduce(jnp.add, squares)
    square = square + part * functools.reduce(jnp.add, [(m - mean) * (m - mean) for m in means])
    return mean, lax.rsqrt(square * (1.0 / (narrow * part)) + EPS)


def stats_kernel(part, slots, projected_ref, out_ref):
    padded = projected_ref.shape[1] // slots
    columns = []
    for slot in range(slots):
        columns += own_stats(projected_ref[:, slot * padded : (slot + 1) * padded], part)
    out_ref[...] = pack_columns(columns)


def column_stats(projected, part, padded, slots):
    rows = projected.shape[0]
    return pl.pallas_call(
        functools.partial(stats_kernel, part, slots),
        grid=(pl.cdiv(rows, QBLOCK),),
        in_specs=[pl.BlockSpec((QBLOCK, slots * padded), lambda i: (i, 0))],
        out_specs=pl.BlockSpec((8, QBLOCK), lambda i: (0, i)),
        out_shape=jax.ShapeDtypeStruct((8, rows), F32),
        compiler_params=pltpu.CompilerParams(vmem_limit_bytes=VMEM_LIMIT),
        cost_estimate=pl.CostEstimate(flops=10 * rows * slots * padded, bytes_accessed=4 * rows * slots * padded, transcendentals=0),
    )(projected)


def heads_kernel(part, query_scale, projected_ref, stats_ref, cos_ref, sin_ref, gains_ref, shifts_ref, out_ref):
    padded = projected_ref.shape[1] // 3
    cosine = wide_table(cos_ref[...], padded)
    sine = wide_table(sin_ref[...], padded)
    columns = as_columns([*joined_stats(stats_ref, part, 0), *joined_stats(stats_ref, part, 1)])
    for slot in range(3):
        place = slice(slot * padded, (slot + 1) * padded)
        value = projected_ref[:, place]
        if slot < 2:
            value = (value - columns[:, 2 * slot : 2 * slot + 1]) * columns[:, 2 * slot + 1 : 2 * slot + 2]
            value = value * gains_ref[slot : slot + 1, :] + shifts_ref[slot : slot + 1, :]
            value = value * cosine + swap_pairs(value) * sine
            if slot == 0:
                value = value * query_scale
        out_ref[:, place] = value.astype(BF16)


def make_heads(projected, stats, cosine, sine, gains, shifts, part, query_scale):
    rows, triple = projected.shape
    padded = triple // 3
    narrow = stats.shape[0]
    return pl.pallas_call(
        functools.partial(heads_kernel, part, query_scale),
        grid=(pl.cdiv(rows, QBLOCK),),
        in_specs=[
            pl.BlockSpec((QBLOCK, triple), lambda i: (i, 0)),
            pl.BlockSpec((narrow, 8, QBLOCK), lambda i: (0, 0, i)),
            pl.BlockSpec((QBLOCK, 128), lambda i: (i, 0)),
            pl.BlockSpec((QBLOCK, 128), lambda i: (i, 0)),
            pl.BlockSpec((2, padded), lambda i: (0, 0)),
            pl.BlockSpec((2, padded), lambda i: (0, 0)),
        ],
        out_specs=pl.BlockSpec((QBLOCK, triple), lambda i: (i, 0)),
        out_shape=jax.ShapeDtypeStruct((rows, triple), BF16),
        compiler_params=pltpu.CompilerParams(vmem_limit_bytes=VMEM_LIMIT),
        cost_estimate=pl.CostEstimate(flops=40 * rows * triple, bytes_accessed=6 * rows * triple, transcendentals=0),
    )(projected, stats, cosine, sine, gains, shifts)


def turned_back(refs, cosine, sine):
    grad = jnp.concatenate([ref[...].astype(F32) for ref in refs], axis=1)
    return grad * cosine - swap_pairs(grad) * sine


def grad_stats_kernel(rows, part, pairs, *refs):
    dq_refs, dk_refs = refs[:pairs], refs[pairs : 2 * pairs]
    projected_ref, stats_ref, cos_ref, sin_ref, gains_ref, out_ref, sums_ref = refs[2 * pairs :]
    step = pl.program_id(0)
    padded = 128 * pairs
    cosine = wide_table(cos_ref[...], padded)
    sine = wide_table(sin_ref[...], padded)
    height = cos_ref.shape[0]
    inside = step * height + lax.broadcasted_iota(jnp.int32, (height, 1), 0) < rows

    @pl.when(step == 0)
    def _():
        sums_ref[...] = jnp.zeros_like(sums_ref)

    columns = as_columns([*joined_stats(stats_ref, part, 0), *joined_stats(stats_ref, part, 1)])
    packed = []
    for slot, grads in enumerate((dq_refs, dk_refs)):
        grad = jnp.where(inside, turned_back(grads, cosine, sine), 0.0)
        unit = (projected_ref[:, slot * padded : (slot + 1) * padded] - columns[:, 2 * slot : 2 * slot + 1])
        unit = jnp.where(inside, unit * columns[:, 2 * slot + 1 : 2 * slot + 2], 0.0)
        both = grad * unit
        sums_ref[2 * slot : 2 * slot + 1, :] += jnp.sum(both, axis=0, keepdims=True)
        sums_ref[2 * slot + 1 : 2 * slot + 2, :] += jnp.sum(grad, axis=0, keepdims=True)
        gain = gains_ref[slot : slot + 1, :]
        packed.append(jnp.sum(grad * gain, axis=1, keepdims=True))
        packed.append(jnp.sum(both * gain, axis=1, keepdims=True))
    out_ref[...] = pack_columns(packed)


def heads_back_kernel(part, pairs, *refs):
    dq_refs, dk_refs, dv_refs = refs[:pairs], refs[pairs : 2 * pairs], refs[2 * pairs : 3 * pairs]
    projected_ref, stats_ref, totals_ref, cos_ref, sin_ref, gains_ref, out_ref = refs[3 * pairs :]
    padded = 128 * pairs
    narrow = stats_ref.shape[0]
    cosine = wide_table(cos_ref[...], padded)
    sine = wide_table(sin_ref[...], padded)
    means = [
        functools.reduce(jnp.add, [totals_ref[i, j : j + 1, :] for i in range(narrow)]) * (1.0 / (narrow * part))
        for j in range(4)
    ]
    columns = as_columns([*joined_stats(stats_ref, part, 0), *joined_stats(stats_ref, part, 1), *means])
    for slot, grads in enumerate((dq_refs, dk_refs)):
        grad = turned_back(grads, cosine, sine) * gains_ref[slot : slot + 1, :]
        inverse = columns[:, 2 * slot + 1 : 2 * slot + 2]
        unit = (projected_ref[:, slot * padded : (slot + 1) * padded] - columns[:, 2 * slot : 2 * slot + 1]) * inverse
        grad = grad - columns[:, 4 + 2 * slot : 5 + 2 * slot] - unit * columns[:, 5 + 2 * slot : 6 + 2 * slot]
        grad = grad * inverse
        if padded != part:
            grad = jnp.where(real_lanes(grad.shape, part), grad, 0.0)
        out_ref[:, slot * padded : (slot + 1) * padded] = grad.astype(BF16)
    for pair, ref in enumerate(dv_refs):
        out_ref[:, 2 * padded + 128 * pair : 2 * padded + 128 * (pair + 1)] = ref[...]


def heads_back(grads, projected, stats, cosine, sine, gains, part, share):
    rows, triple = projected.shape
    padded = triple // 3
    pairs = padded // 128
    narrow = stats.shape[0]
    pair_spec = pl.BlockSpec((QBLOCK, 128), lambda i: (i, 0))
    two_spec = pl.BlockSpec((QBLOCK, 2 * padded), lambda i: (i, 0))
    stat_spec = pl.BlockSpec((narrow, 8, QBLOCK), lambda i: (0, 0, i))
    gain_spec = pl.BlockSpec((2, padded), lambda i: (0, 0))
    own, sums = pl.pallas_call(
        functools.partial(grad_stats_kernel, rows, part, pairs),
        grid=(pl.cdiv(rows, QBLOCK),),
        in_specs=[pair_spec] * (2 * pairs) + [two_spec, stat_spec, pair_spec, pair_spec, gain_spec],
        out_specs=[
            pl.BlockSpec((8, QBLOCK), lambda i: (0, i)),
            pl.BlockSpec((8, padded), lambda i: (0, 0)),
        ],
        out_shape=[jax.ShapeDtypeStruct((8, rows), F32), jax.ShapeDtypeStruct((8, padded), F32)],
        compiler_params=pltpu.CompilerParams(vmem_limit_bytes=VMEM_LIMIT),
        cost_estimate=pl.CostEstimate(flops=40 * rows * triple, bytes_accessed=5 * rows * triple, transcendentals=0),
    )(*grads[0], *grads[1], projected, stats, cosine, sine, gains)
    totals = share(own)
    out = pl.pallas_call(
        functools.partial(heads_back_kernel, part, pairs),
        grid=(pl.cdiv(rows, QBLOCK),),
        in_specs=[pair_spec] * (3 * pairs) + [two_spec, stat_spec, stat_spec, pair_spec, pair_spec, gain_spec],
        out_specs=pl.BlockSpec((QBLOCK, triple), lambda i: (i, 0)),
        out_shape=jax.ShapeDtypeStruct((rows, triple), BF16),
        compiler_params=pltpu.CompilerParams(vmem_limit_bytes=VMEM_LIMIT),
        cost_estimate=pl.CostEstimate(flops=40 * rows * triple, bytes_accessed=7 * rows * triple, transcendentals=0),
    )(*grads[0], *grads[1], *grads[2], projected, stats, totals, cosine, sine, gains)
    return out, sums


def head_lanes(rows, half, head_dim):
    lane = lax.broadcasted_iota(jnp.int32, (rows, 128), 1)
    return (lane >= half * head_dim) & (lane < (half + 1) * head_dim)


def softmax_product(pieces):
    maximum = functools.reduce(jnp.maximum, [jnp.max(s, axis=1, keepdims=True) for s, _ in pieces])
    total, result = 0.0, 0.0
    for scores, values in pieces:
        weight = jnp.exp2(scores - maximum)
        total = total + jnp.sum(weight, axis=1, keepdims=True)
        result = result + low_product(weight.astype(BF16), values)
    return result * (1.0 / total), maximum + jnp.log2(total)


def attend_kernel(
    head_dim, first, most, caption, image_count,
    gate_ref, q_ref, k_ref, v_ref, tk_ref, tv_ref, column_ref, row_ref,
    mixed_ref, self_ref, cross_ref, stats_ref,
):
    count = q_ref.shape[0]
    halves = 128 // head_dim

    def emit(at, rows, outs):
        lanes = [head_lanes(rows, half, head_dim) for half in range(halves)]
        own, cross, gated = 0.0, 0.0, 0.0
        columns = []
        for half, (own_out, own_total, cross_out, cross_total) in enumerate(outs):
            gate = gate_ref[0, half]
            own = own + jnp.where(lanes[half], own_out, 0.0)
            cross = cross + jnp.where(lanes[half], cross_out, 0.0)
            gated = gated + jnp.where(lanes[half], gate * cross_out, 0.0)
            columns += [own_total, cross_total]
        self_ref[pl.ds(at, rows), :] = own
        cross_ref[pl.ds(at, rows), :] = cross
        mixed_ref[pl.ds(at, rows), :] = (own + gated).astype(BF16)
        lane = lax.broadcasted_iota(jnp.int32, (rows, 128), 1)
        packed = jnp.zeros((rows, 128), F32)
        for i, column in enumerate(columns):
            packed = jnp.where(lane == i, column, packed)
        stats_ref[:, pl.ds(at, rows)] = jnp.transpose(packed)[:8, :]

    def clean(block, carry):
        at = pl.multiple_of(block * QBLOCK, QBLOCK)
        queries = q_ref[pl.ds(at, QBLOCK), :]
        outs = []
        for half in range(halves):
            q = jnp.where(head_lanes(QBLOCK, half, head_dim), queries, jnp.zeros_like(queries))
            bias = jnp.where(row_ref[0:1, first:most] == 0, 0.0, MASKED)
            own_out, own_total = softmax_product([
                (times_transposed(q, k_ref[0:first, :]), v_ref[0:first, :]),
                (times_transposed(q, k_ref[first:most, :]) + bias, v_ref[first:most, :]),
            ])
            cross_out, cross_total = softmax_product(
                [(times_transposed(q, tk_ref[0:caption, :]), tv_ref[0:caption, :])]
            )
            outs.append((own_out, own_total, cross_out, cross_total))
        emit(at, QBLOCK, outs)
        return carry

    lax.fori_loop(0, first // QBLOCK, clean, 0)
    rest = count - first
    queries = q_ref[first:count, :]
    image = column_ref[first:count, :]
    outs = []
    for half in range(halves):
        q = jnp.where(head_lanes(rest, half, head_dim), queries, jnp.zeros_like(queries))
        own_out, own_total = softmax_product([
            (jnp.where(image == row_ref[0:1, :], times_transposed(q, k_ref[...]), MASKED), v_ref[...])
        ])
        scores = times_transposed(q, tk_ref[...])
        owner = lax.broadcasted_iota(jnp.int32, (1, scores.shape[1]), 1) // caption
        scores = jnp.where((image == owner) | (image == image_count), scores, MASKED)
        cross_out, cross_total = softmax_product([(scores, tv_ref[...])])
        outs.append((own_out, own_total, cross_out, cross_total))
    emit(first, rest, outs)


def attention_specs(count, texts, pairs):
    return [
        pl.BlockSpec((1, 128 // 64), lambda p: (p, 0), memory_space=pltpu.SMEM),
        pl.BlockSpec((count, 128), lambda p: (0, p)),
        pl.BlockSpec((count, 128), lambda p: (0, pairs + p)),
        pl.BlockSpec((count, 128), lambda p: (0, 2 * pairs + p)),
        pl.BlockSpec((texts, 128), lambda p: (0, p)),
        pl.BlockSpec((texts, 128), lambda p: (0, pairs + p)),
        pl.BlockSpec((count, 1), lambda p: (0, 0)),
        pl.BlockSpec((1, count), lambda p: (0, 0)),
    ]


def attend(gates, packed, text_packed, column, row, head_dim, image_count):
    count, texts = packed.shape[0], text_packed.shape[0]
    pairs = packed.shape[1] // 384
    halves = 128 // head_dim
    specs = attention_specs(count, texts, pairs)
    specs[0] = pl.BlockSpec((None, 1, halves), lambda p: (p, 0, 0), memory_space=pltpu.SMEM)
    most = min(round_up(FIRST_MOST, 128), count)
    flops = 4 * count * (count + texts) * 128 * pairs * halves
    return pl.pallas_call(
        functools.partial(
            attend_kernel, head_dim, FIRST_PATCHES, most, texts // image_count, image_count
        ),
        grid=(pairs,),
        in_specs=specs,
        out_specs=[
            pl.BlockSpec((count, 128), lambda p: (0, p)),
            pl.BlockSpec((count, 128), lambda p: (0, p)),
            pl.BlockSpec((count, 128), lambda p: (0, p)),
            pl.BlockSpec((None, 8, count), lambda p: (p, 0, 0)),
        ],
        out_shape=[
            jax.ShapeDtypeStruct((count, 128 * pairs), BF16),
            jax.ShapeDtypeStruct((count, 128 * pairs), F32),
            jax.ShapeDtypeStruct((count, 128 * pairs), F32),
            jax.ShapeDtypeStruct((pairs, 8, count), F32),
        ],
        compiler_params=pltpu.CompilerParams(vmem_limit_bytes=VMEM_LIMIT),
        cost_estimate=pl.CostEstimate(flops=flops, bytes_accessed=20 * count * 128 * pairs, transcendentals=count * count * pairs * halves),
    )(gates.reshape(pairs, 1, halves), packed, packed, packed, text_packed, text_packed, column, row)


def gate_lanes(gate_ref, head_dim):
    lane = lax.broadcasted_iota(jnp.int32, (1, 128), 1)
    gates = jnp.zeros((1, 128), F32)
    for half in range(128 // head_dim):
        gates = jnp.where(lane // head_dim == half, gate_ref[0, half], gates)
    return gates


def head_picks(head_dim):
    return (
        lax.broadcasted_iota(jnp.int32, (8, 128), 1) // head_dim
        == lax.broadcasted_iota(jnp.int32, (8, 128), 0)
    ).astype(F32)


def rows_back(head_dim, queries, outs, delta, stats, offset, keys, values, key_sum, value_sum, spans):
    rows = queries.shape[0]
    halves = 128 // head_dim
    zero = jnp.zeros((rows, 128), BF16)
    lanes = [head_lanes(rows, half, head_dim) for half in range(halves)]
    q_heads = [jnp.where(lane, queries, zero) for lane in lanes]
    out_heads = [jnp.where(lane, outs, zero) for lane in lanes]
    q_stack = jnp.concatenate(q_heads, axis=0)
    out_stack = jnp.concatenate(out_heads, axis=0)
    dq = [0.0] * halves
    for low, high, mask in spans:
        key_part = keys[low:high, :]
        value_part = values[low:high, :]
        probs, grads = [], []
        for half in range(halves):
            scores = mask(times_transposed(key_part, q_heads[half]))
            prob = jnp.exp2(scores - stats[2 * half + offset : 2 * half + offset + 1, :])
            dprob = times_transposed(value_part, out_heads[half])
            dscore = (prob * (dprob - delta[half : half + 1, :])).astype(BF16)
            probs.append(prob.astype(BF16))
            grads.append(dscore)
            dq[half] = dq[half] + outer_sum(dscore, key_part)
        value_sum[low:high, :] += low_product(jnp.concatenate(probs, axis=1), out_stack)
        key_sum[low:high, :] += low_product(jnp.concatenate(grads, axis=1), q_stack)
    total = 0.0
    for half in range(halves):
        total = total + jnp.where(lanes[half], dq[half], 0.0)
    return total


def cross_back_kernel(
    head_dim, first, caption, image_count, scale,
    gate_ref, q_ref, tk_ref, tv_ref, row_ref, grad_ref, cross_ref, stats_ref,
    dq_ref, dtk_ref, dtv_ref, gate_grad_ref, dtk_sum, dtv_sum,
):
    count = q_ref.shape[0]
    for total in (dtk_sum, dtv_sum, gate_grad_ref):
        total[...] = jnp.zeros_like(total)
    gates = gate_lanes(gate_ref, head_dim)
    picks = head_picks(head_dim)

    def part(at, rows, spans):
        wide = grad_ref[pl.ds(at, rows), :].astype(F32)
        cross = cross_ref[pl.ds(at, rows), :]
        gate_grad_ref[0:1, :] += jnp.sum(wide * cross, axis=0, keepdims=True)
        gated = (wide * gates).astype(BF16)
        delta = exact_transposed(picks, gated.astype(F32) * cross)
        dq = rows_back(
            head_dim, q_ref[pl.ds(at, rows), :], gated, delta, stats_ref[:, pl.ds(at, rows)], 1,
            tk_ref, tv_ref, dtk_sum, dtv_sum, spans,
        )
        dq_ref[pl.ds(at, rows), :] = (dq * scale).astype(BF16)

    def clean(block, carry):
        part(pl.multiple_of(block * QBLOCK, QBLOCK), QBLOCK, [(0, caption, lambda scores: scores)])
        return carry

    lax.fori_loop(0, first // QBLOCK, clean, 0)
    image = row_ref[0:1, first:count]
    owner = lax.broadcasted_iota(jnp.int32, (tk_ref.shape[0], 1), 0) // caption
    allowed = (owner == image) | (image == image_count)
    part(first, count - first, [(0, tk_ref.shape[0], lambda scores: jnp.where(allowed, scores, MASKED))])
    dtk_ref[...] = (dtk_sum[...] * (1.0 / LOG2E)).astype(BF16)
    dtv_ref[...] = dtv_sum[...].astype(BF16)


def cross_back(gates, packed, text_packed, row, grad, cross, stats, head_dim, image_count, scale):
    count, texts = packed.shape[0], text_packed.shape[0]
    pairs = packed.shape[1] // 384
    halves = 128 // head_dim
    tokens = pl.BlockSpec((count, 128), lambda p: (0, p))
    captions = pl.BlockSpec((texts, 128), lambda p: (0, p))
    flops = 10 * count * texts * 64 * pairs * halves
    return pl.pallas_call(
        functools.partial(cross_back_kernel, head_dim, FIRST_PATCHES, texts // image_count, image_count, scale),
        grid=(pairs,),
        in_specs=[
            pl.BlockSpec((None, 1, halves), lambda p: (p, 0, 0), memory_space=pltpu.SMEM),
            tokens,
            captions,
            pl.BlockSpec((texts, 128), lambda p: (0, pairs + p)),
            pl.BlockSpec((1, count), lambda p: (0, 0)),
            tokens,
            tokens,
            pl.BlockSpec((None, 8, count), lambda p: (p, 0, 0)),
        ],
        out_specs=[tokens, captions, captions, pl.BlockSpec((None, 8, 128), lambda p: (p, 0, 0))],
        out_shape=[jax.ShapeDtypeStruct((count, 128 * pairs), BF16)]
        + [jax.ShapeDtypeStruct((texts, 128 * pairs), BF16)] * 2
        + [jax.ShapeDtypeStruct((pairs, 8, 128), F32)],
        scratch_shapes=[pltpu.VMEM((texts, 128), F32), pltpu.VMEM((texts, 128), F32)],
        compiler_params=pltpu.CompilerParams(vmem_limit_bytes=VMEM_LIMIT),
        cost_estimate=pl.CostEstimate(flops=flops, bytes_accessed=12 * count * 128 * pairs, transcendentals=count * texts * pairs),
    )(gates.reshape(pairs, 1, halves), packed, text_packed, text_packed, row, grad, cross, stats)


def self_back_kernel(
    head_dim, first, most, scale,
    q_ref, k_ref, v_ref, column_ref, row_ref, grad_ref, self_ref, stats_ref, more_ref,
    dq_ref, dk_ref, dv_ref, dk_sum, dv_sum,
):
    count = q_ref.shape[0]
    dk_sum[...] = jnp.zeros_like(dk_sum)
    dv_sum[...] = jnp.zeros_like(dv_sum)
    picks = head_picks(head_dim)

    def part(at, rows, spans):
        grad = grad_ref[pl.ds(at, rows), :]
        delta = exact_transposed(picks, grad.astype(F32) * self_ref[pl.ds(at, rows), :])
        dq = rows_back(
            head_dim, q_ref[pl.ds(at, rows), :], grad, delta, stats_ref[:, pl.ds(at, rows)], 0,
            k_ref, v_ref, dk_sum, dv_sum, spans,
        )
        dq_ref[pl.ds(at, rows), :] = (dq * scale + more_ref[pl.ds(at, rows), :].astype(F32)).astype(BF16)

    def clean(block, carry):
        bias = jnp.where(column_ref[first:most, :] == 0, 0.0, MASKED)
        part(
            pl.multiple_of(block * QBLOCK, QBLOCK), QBLOCK,
            [(0, first, lambda scores: scores), (first, most, lambda scores: scores + bias)],
        )
        return carry

    lax.fori_loop(0, first // QBLOCK, clean, 0)
    image = row_ref[0:1, first:count]
    part(first, count - first, [(0, count, lambda scores: jnp.where(column_ref[...] == image, scores, MASKED))])
    dk_ref[...] = (dk_sum[...] * (1.0 / LOG2E)).astype(BF16)
    dv_ref[...] = dv_sum[...].astype(BF16)


def self_back(pair, packed, column, row, grad, own, stats, more, head_dim, scale):
    count = packed.shape[0]
    pairs = packed.shape[1] // 384
    tokens = pl.BlockSpec((count, 128), lambda i: (0, pair))
    out = pl.BlockSpec((count, 128), lambda i: (0, 0))
    most = min(round_up(FIRST_MOST, 128), count)
    flops = 10 * count * count * 128
    return pl.pallas_call(
        functools.partial(self_back_kernel, head_dim, FIRST_PATCHES, most, scale),
        grid=(1,),
        in_specs=[
            tokens,
            pl.BlockSpec((count, 128), lambda i: (0, pairs + pair)),
            pl.BlockSpec((count, 128), lambda i: (0, 2 * pairs + pair)),
            pl.BlockSpec((count, 1), lambda i: (0, 0)),
            pl.BlockSpec((1, count), lambda i: (0, 0)),
            tokens,
            tokens,
            pl.BlockSpec((None, 8, count), lambda i: (pair, 0, 0)),
            tokens,
        ],
        out_specs=[out, out, out],
        out_shape=[jax.ShapeDtypeStruct((count, 128), BF16)] * 3,
        scratch_shapes=[pltpu.VMEM((count, 128), F32), pltpu.VMEM((count, 128), F32)],
        compiler_params=pltpu.CompilerParams(vmem_limit_bytes=VMEM_LIMIT),
        cost_estimate=pl.CostEstimate(flops=flops, bytes_accessed=30 * count * 128, transcendentals=2 * count * count),
    )(packed, packed, packed, column, row, grad, own, stats, more)


def fsdp_share_kernel(narrow, x_ref, out_ref, send_sem, recv_sem):
    me = lax.axis_index("fsdp")
    barrier = pltpu.get_barrier_semaphore()
    for step in range(1, narrow):
        pl.semaphore_signal(
            barrier, inc=1, device_id={"fsdp": lax.rem(me + step, narrow)}, device_id_type=pl.DeviceIdType.MESH
        )
    pl.semaphore_wait(barrier, narrow - 1)
    copies = []
    for step in range(1, narrow):
        copy = pltpu.make_async_remote_copy(
            src_ref=x_ref,
            dst_ref=out_ref.at[me],
            send_sem=send_sem.at[step],
            recv_sem=recv_sem.at[step],
            device_id={"fsdp": lax.rem(me + step, narrow)},
            device_id_type=pl.DeviceIdType.MESH,
        )
        copy.start()
        copies.append(copy)
    out_ref[me] = x_ref[...]
    for copy in copies:
        copy.wait()


def fsdp_share(value, narrow, collective_id):
    return pl.pallas_call(
        functools.partial(fsdp_share_kernel, narrow),
        in_specs=[pl.BlockSpec(memory_space=pltpu.VMEM)],
        out_specs=pl.BlockSpec(memory_space=pltpu.VMEM),
        out_shape=jax.ShapeDtypeStruct((narrow,) + value.shape, value.dtype),
        scratch_shapes=[pltpu.SemaphoreType.DMA((narrow,)), pltpu.SemaphoreType.DMA((narrow,))],
        compiler_params=pltpu.CompilerParams(collective_id=collective_id, has_side_effects=True),
        cost_estimate=pl.CostEstimate(flops=0, bytes_accessed=8 * narrow * value.size, transcendentals=0),
    )(value)


def finish_kernel(narrow, wide, sum_rows, x_ref, out_ref, first_ref, second_ref, sends, recvs):
    me = lax.axis_index("fsdp")
    group = lax.axis_index("z") * 2 + lax.axis_index("core")
    rows = x_ref.shape[1]
    rest = rows - sum_rows
    barrier = pltpu.get_barrier_semaphore()
    places = [{"fsdp": lax.rem(me + step, narrow)} for step in range(1, narrow)]
    peers = [lax.rem(group + step, wide) for step in range(1, wide)]
    partners = [{"z": peer // 2, "core": peer % 2} for peer in peers]
    for place in places + partners:
        pl.semaphore_signal(barrier, inc=1, device_id=place, device_id_type=pl.DeviceIdType.MESH)
    pl.semaphore_wait(barrier, narrow + wide - 2)

    def send_all(targets, source, target, base):
        copies = []
        for i, place in enumerate(targets):
            copy = pltpu.make_async_remote_copy(
                src_ref=source(i),
                dst_ref=target,
                send_sem=sends.at[base + i],
                recv_sem=recvs.at[base + i],
                device_id=place,
                device_id_type=pl.DeviceIdType.MESH,
            )
            copy.start()
            copies.append(copy)
        return copies

    copies = send_all(places, lambda i: x_ref.at[lax.rem(me + i + 1, narrow)], first_ref.at[me], 0)
    first_ref[me] = x_ref[me]
    for copy in copies:
        copy.wait()
    total = first_ref[0]
    for i in range(1, narrow):
        total = total + first_ref[i]
    second_ref[group] = total
    copies = send_all(partners, lambda i: second_ref.at[group], second_ref.at[group], narrow)
    for copy in copies:
        copy.wait()
    total = second_ref[0, :sum_rows, :]
    for i in range(1, wide):
        total = total + second_ref[i, :sum_rows, :]
    out_ref[me, :sum_rows, :] = total
    for i in range(wide):
        out_ref[me, sum_rows + i * rest : sum_rows + (i + 1) * rest, :] = second_ref[i, sum_rows:, :]
    copies = send_all(places, lambda i: out_ref.at[me], out_ref.at[me], narrow + wide)
    for copy in copies:
        copy.wait()


def finish(summed, kept, narrow, wide, collective_id):
    sum_rows = round_up(-(-summed.size // (128 * narrow)), 8)
    kept_rows = round_up(-(-kept.size // (128 * narrow)), 8)

    def chunked(value, rows):
        return jnp.pad(value, (0, narrow * rows * 128 - value.size)).reshape(narrow, rows, 128)

    joined = jnp.concatenate([chunked(summed, sum_rows), chunked(kept, kept_rows)], axis=1)
    rows = sum_rows + kept_rows
    count = 2 * narrow + wide
    out = pl.pallas_call(
        functools.partial(finish_kernel, narrow, wide, sum_rows),
        in_specs=[pl.BlockSpec(memory_space=pltpu.VMEM)],
        out_specs=pl.BlockSpec(memory_space=pltpu.VMEM),
        out_shape=jax.ShapeDtypeStruct((narrow, sum_rows + wide * kept_rows, 128), F32),
        scratch_shapes=[
            pltpu.VMEM((narrow, rows, 128), F32),
            pltpu.VMEM((wide, rows, 128), F32),
            pltpu.SemaphoreType.DMA((count,)),
            pltpu.SemaphoreType.DMA((count,)),
        ],
        compiler_params=pltpu.CompilerParams(collective_id=collective_id, has_side_effects=True),
    )(joined)
    total = out[:, :sum_rows, :].reshape(-1)[: summed.size]
    groups = out[:, sum_rows:, :].reshape(narrow, wide, kept_rows * 128).transpose(1, 0, 2)
    return total, groups.reshape(wide, -1)[:, : kept.size]


def exchange(blocks, axis):
    return lax.all_to_all(blocks, axis, 0, 0, tiled=True)


def core_swap(value):
    return lax.ppermute(value, "core", [(0, 1), (1, 0)])


def by_core(low, high):
    first = lax.axis_index("core") == 0
    return jnp.where(first, low, high), jnp.where(first, high, low)


def in_core_order(own, other):
    first = lax.axis_index("core") == 0
    return jnp.where(first, own, other), jnp.where(first, other, own)


def reduced(own_left, other_left, right):
    came = core_swap(outer_sum(other_left, right).astype(BF16))
    both = (outer_sum(own_left, right) + came.astype(F32)).astype(BF16)
    part = lax.psum_scatter(both, "fsdp", scatter_dimension=0, tiled=True)
    return lax.psum_scatter(part, "z", scatter_dimension=0, tiled=True).astype(F32)


def device_columns(value, deep, narrow):
    rows, width = value.shape
    block = width // (2 * deep * narrow)
    core = lax.axis_index("core")
    if block % 128 == 0:
        blocks = value.reshape(rows, deep, 2, narrow, block).transpose(2, 0, 3, 1, 4).reshape(2, rows, width // 2)
        return tuple(lax.dynamic_index_in_dim(blocks, i, 0, keepdims=False) for i in (core, 1 - core))
    target = jnp.arange(width, dtype=jnp.int32)
    c, f, z, r = (
        target // (narrow * deep * block), target // (deep * block) % narrow, target // block % deep, target % block,
    )
    c = (c + core) % 2
    source = ((z * 2 + c) * narrow + f) * block + r
    pick = (jnp.arange(width, dtype=jnp.int32)[:, None] == source[None, :]).astype(BF16)
    moved = low_product(value, pick).astype(BF16)
    return moved[:, : width // 2], moved[:, width // 2 :]


def whole_weight(shard):
    rows = shard.shape[0] // 2
    half = lax.dynamic_slice_in_dim(shard, lax.axis_index("core") * rows, rows, 0)
    return lax.all_gather(half, ("fsdp", "core"), axis=0, tiled=True)


def shards(
    tokens,
    cotangent,
    text_states,
    conditioning,
    image_sizes,
    ada_weight,
    ada_bias,
    qkv_weight,
    out_weight,
    text_weight,
    gate_up_weight,
    down_weight,
    norm_gains,
    norm_shifts,
    text_gain,
    head_gate,
):
    model_width = tokens.shape[2]
    head_count = head_gate.shape[0]
    head_dim = model_width // head_count
    image_count = text_states.shape[1]
    caption_local = text_states.shape[2]
    caption_width = text_states.shape[3]
    local_tok = tokens.shape[1]
    deep = lax.axis_size("z")
    narrow = lax.axis_size("fsdp")
    wide = 2 * deep
    me = lax.axis_index("fsdp")
    group_tok = local_tok * narrow
    caption_full = caption_local * narrow
    score_scale = head_dim ** (-0.5)
    text_total = image_count * caption_full
    text_local = image_count * caption_local
    part = model_width // narrow
    part_pad = round_up(part, 128)
    heads_here = head_count // narrow
    pairs = part_pad // 128
    halves = 128 // head_dim

    group_sizes = image_sizes[0]
    position = me * local_tok + jnp.arange(local_tok, dtype=jnp.int32)
    image_index = token_layout(group_sizes, position, image_count)[0]
    key_image, key_row, key_col = token_layout(
        group_sizes, jnp.arange(group_tok, dtype=jnp.int32), image_count
    )
    member = [(image_index == i).astype(F32)[:, None] for i in range(image_count)]
    cosine, sine = rope_tables(key_row, key_col, head_dim)

    cond_low = jax.nn.silu(conditioning[0].astype(F32)).astype(BF16)
    cond_rows = ada_weight.shape[0]
    cond_part = lax.dynamic_slice_in_dim(cond_low, me * cond_rows, cond_rows, 1)
    modulation_part = low_product(cond_part, ada_weight)
    modulation = (
        jnp.sum(fsdp_share(modulation_part.reshape(-1, 128), narrow, 0), axis=0).reshape(modulation_part.shape)
        + ada_bias
    )

    def per_token(index):
        rows = modulation[:, index * model_width : (index + 1) * model_width]
        return functools.reduce(
            jnp.add, [member[i] * rows[i : i + 1, :] for i in range(image_count)]
        )

    def per_image(value):
        return jnp.stack([jnp.sum(member[i] * value, axis=0) for i in range(image_count)])

    token_in = tokens[0].astype(F32)
    token_inverse = inverse_rms(token_in)
    normed_low = (
        token_in * token_inverse * norm_gains[0] * (1.0 + per_token(0))
    ).astype(BF16)
    normed_all = lax.all_gather(normed_low, "fsdp", axis=0, tiled=True)

    def widened(value, slots):
        if part == part_pad:
            return value
        lead = value.shape[:-1]
        value = value.reshape(*lead, slots, part)
        pads = [(0, 0)] * (len(lead) + 1) + [(0, part_pad - part)]
        return jnp.pad(value, pads).reshape(*lead, slots * part_pad)

    def narrowed(value, slots):
        if part == part_pad:
            return value
        lead = value.shape[:-1]
        return value.reshape(*lead, slots, part_pad)[..., :part].reshape(*lead, slots * part)

    def own_columns(value):
        return widened(lax.dynamic_slice_in_dim(value, me * part, part, value.ndim - 1), 1)

    qkv_rows = qkv_weight.shape[0] // 2
    qkv_half = lax.dynamic_slice_in_dim(qkv_weight, lax.axis_index("core") * qkv_rows, qkv_rows, 0)
    qkv_half = exchange(
        qkv_half.reshape(qkv_rows, 3, narrow, part).transpose(2, 0, 1, 3).reshape(narrow, qkv_rows, 3 * part), "fsdp"
    )
    own_qkv = widened(
        jnp.concatenate(in_core_order(qkv_half, core_swap(qkv_half)), axis=1).reshape(model_width, 3 * part), 3
    )

    full_out = whole_weight(out_weight)
    full_gate_up = whole_weight(gate_up_weight)
    full_down = whole_weight(down_weight)

    text_in = text_states[0].astype(F32).reshape(text_local, caption_width)
    text_inverse = inverse_rms(text_in)
    text_low = (text_in * text_inverse * text_gain).astype(BF16)
    text_cols = caption_width // narrow
    text_slice = (
        exchange(text_low.reshape(text_local, narrow, text_cols).transpose(1, 0, 2), "fsdp")
        .reshape(narrow, image_count, caption_local, text_cols)
        .transpose(1, 0, 2, 3)
        .reshape(text_total, text_cols)
    )
    own_text_weight = (
        text_weight.reshape(text_cols, 2, narrow, part).transpose(2, 0, 1, 3).reshape(narrow, text_cols, 2 * part)
    )
    text_partial = jnp.stack([low_product(text_slice, own_text_weight[i]).astype(BF16) for i in range(narrow)])
    text_projected = widened(jnp.sum(exchange(text_partial, "fsdp").astype(F32), axis=0), 2)
    text_parts = fsdp_share(column_stats(text_projected[:, :part_pad], part, part_pad, 1), narrow, 1)
    text_means = text_parts[:, 0, :]
    text_mean = jnp.mean(text_means, axis=0)
    text_square = jnp.sum(text_parts[:, 1, :], axis=0) + part * jnp.sum((text_means - text_mean) ** 2, axis=0)
    text_key_inverse = lax.rsqrt(text_square / model_width + EPS)[:, None]
    text_unit = (text_projected[:, :part_pad] - text_mean[:, None]) * text_key_inverse
    text_gains = own_columns(norm_gains[4])
    text_packed = jnp.concatenate(
        [(text_unit * text_gains).astype(BF16), text_projected[:, part_pad:].astype(BF16)], axis=1
    )

    projected = low_product(normed_all, own_qkv)
    stats_all = fsdp_share(column_stats(projected[:, : 2 * part_pad], part, part_pad, 2), narrow, 2)
    head_gains = own_columns(norm_gains[2:4])
    packed = make_heads(
        projected, stats_all, cosine, sine, head_gains, own_columns(norm_shifts), part, score_scale * LOG2E
    )
    gate_tanh = jnp.tanh(head_gate)
    own_gates = lax.dynamic_slice_in_dim(gate_tanh, me * heads_here, heads_here, 0)
    own_gates = jnp.concatenate([own_gates, jnp.ones((pairs * halves - heads_here,), F32)])
    column = key_image[:, None]
    row = key_image[None, :]
    mixed_heads, self_out, cross_out, stats = attend(
        own_gates, packed, text_packed, column, row, head_dim, image_count
    )
    mixed_low = (
        exchange(narrowed(mixed_heads, 1).reshape(narrow, local_tok, part), "fsdp")
        .transpose(1, 0, 2)
        .reshape(local_tok, model_width)
    )

    branch = low_product(mixed_low, full_out)
    branch_inverse = inverse_rms(branch)
    branch_unit = branch * branch_inverse
    gate_attend = jnp.tanh(per_token(1))
    hidden = token_in + gate_attend * (branch_unit * norm_gains[1])
    hidden_inverse = inverse_rms(hidden)
    hidden_unit = hidden * hidden_inverse
    scale_feed = 1.0 + per_token(2)
    normed_feed_low = (hidden_unit * norm_gains[5] * scale_feed).astype(BF16)
    gate_up = low_product(normed_feed_low, full_gate_up)
    hidden_units = gate_up.shape[1] // 2
    gate_half = gate_up[:, :hidden_units]
    up_half = gate_up[:, hidden_units:]
    sigmoid = jax.nn.sigmoid(gate_half)
    activated_low = (gate_half * sigmoid * up_half).astype(BF16)
    down_out = low_product(activated_low, full_down)
    down_inverse = inverse_rms(down_out)
    down_unit = down_out * down_inverse
    gate_feed = jnp.tanh(per_token(3))
    down_normed = down_unit * norm_gains[6]
    result = (hidden + gate_feed * down_normed).astype(BF16)

    grad_result = cotangent[0].astype(F32)
    grad_down_y = grad_result * gate_feed
    grad_gain_six = jnp.sum(grad_down_y * down_unit, axis=0)
    grad_gate_feed = per_image(grad_result * down_normed * (1.0 - gate_feed * gate_feed))
    grad_down_low = norm_pull(grad_down_y * norm_gains[6], down_unit, down_inverse).astype(BF16)
    grad_down_weight = reduced(*device_columns(activated_low, deep, narrow), grad_down_low)
    grad_activated = times_transposed(grad_down_low, full_down)
    grad_gate_up_low = jnp.concatenate(
        [
            (grad_activated * up_half * sigmoid * (1.0 + gate_half * (1.0 - sigmoid))).astype(BF16),
            (grad_activated * gate_half * sigmoid).astype(BF16),
        ],
        axis=1,
    )
    grad_gate_up_weight = reduced(*device_columns(normed_feed_low, deep, narrow), grad_gate_up_low)
    grad_normed_feed = times_transposed(grad_gate_up_low, full_gate_up)
    grad_feed_y = grad_normed_feed * scale_feed
    grad_gain_five = jnp.sum(grad_feed_y * hidden_unit, axis=0)
    grad_scale_feed = per_image(grad_normed_feed * hidden_unit * norm_gains[5])
    grad_hidden = grad_result + norm_pull(grad_feed_y * norm_gains[5], hidden_unit, hidden_inverse)
    grad_branch_y = grad_hidden * gate_attend
    grad_gain_one = jnp.sum(grad_branch_y * branch_unit, axis=0)
    grad_gate_attend = per_image(
        grad_hidden * branch_unit * norm_gains[1] * (1.0 - gate_attend * gate_attend)
    )
    grad_branch_low = norm_pull(grad_branch_y * norm_gains[1], branch_unit, branch_inverse).astype(BF16)
    grad_out_weight = reduced(*device_columns(mixed_low, deep, narrow), grad_branch_low)
    grad_mixed = times_transposed(grad_branch_low, full_out).astype(BF16)
    grad_heads = widened(
        exchange(grad_mixed.reshape(local_tok, narrow, part).transpose(1, 0, 2), "fsdp").reshape(group_tok, part), 1
    )
    dq_cross, dtk, dtv, gate_sums = cross_back(
        own_gates, packed, text_packed, row, grad_heads, cross_out, stats, head_dim, image_count, score_scale
    )

    grad_text_keys = dtk.astype(F32)
    own_gain_four = jnp.sum(grad_text_keys * text_unit, axis=0)
    grad_text_unit = grad_text_keys * text_gains
    text_sums = jnp.stack([jnp.sum(grad_text_unit, axis=1), jnp.sum(grad_text_unit * text_unit, axis=1)])
    text_sums = jnp.sum(
        fsdp_share(jnp.pad(text_sums, ((0, 6), (0, 0))), narrow, 3), axis=0
    ) * (1.0 / model_width)
    grad_text_key_in = (grad_text_unit - text_sums[0][:, None] - text_unit * text_sums[1][:, None]) * text_key_inverse
    grad_text_own = jnp.concatenate(
        [narrowed(grad_text_key_in.astype(BF16), 1), narrowed(dtv, 1)], axis=1
    )
    grad_text_all = lax.all_gather(grad_text_own, "fsdp", axis=0)
    grad_text_columns = (
        grad_text_all.reshape(narrow, text_total, 2, part).transpose(1, 2, 0, 3).reshape(text_total, 2 * model_width)
    )
    text_half = text_cols // 2
    own_text, other_text = by_core(text_slice[:, :text_half], text_slice[:, text_half:])
    came_text = core_swap(outer_sum(other_text, grad_text_columns).astype(BF16))
    text_part = lax.psum_scatter(
        (outer_sum(own_text, grad_text_columns) + came_text.astype(F32)).astype(BF16),
        "z", scatter_dimension=0, tiled=True,
    )
    everyone = ("z", "core", "fsdp")
    grad_text_weight = lax.ppermute(
        text_part,
        everyone,
        [
            ((z * 2 + c) * narrow + f, f * wide + c * deep + z)
            for z in range(deep) for c in range(2) for f in range(narrow)
        ],
    ).astype(F32)
    grad_text_slice = times_transposed(grad_text_columns, text_weight).astype(BF16)
    grad_text_normed = (
        exchange(
            grad_text_slice.reshape(image_count, narrow, caption_local, text_cols)
            .transpose(1, 0, 2, 3)
            .reshape(narrow, text_local, text_cols),
            "fsdp",
        )
        .transpose(1, 0, 2)
        .reshape(text_local, caption_width)
        .astype(F32)
    )
    text_state_unit = text_in * text_inverse
    grad_text_gain = jnp.sum(grad_text_normed * text_state_unit, axis=0)
    grad_text = (
        norm_pull(grad_text_normed * text_gain, text_state_unit, text_inverse)
        .astype(BF16)
        .reshape(image_count, caption_local, caption_width)
    )

    backs = [
        self_back(pair, packed, column, row, grad_heads, self_out, stats, dq_cross, head_dim, score_scale)
        for pair in range(pairs)
    ]
    own_gate_grad = jnp.sum(gate_sums[:, 0, :].reshape(pairs * halves, head_dim), axis=1)[:heads_here]
    grad_head_gate = lax.dynamic_update_slice_in_dim(
        jnp.zeros((head_count,), F32), own_gate_grad, me * heads_here, 0
    ) * (1.0 - gate_tanh * gate_tanh)
    grad_projected_low, head_sums = heads_back(
        list(zip(*backs)), projected, stats_all, cosine, sine, head_gains, part,
        lambda value: fsdp_share(value, narrow, 4),
    )
    grad_normed = lax.psum_scatter(
        times_transposed(grad_projected_low, own_qkv).astype(BF16), "fsdp", scatter_dimension=0, tiled=True
    ).astype(F32)

    qkv_grad = outer_sum(normed_all, grad_projected_low).astype(BF16).reshape(deep, 2, model_width // wide, 3 * part_pad)
    own_grad, other_grad = by_core(qkv_grad[:, 0], qkv_grad[:, 1])
    own_grad = own_grad.astype(F32) + core_swap(other_grad).astype(F32)
    own_grad = jnp.sum(exchange(own_grad.astype(BF16), "z").astype(F32), axis=0)
    grad_qkv_weight = (
        exchange(narrowed(own_grad.astype(BF16), 3).reshape(narrow, -1, 3 * part), "fsdp")
        .reshape(narrow, -1, 3, part)
        .transpose(1, 2, 0, 3)
        .reshape(-1, 3 * model_width)
        .astype(F32)
    )

    token_unit = token_in * token_inverse
    scale_attend = 1.0 + per_token(0)
    grad_normed_y = grad_normed * scale_attend
    grad_gain_zero = jnp.sum(grad_normed_y * token_unit, axis=0)
    grad_scale_attend = per_image(grad_normed * token_unit * norm_gains[0])
    grad_tokens = (
        grad_hidden + norm_pull(grad_normed_y * norm_gains[0], token_unit, token_inverse)
    ).astype(BF16)

    def placed_columns(value):
        return lax.dynamic_update_slice_in_dim(
            jnp.zeros((model_width,), F32), narrowed(value, 1), me * part, 0
        )

    grad_modulation = jnp.concatenate(
        [grad_scale_attend, grad_gate_attend, grad_scale_feed, grad_gate_feed], axis=1
    )
    group = lax.axis_index("z") * 2 + lax.axis_index("core")
    summed = jnp.concatenate(
        [
            grad_gain_zero,
            grad_gain_one,
            placed_columns(head_sums[0]),
            placed_columns(head_sums[2]),
            placed_columns(own_gain_four),
            grad_gain_five,
            grad_gain_six,
            placed_columns(head_sums[1]),
            placed_columns(head_sums[3]),
            grad_text_gain,
            grad_head_gate,
        ]
    )
    kept = jnp.concatenate(
        [grad_modulation.reshape(-1), jnp.where(me == 0, cond_low.astype(F32), 0.0).reshape(-1)]
    )
    summed, kept = finish(summed, kept, narrow, wide, 5)
    gain_count = norm_gains.size
    shift_end = gain_count + norm_shifts.size
    text_end = shift_end + text_gain.size
    grad_gains = summed[:gain_count].reshape(norm_gains.shape)
    grad_shifts = summed[gain_count:shift_end].reshape(norm_shifts.shape)
    grad_text_gain = summed[shift_end:text_end]
    grad_head_gate = summed[text_end:]
    every_image = wide * image_count
    slots = kept[:, : grad_modulation.size].reshape(every_image, grad_modulation.shape[1])
    cond_slots = kept[:, grad_modulation.size :].reshape(every_image, cond_low.shape[1])
    grad_ada_bias = jnp.sum(slots, axis=0)
    ada_rows = cond_rows // wide
    own_cond = lax.dynamic_slice_in_dim(cond_slots, (group * narrow + me) * ada_rows, ada_rows, 1)
    grad_ada_weight = exact_outer(own_cond, slots)
    return (
        result[None],
        grad_tokens[None],
        grad_text[None],
        grad_ada_weight,
        grad_qkv_weight,
        grad_out_weight,
        grad_text_weight,
        grad_gate_up_weight,
        grad_down_weight,
        grad_ada_bias,
        grad_gains,
        grad_shifts,
        grad_text_gain,
        grad_head_gate,
    )


def solution(mesh):
    wide, narrow = mesh.devices.shape
    fine = Mesh(mesh.devices.reshape(wide // 2, 2, narrow), ("z", "core", "fsdp"))
    groups = ("z", "core")
    every = ("z", "core", "fsdp")
    placed = (
        P(groups, "fsdp", None),
        P(groups, "fsdp", None),
        P(groups, None, "fsdp", None),
        P(groups, None, None),
        P(groups, None, None),
        P("fsdp", None),
        P(),
        P("fsdp", None),
        P("fsdp", None),
        P("fsdp", None),
        P("fsdp", None),
        P("fsdp", None),
        P(),
        P(),
        P(),
        P(),
    )
    return jax.shard_map(
        shards,
        mesh=fine,
        in_specs=placed,
        out_specs=(
            P(groups, "fsdp", None),
            P(groups, "fsdp", None),
            P(groups, None, "fsdp", None),
            P(every, None),
            P(every, None),
            P(every, None),
            P(every, None),
            P(every, None),
            P(every, None),
            P(),
            P(),
            P(),
            P(),
            P(),
        ),
        check_vma=False,
    )
```

time: 3570 us -> 1240 us (0.35)
  waiting for transfers between devices: 1750 us -> 231 us
  matrix products: 1130 us -> 252 us
  Pallas kernels: 0 us -> 407 us
  local copies, waits for them, and re-layouts: 336 us -> 122 us
  other arithmetic: 301 us -> 109 us
  blocking collectives: 0 us -> 65.1 us
    reduce_scatter x14 -> x8, waiting for transfers between devices: 1020 us -> 85.1 us  [the longest x3 55.8 us: reduced(): lax.psum_scatter(part, 'z', scatter_dimension=0, tiled=True).astype(F32)]
    all_gather x10 -> x5, waiting for transfers between devices: 600 us -> 0.06 us  [the longest x3 0.04 us: whole_weight(): return lax.all_gather(half, ('fsdp', 'core'), axis=0, tiled=True)]
    pallas_call x0 -> x16, Pallas kernels: none -> 407 us  [the longest x3 138 us: self_back(): pl.pallas_call(functools.partial(self_back_kernel, head_dim, FIRST_PATCHE...]
    dot_general x149 -> x5, matrix products: 468 us -> 77.3 us  [times_transposed(): lax.dot_general(left, right, (((1,), (1,)), ((), ())), preferred_element_...]
    dot_general x103 -> x11, matrix products: 331 us -> 84 us  [low_product(): return jnp.dot(left, right, preferred_element_type=F32)]
    dot_general x101 -> x9, matrix products: 309 us -> 89 us  [outer_sum(): lax.dot_general(left, right, (((0,), (0,)), ((), ())), preferred_element_...]
    psum x1 -> x0, waiting for transfers between devices: 127 us -> none  [shards(): lax.psum((grad_gains, grad_shifts, grad_text_gain, grad_ada_bias, grad_he...]
    all_to_all x0 -> x6, waiting for transfers between devices: none -> 125 us  [exchange(): return lax.all_to_all(blocks, axis, 0, 0, tiled=True)]
  transfers between devices with their start and end apart: 26 -> 26, of which waited for: 16 -> 10; matrix products, arithmetic and copies ran while one was open for 31% -> 29% of each run, Pallas kernels for 0% -> 29%
where the time goes in v1:
time: 1240 us; the launch traced here: 1230 us
  Pallas kernels  407 us (33%)
  matrix products  252 us (20%)
  waiting for transfers between devices  231 us (19%)
  local copies, waits for them, and re-layouts  122 us (10%)
  other arithmetic  109 us (9%)
  blocking collectives  65.1 us (5%)
  starting transfers between devices  28.6 us (2%)
  between operations  18.5 us (1%)
    pallas_call x3, Pallas kernels, self_back(): pl.pallas_call(functools.partial(self_back_kernel, head_dim, FIRST_PATCHE...  138 us
    all_to_all x6, waiting for transfers between devices, exchange(): return lax.all_to_all(blocks, axis, 0, 0, tiled=True)  125 us
    dot_general x9, matrix products, outer_sum(): lax.dot_general(left, right, (((0,), (0,)), ((), ())), preferred_element_...  89 us
    pallas_call x1, Pallas kernels, attend(): pl.pallas_call(functools.partial(attend_kernel, head_dim, FIRST_PATCHES,...  84.8 us
    dot_general x11, matrix products, low_product(): return jnp.dot(left, right, preferred_element_type=F32)  84 us
    dot_general x5, matrix products, times_transposed(): lax.dot_general(left, right, (((1,), (1,)), ((), ())), preferred_element_...  77.3 us
    all_to_all x2, blocking collectives, exchange(): return lax.all_to_all(blocks, axis, 0, 0, tiled=True)  65.1 us
    reduce_scatter x3, waiting for transfers between devices, reduced(): lax.psum_scatter(part, 'z', scatter_dimension=0, tiled=True).astype(F32)  55.8 us
  transfers between devices with their start and end apart: 26, of which 10 were waited for; matrix products, arithmetic and copies ran while one was open for 29% of the time, Pallas kernels for 29%

profile of v1, /device:TPU:0, one launch (start us, length us, event | category | flops | bytes accessed | tf_op | source)
XLA Modules:
  0.0 1233.4 jit_solution(11724745994176810010)
XLA Ops:
  105.1 30.1 %all-to-all-done = bf16[4,192,1152]{2,1,0:T(8,128)(2,1)S(1)} async-done(((bf16[4,192,1152]{2,1,0:T(8,128)(2,1)}), bf16[4,192,1152]{2,1,0:T(8,128)(2,1)S(1)}, u32[]{:S(2)}, u32[]{:S(2)}) %all-to-all-start) | async-done | bytes 1769504 | tf_op jit(solution)/shard_map/all_to_all | solution.py:706
  146.4 10.5 negate_select_fusion
  160.9 27.0 %all-to-all-done.2 = bf16[4,512,768]{2,1,0:T(8,128)(2,1)} async-done(((bf16[4,512,768]{2,1,0:T(8,128)(2,1)}), bf16[4,512,768]{2,1,0:T(8,128)(2,1)}, u32[]{:S(2)}, u32[]{:S(2)}) %all-to-all-start.2) | async-done | bytes 3145760 | tf_op jit(solution)/shard_map/all_to_all | solution.py:706
  201.9 14.2 %fusion.151.projected_ref.refs_6_.refs_9_ = f32[2624,1152]{1,0:T(8,128)S(1)} fusion(bf16[2624,1536]{1,0:T(8,128)(2,1)} %all-gather.7.cloned.1.call-done, bf16[1536,1152]{1,0:T(8,128)(2,1)} %bitcast.201), kind=kOutput, calls=%fused_computation.341 | convolution fusion | flops 9286189056 | bytes 23691264 | tf_op jit(solution)/shard_map/dot_general | solution.py:28
  224.3 10.0 shard_map.264.x_ref
  234.3 12.8 %shard_map.265.stats_ref.refs_7_.refs_10_ = f32[4,8,2624]{2,1,0:T(8,128)} custom-call(f32[8,2624]{1,0:T(8,128)} %shard_map.264.x_ref), custom_call_target="tpu_custom_call" | custom-call | bytes 671744 | tf_op jit(solution)/shard_map/pallas_call | solution.py:616
  247.0 15.5 %shard_map.266.q_ref.k_ref.v_ref = bf16[2624,1152]{1,0:T(8,128)(2,1)} custom-call(f32[2624,1152]{1,0:T(8,128)} %copy-done.2, f32[4,8,2624]{2,1,0:T(8,128)} %shard_map.265.stats_ref.refs_7_.refs_10_, f32[2624,128]{1,0:T(8,128)} %get-tuple-element.112.cos_ref.refs_8_.refs_12_, f32[2624,128]{1,0:T(8,128)} %get-tuple-element.111.sin_ref.refs_9_.refs_13_, ...), custom_call_target="tpu_custom_call" | custom-call | flops 120913920 | bytes 18137088 | tf_op jit(solution)/shard_map/pallas_call | solution.py:183
  262.6 84.8 %shard_map.269 = (bf16[2624,384]{1,0:T(8,128)(2,1)}, f32[2624,384]{1,0:T(8,128)}, f32[2624,384]{1,0:T(8,128)}, f32[3,8,2624]{2,1,0:T(8,128)}) custom-call(f32[3,1,2]{2,1,0:T(1,128)} %reshape.612.gate_ref, bf16[2624,1152]{1,0:T(8,128)(2,1)} %shard_map.266.q_ref.k_ref.v_ref, bf16[2624,1152]{1,0:T(8,128)(2,1)} %shard_map.266.q_ref.k_ref.v_ref, ...), custom_call_target="tpu_custom_call" | custom-call | flops 25279070208 | bytes 20152320 | tf_op jit(solution)/shard_map/pallas_call | solution.py:393
  347.4 41.6 %all_to_all.40 = bf16[4,656,384]{2,1,0:T(8,128)(2,1)S(1)} all-to-all(bf16[4,656,384]{2,1,0:T(8,128)(2,1)} %bitcast.212), channel_id=1, replica_groups=mesh['z'=4,'core'=2,'fsdp'=4] {'fsdp'}, dimensions={0} | all-to-all | bytes 4030464 | tf_op jit(solution)/shard_map/all_to_all | solution.py:706
  402.2 26.2 %fusion.152 = f32[656,8192]{1,0:T(8,128)} fusion(bf16[656,1536]{1,0:T(8,128)(2,1)S(1)} %multiply_convert_fusion.5, bf16[1536,8192]{1,0:T(8,128)(2,1)} %all-gather.11.cloned.1.call-done), kind=kOutput, calls=%fused_computation.342 | convolution fusion | flops 16508780544 | bytes 48676864 | tf_op jit(solution)/shard_map/dot_general | solution.py:28
  428.4 11.1 multiply_convert_fusion.2
  439.6 13.3 %multiply_reduce_fusion.14 = (f32[656]{0:T(1024)S(1)}, f32[656,1536]{1,0:T(8,128)S(1)}) fusion(bf16[656,4096]{1,0:T(8,128)(2,1)} %multiply_convert_fusion.2, bf16[4096,1536]{1,0:T(8,128)(2,1)} %all-gather.13.cloned.1.call-done), kind=kOutput, calls=%fused_computation.63 | convolution fusion | flops 8256404992 | bytes 21989952 | tf_op jit(solution)/shard_map/dot_general | solution.py:28
  461.8 21.5 %multiply_convert_fusion.1 = (bf16[656,4096]{1,0:T(8,128)(2,1)}, bf16[656,4096]{1,0:T(8,128)(2,1)}) fusion(f32[656,8192]{1,0:T(8,128)} %fusion.152, bf16[656,1536]{1,0:T(8,128)(2,1)S(1)} %get-tuple-element.105, bf16[4096,1536]{1,0:T(8,128)(2,1)} %all-gather.13.cloned.1.call-done), kind=kOutput, calls=%fused_computation.6 | convolution fusion | flops 8289320960 | bytes 46841856 | tf_op jit(solution)/shard_map/dot_general | solution.py:32
  483.3 29.1 %multiply_reduce_fusion.9 = (f32[1536]{0:T(1024)}, f32[656]{0:T(1024)S(1)}, f32[1536]{0:T(1024)}, f32[1536]{0:T(1024)}, f32[656,1536]{1,0:T(8,128)}) fusion(f32[656,1536]{1,0:T(8,128)} %copy-done.6, f32[656]{0:T(1024)S(1)} %add_rsqrt_fusion.1, f32[1536]{0:T(1024)S(1)} %copy-done.46, f32[656]{0:T(1024)S(1)} %get-tuple-element.127, f32[1536]{0:T(1024)S(1)} %copy-done.47, ...), kind=kOutput, calls=%fused_computation.55 | convolution fusion | flops 16547399680 | bytes 44022016 | tf_op jit(solution)/shard_map/dot_general | solution.py:32
  528.8 23.5 %all_to_all.41 = bf16[4,656,384]{2,1,0:T(8,128)(2,1)} all-to-all(bf16[4,656,384]{2,1,0:T(8,128)(2,1)S(1)} %bitcast.198), channel_id=1, replica_groups=mesh['z'=4,'core'=2,'fsdp'=4] {'fsdp'}, dimensions={0} | all-to-all | bytes 4030464 | tf_op jit(solution)/shard_map/all_to_all | solution.py:706
  552.3 35.1 %shard_map.270 = (bf16[2624,384]{1,0:T(8,128)(2,1)}, bf16[512,384]{1,0:T(8,128)(2,1)}, bf16[512,384]{1,0:T(8,128)(2,1)}, f32[3,8,128]{2,1,0:T(8,128)}) custom-call(f32[3,1,2]{2,1,0:T(1,128)} %reshape.612.gate_ref, bf16[2624,1152]{1,0:T(8,128)(2,1)} %shard_map.266.q_ref.k_ref.v_ref, bf16[512,768]{1,0:T(8,128)(2,1)} %pad_maximum_fusion.8.tk_ref.tv_ref, ...), custom_call_target="tpu_custom_call" | custom-call | flops 5158993920 | bytes 12091392 | tf_op jit(solution)/shard_map/pallas_call | solution.py:504
  606.6 12.2 reshape.596
  628.8 10.0 reshape.597
  659.9 17.2 %convolution_convert_fusion = bf16[768,8192]{1,0:T(8,128)(2,1)} fusion(bf16[656,4096]{1,0:T(8,128)(2,1)} %get-tuple-element.100, bf16[656,4096]{1,0:T(8,128)(2,1)} %get-tuple-element.99, bf16[656,1536]{1,0:T(8,128)(2,1)} %fusion.26), kind=kOutput, calls=%fused_computation.1 | convolution fusion | flops 8282177536 | bytes 24338432 | tf_op jit(solution)/shard_map/dot_general | solution.py:36
  696.6 19.6 %add_convert_fusion = bf16[768,8192]{1,0:T(8,128)(2,1)} fusion(bf16[768,8192]{1,0:T(8,128)(2,1)} %collective-permute-done.5, bf16[656,4096]{1,0:T(8,128)(2,1)} %get-tuple-element.100, bf16[656,4096]{1,0:T(8,128)(2,1)} %get-tuple-element.99, bf16[656,1536]{1,0:T(8,128)(2,1)S(1)} %copy-done.77), kind=kOutput, calls=%fused_computation | convolution fusion | flops 8294760448 | bytes 36921344 | tf_op jit(solution)/shard_map/dot_general | solution.py:36
  742.7 46.2 %shard_map.271 = (bf16[2624,128]{1,0:T(8,128)(2,1)}, bf16[2624,128]{1,0:T(8,128)(2,1)}, bf16[2624,128]{1,0:T(8,128)(2,1)}) custom-call(bf16[2624,1152]{1,0:T(8,128)(2,1)} %shard_map.266.q_ref.k_ref.v_ref, bf16[2624,1152]{1,0:T(8,128)(2,1)} %shard_map.266.q_ref.k_ref.v_ref, bf16[2624,1152]{1,0:T(8,128)(2,1)} %shard_map.266.q_ref.k_ref.v_ref, ...), custom_call_target="tpu_custom_call" | custom-call | flops 8813281280 | bytes 10076160 | tf_op jit(solution)/shard_map/pallas_call | solution.py:568
  788.9 46.0 %shard_map.272 = (bf16[2624,128]{1,0:T(8,128)(2,1)}, bf16[2624,128]{1,0:T(8,128)(2,1)}, bf16[2624,128]{1,0:T(8,128)(2,1)}) custom-call(bf16[2624,1152]{1,0:T(8,128)(2,1)} %shard_map.266.q_ref.k_ref.v_ref, bf16[2624,1152]{1,0:T(8,128)(2,1)} %shard_map.266.q_ref.k_ref.v_ref, bf16[2624,1152]{1,0:T(8,128)(2,1)} %shard_map.266.q_ref.k_ref.v_ref, ...), custom_call_target="tpu_custom_call" | custom-call | flops 8813281280 | bytes 10076160 | tf_op jit(solution)/shard_map/pallas_call | solution.py:568
  834.9 46.0 %shard_map.273 = (bf16[2624,128]{1,0:T(8,128)(2,1)}, bf16[2624,128]{1,0:T(8,128)(2,1)}, bf16[2624,128]{1,0:T(8,128)(2,1)}) custom-call(bf16[2624,1152]{1,0:T(8,128)(2,1)} %shard_map.266.q_ref.k_ref.v_ref, bf16[2624,1152]{1,0:T(8,128)(2,1)} %shard_map.266.q_ref.k_ref.v_ref, bf16[2624,1152]{1,0:T(8,128)(2,1)} %shard_map.266.q_ref.k_ref.v_ref, ...), custom_call_target="tpu_custom_call" | custom-call | flops 8813281280 | bytes 10076160 | tf_op jit(solution)/shard_map/pallas_call | solution.py:568
  880.9 15.1 %shard_map.274 = (f32[8,2624]{1,0:T(8,128)}, f32[8,384]{1,0:T(8,128)}) custom-call(bf16[2624,128]{1,0:T(8,128)(2,1)} %get-tuple-element.38.refs_0_, bf16[2624,128]{1,0:T(8,128)(2,1)} %get-tuple-element.39.refs_1_, bf16[2624,128]{1,0:T(8,128)(2,1)} %get-tuple-element.40.refs_2_, bf16[2624,128]{1,0:T(8,128)(2,1)} %get-tuple-element.41.refs_3_, ...), custom_call_target="tpu_custom_call" | custom-call | flops 120913920 | bytes 15114240 | tf_op jit(solution)/shard_map/pallas_call | solution.py:269
  905.2 15.7 %shard_map.276 = bf16[2624,1152]{1,0:T(8,128)(2,1)} custom-call(bf16[2624,128]{1,0:T(8,128)(2,1)} %get-tuple-element.38.refs_0_, bf16[2624,128]{1,0:T(8,128)(2,1)} %get-tuple-element.39.refs_1_, bf16[2624,128]{1,0:T(8,128)(2,1)} %get-tuple-element.40.refs_2_, bf16[2624,128]{1,0:T(8,128)(2,1)} %get-tuple-element.41.refs_3_, ...), custom_call_target="tpu_custom_call" | custom-call | flops 120913920 | bytes 21159936 | tf_op jit(solution)/shard_map/pallas_call | solution.py:282
  921.1 15.6 %convolution_convert_fusion.1 = bf16[2624,1536]{1,0:T(8,128)(2,1)} fusion(bf16[2624,1152]{1,0:T(8,128)(2,1)} %shard_map.276, bf16[1536,1152]{1,0:T(8,128)(2,1)S(1)} %bitcast.202), kind=kOutput, calls=%fused_computation.3 | convolution fusion | flops 9290219520 | bytes 17645568 | tf_op jit(solution)/shard_map/dot_general | solution.py:32
  936.6 15.5 %convolution_convert_fusion.3 = bf16[1536,1152]{1,0:T(8,128)(2,1)S(1)} fusion(bf16[2624,1536]{1,0:T(8,128)(2,1)} %all-gather.7.cloned.1.call-done, bf16[2624,1152]{1,0:T(8,128)(2,1)} %shard_map.276), kind=kOutput, calls=%fused_computation.13 | convolution fusion | flops 9287958528 | bytes 17645568 | tf_op jit(solution)/shard_map/dot_general | solution.py:36
  963.0 46.4 %all-to-all-done.6 = bf16[4,192,1152]{2,1,0:T(8,128)(2,1)S(1)} async-done(((bf16[4,192,1152]{2,1,0:T(8,128)(2,1)}), bf16[4,192,1152]{2,1,0:T(8,128)(2,1)S(1)}, u32[]{:S(2)}, u32[]{:S(2)}) %all-to-all-start.6) | async-done | bytes 1769504 | tf_op jit(solution)/shard_map/all_to_all | solution.py:706
  1036.3 17.7 %all-to-all-done.5 = bf16[4,128,1024]{2,1,0:T(8,128)(2,1)S(1)} async-done(((bf16[4,128,1024]{2,1,0:T(8,128)(2,1)}), bf16[4,128,1024]{2,1,0:T(8,128)(2,1)S(1)}, u32[]{:S(2)}, u32[]{:S(2)}) %all-to-all-start.5) | async-done | bytes 1048608 | tf_op jit(solution)/shard_map/all_to_all | solution.py:706
  1071.1 29.2 %reduce-scatter.9.cloned.1.call-done = bf16[656,1536]{1,0:T(8,128)(2,1)} async-done(((bf16[2624,1536]{1,0:T(8,128)(2,1)}), bf16[656,1536]{1,0:T(8,128)(2,1)}) %reduce-scatter.9.cloned.1.call-update) | async-done | bytes 2015248 | tf_op jit(solution)/shard_map/reduce_scatter | solution.py:1024
  1105.9 47.9 %shard_map.278 = f32[4,296,128]{2,1,0:T(8,128)} custom-call(f32[4,72,128]{2,1,0:T(8,128)} %pad_maximum_fusion.10.x_ref), custom_call_target="tpu_custom_call" | custom-call | tf_op jit(solution)/shard_map/pallas_call | solution.py:687
  1168.3 55.8 %reduce-scatter.19.cloned.1.call-done = bf16[48,8192]{1,0:T(8,128)(2,1)} async-done(((bf16[192,8192]{1,0:T(8,128)(2,1)}), bf16[48,8192]{1,0:T(8,128)(2,1)}) %reduce-scatter.19.cloned.1.call-update) | async-done | bytes 786448 | tf_op jit(solution)/shard_map/reduce_scatter | solution.py:727
  (397 shorter events, 352.6 us)
Async XLA Ops:
  7.2 58.6 %copy-start = (bf16[384,4608]{1,0:T(8,128)(2,1)S(1)}, bf16[384,4608]{1,0:T(8,128)(2,1)}, u32[]{:S(2)}) copy-start(bf16[384,4608]{1,0:T(8,128)(2,1)} %param.23) | copy-start | bytes 10616836
  7.2 194.7 %all-gather.7.cloned.1.call-start = ((), (), s32[]{:S(2)}) async-start(), calls=%async_computation.16 | async-start | bytes 10076160 | tf_op jit(solution)/shard_map/all_gather | solution.py:826
  32.5 364.3 %copy-start.34 = (f32[1536]{0:T(1024)}, f32[1536]{0:T(1024)S(1)}, u32[]{:S(2)}) copy-start(f32[1536]{0:T(1024)S(1)} %get-tuple-element.81) | copy-start | bytes 18436
  33.8 489.1 %copy-start.30 = (f32[656]{0:T(1024)}, f32[656]{0:T(1024)S(1)}, u32[]{:S(2)}) copy-start(f32[656]{0:T(1024)S(1)} %get-tuple-element.126) | copy-start | bytes 7876
  33.8 489.1 %copy-start.32 = (f32[656]{0:T(1024)}, f32[656]{0:T(1024)S(1)}, u32[]{:S(2)}) copy-start(f32[656]{0:T(1024)S(1)} %get-tuple-element.127) | copy-start | bytes 7876
  37.9 352.5 %all-gather.9.cloned.1.call-start = ((), (), s32[]{:S(2)}) async-start(), calls=%async_computation.17 | async-start | bytes 5308416 | tf_op jit(solution)/shard_map/all_gather | solution.py:751
  40.0 362.2 %all-gather.11.cloned.1.call-start = ((), (), s32[]{:S(2)}) async-start(), calls=%async_computation.18 | async-start | bytes 28311552 | tf_op jit(solution)/shard_map/all_gather | solution.py:751
  43.9 395.7 %all-gather.13.cloned.1.call-start = ((), (), s32[]{:S(2)}) async-start(), calls=%async_computation.19 | async-start | bytes 14155776 | tf_op jit(solution)/shard_map/all_gather | solution.py:751
  58.9 31.2 %all-to-all-start.1 = ((bf16[4,128,1024]{2,1,0:T(8,128)(2,1)}), bf16[4,128,1024]{2,1,0:T(8,128)(2,1)}, u32[]{:S(2)}, u32[]{:S(2)}) async-start(bf16[4,128,1024]{2,1,0:T(8,128)(2,1)} %fusion.46), calls=%async_computation.1 | async-start | bytes 2097152 | tf_op jit(solution)/shard_map/all_to_all | solution.py:706
  90.1 45.1 %all-to-all-start = ((bf16[4,192,1152]{2,1,0:T(8,128)(2,1)}), bf16[4,192,1152]{2,1,0:T(8,128)(2,1)S(1)}, u32[]{:S(2)}, u32[]{:S(2)}) async-start(bf16[4,192,1152]{2,1,0:T(8,128)(2,1)} %reshape.574), calls=%async_computation | async-start | bytes 3538944 | tf_op jit(solution)/shard_map/all_to_all | solution.py:706
  135.2 21.7 %collective-permute-start = (bf16[4,192,1152]{2,1,0:T(8,128)(2,1)S(1)}, bf16[4,192,1152]{2,1,0:T(8,128)(2,1)}, u32[]{:S(2)}, u32[]{:S(2)}) collective-permute-start(bf16[4,192,1152]{2,1,0:T(8,128)(2,1)S(1)} %all-to-all-done), channel_id=1, source_target_pairs={{0,4},{4,0},{1,5},{5,1},{2,6},{6,2},{3,7},{7,3},{8,12},{12,8},{9,1... | collective-permute-start | bytes 5308424 | tf_op jit(solution)/shard_map/ppermute | solution.py:710
  140.2 47.6 %all-to-all-start.2 = ((bf16[4,512,768]{2,1,0:T(8,128)(2,1)}), bf16[4,512,768]{2,1,0:T(8,128)(2,1)}, u32[]{:S(2)}, u32[]{:S(2)}) async-start(bf16[4,512,768]{2,1,0:T(8,128)(2,1)} %pad_maximum_fusion.2), calls=%async_computation.2 | async-start | bytes 6291456 | tf_op jit(solution)/shard_map/all_to_all | solution.py:706
  144.9 571.4 %all-gather.15.cloned.1.call-start = ((), (), s32[]{:S(2)}) async-start(), calls=%async_computation.28 | async-start | bytes 3932160 | tf_op jit(solution)/shard_map/all_gather | solution.py:972
  160.9 39.8 %copy-start.58 = (f32[384]{0:T(512)S(1)}, f32[384]{0:T(512)}, u32[]{:S(2)}) copy-start(f32[384]{0:T(512)} %fusion.134) | copy-start | bytes 4612
  600.4 320.6 %reduce-scatter.11.cloned.1.call-start = ((), (), s32[]{:S(2)}) async-start(), calls=%async_computation.21 | async-start | bytes 2949120 | tf_op jit(solution)/shard_map/reduce_scatter | solution.py:726
  623.6 25.0 %collective-permute-start.2 = (bf16[768,1536]{1,0:T(8,128)(2,1)}, bf16[768,1536]{1,0:T(8,128)(2,1)}, u32[]{:S(2)}, u32[]{:S(2)}) collective-permute-start(bf16[768,1536]{1,0:T(8,128)(2,1)} %convolution_convert_fusion.5), channel_id=1, source_target_pairs={{0,4},{4,0},{1,5},{5,1},{2,6},{6,2},{3,7},{7,3},{8,12},{12,8},{9,1... | collective-permute-start | bytes 7077896 | tf_op jit(solution)/shard_map/ppermute | solution.py:710
  648.0 29.2 %collective-permute-start.6 = (bf16[2048,1536]{1,0:T(8,128)(2,1)}, bf16[2048,1536]{1,0:T(8,128)(2,1)}, u32[]{:S(2)}, u32[]{:S(2)}) collective-permute-start(bf16[2048,1536]{1,0:T(8,128)(2,1)} %convolution_convert_fusion.2), channel_id=1, source_target_pairs={{0,4},{4,0},{1,5},{5,1},{2,6},{6,2},{3,7},{7,3},{8,12},{12,8},{9,1... | collective-permute-start | bytes 18874376 | tf_op jit(solution)/shard_map/ppermute | solution.py:710
  653.7 308.7 %reduce-scatter.21.cloned.1.call-start = ((), (), s32[]{:S(2)}) async-start(), calls=%async_computation.26 | async-start | bytes 7864320 | tf_op jit(solution)/shard_map/reduce_scatter | solution.py:726
  677.1 19.5 %collective-permute-start.5 = (bf16[768,8192]{1,0:T(8,128)(2,1)}, bf16[768,8192]{1,0:T(8,128)(2,1)}, u32[]{:S(2)}, u32[]{:S(2)}) collective-permute-start(bf16[768,8192]{1,0:T(8,128)(2,1)} %convolution_convert_fusion), channel_id=1, source_target_pairs={{0,4},{4,0},{1,5},{5,1},{2,6},{6,2},{3,7},{7,3},{8,12},{12,8},{9,1... | collective-permute-start | bytes 37748744 | tf_op jit(solution)/shard_map/ppermute | solution.py:710
  687.0 343.6 %reduce-scatter.17.cloned.1.call-start = ((), (), s32[]{:S(2)}) async-start(), calls=%async_computation.24 | async-start | bytes 15728640 | tf_op jit(solution)/shard_map/reduce_scatter | solution.py:726
  716.2 346.3 %reduce-scatter.15.cloned.1.call-start = ((), (), s32[]{:S(2)}) async-start(), calls=%async_computation.23 | async-start | bytes 3932160 | tf_op jit(solution)/shard_map/reduce_scatter | solution.py:979
  733.3 5.7 collective-permute-start.3
  742.6 325.5 %reduce-scatter.13.cloned.1.call-start = ((), (), s32[]{:S(2)}) async-start(), calls=%async_computation.22 | async-start | bytes 737280 | tf_op jit(solution)/shard_map/reduce_scatter | solution.py:727
  921.0 179.3 %reduce-scatter.9.cloned.1.call-start = ((), (), s32[]{:S(2)}) async-start(), calls=%async_computation.20 | async-start | bytes 10076160 | tf_op jit(solution)/shard_map/reduce_scatter | solution.py:1024
  952.3 3.8 collective-permute-start.1
  957.9 51.5 %all-to-all-start.6 = ((bf16[4,192,1152]{2,1,0:T(8,128)(2,1)}), bf16[4,192,1152]{2,1,0:T(8,128)(2,1)S(1)}, u32[]{:S(2)}, u32[]{:S(2)}) async-start(bf16[4,192,1152]{2,1,0:T(8,128)(2,1)} %fusion.24), calls=%async_computation.7 | async-start | bytes 3538944 | tf_op jit(solution)/shard_map/all_to_all | solution.py:706
  962.4 203.9 %reduce-scatter.23.cloned.1.call-start = ((), (), s32[]{:S(2)}) async-start(), calls=%async_computation.27 | async-start | bytes 1966080 | tf_op jit(solution)/shard_map/reduce_scatter | solution.py:727
  1010.5 16.5 %all-to-all-start.7 = ((bf16[4,48,1152]{2,1,0:T(8,128)(2,1)}), bf16[4,48,1152]{2,1,0:T(8,128)(2,1)S(1)}, u32[]{:S(2)}, u32[]{:S(2)}) async-start(bf16[4,48,1152]{2,1,0:T(8,128)(2,1)} %bitcast.54), calls=%async_computation.8 | async-start | bytes 884736 | tf_op jit(solution)/shard_map/all_to_all | solution.py:706
  1027.0 27.0 %all-to-all-start.5 = ((bf16[4,128,1024]{2,1,0:T(8,128)(2,1)}), bf16[4,128,1024]{2,1,0:T(8,128)(2,1)S(1)}, u32[]{:S(2)}, u32[]{:S(2)}) async-start(bf16[4,128,1024]{2,1,0:T(8,128)(2,1)} %bitcast.41), calls=%async_computation.6 | async-start | bytes 2097152 | tf_op jit(solution)/shard_map/all_to_all | solution.py:706
  1030.6 193.5 %reduce-scatter.19.cloned.1.call-start = ((), (), s32[]{:S(2)}) async-start(), calls=%async_computation.25 | async-start | bytes 3932160 | tf_op jit(solution)/shard_map/reduce_scatter | solution.py:727
  1062.5 7.2 collective-permute-start.4
  1160.8 65.7 %copy-start.1 = (bf16[384,4608]{1,0:T(8,128)(2,1)S(1)}, bf16[384,4608]{1,0:T(8,128)(2,1)}, u32[]{:S(2)}) copy-start(bf16[384,4608]{1,0:T(8,128)(2,1)} %param.23) | copy-start | bytes 10616836
  (74 other events, 1175.2 us)
Sparse Core Ops, SparseCore 0:
  38.1 139.4 all-gather.6
  179.5 38.0 all-gather.8
  219.4 129.0 all-gather.10
  350.8 83.7 all-gather.12
  600.5 43.3 all-gather.14
  653.9 36.7 reduce-scatter.10
  693.7 70.1 reduce-scatter.20
  767.0 120.7 reduce-scatter.16
  890.0 60.2 reduce-scatter.14
  952.5 30.9 reduce-scatter.12
  986.6 113.6 reduce-scatter.8
  1102.5 59.2 reduce-scatter.22
  1164.1 59.8 reduce-scatter.18

commit v2 on v1

--- a/solution.py
+++ b/solution.py
@@ -369,47 +369,37 @@
     emit(first, rest, outs)
 
 
-def attention_specs(count, texts, pairs):
-    return [
-        pl.BlockSpec((1, 128 // 64), lambda p: (p, 0), memory_space=pltpu.SMEM),
-        pl.BlockSpec((count, 128), lambda p: (0, p)),
-        pl.BlockSpec((count, 128), lambda p: (0, pairs + p)),
-        pl.BlockSpec((count, 128), lambda p: (0, 2 * pairs + p)),
-        pl.BlockSpec((texts, 128), lambda p: (0, p)),
-        pl.BlockSpec((texts, 128), lambda p: (0, pairs + p)),
-        pl.BlockSpec((count, 1), lambda p: (0, 0)),
-        pl.BlockSpec((1, count), lambda p: (0, 0)),
-    ]
-
-
-def attend(gates, packed, text_packed, column, row, head_dim, image_count):
+def attend(pair, gates, packed, text_packed, column, row, head_dim, image_count):
     count, texts = packed.shape[0], text_packed.shape[0]
     pairs = packed.shape[1] // 384
     halves = 128 // head_dim
-    specs = attention_specs(count, texts, pairs)
-    specs[0] = pl.BlockSpec((None, 1, halves), lambda p: (p, 0, 0), memory_space=pltpu.SMEM)
+    out = pl.BlockSpec((count, 128), lambda i: (0, 0))
     most = min(round_up(FIRST_MOST, 128), count)
-    flops = 4 * count * (count + texts) * 128 * pairs * halves
+    flops = 4 * count * (count + texts) * 128
     return pl.pallas_call(
         functools.partial(
             attend_kernel, head_dim, FIRST_PATCHES, most, texts // image_count, image_count
         ),
-        grid=(pairs,),
-        in_specs=specs,
-        out_specs=[
-            pl.BlockSpec((count, 128), lambda p: (0, p)),
-            pl.BlockSpec((count, 128), lambda p: (0, p)),
-            pl.BlockSpec((count, 128), lambda p: (0, p)),
-            pl.BlockSpec((None, 8, count), lambda p: (p, 0, 0)),
+        grid=(1,),
+        in_specs=[
+            pl.BlockSpec((None, 1, halves), lambda i: (pair, 0, 0), memory_space=pltpu.SMEM),
+            pl.BlockSpec((count, 128), lambda i: (0, pair)),
+            pl.BlockSpec((count, 128), lambda i: (0, pairs + pair)),
+            pl.BlockSpec((count, 128), lambda i: (0, 2 * pairs + pair)),
+            pl.BlockSpec((texts, 128), lambda i: (0, pair)),
+            pl.BlockSpec((texts, 128), lambda i: (0, pairs + pair)),
+            pl.BlockSpec((count, 1), lambda i: (0, 0)),
+            pl.BlockSpec((1, count), lambda i: (0, 0)),
         ],
+        out_specs=[out, out, out, pl.BlockSpec((8, count), lambda i: (0, 0))],
         out_shape=[
-            jax.ShapeDtypeStruct((count, 128 * pairs), BF16),
-            jax.ShapeDtypeStruct((count, 128 * pairs), F32),
-            jax.ShapeDtypeStruct((count, 128 * pairs), F32),
-            jax.ShapeDtypeStruct((pairs, 8, count), F32),
+            jax.ShapeDtypeStruct((count, 128), BF16),
+            jax.ShapeDtypeStruct((count, 128), F32),
+            jax.ShapeDtypeStruct((count, 128), F32),
+            jax.ShapeDtypeStruct((8, count), F32),
         ],
         compiler_params=pltpu.CompilerParams(vmem_limit_bytes=VMEM_LIMIT),
-        cost_estimate=pl.CostEstimate(flops=flops, bytes_accessed=20 * count * 128 * pairs, transcendentals=count * count * pairs * halves),
+        cost_estimate=pl.CostEstimate(flops=flops, bytes_accessed=20 * count * 128, transcendentals=2 * count * count),
     )(gates.reshape(pairs, 1, halves), packed, packed, packed, text_packed, text_packed, column, row)
 
 
@@ -494,33 +484,37 @@
     dtv_ref[...] = dtv_sum[...].astype(BF16)
 
 
-def cross_back(gates, packed, text_packed, row, grad, cross, stats, head_dim, image_count, scale):
+def cross_back(pair, gates, packed, text_packed, row, grad, cross, stats, head_dim, image_count, scale):
     count, texts = packed.shape[0], text_packed.shape[0]
     pairs = packed.shape[1] // 384
     halves = 128 // head_dim
-    tokens = pl.BlockSpec((count, 128), lambda p: (0, p))
-    captions = pl.BlockSpec((texts, 128), lambda p: (0, p))
-    flops = 10 * count * texts * 64 * pairs * halves
+    tokens = pl.BlockSpec((count, 128), lambda i: (0, pair))
+    own_tokens = pl.BlockSpec((count, 128), lambda i: (0, 0))
+    captions = pl.BlockSpec((texts, 128), lambda i: (0, 0))
+    flops = 10 * count * texts * 128
     return pl.pallas_call(
         functools.partial(cross_back_kernel, head_dim, FIRST_PATCHES, texts // image_count, image_count, scale),
-        grid=(pairs,),
+        grid=(1,),
         in_specs=[
-            pl.BlockSpec((None, 1, halves), lambda p: (p, 0, 0), memory_space=pltpu.SMEM),
+            pl.BlockSpec((None, 1, halves), lambda i: (pair, 0, 0), memory_space=pltpu.SMEM),
             tokens,
-            captions,
-            pl.BlockSpec((texts, 128), lambda p: (0, pairs + p)),
-            pl.BlockSpec((1, count), lambda p: (0, 0)),
-            tokens,
-            tokens,
-            pl.BlockSpec((None, 8, count), lambda p: (p, 0, 0)),
+            pl.BlockSpec((texts, 128), lambda i: (0, pair)),
+            pl.BlockSpec((texts, 128), lambda i: (0, pairs + pair)),
+            pl.BlockSpec((1, count), lambda i: (0, 0)),
+            own_tokens,
+            own_tokens,
+            pl.BlockSpec((8, count), lambda i: (0, 0)),
         ],
-        out_specs=[tokens, captions, captions, pl.BlockSpec((None, 8, 128), lambda p: (p, 0, 0))],
-        out_shape=[jax.ShapeDtypeStruct((count, 128 * pairs), BF16)]
-        + [jax.ShapeDtypeStruct((texts, 128 * pairs), BF16)] * 2
-        + [jax.ShapeDtypeStruct((pairs, 8, 128), F32)],
+        out_specs=[own_tokens, captions, captions, pl.BlockSpec((8, 128), lambda i: (0, 0))],
+        out_shape=[
+            jax.ShapeDtypeStruct((count, 128), BF16),
+            jax.ShapeDtypeStruct((texts, 128), BF16),
+            jax.ShapeDtypeStruct((texts, 128), BF16),
+            jax.ShapeDtypeStruct((8, 128), F32),
+        ],
         scratch_shapes=[pltpu.VMEM((texts, 128), F32), pltpu.VMEM((texts, 128), F32)],
         compiler_params=pltpu.CompilerParams(vmem_limit_bytes=VMEM_LIMIT),
-        cost_estimate=pl.CostEstimate(flops=flops, bytes_accessed=12 * count * 128 * pairs, transcendentals=count * texts * pairs),
+        cost_estimate=pl.CostEstimate(flops=flops, bytes_accessed=12 * count * 128, transcendentals=count * texts),
     )(gates.reshape(pairs, 1, halves), packed, text_packed, text_packed, row, grad, cross, stats)
 
 
@@ -574,10 +568,10 @@
             pl.BlockSpec((count, 128), lambda i: (0, 2 * pairs + pair)),
             pl.BlockSpec((count, 1), lambda i: (0, 0)),
             pl.BlockSpec((1, count), lambda i: (0, 0)),
-            tokens,
-            tokens,
-            pl.BlockSpec((None, 8, count), lambda i: (pair, 0, 0)),
-            tokens,
+            out,
+            out,
+            pl.BlockSpec((8, count), lambda i: (0, 0)),
+            out,
         ],
         out_specs=[out, out, out],
         out_shape=[jax.ShapeDtypeStruct((count, 128), BF16)] * 3,
@@ -720,11 +714,17 @@
     return jnp.where(first, own, other), jnp.where(first, other, own)
 
 
-def reduced(own_left, other_left, right):
+def chip_sum(own_left, other_left, right):
     came = core_swap(outer_sum(other_left, right).astype(BF16))
-    both = (outer_sum(own_left, right) + came.astype(F32)).astype(BF16)
-    part = lax.psum_scatter(both, "fsdp", scatter_dimension=0, tiled=True)
-    return lax.psum_scatter(part, "z", scatter_dimension=0, tiled=True).astype(F32)
+    return (outer_sum(own_left, right) + came.astype(F32)).astype(BF16)
+
+
+def fsdp_sum(both):
+    return lax.psum_scatter(both, "fsdp", scatter_dimension=0, tiled=True)
+
+
+def z_sum(part, deep):
+    return jnp.sum(exchange(part.reshape(deep, -1, part.shape[1]), "z").astype(F32), axis=0)
 
 
 def device_columns(value, deep, narrow):
@@ -732,8 +732,18 @@
     block = width // (2 * deep * narrow)
     core = lax.axis_index("core")
     if block % 128 == 0:
-        blocks = value.reshape(rows, deep, 2, narrow, block).transpose(2, 0, 3, 1, 4).reshape(2, rows, width // 2)
-        return tuple(lax.dynamic_index_in_dim(blocks, i, 0, keepdims=False) for i in (core, 1 - core))
+        low, high = (
+            jnp.concatenate(
+                [
+                    value[:, ((z * 2 + c) * narrow + f) * block : ((z * 2 + c) * narrow + f + 1) * block]
+                    for f in range(narrow)
+                    for z in range(deep)
+                ],
+                axis=1,
+            )
+            for c in range(2)
+        )
+        return by_core(low, high)
     target = jnp.arange(width, dtype=jnp.int32)
     c, f, z, r = (
         target // (narrow * deep * block), target // (deep * block) % narrow, target // block % deep, target % block,
@@ -820,11 +830,7 @@
 
     token_in = tokens[0].astype(F32)
     token_inverse = inverse_rms(token_in)
-    normed_low = (
-        token_in * token_inverse * norm_gains[0] * (1.0 + per_token(0))
-    ).astype(BF16)
-    normed_all = lax.all_gather(normed_low, "fsdp", axis=0, tiled=True)
-
+    tokens_all = lax.all_gather(tokens[0], "fsdp", axis=0, tiled=True)
     def widened(value, slots):
         if part == part_pad:
             return value
@@ -869,6 +875,7 @@
         text_weight.reshape(text_cols, 2, narrow, part).transpose(2, 0, 1, 3).reshape(narrow, text_cols, 2 * part)
     )
     text_partial = jnp.stack([low_product(text_slice, own_text_weight[i]).astype(BF16) for i in range(narrow)])
+    text_partial, tokens_all = lax.optimization_barrier((text_partial, tokens_all))
     text_projected = widened(jnp.sum(exchange(text_partial, "fsdp").astype(F32), axis=0), 2)
     text_parts = fsdp_share(column_stats(text_projected[:, :part_pad], part, part_pad, 1), narrow, 1)
     text_means = text_parts[:, 0, :]
@@ -881,6 +888,13 @@
         [(text_unit * text_gains).astype(BF16), text_projected[:, part_pad:].astype(BF16)], axis=1
     )
 
+    wide_tokens = tokens_all.astype(F32)
+    wide_scale = functools.reduce(
+        jnp.add,
+        [(key_image == i).astype(F32)[:, None] * modulation[i : i + 1, :model_width] for i in range(image_count)],
+    )
+    normed_all = (wide_tokens * inverse_rms(wide_tokens) * norm_gains[0] * (1.0 + wide_scale)).astype(BF16)
+
     projected = low_product(normed_all, own_qkv)
     stats_all = fsdp_share(column_stats(projected[:, : 2 * part_pad], part, part_pad, 2), narrow, 2)
     head_gains = own_columns(norm_gains[2:4])
@@ -892,13 +906,15 @@
     own_gates = jnp.concatenate([own_gates, jnp.ones((pairs * halves - heads_here,), F32)])
     column = key_image[:, None]
     row = key_image[None, :]
-    mixed_heads, self_out, cross_out, stats = attend(
-        own_gates, packed, text_packed, column, row, head_dim, image_count
-    )
+    attended = [
+        attend(pair, own_gates, packed, text_packed, column, row, head_dim, image_count) for pair in range(pairs)
+    ]
+    mixed_pairs = [exchange(one[0].reshape(narrow, local_tok, 128), "fsdp") for one in attended]
+    self_outs = [one[1] for one in attended]
+    cross_outs = [one[2] for one in attended]
+    stats = [one[3] for one in attended]
     mixed_low = (
-        exchange(narrowed(mixed_heads, 1).reshape(narrow, local_tok, part), "fsdp")
-        .transpose(1, 0, 2)
-        .reshape(local_tok, model_width)
+        narrowed(jnp.concatenate(mixed_pairs, axis=2), 1).transpose(1, 0, 2).reshape(local_tok, model_width)
     )
 
     branch = low_product(mixed_low, full_out)
@@ -928,7 +944,7 @@
     grad_gain_six = jnp.sum(grad_down_y * down_unit, axis=0)
     grad_gate_feed = per_image(grad_result * down_normed * (1.0 - gate_feed * gate_feed))
     grad_down_low = norm_pull(grad_down_y * norm_gains[6], down_unit, down_inverse).astype(BF16)
-    grad_down_weight = reduced(*device_columns(activated_low, deep, narrow), grad_down_low)
+    down_both = chip_sum(*device_columns(activated_low, deep, narrow), grad_down_low)
     grad_activated = times_transposed(grad_down_low, full_down)
     grad_gate_up_low = jnp.concatenate(
         [
@@ -937,7 +953,10 @@
         ],
         axis=1,
     )
-    grad_gate_up_weight = reduced(*device_columns(normed_feed_low, deep, narrow), grad_gate_up_low)
+    gate_up_both = chip_sum(*device_columns(normed_feed_low, deep, narrow), grad_gate_up_low)
+    grad_gate_up_low, down_both, gate_up_both = lax.optimization_barrier((grad_gate_up_low, down_both, gate_up_both))
+    down_part = fsdp_sum(down_both)
+    gate_up_part = fsdp_sum(gate_up_both)
     grad_normed_feed = times_transposed(grad_gate_up_low, full_gate_up)
     grad_feed_y = grad_normed_feed * scale_feed
     grad_gain_five = jnp.sum(grad_feed_y * hidden_unit, axis=0)
@@ -949,14 +968,26 @@
         grad_hidden * branch_unit * norm_gains[1] * (1.0 - gate_attend * gate_attend)
     )
     grad_branch_low = norm_pull(grad_branch_y * norm_gains[1], branch_unit, branch_inverse).astype(BF16)
-    grad_out_weight = reduced(*device_columns(mixed_low, deep, narrow), grad_branch_low)
+    out_both = chip_sum(*device_columns(mixed_low, deep, narrow), grad_branch_low)
+    out_part = fsdp_sum(out_both)
     grad_mixed = times_transposed(grad_branch_low, full_out).astype(BF16)
-    grad_heads = widened(
-        exchange(grad_mixed.reshape(local_tok, narrow, part).transpose(1, 0, 2), "fsdp").reshape(group_tok, part), 1
-    )
-    dq_cross, dtk, dtv, gate_sums = cross_back(
-        own_gates, packed, text_packed, row, grad_heads, cross_out, stats, head_dim, image_count, score_scale
-    )
+    grad_blocks = widened(grad_mixed.reshape(local_tok, narrow, part).transpose(1, 0, 2), 1)
+    grad_heads = [
+        exchange(grad_blocks[:, :, 128 * pair : 128 * (pair + 1)], "fsdp").reshape(group_tok, 128)
+        for pair in range(pairs)
+    ]
+    grad_heads[0], down_part = lax.optimization_barrier((grad_heads[0], down_part))
+    crossed = [
+        cross_back(
+            pair, own_gates, packed, text_packed, row, grad_heads[pair], cross_outs[pair], stats[pair],
+            head_dim, image_count, score_scale,
+        )
+        for pair in range(pairs)
+    ]
+    grad_down_weight = z_sum(down_part, deep)
+    dtk = jnp.concatenate([one[1] for one in crossed], axis=1)
+    dtv = jnp.concatenate([one[2] for one in crossed], axis=1)
+    gate_sums = jnp.stack([one[3] for one in crossed])
 
     grad_text_keys = dtk.astype(F32)
     own_gain_four = jnp.sum(grad_text_keys * text_unit, axis=0)
@@ -969,6 +1000,25 @@
     grad_text_own = jnp.concatenate(
         [narrowed(grad_text_key_in.astype(BF16), 1), narrowed(dtv, 1)], axis=1
     )
+    backs = []
+    for pair in range(pairs):
+        backs.append(
+            self_back(
+                pair, packed, column, row, grad_heads[pair], self_outs[pair], stats[pair], crossed[pair][0],
+                head_dim, score_scale,
+            )
+        )
+        if pair == 0:
+            grad_heads[1], gate_up_part, grad_down_weight, first, grad_text_own = lax.optimization_barrier(
+                (grad_heads[1], gate_up_part, grad_down_weight, backs[0][0], grad_text_own)
+            )
+            backs[0] = (first, *backs[0][1:])
+            grad_gate_up_weight = z_sum(gate_up_part, deep)
+        if pair == 1 and pairs > 2:
+            grad_heads[2], out_part, second = lax.optimization_barrier((grad_heads[2], out_part, backs[1][0]))
+            backs[1] = (second, *backs[1][1:])
+    grad_out_weight = z_sum(out_part, deep)
+
     grad_text_all = lax.all_gather(grad_text_own, "fsdp", axis=0)
     grad_text_columns = (
         grad_text_all.reshape(narrow, text_total, 2, part).transpose(1, 2, 0, 3).reshape(text_total, 2 * model_width)
@@ -976,10 +1026,10 @@
     text_half = text_cols // 2
     own_text, other_text = by_core(text_slice[:, :text_half], text_slice[:, text_half:])
     came_text = core_swap(outer_sum(other_text, grad_text_columns).astype(BF16))
-    text_part = lax.psum_scatter(
-        (outer_sum(own_text, grad_text_columns) + came_text.astype(F32)).astype(BF16),
-        "z", scatter_dimension=0, tiled=True,
-    )
+    text_both = (outer_sum(own_text, grad_text_columns) + came_text.astype(F32)).astype(BF16)
+    text_part = jnp.sum(
+        exchange(text_both.reshape(deep, -1, 2 * model_width), "z").astype(F32), axis=0
+    ).astype(BF16)
     everyone = ("z", "core", "fsdp")
     grad_text_weight = lax.ppermute(
         text_part,
@@ -1009,10 +1059,6 @@
         .reshape(image_count, caption_local, caption_width)
     )
 
-    backs = [
-        self_back(pair, packed, column, row, grad_heads, self_out, stats, dq_cross, head_dim, score_scale)
-        for pair in range(pairs)
-    ]
     own_gate_grad = jnp.sum(gate_sums[:, 0, :].reshape(pairs * halves, head_dim), axis=1)[:heads_here]
     grad_head_gate = lax.dynamic_update_slice_in_dim(
         jnp.zeros((head_count,), F32), own_gate_grad, me * heads_here, 0

time: 1240 us -> 1310 us (1.056)
  Pallas kernels: 407 us -> 460 us
  waiting for transfers between devices: 231 us -> 188 us
  starting transfers between devices: 28.6 us -> 59.4 us
  blocking collectives: 65.1 us -> 81.2 us
  other arithmetic: 109 us -> 125 us
    reduce_scatter x7 -> x3, waiting for transfers between devices: 55.8 us -> 0.02 us  [fsdp_sum(): return lax.psum_scatter(both, 'fsdp', scatter_dimension=0, tiled=True)]
    all_to_all x6 -> x13, waiting for transfers between devices: 125 us -> 157 us  [exchange(): return lax.all_to_all(blocks, axis, 0, 0, tiled=True)]
    all_to_all x6 -> x13, starting transfers between devices: 25.1 us -> 56.1 us  [exchange(): return lax.all_to_all(blocks, axis, 0, 0, tiled=True)]
    unnamed x172 -> x233, local copies, waits for them, and re-layouts: 15.8 us -> 46.2 us
    reduce_scatter x1, waiting for transfers between devices: 29.2 us -> 0.01 us  [shards(): lax.psum_scatter(times_transposed(grad_projected_low, own_qkv).astype(BF1...]
    reshape x4 -> x1, local copies, waits for them, and re-layouts: 28.9 us -> 1.5 us  [shards(): narrowed(jnp.concatenate(mixed_pairs, axis=2), 1).transpose(1, 0, 2)]
    pallas_call x1, Pallas kernels: 47.9 us -> 71.8 us  [finish(): pl.pallas_call(functools.partial(finish_kernel, narrow, wide, sum_rows),...]
    all_gather x3, waiting for transfers between devices: 0.04 us -> 20.3 us  [whole_weight(): return lax.all_gather(half, ('fsdp', 'core'), axis=0, tiled=True)]
  transfers between devices with their start and end apart: 26 -> 29, of which waited for: 10 -> 11; matrix products, arithmetic and copies ran while one was open for 29% -> 30% of each run, Pallas kernels for 29% -> 30%
where the time goes in v2:
time: 1310 us; the launch traced here: 1300 us
  Pallas kernels  460 us (35%)
  matrix products  247 us (19%)
  waiting for transfers between devices  188 us (14%)
  other arithmetic  125 us (10%)
  local copies, waits for them, and re-layouts  122 us (9%)
  blocking collectives  81.2 us (6%)
  starting transfers between devices  59.4 us (5%)
  between operations  18.8 us (1%)
    all_to_all x13, waiting for transfers between devices, exchange(): return lax.all_to_all(blocks, axis, 0, 0, tiled=True)  157 us
    pallas_call x3, Pallas kernels, self_back(): pl.pallas_call(functools.partial(self_back_kernel, head_dim, FIRST_PATCHE...  137 us
    dot_general x9, matrix products, outer_sum(): lax.dot_general(left, right, (((0,), (0,)), ((), ())), preferred_element_...  92.2 us
    pallas_call x3, Pallas kernels, attend(): pl.pallas_call(functools.partial(attend_kernel, head_dim, FIRST_PATCHES,...  91.3 us
    all_to_all x3, blocking collectives, exchange(): return lax.all_to_all(blocks, axis, 0, 0, tiled=True)  81.2 us
    dot_general x5, matrix products, times_transposed(): lax.dot_general(left, right, (((1,), (1,)), ((), ())), preferred_element_...  76.2 us
    dot_general x11, matrix products, low_product(): return jnp.dot(left, right, preferred_element_type=F32)  75.6 us
    pallas_call x1, Pallas kernels, finish(): pl.pallas_call(functools.partial(finish_kernel, narrow, wide, sum_rows),...  71.8 us
  transfers between devices with their start and end apart: 29, of which 11 were waited for; matrix products, arithmetic and copies ran while one was open for 30% of the time, Pallas kernels for 30%

profile of v2, /device:TPU:0, one launch (start us, length us, event | category | flops | bytes accessed | tf_op | source)
XLA Modules:
  0.0 1301.6 jit_solution(13778097128207653003)
XLA Ops:
  42.9 24.9 %shard_map.263 = f32[4,96,128]{2,1,0:T(8,128)} custom-call(f32[96,128]{1,0:T(8,128)} %reshape.608.x_ref), custom_call_target="tpu_custom_call" | custom-call | bytes 393216 | tf_op jit(solution)/shard_map/pallas_call | solution.py:610
  174.5 14.5 %shard_map.265.stats_ref.refs_7_.refs_10_ = f32[4,8,2624]{2,1,0:T(8,128)} custom-call(f32[8,2624]{1,0:T(8,128)} %shard_map.264.x_ref), custom_call_target="tpu_custom_call" | custom-call | bytes 671744 | tf_op jit(solution)/shard_map/pallas_call | solution.py:610
  189.1 15.7 %shard_map.266.q_ref.k_ref.v_ref = bf16[2624,1152]{1,0:T(8,128)(2,1)} custom-call(f32[2624,1152]{1,0:T(8,128)} %copy-done.2, f32[4,8,2624]{2,1,0:T(8,128)} %shard_map.265.stats_ref.refs_7_.refs_10_, f32[2624,128]{1,0:T(8,128)} %get-tuple-element.209.cos_ref.refs_8_.refs_12_, f32[2624,128]{1,0:T(8,128)} %get-tuple-element.208.sin_ref.refs_9_.refs_13_, ...), custom_call_target="tpu_custom_call" | custom-call | flops 120913920 | bytes 18137088 | tf_op jit(solution)/shard_map/pallas_call | solution.py:183
  220.4 30.5 %shard_map.269 = (bf16[2624,128]{1,0:T(8,128)(2,1)}, f32[2624,128]{1,0:T(8,128)}, f32[2624,128]{1,0:T(8,128)}, f32[8,2624]{1,0:T(8,128)}) custom-call(f32[3,1,2]{2,1,0:T(1,128)} %reshape.657.gate_ref, bf16[2624,1152]{1,0:T(8,128)(2,1)} %shard_map.266.q_ref.k_ref.v_ref, bf16[2624,1152]{1,0:T(8,128)(2,1)} %shard_map.266.q_ref.k_ref.v_ref, ...), custom_call_target="tpu_custom_call" | custom-call | flops 4213178368 | bytes 6717440 | tf_op jit(solution)/shard_map/pallas_call | solution.py:379
  254.7 30.4 %shard_map.270 = (bf16[2624,128]{1,0:T(8,128)(2,1)}, f32[2624,128]{1,0:T(8,128)}, f32[2624,128]{1,0:T(8,128)}, f32[8,2624]{1,0:T(8,128)}) custom-call(f32[3,1,2]{2,1,0:T(1,128)} %reshape.657.gate_ref, bf16[2624,1152]{1,0:T(8,128)(2,1)} %shard_map.266.q_ref.k_ref.v_ref, bf16[2624,1152]{1,0:T(8,128)(2,1)} %shard_map.266.q_ref.k_ref.v_ref, ...), custom_call_target="tpu_custom_call" | custom-call | flops 4213178368 | bytes 6717440 | tf_op jit(solution)/shard_map/pallas_call | solution.py:379
  289.5 30.4 %shard_map.271 = (bf16[2624,128]{1,0:T(8,128)(2,1)}, f32[2624,128]{1,0:T(8,128)}, f32[2624,128]{1,0:T(8,128)}, f32[8,2624]{1,0:T(8,128)}) custom-call(f32[3,1,2]{2,1,0:T(1,128)} %reshape.657.gate_ref, bf16[2624,1152]{1,0:T(8,128)(2,1)} %shard_map.266.q_ref.k_ref.v_ref, bf16[2624,1152]{1,0:T(8,128)(2,1)} %shard_map.266.q_ref.k_ref.v_ref, ...), custom_call_target="tpu_custom_call" | custom-call | flops 4213178368 | bytes 6717440 | tf_op jit(solution)/shard_map/pallas_call | solution.py:379
  324.3 16.9 %all-to-all-done.5 = bf16[4,656,128]{2,1,0:T(8,128)(2,1)} async-done(((bf16[4,656,128]{2,1,0:T(8,128)(2,1)}), bf16[4,656,128]{2,1,0:T(8,128)(2,1)}, u32[]{:S(2)}, u32[]{:S(2)}) %all-to-all-start.5) | async-done | bytes 671776 | tf_op jit(solution)/shard_map/all_to_all | solution.py:700
  361.3 25.5 %fusion.156 = f32[656,8192]{1,0:T(8,128)} fusion(bf16[656,1536]{1,0:T(8,128)(2,1)S(1)} %multiply_convert_fusion.5, bf16[1536,8192]{1,0:T(8,128)(2,1)} %all-gather.10.cloned.1.call-done), kind=kOutput, calls=%fused_computation.384 | convolution fusion | flops 16508780544 | bytes 48676864 | tf_op jit(solution)/shard_map/dot_general | solution.py:28
  398.9 20.3 %all-gather.12.cloned.1.call-done = bf16[4096,1536]{1,0:T(8,128)(2,1)} async-done(((bf16[512,1536]{1,0:T(8,128)(2,1)}), bf16[4096,1536]{1,0:T(8,128)(2,1)}) %all-gather.12.cloned.1.call-update) | async-done | bytes 12582928 | tf_op jit(solution)/shard_map/all_gather | solution.py:761
  419.2 13.1 %multiply_reduce_fusion.14 = (f32[656]{0:T(1024)S(1)}, f32[656,1536]{1,0:T(8,128)S(1)}) fusion(bf16[656,4096]{1,0:T(8,128)(2,1)} %copy-done.11, bf16[4096,1536]{1,0:T(8,128)(2,1)} %all-gather.12.cloned.1.call-done), kind=kOutput, calls=%fused_computation.66 | convolution fusion | flops 8256404992 | bytes 21989952 | tf_op jit(solution)/shard_map/dot_general | solution.py:28
  438.9 22.7 %multiply_convert_fusion.1 = (bf16[656,4096]{1,0:T(8,128)(2,1)}, bf16[656,4096]{1,0:T(8,128)(2,1)}) fusion(f32[656,8192]{1,0:T(8,128)} %fusion.156, bf16[4096,1536]{1,0:T(8,128)(2,1)} %all-gather.12.cloned.1.call-done, f32[656,1536]{1,0:T(8,128)} %copy-done.21, bf16[1,656,1536]{2,1,0:T(8,128)(2,1)S(1)} %copy-done.19, f32[656]{0:T(1024)S(1)} %broadcast_multiply_fusion.4, ...), kind=kOutput, calls=%fused_computation.12 | convolution fusion | flops 8300404736 | bytes 50901248 | tf_op jit(solution)/shard_map/dot_general | solution.py:32
  461.6 17.4 %convolution_convert_fusion = bf16[768,8192]{1,0:T(8,128)(2,1)} fusion(bf16[656,1536]{1,0:T(8,128)(2,1)} %fusion.26, bf16[656,4096]{1,0:T(8,128)(2,1)} %get-tuple-element.162, bf16[656,4096]{1,0:T(8,128)(2,1)} %get-tuple-element.161), kind=kOutput, calls=%fused_computation.7 | convolution fusion | flops 8282177536 | bytes 24338432 | tf_op jit(solution)/shard_map/dot_general | solution.py:36
  528.6 12.2 add_convert_fusion.1
  540.8 18.2 %add_convert_fusion = bf16[768,8192]{1,0:T(8,128)(2,1)} fusion(bf16[768,8192]{1,0:T(8,128)(2,1)} %collective-permute-done.2, bf16[656,1536]{1,0:T(8,128)(2,1)} %fusion.26, bf16[656,4096]{1,0:T(8,128)(2,1)} %get-tuple-element.162, bf16[656,4096]{1,0:T(8,128)(2,1)} %get-tuple-element.161), kind=kOutput, calls=%fused_computation | convolution fusion | flops 8294760448 | bytes 36921344 | tf_op jit(solution)/shard_map/dot_general | solution.py:36
  566.2 27.8 %multiply_reduce_fusion.9 = (f32[1536]{0:T(1024)}, f32[656]{0:T(1024)S(1)}, f32[1536]{0:T(1024)}, f32[1536]{0:T(1024)}, f32[656,1536]{1,0:T(8,128)}) fusion(f32[656,1536]{1,0:T(8,128)} %copy-done.6, f32[656]{0:T(1024)S(1)} %copy-done.63, f32[1536]{0:T(1024)S(1)} %copy-done.49, f32[656]{0:T(1024)S(1)} %get-tuple-element.224, f32[1536]{0:T(1024)S(1)} %copy-done.51, ...), kind=kOutput, calls=%fused_computation.58 | convolution fusion | flops 16525903872 | bytes 44022016 | tf_op jit(solution)/shard_map/dot_general | solution.py:32
  624.4 14.8 %all_to_all.80 = bf16[4,656,128]{2,1,0:T(8,128)(2,1)} all-to-all(bf16[4,656,128]{2,1,0:T(8,128)(2,1)S(1)} %get-tuple-element.205), channel_id=1, replica_groups=mesh['z'=4,'core'=2,'fsdp'=4] {'fsdp'}, dimensions={0} | all-to-all | bytes 1343488 | tf_op jit(solution)/shard_map/all_to_all | solution.py:700
  639.2 21.3 %all_to_all.81 = bf16[4,656,128]{2,1,0:T(8,128)(2,1)} all-to-all(bf16[4,656,128]{2,1,0:T(8,128)(2,1)S(1)} %get-tuple-element.204), channel_id=1, replica_groups=mesh['z'=4,'core'=2,'fsdp'=4] {'fsdp'}, dimensions={0} | all-to-all | bytes 1343488 | tf_op jit(solution)/shard_map/all_to_all | solution.py:700
  664.1 17.1 %all-to-all-done.9 = bf16[4,656,128]{2,1,0:T(8,128)(2,1)S(1)} async-done(((bf16[4,656,128]{2,1,0:T(8,128)(2,1)}), bf16[4,656,128]{2,1,0:T(8,128)(2,1)S(1)}, u32[]{:S(2)}, u32[]{:S(2)}) %all-to-all-start.9) | async-done | bytes 671776 | tf_op jit(solution)/shard_map/all_to_all | solution.py:700
  685.8 13.7 %shard_map.274 = (bf16[2624,128]{1,0:T(8,128)(2,1)}, bf16[512,128]{1,0:T(8,128)(2,1)}, bf16[512,128]{1,0:T(8,128)(2,1)}, f32[8,128]{1,0:T(8,128)}) custom-call(f32[3,1,2]{2,1,0:T(1,128)} %reshape.657.gate_ref, bf16[2624,1152]{1,0:T(8,128)(2,1)} %shard_map.266.q_ref.k_ref.v_ref, bf16[512,768]{1,0:T(8,128)(2,1)} %pad_maximum_fusion.3.tk_ref.tv_ref, ...), custom_call_target="tpu_custom_call" | custom-call | flops 1719664640 | bytes 4030464 | tf_op jit(solution)/shard_map/pallas_call | solution.py:495
  699.5 13.4 %shard_map.275 = (bf16[2624,128]{1,0:T(8,128)(2,1)}, bf16[512,128]{1,0:T(8,128)(2,1)}, bf16[512,128]{1,0:T(8,128)(2,1)}, f32[8,128]{1,0:T(8,128)}) custom-call(f32[3,1,2]{2,1,0:T(1,128)} %reshape.657.gate_ref, bf16[2624,1152]{1,0:T(8,128)(2,1)} %shard_map.266.q_ref.k_ref.v_ref, bf16[512,768]{1,0:T(8,128)(2,1)} %pad_maximum_fusion.3.tk_ref.tv_ref, ...), custom_call_target="tpu_custom_call" | custom-call | flops 1719664640 | bytes 4030464 | tf_op jit(solution)/shard_map/pallas_call | solution.py:495
  712.9 13.4 %shard_map.272 = (bf16[2624,128]{1,0:T(8,128)(2,1)}, bf16[512,128]{1,0:T(8,128)(2,1)}, bf16[512,128]{1,0:T(8,128)(2,1)}, f32[8,128]{1,0:T(8,128)}) custom-call(f32[3,1,2]{2,1,0:T(1,128)} %reshape.657.gate_ref, bf16[2624,1152]{1,0:T(8,128)(2,1)} %shard_map.266.q_ref.k_ref.v_ref, bf16[512,768]{1,0:T(8,128)(2,1)} %pad_maximum_fusion.3.tk_ref.tv_ref, ...), custom_call_target="tpu_custom_call" | custom-call | flops 1719664640 | bytes 4030464 | tf_op jit(solution)/shard_map/pallas_call | solution.py:495
  740.1 45.7 %shard_map.273 = (bf16[2624,128]{1,0:T(8,128)(2,1)}, bf16[2624,128]{1,0:T(8,128)(2,1)}, bf16[2624,128]{1,0:T(8,128)(2,1)}) custom-call(bf16[2624,1152]{1,0:T(8,128)(2,1)} %shard_map.266.q_ref.k_ref.v_ref, bf16[2624,1152]{1,0:T(8,128)(2,1)} %shard_map.266.q_ref.k_ref.v_ref, bf16[2624,1152]{1,0:T(8,128)(2,1)} %shard_map.266.q_ref.k_ref.v_ref, ...), custom_call_target="tpu_custom_call" | custom-call | flops 8813281280 | bytes 10076160 | tf_op jit(solution)/shard_map/pallas_call | solution.py:562
  787.0 45.8 %shard_map.277 = (bf16[2624,128]{1,0:T(8,128)(2,1)}, bf16[2624,128]{1,0:T(8,128)(2,1)}, bf16[2624,128]{1,0:T(8,128)(2,1)}) custom-call(bf16[2624,1152]{1,0:T(8,128)(2,1)} %shard_map.266.q_ref.k_ref.v_ref, bf16[2624,1152]{1,0:T(8,128)(2,1)} %shard_map.266.q_ref.k_ref.v_ref, bf16[2624,1152]{1,0:T(8,128)(2,1)} %shard_map.266.q_ref.k_ref.v_ref, ...), custom_call_target="tpu_custom_call" | custom-call | flops 8813281280 | bytes 10076160 | tf_op jit(solution)/shard_map/pallas_call | solution.py:562
  832.8 45.8 %shard_map.278 = (bf16[2624,128]{1,0:T(8,128)(2,1)}, bf16[2624,128]{1,0:T(8,128)(2,1)}, bf16[2624,128]{1,0:T(8,128)(2,1)}) custom-call(bf16[2624,1152]{1,0:T(8,128)(2,1)} %shard_map.266.q_ref.k_ref.v_ref, bf16[2624,1152]{1,0:T(8,128)(2,1)} %shard_map.266.q_ref.k_ref.v_ref, bf16[2624,1152]{1,0:T(8,128)(2,1)} %shard_map.266.q_ref.k_ref.v_ref, ...), custom_call_target="tpu_custom_call" | custom-call | flops 8813281280 | bytes 10076160 | tf_op jit(solution)/shard_map/pallas_call | solution.py:562
  878.6 15.2 %shard_map.279 = (f32[8,2624]{1,0:T(8,128)}, f32[8,384]{1,0:T(8,128)}) custom-call(bf16[2624,128]{1,0:T(8,128)(2,1)} %get-tuple-element.89.refs_0_, bf16[2624,128]{1,0:T(8,128)(2,1)} %get-tuple-element.94.refs_1_, bf16[2624,128]{1,0:T(8,128)(2,1)} %get-tuple-element.98.refs_2_, bf16[2624,128]{1,0:T(8,128)(2,1)} %get-tuple-element.99.refs_3_, ...), custom_call_target="tpu_custom_call" | custom-call | flops 120913920 | bytes 15114240 | tf_op jit(solution)/shard_map/pallas_call | solution.py:269
  901.9 15.6 %shard_map.281 = bf16[2624,1152]{1,0:T(8,128)(2,1)} custom-call(bf16[2624,128]{1,0:T(8,128)(2,1)} %get-tuple-element.89.refs_0_, bf16[2624,128]{1,0:T(8,128)(2,1)} %get-tuple-element.94.refs_1_, bf16[2624,128]{1,0:T(8,128)(2,1)} %get-tuple-element.98.refs_2_, bf16[2624,128]{1,0:T(8,128)(2,1)} %get-tuple-element.99.refs_3_, ...), custom_call_target="tpu_custom_call" | custom-call | flops 120913920 | bytes 21159936 | tf_op jit(solution)/shard_map/pallas_call | solution.py:282
  917.5 15.5 %convolution_convert_fusion.3 = bf16[1536,1152]{1,0:T(8,128)(2,1)S(1)} fusion(bf16[2624,1536]{1,0:T(8,128)(2,1)} %copy-done.18, bf16[2624,1152]{1,0:T(8,128)(2,1)} %shard_map.281), kind=kOutput, calls=%fused_computation.19 | convolution fusion | flops 9287958528 | bytes 17645568 | tf_op jit(solution)/shard_map/dot_general | solution.py:36
  935.6 12.7 convolution_convert_fusion.1
  968.7 45.1 %all_to_all.82 = bf16[4,192,1152]{2,1,0:T(8,128)(2,1)} all-to-all(bf16[4,192,1152]{2,1,0:T(8,128)(2,1)} %fusion.25), channel_id=1, replica_groups=mesh['z'=4,'core'=2,'fsdp'=4] {'z'}, dimensions={0} | all-to-all | bytes 3538944 | tf_op jit(solution)/shard_map/all_to_all | solution.py:700
  1041.7 45.7 %all-to-all-done.15 = bf16[4,48,8192]{2,1,0:T(8,128)(2,1)S(1)} async-done(((bf16[4,48,8192]{2,1,0:T(8,128)(2,1)}), bf16[4,48,8192]{2,1,0:T(8,128)(2,1)S(1)}, u32[]{:S(2)}, u32[]{:S(2)}) %all-to-all-start.15) | async-done | bytes 3145760 | tf_op jit(solution)/shard_map/all_to_all | solution.py:700
  1142.0 50.3 %all-to-all-done.14 = bf16[4,128,3072]{2,1,0:T(8,128)(2,1)} async-done(((bf16[4,128,3072]{2,1,0:T(8,128)(2,1)}), bf16[4,128,3072]{2,1,0:T(8,128)(2,1)}, u32[]{:S(2)}, u32[]{:S(2)}) %all-to-all-start.14) | async-done | bytes 3145760 | tf_op jit(solution)/shard_map/all_to_all | solution.py:700
  1208.0 71.8 %shard_map.282 = f32[4,296,128]{2,1,0:T(8,128)} custom-call(f32[4,72,128]{2,1,0:T(8,128)} %pad_maximum_fusion.6.x_ref), custom_call_target="tpu_custom_call" | custom-call | tf_op jit(solution)/shard_map/pallas_call | solution.py:681
  (470 shorter events, 459.5 us)
Async XLA Ops:
  7.2 122.6 %all-gather.14.cloned.1.call-start = ((), (), s32[]{:S(2)}) async-start(), calls=%async_computation.27 | async-start | bytes 10076160 | tf_op jit(solution)/shard_map/all_gather | solution.py:833
  7.9 336.1 %all-gather.8.cloned.1.call-start = ((), (), s32[]{:S(2)}) async-start(), calls=%async_computation.20 | async-start | bytes 5308416 | tf_op jit(solution)/shard_map/all_gather | solution.py:761
  10.2 351.1 %all-gather.10.cloned.1.call-start = ((), (), s32[]{:S(2)}) async-start(), calls=%async_computation.21 | async-start | bytes 28311552 | tf_op jit(solution)/shard_map/all_gather | solution.py:761
  25.0 60.0 %all-to-all-start.1 = ((bf16[4,192,1152]{2,1,0:T(8,128)(2,1)}), bf16[4,192,1152]{2,1,0:T(8,128)(2,1)}, u32[]{:S(2)}, u32[]{:S(2)}) async-start(bf16[4,192,1152]{2,1,0:T(8,128)(2,1)} %reshape.615), calls=%async_computation.1 | async-start | bytes 3538944 | tf_op jit(solution)/shard_map/all_to_all | solution.py:700
  30.3 388.9 %all-gather.12.cloned.1.call-start = ((), (), s32[]{:S(2)}) async-start(), calls=%async_computation.22 | async-start | bytes 14155776 | tf_op jit(solution)/shard_map/all_gather | solution.py:761
  69.5 70.1 %copy-start.40 = (f32[1536]{0:T(1024)}, f32[1536]{0:T(1024)S(1)}, u32[]{:S(2)}) copy-start(f32[1536]{0:T(1024)S(1)} %get-tuple-element.141) | copy-start | bytes 18436
  69.5 281.2 %copy-start.32 = (f32[1536]{0:T(1024)}, f32[1536]{0:T(1024)S(1)}, u32[]{:S(2)}) copy-start(f32[1536]{0:T(1024)S(1)} %get-tuple-element.143) | copy-start | bytes 18436
  85.0 29.5 %all-to-all-start = ((bf16[4,128,1024]{2,1,0:T(8,128)(2,1)}), bf16[4,128,1024]{2,1,0:T(8,128)(2,1)S(1)}, u32[]{:S(2)}, u32[]{:S(2)}) async-start(bf16[4,128,1024]{2,1,0:T(8,128)(2,1)} %fusion.45), calls=%async_computation | async-start | bytes 2097152 | tf_op jit(solution)/shard_map/all_to_all | solution.py:700
  105.6 17.0 %collective-permute-start = (bf16[4,192,1152]{2,1,0:T(8,128)(2,1)}, bf16[4,192,1152]{2,1,0:T(8,128)(2,1)}, u32[]{:S(2)}, u32[]{:S(2)}) collective-permute-start(bf16[4,192,1152]{2,1,0:T(8,128)(2,1)} %all-to-all-done.1), channel_id=1, source_target_pairs={{0,4},{4,0},{1,5},{5,1},{2,6},{6,2},{3,7},{7,3},{8,12},{12,8},{9,1... | collective-permute-start | bytes 5308424 | tf_op jit(solution)/shard_map/ppermute | solution.py:704
  129.8 75.0 %all-to-all-start.2 = ((bf16[4,512,768]{2,1,0:T(8,128)(2,1)}), bf16[4,512,768]{2,1,0:T(8,128)(2,1)}, u32[]{:S(2)}, u32[]{:S(2)}) async-start(bf16[4,512,768]{2,1,0:T(8,128)(2,1)} %pad_maximum_fusion.2), calls=%async_computation.2 | async-start | bytes 6291456 | tf_op jit(solution)/shard_map/all_to_all | solution.py:700
  250.9 34.2 %all-to-all-start.3 = ((bf16[4,656,128]{2,1,0:T(8,128)(2,1)}), bf16[4,656,128]{2,1,0:T(8,128)(2,1)S(1)}, u32[]{:S(2)}, u32[]{:S(2)}) async-start(bf16[4,656,128]{2,1,0:T(8,128)(2,1)} %bitcast.246), calls=%async_computation.3 | async-start | bytes 1343488 | tf_op jit(solution)/shard_map/all_to_all | solution.py:700
  285.1 34.8 %all-to-all-start.4 = ((bf16[4,656,128]{2,1,0:T(8,128)(2,1)}), bf16[4,656,128]{2,1,0:T(8,128)(2,1)S(1)}, u32[]{:S(2)}, u32[]{:S(2)}) async-start(bf16[4,656,128]{2,1,0:T(8,128)(2,1)} %bitcast.245), calls=%async_computation.4 | async-start | bytes 1343488 | tf_op jit(solution)/shard_map/all_to_all | solution.py:700
  319.9 21.2 %all-to-all-start.5 = ((bf16[4,656,128]{2,1,0:T(8,128)(2,1)}), bf16[4,656,128]{2,1,0:T(8,128)(2,1)}, u32[]{:S(2)}, u32[]{:S(2)}) async-start(bf16[4,656,128]{2,1,0:T(8,128)(2,1)} %bitcast.244), calls=%async_computation.5 | async-start | bytes 1343488 | tf_op jit(solution)/shard_map/all_to_all | solution.py:700
  324.1 340.0 %reduce-scatter.7.cloned.1.call-start = ((), (), s32[]{:S(2)}) async-start(), calls=%async_computation.24 | async-start | bytes 7864320 | tf_op jit(solution)/shard_map/reduce_scatter | solution.py:723
  479.0 61.9 %collective-permute-start.2 = (bf16[768,8192]{1,0:T(8,128)(2,1)}, bf16[768,8192]{1,0:T(8,128)(2,1)}, u32[]{:S(2)}, u32[]{:S(2)}) collective-permute-start(bf16[768,8192]{1,0:T(8,128)(2,1)} %convolution_convert_fusion), channel_id=1, source_target_pairs={{0,4},{4,0},{1,5},{5,1},{2,6},{6,2},{3,7},{7,3},{8,12},{12,8},{9,1... | collective-permute-start | bytes 37748744 | tf_op jit(solution)/shard_map/ppermute | solution.py:704
  518.1 10.5 collective-permute-start.1
  559.1 227.9 %reduce-scatter.5.cloned.1.call-start = ((), (), s32[]{:S(2)}) async-start(), calls=%async_computation.23 | async-start | bytes 15728640 | tf_op jit(solution)/shard_map/reduce_scatter | solution.py:723
  559.7 273.1 %reduce-scatter.9.cloned.1.call-start = ((), (), s32[]{:S(2)}) async-start(), calls=%async_computation.25 | async-start | bytes 2949120 | tf_op jit(solution)/shard_map/reduce_scatter | solution.py:723
  608.9 4.6 collective-permute-start.3
  660.5 20.7 %all-to-all-start.9 = ((bf16[4,656,128]{2,1,0:T(8,128)(2,1)}), bf16[4,656,128]{2,1,0:T(8,128)(2,1)S(1)}, u32[]{:S(2)}, u32[]{:S(2)}) async-start(bf16[4,656,128]{2,1,0:T(8,128)(2,1)} %get-tuple-element.203), calls=%async_computation.11 | async-start | bytes 1343488 | tf_op jit(solution)/shard_map/all_to_all | solution.py:700
  681.2 104.6 %all-to-all-start.8 = ((bf16[4,128,1536]{2,1,0:T(8,128)(2,1)}), bf16[4,128,1536]{2,1,0:T(8,128)(2,1)S(1)}, u32[]{:S(2)}, u32[]{:S(2)}) async-start(bf16[4,128,1536]{2,1,0:T(8,128)(2,1)} %bitcast.236), calls=%async_computation.10 | async-start | bytes 3145728 | tf_op jit(solution)/shard_map/all_to_all | solution.py:700
  685.8 331.8 %all-gather.16.cloned.1.call-start = ((), (), s32[]{:S(2)}) async-start(), calls=%async_computation.28 | async-start | bytes 3932160 | tf_op jit(solution)/shard_map/all_gather | solution.py:1022
  787.0 415.5 %reduce-scatter.11.cloned.1.call-start = ((), (), s32[]{:S(2)}) async-start(), calls=%async_computation.26 | async-start | bytes 10076160 | tf_op jit(solution)/shard_map/reduce_scatter | solution.py:1070
  934.4 18.9 %collective-permute-start.4 = (bf16[4,192,1152]{2,1,0:T(8,128)(2,1)}, bf16[4,192,1152]{2,1,0:T(8,128)(2,1)}, u32[]{:S(2)}, u32[]{:S(2)}) collective-permute-start(bf16[4,192,1152]{2,1,0:T(8,128)(2,1)} %fusion.37), channel_id=1, source_target_pairs={{0,4},{4,0},{1,5},{5,1},{2,6},{6,2},{3,7},{7,3},{8,12},{12,8},{9,1... | collective-permute-start | bytes 5308424 | tf_op jit(solution)/shard_map/ppermute | solution.py:704
  948.3 20.4 %all-to-all-start.13 = ((bf16[4,48,1536]{2,1,0:T(8,128)(2,1)}), bf16[4,48,1536]{2,1,0:T(8,128)(2,1)}, u32[]{:S(2)}, u32[]{:S(2)}) async-start(bf16[4,48,1536]{2,1,0:T(8,128)(2,1)} %bitcast.247), calls=%async_computation.17 | async-start | bytes 1179648 | tf_op jit(solution)/shard_map/all_to_all | solution.py:700
  1013.8 73.6 %all-to-all-start.15 = ((bf16[4,48,8192]{2,1,0:T(8,128)(2,1)}), bf16[4,48,8192]{2,1,0:T(8,128)(2,1)S(1)}, u32[]{:S(2)}, u32[]{:S(2)}) async-start(bf16[4,48,8192]{2,1,0:T(8,128)(2,1)} %bitcast.215), calls=%async_computation.19 | async-start | bytes 6291456 | tf_op jit(solution)/shard_map/all_to_all | solution.py:700
  1039.1 65.2 %collective-permute-start.5 = (bf16[512,3072]{1,0:T(8,128)(2,1)}, bf16[512,3072]{1,0:T(8,128)(2,1)}, u32[]{:S(2)}, u32[]{:S(2)}) collective-permute-start(bf16[512,3072]{1,0:T(8,128)(2,1)} %convolution_convert_fusion.4), channel_id=1, source_target_pairs={{0,4},{4,0},{1,5},{5,1},{2,6},{6,2},{3,7},{7,3},{8,12},{12,8},{9,1... | collective-permute-start | bytes 9437192 | tf_op jit(solution)/shard_map/ppermute | solution.py:704
  1087.4 12.6 all-to-all-start.12
  1100.0 17.4 %all-to-all-start.10 = ((bf16[4,128,1024]{2,1,0:T(8,128)(2,1)}), bf16[4,128,1024]{2,1,0:T(8,128)(2,1)}, u32[]{:S(2)}, u32[]{:S(2)}) async-start(bf16[4,128,1024]{2,1,0:T(8,128)(2,1)} %bitcast.212), calls=%async_computation.14 | async-start | bytes 2097152 | tf_op jit(solution)/shard_map/all_to_all | solution.py:700
  1117.5 74.9 %all-to-all-start.14 = ((bf16[4,128,3072]{2,1,0:T(8,128)(2,1)}), bf16[4,128,3072]{2,1,0:T(8,128)(2,1)}, u32[]{:S(2)}, u32[]{:S(2)}) async-start(bf16[4,128,3072]{2,1,0:T(8,128)(2,1)} %bitcast.216), calls=%async_computation.18 | async-start | bytes 6291456 | tf_op jit(solution)/shard_map/all_to_all | solution.py:700
  1122.2 80.3 %copy-start.61 = (f32[656]{0:T(1024)}, f32[656]{0:T(1024)S(1)}, u32[]{:S(2)}) copy-start(f32[656]{0:T(1024)S(1)} %add_rsqrt_fusion.1) | copy-start | bytes 7876
  1195.9 5.3 collective-permute-start.6
  (100 other events, 1439.4 us)
Sparse Core Ops, SparseCore 0:
  9.9 119.8 all-gather.13
  131.7 63.4 all-gather.7
  197.1 147.6 all-gather.9
  347.0 72.1 all-gather.11
  559.2 70.2 reduce-scatter.6
  632.4 135.4 reduce-scatter.4
  771.0 37.3 reduce-scatter.8
  810.8 43.9 all-gather.15
  948.5 84.0 reduce-scatter.10

commit v3 on v2

--- a/solution.py
+++ b/solution.py
@@ -501,7 +501,7 @@
             pl.BlockSpec((texts, 128), lambda i: (0, pair)),
             pl.BlockSpec((texts, 128), lambda i: (0, pairs + pair)),
             pl.BlockSpec((1, count), lambda i: (0, 0)),
-            own_tokens,
+            tokens,
             own_tokens,
             pl.BlockSpec((8, count), lambda i: (0, 0)),
         ],
@@ -568,7 +568,7 @@
             pl.BlockSpec((count, 128), lambda i: (0, 2 * pairs + pair)),
             pl.BlockSpec((count, 1), lambda i: (0, 0)),
             pl.BlockSpec((1, count), lambda i: (0, 0)),
-            out,
+            tokens,
             out,
             pl.BlockSpec((8, count), lambda i: (0, 0)),
             out,
@@ -579,6 +579,43 @@
         compiler_params=pltpu.CompilerParams(vmem_limit_bytes=VMEM_LIMIT),
         cost_estimate=pl.CostEstimate(flops=flops, bytes_accessed=30 * count * 128, transcendentals=2 * count * count),
     )(packed, packed, packed, column, row, grad, own, stats, more)
+
+
+def swiglu_kernel(core_ref, gate_ref, up_ref, out_ref, moved_ref):
+    gate = gate_ref[...]
+    value = (gate * up_ref[...] / (1.0 + jnp.exp(-gate))).astype(BF16)
+    out_ref[...] = value
+    moved_ref[...] = value
+
+
+def swiglu(gate_up, core, deep, narrow):
+    rows, double = gate_up.shape
+    width = double // 2
+    blocks = 2 * deep * narrow
+    block = width // blocks
+
+    def moved_place(i, core_ref):
+        z, c, f = i // (2 * narrow), (i // narrow) % 2, i % narrow
+        return (0, ((c + core_ref[0]) % 2) * (deep * narrow) + f * deep + z)
+
+    return pl.pallas_call(
+        swiglu_kernel,
+        grid_spec=pltpu.PrefetchScalarGridSpec(
+            num_scalar_prefetch=1,
+            grid=(blocks,),
+            in_specs=[
+                pl.BlockSpec((rows, block), lambda i, core_ref: (0, i)),
+                pl.BlockSpec((rows, block), lambda i, core_ref: (0, blocks + i)),
+            ],
+            out_specs=[
+                pl.BlockSpec((rows, block), lambda i, core_ref: (0, i)),
+                pl.BlockSpec((rows, block), moved_place),
+            ],
+        ),
+        out_shape=[jax.ShapeDtypeStruct((rows, width), BF16)] * 2,
+        compiler_params=pltpu.CompilerParams(vmem_limit_bytes=VMEM_LIMIT),
+        cost_estimate=pl.CostEstimate(flops=6 * rows * width, bytes_accessed=12 * rows * width, transcendentals=rows * width),
+    )(core.reshape(1), gate_up, gate_up)
 
 
 def fsdp_share_kernel(narrow, x_ref, out_ref, send_sem, recv_sem):
@@ -723,27 +760,36 @@
     return lax.psum_scatter(both, "fsdp", scatter_dimension=0, tiled=True)
 
 
-def z_sum(part, deep):
-    return jnp.sum(exchange(part.reshape(deep, -1, part.shape[1]), "z").astype(F32), axis=0)
+def z_sum(blocks, deep):
+    me = lax.axis_index("z")
+    total = lax.dynamic_index_in_dim(blocks, me, 0, keepdims=False).astype(F32)
+    for step in range(1, deep):
+        sent = lax.dynamic_index_in_dim(blocks, me ^ step, 0, keepdims=False)
+        total = total + lax.ppermute(sent, "z", [(i, i ^ step) for i in range(deep)]).astype(F32)
+    return total
+
+
+def to_all(block, narrow):
+    return [
+        lax.ppermute(block, "fsdp", [(i, i ^ step) for i in range(narrow)]) for step in range(1, narrow)
+    ]
+
+
+def in_order(block, came):
+    me = lax.axis_index("fsdp")
+    narrow = len(came) + 1
+    result = lax.dynamic_update_slice_in_dim(
+        jnp.zeros((narrow,) + block.shape, block.dtype), block[None], me, 0
+    )
+    for step in range(1, narrow):
+        result = lax.dynamic_update_slice_in_dim(result, came[step - 1][None], me ^ step, 0)
+    return result
 
 
 def device_columns(value, deep, narrow):
     rows, width = value.shape
     block = width // (2 * deep * narrow)
     core = lax.axis_index("core")
-    if block % 128 == 0:
-        low, high = (
-            jnp.concatenate(
-                [
-                    value[:, ((z * 2 + c) * narrow + f) * block : ((z * 2 + c) * narrow + f + 1) * block]
-                    for f in range(narrow)
-                    for z in range(deep)
-                ],
-                axis=1,
-            )
-            for c in range(2)
-        )
-        return by_core(low, high)
     target = jnp.arange(width, dtype=jnp.int32)
     c, f, z, r = (
         target // (narrow * deep * block), target // (deep * block) % narrow, target // block % deep, target % block,
@@ -877,7 +923,7 @@
     text_partial = jnp.stack([low_product(text_slice, own_text_weight[i]).astype(BF16) for i in range(narrow)])
     text_partial, tokens_all = lax.optimization_barrier((text_partial, tokens_all))
     text_projected = widened(jnp.sum(exchange(text_partial, "fsdp").astype(F32), axis=0), 2)
-    text_parts = fsdp_share(column_stats(text_projected[:, :part_pad], part, part_pad, 1), narrow, 1)
+    text_parts = fsdp_share(column_stats(text_projected, part, part_pad, 1), narrow, 1)
     text_means = text_parts[:, 0, :]
     text_mean = jnp.mean(text_means, axis=0)
     text_square = jnp.sum(text_parts[:, 1, :], axis=0) + part * jnp.sum((text_means - text_mean) ** 2, axis=0)
@@ -896,7 +942,7 @@
     normed_all = (wide_tokens * inverse_rms(wide_tokens) * norm_gains[0] * (1.0 + wide_scale)).astype(BF16)
 
     projected = low_product(normed_all, own_qkv)
-    stats_all = fsdp_share(column_stats(projected[:, : 2 * part_pad], part, part_pad, 2), narrow, 2)
+    stats_all = fsdp_share(column_stats(projected, part, part_pad, 2), narrow, 2)
     head_gains = own_columns(norm_gains[2:4])
     packed = make_heads(
         projected, stats_all, cosine, sine, head_gains, own_columns(norm_shifts), part, score_scale * LOG2E
@@ -931,7 +977,12 @@
     gate_half = gate_up[:, :hidden_units]
     up_half = gate_up[:, hidden_units:]
     sigmoid = jax.nn.sigmoid(gate_half)
-    activated_low = (gate_half * sigmoid * up_half).astype(BF16)
+    if hidden_units // (wide * narrow) % 128 == 0:
+        activated_low, moved = swiglu(gate_up, lax.axis_index("core"), deep, narrow)
+        down_columns = (moved[:, : hidden_units // 2], moved[:, hidden_units // 2 :])
+    else:
+        activated_low = (gate_half * sigmoid * up_half).astype(BF16)
+        down_columns = device_columns(activated_low, deep, narrow)
     down_out = low_product(activated_low, full_down)
     down_inverse = inverse_rms(down_out)
     down_unit = down_out * down_inverse
@@ -944,7 +995,6 @@
     grad_gain_six = jnp.sum(grad_down_y * down_unit, axis=0)
     grad_gate_feed = per_image(grad_result * down_normed * (1.0 - gate_feed * gate_feed))
     grad_down_low = norm_pull(grad_down_y * norm_gains[6], down_unit, down_inverse).astype(BF16)
-    down_both = chip_sum(*device_columns(activated_low, deep, narrow), grad_down_low)
     grad_activated = times_transposed(grad_down_low, full_down)
     grad_gate_up_low = jnp.concatenate(
         [
@@ -953,10 +1003,6 @@
         ],
         axis=1,
     )
-    gate_up_both = chip_sum(*device_columns(normed_feed_low, deep, narrow), grad_gate_up_low)
-    grad_gate_up_low, down_both, gate_up_both = lax.optimization_barrier((grad_gate_up_low, down_both, gate_up_both))
-    down_part = fsdp_sum(down_both)
-    gate_up_part = fsdp_sum(gate_up_both)
     grad_normed_feed = times_transposed(grad_gate_up_low, full_gate_up)
     grad_feed_y = grad_normed_feed * scale_feed
     grad_gain_five = jnp.sum(grad_feed_y * hidden_unit, axis=0)
@@ -968,23 +1014,29 @@
         grad_hidden * branch_unit * norm_gains[1] * (1.0 - gate_attend * gate_attend)
     )
     grad_branch_low = norm_pull(grad_branch_y * norm_gains[1], branch_unit, branch_inverse).astype(BF16)
-    out_both = chip_sum(*device_columns(mixed_low, deep, narrow), grad_branch_low)
-    out_part = fsdp_sum(out_both)
     grad_mixed = times_transposed(grad_branch_low, full_out).astype(BF16)
     grad_blocks = widened(grad_mixed.reshape(local_tok, narrow, part).transpose(1, 0, 2), 1)
-    grad_heads = [
-        exchange(grad_blocks[:, :, 128 * pair : 128 * (pair + 1)], "fsdp").reshape(group_tok, 128)
-        for pair in range(pairs)
-    ]
-    grad_heads[0], down_part = lax.optimization_barrier((grad_heads[0], down_part))
+    grad_heads = exchange(grad_blocks, "fsdp").reshape(group_tok, part_pad)
+    def by_z(value):
+        return value.reshape(deep, -1, value.shape[1])
+
+    down_both = chip_sum(*down_columns, grad_down_low)
+    gate_up_both = chip_sum(*device_columns(normed_feed_low, deep, narrow), grad_gate_up_low)
+    out_both = chip_sum(*device_columns(mixed_low, deep, narrow), grad_branch_low)
+    down_part = fsdp_sum(down_both)
+    grad_heads, gate_up_both, out_both, down_part = lax.optimization_barrier(
+        (grad_heads, gate_up_both, out_both, down_part)
+    )
+    came_downs = exchange(by_z(down_part), "z")
+    gate_up_part = fsdp_sum(gate_up_both)
+    out_part = fsdp_sum(out_both)
     crossed = [
         cross_back(
-            pair, own_gates, packed, text_packed, row, grad_heads[pair], cross_outs[pair], stats[pair],
+            pair, own_gates, packed, text_packed, row, grad_heads, cross_outs[pair], stats[pair],
             head_dim, image_count, score_scale,
         )
         for pair in range(pairs)
     ]
-    grad_down_weight = z_sum(down_part, deep)
     dtk = jnp.concatenate([one[1] for one in crossed], axis=1)
     dtv = jnp.concatenate([one[2] for one in crossed], axis=1)
     gate_sums = jnp.stack([one[3] for one in crossed])
@@ -1000,26 +1052,17 @@
     grad_text_own = jnp.concatenate(
         [narrowed(grad_text_key_in.astype(BF16), 1), narrowed(dtv, 1)], axis=1
     )
-    backs = []
-    for pair in range(pairs):
-        backs.append(
-            self_back(
-                pair, packed, column, row, grad_heads[pair], self_outs[pair], stats[pair], crossed[pair][0],
-                head_dim, score_scale,
-            )
+    def self_pair(pair):
+        return self_back(
+            pair, packed, column, row, grad_heads, self_outs[pair], stats[pair], crossed[pair][0], head_dim, score_scale
         )
-        if pair == 0:
-            grad_heads[1], gate_up_part, grad_down_weight, first, grad_text_own = lax.optimization_barrier(
-                (grad_heads[1], gate_up_part, grad_down_weight, backs[0][0], grad_text_own)
-            )
-            backs[0] = (first, *backs[0][1:])
-            grad_gate_up_weight = z_sum(gate_up_part, deep)
-        if pair == 1 and pairs > 2:
-            grad_heads[2], out_part, second = lax.optimization_barrier((grad_heads[2], out_part, backs[1][0]))
-            backs[1] = (second, *backs[1][1:])
-    grad_out_weight = z_sum(out_part, deep)
-
-    grad_text_all = lax.all_gather(grad_text_own, "fsdp", axis=0)
+
+    came_texts = to_all(grad_text_own, narrow)
+    backs = [self_pair(0)]
+    first, came_downs, *came_texts = lax.optimization_barrier((backs[0][0], came_downs, *came_texts))
+    grad_down_weight = jnp.sum(came_downs.astype(F32), axis=0)
+    backs[0] = (first, *backs[0][1:])
+    grad_text_all = in_order(grad_text_own, came_texts)
     grad_text_columns = (
         grad_text_all.reshape(narrow, text_total, 2, part).transpose(1, 2, 0, 3).reshape(text_total, 2 * model_width)
     )
@@ -1027,18 +1070,15 @@
     own_text, other_text = by_core(text_slice[:, :text_half], text_slice[:, text_half:])
     came_text = core_swap(outer_sum(other_text, grad_text_columns).astype(BF16))
     text_both = (outer_sum(own_text, grad_text_columns) + came_text.astype(F32)).astype(BF16)
-    text_part = jnp.sum(
-        exchange(text_both.reshape(deep, -1, 2 * model_width), "z").astype(F32), axis=0
-    ).astype(BF16)
-    everyone = ("z", "core", "fsdp")
-    grad_text_weight = lax.ppermute(
-        text_part,
-        everyone,
-        [
-            ((z * 2 + c) * narrow + f, f * wide + c * deep + z)
-            for z in range(deep) for c in range(2) for f in range(narrow)
-        ],
-    ).astype(F32)
+    grad_heads, text_both, first = lax.optimization_barrier((grad_heads, text_both, backs[0][0]))
+    backs[0] = (first, *backs[0][1:])
+    text_part = z_sum(by_z(text_both), deep).astype(BF16)
+    backs.append(self_pair(1))
+    if pairs > 2:
+        grad_heads, gate_up_part, second = lax.optimization_barrier((grad_heads, gate_up_part, backs[1][0]))
+        backs[1] = (second, *backs[1][1:])
+        backs += [self_pair(pair) for pair in range(2, pairs)]
+    grad_gate_up_weight = z_sum(by_z(gate_up_part), deep)
     grad_text_slice = times_transposed(grad_text_columns, text_weight).astype(BF16)
     grad_text_normed = (
         exchange(
@@ -1067,6 +1107,19 @@
         list(zip(*backs)), projected, stats_all, cosine, sine, head_gains, part,
         lambda value: fsdp_share(value, narrow, 4),
     )
+    grad_projected_low, grad_gate_up_weight, text_part, out_part = lax.optimization_barrier(
+        (grad_projected_low, grad_gate_up_weight, text_part, out_part)
+    )
+    everyone = ("z", "core", "fsdp")
+    grad_text_weight = lax.ppermute(
+        text_part,
+        everyone,
+        [
+            ((z * 2 + c) * narrow + f, f * wide + c * deep + z)
+            for z in range(deep) for c in range(2) for f in range(narrow)
+        ],
+    ).astype(F32)
+    grad_out_weight = z_sum(by_z(out_part), deep)
     grad_normed = lax.psum_scatter(
         times_transposed(grad_projected_low, own_qkv).astype(BF16), "fsdp", scatter_dimension=0, tiled=True
     ).astype(F32)
@@ -1074,7 +1127,7 @@
     qkv_grad = outer_sum(normed_all, grad_projected_low).astype(BF16).reshape(deep, 2, model_width // wide, 3 * part_pad)
     own_grad, other_grad = by_core(qkv_grad[:, 0], qkv_grad[:, 1])
     own_grad = own_grad.astype(F32) + core_swap(other_grad).astype(F32)
-    own_grad = jnp.sum(exchange(own_grad.astype(BF16), "z").astype(F32), axis=0)
+    own_grad = z_sum(own_grad.astype(BF16), deep)
     grad_qkv_weight = (
         exchange(narrowed(own_grad.astype(BF16), 3).reshape(narrow, -1, 3 * part), "fsdp")
         .reshape(narrow, -1, 3, part)

time: 1310 us -> 1150 us (0.88)
  blocking collectives: 81.2 us -> 0 us
  waiting for transfers between devices: 188 us -> 117 us
  starting transfers between devices: 59.4 us -> 85.7 us
  local copies, waits for them, and re-layouts: 122 us -> 99.5 us
    all_to_all x13 -> x10, waiting for transfers between devices: 157 us -> 52.3 us  [exchange(): return lax.all_to_all(blocks, axis, 0, 0, tiled=True)]
    all_to_all x3 -> x0, blocking collectives: 81.2 us -> none  [exchange(): return lax.all_to_all(blocks, axis, 0, 0, tiled=True)]
    ppermute x0 -> x15, waiting for transfers between devices: none -> 51.9 us  [the longest x12 48.8 us: z_sum(): lax.ppermute(sent, 'z', [(i, i ^ step) for i in range(deep)]).astype(F32)]
    ppermute x0 -> x15, starting transfers between devices: none -> 38.1 us  [the longest x12 34.6 us: z_sum(): lax.ppermute(sent, 'z', [(i, i ^ step) for i in range(deep)]).astype(F32)]
    unnamed x233 -> x276, local copies, waits for them, and re-layouts: 46.2 us -> 20.7 us
    pallas_call x0 -> x1, Pallas kernels: none -> 23.6 us  [swiglu(): pl.pallas_call(swiglu_kernel, grid_spec=pltpu.PrefetchScalarGridSpec(num_...]
    pallas_call x1, Pallas kernels: 71.8 us -> 52 us  [finish(): pl.pallas_call(functools.partial(finish_kernel, narrow, wide, sum_rows),...]
    all_gather x3, waiting for transfers between devices: 20.3 us -> 3.09 us  [whole_weight(): return lax.all_gather(half, ('fsdp', 'core'), axis=0, tiled=True)]
  transfers between devices with their start and end apart: 29 -> 40, of which waited for: 11 -> 13; matrix products, arithmetic and copies ran while one was open for 30% -> 33% of each run, Pallas kernels for 30% -> 36%
where the time goes in v3:
time: 1150 us; the launch traced here: 1140 us
  Pallas kernels  467 us (41%)
  matrix products  240 us (21%)
  waiting for transfers between devices  117 us (10%)
  other arithmetic  112 us (10%)
  local copies, waits for them, and re-layouts  99.5 us (9%)
  starting transfers between devices  85.7 us (7%)
  between operations  19.1 us (2%)
    pallas_call x3, Pallas kernels, self_back(): pl.pallas_call(functools.partial(self_back_kernel, head_dim, FIRST_PATCHE...  138 us
    pallas_call x3, Pallas kernels, attend(): pl.pallas_call(functools.partial(attend_kernel, head_dim, FIRST_PATCHES,...  91.8 us
    dot_general x9, matrix products, outer_sum(): lax.dot_general(left, right, (((0,), (0,)), ((), ())), preferred_element_...  85.1 us
    dot_general x11, matrix products, low_product(): return jnp.dot(left, right, preferred_element_type=F32)  77.2 us
    dot_general x5, matrix products, times_transposed(): lax.dot_general(left, right, (((1,), (1,)), ((), ())), preferred_element_...  75.1 us
    pallas_call x5, Pallas kernels, fsdp_share(): pl.pallas_call(functools.partial(fsdp_share_kernel, narrow), in_specs=[pl...  63.6 us
    all_to_all x10, waiting for transfers between devices, exchange(): return lax.all_to_all(blocks, axis, 0, 0, tiled=True)  52.3 us
    pallas_call x1, Pallas kernels, finish(): pl.pallas_call(functools.partial(finish_kernel, narrow, wide, sum_rows),...  52 us
  transfers between devices with their start and end apart: 40, of which 13 were waited for; matrix products, arithmetic and copies ran while one was open for 33% of the time, Pallas kernels for 36%

profile of v3, /device:TPU:0, one launch (start us, length us, event | category | flops | bytes accessed | tf_op | source)
XLA Modules:
  0.0 1140.1 jit_solution(15935699407384984720)
XLA Ops:
  41.0 26.8 %shard_map.263 = f32[4,96,128]{2,1,0:T(8,128)} custom-call(f32[96,128]{1,0:T(8,128)} %reshape.613.x_ref), custom_call_target="tpu_custom_call" | custom-call | bytes 393216 | tf_op jit(solution)/shard_map/pallas_call | solution.py:647
  150.4 13.6 %fusion.168.projected_ref.refs_6_.refs_9_ = f32[2624,1152]{1,0:T(8,128)} fusion(bf16[2624,1536]{1,0:T(8,128)(2,1)S(1)} %fusion.3, bf16[1536,1152]{1,0:T(8,128)(2,1)S(1)} %bitcast.251), kind=kOutput, calls=%fused_computation.383 | convolution fusion | flops 9286189056 | bytes 23691264 | tf_op jit(solution)/shard_map/dot_general | solution.py:28
  173.4 16.1 %shard_map.265.stats_ref.refs_7_.refs_10_ = f32[4,8,2624]{2,1,0:T(8,128)} custom-call(f32[8,2624]{1,0:T(8,128)} %shard_map.264.x_ref), custom_call_target="tpu_custom_call" | custom-call | bytes 671744 | tf_op jit(solution)/shard_map/pallas_call | solution.py:647
  189.5 15.5 %shard_map.266.q_ref.k_ref.v_ref = bf16[2624,1152]{1,0:T(8,128)(2,1)} custom-call(f32[2624,1152]{1,0:T(8,128)} %fusion.168.projected_ref.refs_6_.refs_9_, f32[4,8,2624]{2,1,0:T(8,128)} %shard_map.265.stats_ref.refs_7_.refs_10_, f32[2624,128]{1,0:T(8,128)} %get-tuple-element.205.cos_ref.refs_8_.refs_12_, ...), custom_call_target="tpu_custom_call" | custom-call | flops 120913920 | bytes 18137088 | tf_op jit(solution)/shard_map/pallas_call | solution.py:183
  221.7 31.0 %shard_map.271 = (bf16[2624,128]{1,0:T(8,128)(2,1)}, f32[2624,128]{1,0:T(8,128)}, f32[2624,128]{1,0:T(8,128)}, f32[8,2624]{1,0:T(8,128)}) custom-call(f32[3,1,2]{2,1,0:T(1,128)} %reshape.663.gate_ref, bf16[2624,1152]{1,0:T(8,128)(2,1)} %shard_map.266.q_ref.k_ref.v_ref, bf16[2624,1152]{1,0:T(8,128)(2,1)} %shard_map.266.q_ref.k_ref.v_ref, ...), custom_call_target="tpu_custom_call" | custom-call | flops 4213178368 | bytes 6717440 | tf_op jit(solution)/shard_map/pallas_call | solution.py:379
  256.4 30.4 %shard_map.270 = (bf16[2624,128]{1,0:T(8,128)(2,1)}, f32[2624,128]{1,0:T(8,128)}, f32[2624,128]{1,0:T(8,128)}, f32[8,2624]{1,0:T(8,128)}) custom-call(f32[3,1,2]{2,1,0:T(1,128)} %reshape.663.gate_ref, bf16[2624,1152]{1,0:T(8,128)(2,1)} %shard_map.266.q_ref.k_ref.v_ref, bf16[2624,1152]{1,0:T(8,128)(2,1)} %shard_map.266.q_ref.k_ref.v_ref, ...), custom_call_target="tpu_custom_call" | custom-call | flops 4213178368 | bytes 6717440 | tf_op jit(solution)/shard_map/pallas_call | solution.py:379
  291.1 30.4 %shard_map.269 = (bf16[2624,128]{1,0:T(8,128)(2,1)}, f32[2624,128]{1,0:T(8,128)}, f32[2624,128]{1,0:T(8,128)}, f32[8,2624]{1,0:T(8,128)}) custom-call(f32[3,1,2]{2,1,0:T(1,128)} %reshape.663.gate_ref, bf16[2624,1152]{1,0:T(8,128)(2,1)} %shard_map.266.q_ref.k_ref.v_ref, bf16[2624,1152]{1,0:T(8,128)(2,1)} %shard_map.266.q_ref.k_ref.v_ref, ...), custom_call_target="tpu_custom_call" | custom-call | flops 4213178368 | bytes 6717440 | tf_op jit(solution)/shard_map/pallas_call | solution.py:379
  325.8 16.2 %all-to-all-done.3 = bf16[4,656,128]{2,1,0:T(8,128)(2,1)} async-done(((bf16[4,656,128]{2,1,0:T(8,128)(2,1)}), bf16[4,656,128]{2,1,0:T(8,128)(2,1)}, u32[]{:S(2)}, u32[]{:S(2)}) %all-to-all-start.3) | async-done | bytes 671776 | tf_op jit(solution)/shard_map/all_to_all | solution.py:737
  366.4 26.5 %fusion.169.gate_ref.up_ref = f32[656,8192]{1,0:T(8,128)} fusion(bf16[656,1536]{1,0:T(8,128)(2,1)} %copy-done.30, bf16[1536,8192]{1,0:T(8,128)(2,1)} %all-gather.8.cloned.1.call-done), kind=kOutput, calls=%fused_computation.384 | convolution fusion | flops 16508780544 | bytes 48676864 | tf_op jit(solution)/shard_map/dot_general | solution.py:28
  392.9 23.6 %shard_map.272 = (bf16[656,4096]{1,0:T(8,128)(2,1)}, bf16[656,4096]{1,0:T(8,128)(2,1)}) custom-call(s32[1]{0:T(128)} %bitcast.29.core_ref, f32[656,8192]{1,0:T(8,128)} %fusion.169.gate_ref.up_ref, f32[656,8192]{1,0:T(8,128)} %fusion.169.gate_ref.up_ref), custom_call_target="tpu_custom_call" | custom-call | flops 16121856 | bytes 32243712 | tf_op jit(solution)/shard_map/pallas_call | solution.py:601
  419.6 13.1 %multiply_reduce_fusion.14 = (f32[656]{0:T(1024)S(1)}, f32[656,1536]{1,0:T(8,128)S(1)}) fusion(bf16[656,4096]{1,0:T(8,128)(2,1)} %get-tuple-element.77, bf16[4096,1536]{1,0:T(8,128)(2,1)} %all-gather.10.cloned.1.call-done), kind=kOutput, calls=%fused_computation.67 | convolution fusion | flops 8256404992 | bytes 21989952 | tf_op jit(solution)/shard_map/dot_general | solution.py:28
  449.2 20.9 %fusion.6 = (bf16[656,4096]{1,0:T(8,128)(2,1)}, bf16[656,4096]{1,0:T(8,128)(2,1)}) fusion(f32[656,8192]{1,0:T(8,128)} %fusion.169.gate_ref.up_ref, bf16[656,1536]{1,0:T(8,128)(2,1)S(1)} %get-tuple-element.183, bf16[4096,1536]{1,0:T(8,128)(2,1)} %all-gather.10.cloned.1.call-done), kind=kOutput, calls=%fused_computation.13 | convolution fusion | flops 8289320960 | bytes 46841856 | tf_op jit(solution)/shard_map/dot_general | solution.py:32
  470.1 17.2 %convolution_convert_fusion = bf16[768,8192]{1,0:T(8,128)(2,1)} fusion(bf16[656,4096]{1,0:T(8,128)(2,1)} %get-tuple-element.178, bf16[656,4096]{1,0:T(8,128)(2,1)} %get-tuple-element.177, bf16[656,1536]{1,0:T(8,128)(2,1)} %fusion.29), kind=kOutput, calls=%fused_computation.7 | convolution fusion | flops 8282177536 | bytes 24338432 | tf_op jit(solution)/shard_map/dot_general | solution.py:36
  498.4 28.7 %multiply_reduce_fusion.9 = (f32[1536]{0:T(1024)}, f32[656]{0:T(1024)S(1)}, f32[1536]{0:T(1024)}, f32[1536]{0:T(1024)}, f32[656,1536]{1,0:T(8,128)}) fusion(f32[656,1536]{1,0:T(8,128)} %copy-done.5, f32[656]{0:T(1024)S(1)} %copy-done.78, f32[1536]{0:T(1024)S(1)} %copy-done.60, f32[656]{0:T(1024)S(1)} %get-tuple-element.222, f32[1536]{0:T(1024)S(1)} %copy-done.62, ...), kind=kOutput, calls=%fused_computation.59 | convolution fusion | flops 16547399680 | bytes 44022016 | tf_op jit(solution)/shard_map/dot_general | solution.py:32
  558.5 18.3 %add_convert_fusion = bf16[768,8192]{1,0:T(8,128)(2,1)} fusion(bf16[768,8192]{1,0:T(8,128)(2,1)} %collective-permute-done.1, bf16[656,4096]{1,0:T(8,128)(2,1)} %get-tuple-element.178, bf16[656,4096]{1,0:T(8,128)(2,1)} %get-tuple-element.177, bf16[656,1536]{1,0:T(8,128)(2,1)} %fusion.29), kind=kOutput, calls=%fused_computation | convolution fusion | flops 8294760448 | bytes 36921344 | tf_op jit(solution)/shard_map/dot_general | solution.py:36
  576.9 10.9 all-to-all-done.6
  594.0 13.5 %shard_map.275 = (bf16[2624,128]{1,0:T(8,128)(2,1)}, bf16[512,128]{1,0:T(8,128)(2,1)}, bf16[512,128]{1,0:T(8,128)(2,1)}, f32[8,128]{1,0:T(8,128)}) custom-call(f32[3,1,2]{2,1,0:T(1,128)} %reshape.663.gate_ref, bf16[2624,1152]{1,0:T(8,128)(2,1)} %shard_map.266.q_ref.k_ref.v_ref, bf16[512,768]{1,0:T(8,128)(2,1)} %pad_maximum_fusion.8.tk_ref.tv_ref, ...), custom_call_target="tpu_custom_call" | custom-call | flops 1719664640 | bytes 4030464 | tf_op jit(solution)/shard_map/pallas_call | solution.py:495
  607.5 13.3 %shard_map.274 = (bf16[2624,128]{1,0:T(8,128)(2,1)}, bf16[512,128]{1,0:T(8,128)(2,1)}, bf16[512,128]{1,0:T(8,128)(2,1)}, f32[8,128]{1,0:T(8,128)}) custom-call(f32[3,1,2]{2,1,0:T(1,128)} %reshape.663.gate_ref, bf16[2624,1152]{1,0:T(8,128)(2,1)} %shard_map.266.q_ref.k_ref.v_ref, bf16[512,768]{1,0:T(8,128)(2,1)} %pad_maximum_fusion.8.tk_ref.tv_ref, ...), custom_call_target="tpu_custom_call" | custom-call | flops 1719664640 | bytes 4030464 | tf_op jit(solution)/shard_map/pallas_call | solution.py:495
  620.9 13.4 %shard_map.273 = (bf16[2624,128]{1,0:T(8,128)(2,1)}, bf16[512,128]{1,0:T(8,128)(2,1)}, bf16[512,128]{1,0:T(8,128)(2,1)}, f32[8,128]{1,0:T(8,128)}) custom-call(f32[3,1,2]{2,1,0:T(1,128)} %reshape.663.gate_ref, bf16[2624,1152]{1,0:T(8,128)(2,1)} %shard_map.266.q_ref.k_ref.v_ref, bf16[512,768]{1,0:T(8,128)(2,1)} %pad_maximum_fusion.8.tk_ref.tv_ref, ...), custom_call_target="tpu_custom_call" | custom-call | flops 1719664640 | bytes 4030464 | tf_op jit(solution)/shard_map/pallas_call | solution.py:495
  653.6 46.2 %shard_map.277 = (bf16[2624,128]{1,0:T(8,128)(2,1)}, bf16[2624,128]{1,0:T(8,128)(2,1)}, bf16[2624,128]{1,0:T(8,128)(2,1)}) custom-call(bf16[2624,1152]{1,0:T(8,128)(2,1)} %shard_map.266.q_ref.k_ref.v_ref, bf16[2624,1152]{1,0:T(8,128)(2,1)} %shard_map.266.q_ref.k_ref.v_ref, bf16[2624,1152]{1,0:T(8,128)(2,1)} %shard_map.266.q_ref.k_ref.v_ref, ...), custom_call_target="tpu_custom_call" | custom-call | flops 8813281280 | bytes 10076160 | tf_op jit(solution)/shard_map/pallas_call | solution.py:562
  733.0 45.7 %shard_map.278 = (bf16[2624,128]{1,0:T(8,128)(2,1)}, bf16[2624,128]{1,0:T(8,128)(2,1)}, bf16[2624,128]{1,0:T(8,128)(2,1)}) custom-call(bf16[2624,1152]{1,0:T(8,128)(2,1)} %shard_map.266.q_ref.k_ref.v_ref, bf16[2624,1152]{1,0:T(8,128)(2,1)} %shard_map.266.q_ref.k_ref.v_ref, bf16[2624,1152]{1,0:T(8,128)(2,1)} %shard_map.266.q_ref.k_ref.v_ref, ...), custom_call_target="tpu_custom_call" | custom-call | flops 8813281280 | bytes 10076160 | tf_op jit(solution)/shard_map/pallas_call | solution.py:562
  778.7 21.1 %collective-permute-done.12 = bf16[128,3072]{1,0:T(8,128)(2,1)} collective-permute-done((bf16[128,3072]{1,0:T(8,128)(2,1)}, bf16[128,3072]{1,0:T(8,128)(2,1)}, u32[]{:S(2)}, u32[]{:S(2)}) %collective-permute-start.12) | collective-permute-done | bytes 786464 | tf_op jit(solution)/shard_map/ppermute | solution.py:768
  810.2 45.6 %shard_map.279 = (bf16[2624,128]{1,0:T(8,128)(2,1)}, bf16[2624,128]{1,0:T(8,128)(2,1)}, bf16[2624,128]{1,0:T(8,128)(2,1)}) custom-call(bf16[2624,1152]{1,0:T(8,128)(2,1)} %shard_map.266.q_ref.k_ref.v_ref, bf16[2624,1152]{1,0:T(8,128)(2,1)} %shard_map.266.q_ref.k_ref.v_ref, bf16[2624,1152]{1,0:T(8,128)(2,1)} %shard_map.266.q_ref.k_ref.v_ref, ...), custom_call_target="tpu_custom_call" | custom-call | flops 8813281280 | bytes 10076160 | tf_op jit(solution)/shard_map/pallas_call | solution.py:562
  855.8 15.2 %shard_map.280 = (f32[8,2624]{1,0:T(8,128)}, f32[8,384]{1,0:T(8,128)}) custom-call(bf16[2624,128]{1,0:T(8,128)(2,1)} %get-tuple-element.100.refs_0_, bf16[2624,128]{1,0:T(8,128)(2,1)} %get-tuple-element.106.refs_1_, bf16[2624,128]{1,0:T(8,128)(2,1)} %get-tuple-element.110.refs_2_, bf16[2624,128]{1,0:T(8,128)(2,1)} %get-tuple-element.111.refs_3_, ...), custom_call_target="tpu_custom_call" | custom-call | flops 120913920 | bytes 15114240 | tf_op jit(solution)/shard_map/pallas_call | solution.py:269
  878.4 15.8 %shard_map.282 = bf16[2624,1152]{1,0:T(8,128)(2,1)} custom-call(bf16[2624,128]{1,0:T(8,128)(2,1)} %get-tuple-element.100.refs_0_, bf16[2624,128]{1,0:T(8,128)(2,1)} %get-tuple-element.106.refs_1_, bf16[2624,128]{1,0:T(8,128)(2,1)} %get-tuple-element.110.refs_2_, bf16[2624,128]{1,0:T(8,128)(2,1)} %get-tuple-element.111.refs_3_, ...), custom_call_target="tpu_custom_call" | custom-call | flops 120913920 | bytes 21159936 | tf_op jit(solution)/shard_map/pallas_call | solution.py:282
  897.8 15.5 %convolution_convert_fusion.1 = bf16[2624,1536]{1,0:T(8,128)(2,1)} fusion(bf16[2624,1152]{1,0:T(8,128)(2,1)} %shard_map.282, bf16[1536,1152]{1,0:T(8,128)(2,1)S(1)} %bitcast.252), kind=kOutput, calls=%fused_computation.9 | convolution fusion | flops 9290219520 | bytes 17645568 | tf_op jit(solution)/shard_map/dot_general | solution.py:32
  913.3 15.4 %convolution_convert_fusion.3 = bf16[1536,1152]{1,0:T(8,128)(2,1)S(1)} fusion(bf16[2624,1536]{1,0:T(8,128)(2,1)} %copy-done.20, bf16[2624,1152]{1,0:T(8,128)(2,1)} %shard_map.282), kind=kOutput, calls=%fused_computation.21 | convolution fusion | flops 9287958528 | bytes 17645568 | tf_op jit(solution)/shard_map/dot_general | solution.py:36
  952.2 17.0 %all-to-all-done.8 = bf16[4,128,1024]{2,1,0:T(8,128)(2,1)S(1)} async-done(((bf16[4,128,1024]{2,1,0:T(8,128)(2,1)}), bf16[4,128,1024]{2,1,0:T(8,128)(2,1)S(1)}, u32[]{:S(2)}, u32[]{:S(2)}) %all-to-all-start.8) | async-done | bytes 1048608 | tf_op jit(solution)/shard_map/all_to_all | solution.py:737
  998.1 18.9 %collective-permute-start.18 = (bf16[48,1536]{1,0:T(8,128)(2,1)S(1)}, bf16[48,1536]{1,0:T(8,128)(2,1)S(1)}, u32[]{:S(2)}, u32[]{:S(2)}) collective-permute-start(bf16[48,1536]{1,0:T(8,128)(2,1)S(1)} %get-tuple-element.199), channel_id=1, source_target_pairs={{0,8},{8,0},{16,24},{24,16},{1,9},{9,1},{17,25},{25,17},{2,10},{10... | collective-permute-start | bytes 442376 | tf_op jit(solution)/shard_map/ppermute | solution.py:768
  1017.0 12.1 %collective-permute-done.16 = bf16[192,1152]{1,0:T(8,128)(2,1)} collective-permute-done((bf16[192,1152]{1,0:T(8,128)(2,1)}, bf16[192,1152]{1,0:T(8,128)(2,1)}, u32[]{:S(2)}, u32[]{:S(2)}) %collective-permute-start.16) | collective-permute-done | bytes 442400 | tf_op jit(solution)/shard_map/ppermute | solution.py:768
  1039.8 12.0 %collective-permute-done.19 = bf16[48,1536]{1,0:T(8,128)(2,1)S(1)} collective-permute-done((bf16[48,1536]{1,0:T(8,128)(2,1)S(1)}, bf16[48,1536]{1,0:T(8,128)(2,1)S(1)}, u32[]{:S(2)}, u32[]{:S(2)}) %collective-permute-start.19) | collective-permute-done | bytes 147488 | tf_op jit(solution)/shard_map/ppermute | solution.py:768
  1066.2 52.0 %shard_map.283 = f32[4,296,128]{2,1,0:T(8,128)} custom-call(f32[4,72,128]{2,1,0:T(8,128)} %pad_maximum_fusion.11.x_ref), custom_call_target="tpu_custom_call" | custom-call | tf_op jit(solution)/shard_map/pallas_call | solution.py:718
  (538 shorter events, 409.1 us)
Async XLA Ops:
  7.2 122.6 %all-gather.12.cloned.1.call-start = ((), (), s32[]{:S(2)}) async-start(), calls=%async_computation.21 | async-start | bytes 10076160 | tf_op jit(solution)/shard_map/all_gather | solution.py:879
  7.9 336.9 %all-gather.6.cloned.1.call-start = ((), (), s32[]{:S(2)}) async-start(), calls=%async_computation.14 | async-start | bytes 5308416 | tf_op jit(solution)/shard_map/all_gather | solution.py:807
  10.2 356.2 %all-gather.8.cloned.1.call-start = ((), (), s32[]{:S(2)}) async-start(), calls=%async_computation.15 | async-start | bytes 28311552 | tf_op jit(solution)/shard_map/all_gather | solution.py:807
  25.0 61.4 %all-to-all-start.1 = ((bf16[4,192,1152]{2,1,0:T(8,128)(2,1)}), bf16[4,192,1152]{2,1,0:T(8,128)(2,1)}, u32[]{:S(2)}, u32[]{:S(2)}) async-start(bf16[4,192,1152]{2,1,0:T(8,128)(2,1)} %reshape.620), calls=%async_computation.1 | async-start | bytes 3538944 | tf_op jit(solution)/shard_map/all_to_all | solution.py:737
  30.3 389.3 %all-gather.10.cloned.1.call-start = ((), (), s32[]{:S(2)}) async-start(), calls=%async_computation.16 | async-start | bytes 14155776 | tf_op jit(solution)/shard_map/all_gather | solution.py:807
  86.4 29.5 %all-to-all-start = ((bf16[4,128,1024]{2,1,0:T(8,128)(2,1)}), bf16[4,128,1024]{2,1,0:T(8,128)(2,1)S(1)}, u32[]{:S(2)}, u32[]{:S(2)}) async-start(bf16[4,128,1024]{2,1,0:T(8,128)(2,1)} %fusion.53), calls=%async_computation | async-start | bytes 2097152 | tf_op jit(solution)/shard_map/all_to_all | solution.py:737
  129.8 75.2 %all-to-all-start.2 = ((bf16[4,512,768]{2,1,0:T(8,128)(2,1)}), bf16[4,512,768]{2,1,0:T(8,128)(2,1)}, u32[]{:S(2)}, u32[]{:S(2)}) async-start(bf16[4,512,768]{2,1,0:T(8,128)(2,1)} %pad_maximum_fusion.2), calls=%async_computation.2 | async-start | bytes 6291456 | tf_op jit(solution)/shard_map/all_to_all | solution.py:737
  252.8 34.0 %all-to-all-start.5 = ((bf16[4,656,128]{2,1,0:T(8,128)(2,1)}), bf16[4,656,128]{2,1,0:T(8,128)(2,1)S(1)}, u32[]{:S(2)}, u32[]{:S(2)}) async-start(bf16[4,656,128]{2,1,0:T(8,128)(2,1)} %bitcast.279), calls=%async_computation.5 | async-start | bytes 1343488 | tf_op jit(solution)/shard_map/all_to_all | solution.py:737
  286.8 34.8 %all-to-all-start.4 = ((bf16[4,656,128]{2,1,0:T(8,128)(2,1)}), bf16[4,656,128]{2,1,0:T(8,128)(2,1)S(1)}, u32[]{:S(2)}, u32[]{:S(2)}) async-start(bf16[4,656,128]{2,1,0:T(8,128)(2,1)} %bitcast.278), calls=%async_computation.4 | async-start | bytes 1343488 | tf_op jit(solution)/shard_map/all_to_all | solution.py:737
  325.7 263.6 %reduce-scatter.5.cloned.1.call-start = ((), (), s32[]{:S(2)}) async-start(), calls=%async_computation.17 | async-start | bytes 7864320 | tf_op jit(solution)/shard_map/reduce_scatter | solution.py:760
  449.0 38.6 %collective-permute-start.3 = (bf16[2048,1536]{1,0:T(8,128)(2,1)}, bf16[2048,1536]{1,0:T(8,128)(2,1)}, u32[]{:S(2)}, u32[]{:S(2)}) collective-permute-start(bf16[2048,1536]{1,0:T(8,128)(2,1)} %convolution_convert_fusion.2), channel_id=1, source_target_pairs={{0,4},{4,0},{1,5},{5,1},{2,6},{6,2},{3,7},{7,3},{8,12},{12,8},{9,1... | collective-permute-start | bytes 18874376 | tf_op jit(solution)/shard_map/ppermute | solution.py:741
  487.3 71.2 %collective-permute-start.1 = (bf16[768,8192]{1,0:T(8,128)(2,1)}, bf16[768,8192]{1,0:T(8,128)(2,1)}, u32[]{:S(2)}, u32[]{:S(2)}) collective-permute-start(bf16[768,8192]{1,0:T(8,128)(2,1)} %convolution_convert_fusion), channel_id=1, source_target_pairs={{0,4},{4,0},{1,5},{5,1},{2,6},{6,2},{3,7},{7,3},{8,12},{12,8},{9,1... | collective-permute-start | bytes 37748744 | tf_op jit(solution)/shard_map/ppermute | solution.py:741
  548.8 39.0 %all-to-all-start.6 = ((bf16[4,656,384]{2,1,0:T(8,128)(2,1)}), bf16[4,656,384]{2,1,0:T(8,128)(2,1)S(1)}, u32[]{:S(2)}, u32[]{:S(2)}) async-start(bf16[4,656,384]{2,1,0:T(8,128)(2,1)} %bitcast.247), calls=%async_computation.6 | async-start | bytes 4030464 | tf_op jit(solution)/shard_map/all_to_all | solution.py:737
  552.4 250.3 %reduce-scatter.7.cloned.1.call-start = ((), (), s32[]{:S(2)}) async-start(), calls=%async_computation.18 | async-start | bytes 15728640 | tf_op jit(solution)/shard_map/reduce_scatter | solution.py:760
  589.4 113.6 %all-to-all-start.7 = ((bf16[4,128,1536]{2,1,0:T(8,128)(2,1)}), bf16[4,128,1536]{2,1,0:T(8,128)(2,1)}, u32[]{:S(2)}, u32[]{:S(2)}) async-start(bf16[4,128,1536]{2,1,0:T(8,128)(2,1)} %bitcast.269), calls=%async_computation.8 | async-start | bytes 3145728 | tf_op jit(solution)/shard_map/all_to_all | solution.py:737
  594.0 303.7 %reduce-scatter.9.cloned.1.call-start = ((), (), s32[]{:S(2)}) async-start(), calls=%async_computation.19 | async-start | bytes 2949120 | tf_op jit(solution)/shard_map/reduce_scatter | solution.py:760
  647.5 52.3 %collective-permute-start.4 = (bf16[512,768]{1,0:T(8,128)(2,1)}, bf16[512,768]{1,0:T(8,128)(2,1)}, u32[]{:S(2)}, u32[]{:S(2)}) collective-permute-start(bf16[512,768]{1,0:T(8,128)(2,1)} %get-tuple-element.197), channel_id=1, source_target_pairs={{0,1},{1,0},{2,3},{3,2},{4,5},{5,4},{6,7},{7,6},{8,9},{9,8},{10,11... | collective-permute-start | bytes 2359304 | tf_op jit(solution)/shard_map/ppermute | solution.py:774
  649.0 50.9 %collective-permute-start.5 = (bf16[512,768]{1,0:T(8,128)(2,1)}, bf16[512,768]{1,0:T(8,128)(2,1)}, u32[]{:S(2)}, u32[]{:S(2)}) collective-permute-start(bf16[512,768]{1,0:T(8,128)(2,1)} %get-tuple-element.197), channel_id=1, source_target_pairs={{0,2},{1,3},{2,0},{3,1},{4,6},{5,7},{6,4},{7,5},{8,10},{9,11},{10,... | collective-permute-start | bytes 2359304 | tf_op jit(solution)/shard_map/ppermute | solution.py:774
  649.5 53.4 %collective-permute-start.6 = (bf16[512,768]{1,0:T(8,128)(2,1)}, bf16[512,768]{1,0:T(8,128)(2,1)}, u32[]{:S(2)}, u32[]{:S(2)}) collective-permute-start(bf16[512,768]{1,0:T(8,128)(2,1)} %get-tuple-element.197), channel_id=1, source_target_pairs={{0,3},{1,2},{2,1},{3,0},{4,7},{5,6},{6,5},{7,4},{8,11},{9,10},{10,... | collective-permute-start | bytes 2359304 | tf_op jit(solution)/shard_map/ppermute | solution.py:774
  716.0 344.5 %reduce-scatter.11.cloned.1.call-start = ((), (), s32[]{:S(2)}) async-start(), calls=%async_computation.20 | async-start | bytes 10076160 | tf_op jit(solution)/shard_map/reduce_scatter | solution.py:1123
  728.6 50.1 %collective-permute-start.13 = (bf16[128,3072]{1,0:T(8,128)(2,1)}, bf16[128,3072]{1,0:T(8,128)(2,1)}, u32[]{:S(2)}, u32[]{:S(2)}) collective-permute-start(bf16[128,3072]{1,0:T(8,128)(2,1)} %get-tuple-element.188), channel_id=1, source_target_pairs={{0,24},{8,16},{16,8},{24,0},{1,25},{9,17},{17,9},{25,1},{2,26},{10... | collective-permute-start | bytes 2359304 | tf_op jit(solution)/shard_map/ppermute | solution.py:768
  731.8 68.0 %collective-permute-start.12 = (bf16[128,3072]{1,0:T(8,128)(2,1)}, bf16[128,3072]{1,0:T(8,128)(2,1)}, u32[]{:S(2)}, u32[]{:S(2)}) collective-permute-start(bf16[128,3072]{1,0:T(8,128)(2,1)} %get-tuple-element.189), channel_id=1, source_target_pairs={{0,16},{8,24},{16,0},{24,8},{1,17},{9,25},{17,1},{25,9},{2,18},{10... | collective-permute-start | bytes 2359304 | tf_op jit(solution)/shard_map/ppermute | solution.py:768
  731.8 68.0 %collective-permute-start.11 = (bf16[128,3072]{1,0:T(8,128)(2,1)}, bf16[128,3072]{1,0:T(8,128)(2,1)}, u32[]{:S(2)}, u32[]{:S(2)}) collective-permute-start(bf16[128,3072]{1,0:T(8,128)(2,1)} %get-tuple-element.187), channel_id=1, source_target_pairs={{0,8},{8,0},{16,24},{24,16},{1,9},{9,1},{17,25},{25,17},{2,10},{10... | collective-permute-start | bytes 2359304 | tf_op jit(solution)/shard_map/ppermute | solution.py:768
  805.8 88.4 %collective-permute-start.10 = (bf16[48,8192]{1,0:T(8,128)(2,1)}, bf16[48,8192]{1,0:T(8,128)(2,1)}, u32[]{:S(2)}, u32[]{:S(2)}) collective-permute-start(bf16[48,8192]{1,0:T(8,128)(2,1)} %get-tuple-element.191), channel_id=1, source_target_pairs={{0,24},{8,16},{16,8},{24,0},{1,25},{9,17},{17,9},{25,1},{2,26},{10... | collective-permute-start | bytes 2359304 | tf_op jit(solution)/shard_map/ppermute | solution.py:768
  808.2 86.0 %collective-permute-start.9 = (bf16[48,8192]{1,0:T(8,128)(2,1)}, bf16[48,8192]{1,0:T(8,128)(2,1)}, u32[]{:S(2)}, u32[]{:S(2)}) collective-permute-start(bf16[48,8192]{1,0:T(8,128)(2,1)} %get-tuple-element.192), channel_id=1, source_target_pairs={{0,16},{8,24},{16,0},{24,8},{1,17},{9,25},{17,1},{25,9},{2,18},{10... | collective-permute-start | bytes 2359304 | tf_op jit(solution)/shard_map/ppermute | solution.py:768
  808.2 86.0 %collective-permute-start.8 = (bf16[48,8192]{1,0:T(8,128)(2,1)}, bf16[48,8192]{1,0:T(8,128)(2,1)}, u32[]{:S(2)}, u32[]{:S(2)}) collective-permute-start(bf16[48,8192]{1,0:T(8,128)(2,1)} %get-tuple-element.190), channel_id=1, source_target_pairs={{0,8},{8,0},{16,24},{24,16},{1,9},{9,1},{17,25},{25,17},{2,10},{10... | collective-permute-start | bytes 2359304 | tf_op jit(solution)/shard_map/ppermute | solution.py:768
  930.1 48.1 %collective-permute-start.14 = (bf16[4,192,1152]{2,1,0:T(8,128)(2,1)}, bf16[4,192,1152]{2,1,0:T(8,128)(2,1)}, u32[]{:S(2)}, u32[]{:S(2)}) collective-permute-start(bf16[4,192,1152]{2,1,0:T(8,128)(2,1)} %fusion.40), channel_id=1, source_target_pairs={{0,4},{4,0},{1,5},{5,1},{2,6},{6,2},{3,7},{7,3},{8,12},{12,8},{9,1... | collective-permute-start | bytes 5308424 | tf_op jit(solution)/shard_map/ppermute | solution.py:741
  985.3 43.7 %collective-permute-start.16 = (bf16[192,1152]{1,0:T(8,128)(2,1)}, bf16[192,1152]{1,0:T(8,128)(2,1)}, u32[]{:S(2)}, u32[]{:S(2)}) collective-permute-start(bf16[192,1152]{1,0:T(8,128)(2,1)} %get-tuple-element.196), channel_id=1, source_target_pairs={{0,16},{8,24},{16,0},{24,8},{1,17},{9,25},{17,1},{25,9},{2,18},{10... | collective-permute-start | bytes 1327112 | tf_op jit(solution)/shard_map/ppermute | solution.py:768
  985.3 45.5 %collective-permute-start.15 = (bf16[192,1152]{1,0:T(8,128)(2,1)}, bf16[192,1152]{1,0:T(8,128)(2,1)}, u32[]{:S(2)}, u32[]{:S(2)}) collective-permute-start(bf16[192,1152]{1,0:T(8,128)(2,1)} %get-tuple-element.194), channel_id=1, source_target_pairs={{0,8},{8,0},{16,24},{24,16},{1,9},{9,1},{17,25},{25,17},{2,10},{10... | collective-permute-start | bytes 1327112 | tf_op jit(solution)/shard_map/ppermute | solution.py:768
  992.0 47.8 %collective-permute-start.20 = (bf16[48,1536]{1,0:T(8,128)(2,1)S(1)}, bf16[48,1536]{1,0:T(8,128)(2,1)S(1)}, u32[]{:S(2)}, u32[]{:S(2)}) collective-permute-start(bf16[48,1536]{1,0:T(8,128)(2,1)S(1)} %get-tuple-element.200), channel_id=1, source_target_pairs={{0,24},{8,16},{16,8},{24,0},{1,25},{9,17},{17,9},{25,1},{2,26},{10... | collective-permute-start | bytes 442376 | tf_op jit(solution)/shard_map/ppermute | solution.py:768
  994.5 57.4 %collective-permute-start.19 = (bf16[48,1536]{1,0:T(8,128)(2,1)S(1)}, bf16[48,1536]{1,0:T(8,128)(2,1)S(1)}, u32[]{:S(2)}, u32[]{:S(2)}) collective-permute-start(bf16[48,1536]{1,0:T(8,128)(2,1)S(1)} %get-tuple-element.201), channel_id=1, source_target_pairs={{0,16},{8,24},{16,0},{24,8},{1,17},{9,25},{17,1},{25,9},{2,18},{10... | collective-permute-start | bytes 442376 | tf_op jit(solution)/shard_map/ppermute | solution.py:768
  998.1 53.8 %collective-permute-start.18 = (bf16[48,1536]{1,0:T(8,128)(2,1)S(1)}, bf16[48,1536]{1,0:T(8,128)(2,1)S(1)}, u32[]{:S(2)}, u32[]{:S(2)}) collective-permute-start(bf16[48,1536]{1,0:T(8,128)(2,1)S(1)} %get-tuple-element.199), channel_id=1, source_target_pairs={{0,8},{8,0},{16,24},{24,16},{1,9},{9,1},{17,25},{25,17},{2,10},{10... | collective-permute-start | bytes 442376 | tf_op jit(solution)/shard_map/ppermute | solution.py:768
  (140 other events, 2347.9 us)
Sparse Core Ops, SparseCore 0:
  9.9 119.8 all-gather.11
  131.7 63.8 all-gather.5
  197.5 147.6 all-gather.7
  347.5 72.1 all-gather.9
  497.8 91.5 reduce-scatter.4
  592.3 151.4 reduce-scatter.6
  746.9 37.3 reduce-scatter.8
  913.4 94.0 reduce-scatter.10

commit v4 on v3

--- a/solution.py
+++ b/solution.py
@@ -583,7 +583,8 @@
 
 def swiglu_kernel(core_ref, gate_ref, up_ref, out_ref, moved_ref):
     gate = gate_ref[...]
-    value = (gate * up_ref[...] / (1.0 + jnp.exp(-gate))).astype(BF16)
+    half = 0.5 * gate
+    value = ((half + half * jnp.tanh(half)) * up_ref[...]).astype(BF16)
     out_ref[...] = value
     moved_ref[...] = value
 
@@ -760,13 +761,18 @@
     return lax.psum_scatter(both, "fsdp", scatter_dimension=0, tiled=True)
 
 
-def z_sum(blocks, deep):
+def z_pieces(blocks, deep):
     me = lax.axis_index("z")
-    total = lax.dynamic_index_in_dim(blocks, me, 0, keepdims=False).astype(F32)
-    for step in range(1, deep):
-        sent = lax.dynamic_index_in_dim(blocks, me ^ step, 0, keepdims=False)
-        total = total + lax.ppermute(sent, "z", [(i, i ^ step) for i in range(deep)]).astype(F32)
-    return total
+    return [lax.dynamic_index_in_dim(blocks, me, 0, keepdims=False)] + [
+        lax.ppermute(
+            lax.dynamic_index_in_dim(blocks, me ^ step, 0, keepdims=False), "z", [(i, i ^ step) for i in range(deep)]
+        )
+        for step in range(1, deep)
+    ]
+
+
+def added(pieces):
+    return functools.reduce(jnp.add, [piece.astype(F32) for piece in pieces])
 
 
 def to_all(block, narrow):
@@ -1072,33 +1078,19 @@
     text_both = (outer_sum(own_text, grad_text_columns) + came_text.astype(F32)).astype(BF16)
     grad_heads, text_both, first = lax.optimization_barrier((grad_heads, text_both, backs[0][0]))
     backs[0] = (first, *backs[0][1:])
-    text_part = z_sum(by_z(text_both), deep).astype(BF16)
+    came_text_z = exchange(by_z(text_both), "z")
     backs.append(self_pair(1))
     if pairs > 2:
-        grad_heads, gate_up_part, second = lax.optimization_barrier((grad_heads, gate_up_part, backs[1][0]))
+        grad_heads, gate_up_part, out_part, second = lax.optimization_barrier(
+            (grad_heads, gate_up_part, out_part, backs[1][0])
+        )
         backs[1] = (second, *backs[1][1:])
         backs += [self_pair(pair) for pair in range(2, pairs)]
-    grad_gate_up_weight = z_sum(by_z(gate_up_part), deep)
-    grad_text_slice = times_transposed(grad_text_columns, text_weight).astype(BF16)
-    grad_text_normed = (
-        exchange(
-            grad_text_slice.reshape(image_count, narrow, caption_local, text_cols)
-            .transpose(1, 0, 2, 3)
-            .reshape(narrow, text_local, text_cols),
-            "fsdp",
-        )
-        .transpose(1, 0, 2)
-        .reshape(text_local, caption_width)
-        .astype(F32)
-    )
-    text_state_unit = text_in * text_inverse
-    grad_text_gain = jnp.sum(grad_text_normed * text_state_unit, axis=0)
-    grad_text = (
-        norm_pull(grad_text_normed * text_gain, text_state_unit, text_inverse)
-        .astype(BF16)
-        .reshape(image_count, caption_local, caption_width)
-    )
-
+    grad_gate_up_weight = added(z_pieces(by_z(gate_up_part), deep))
+    last, came_text_z = lax.optimization_barrier((backs[-1][0], came_text_z))
+    backs[-1] = (last, *backs[-1][1:])
+    text_part = jnp.sum(came_text_z.astype(F32), axis=0).astype(BF16)
+    came_out_z = exchange(by_z(out_part), "z")
     own_gate_grad = jnp.sum(gate_sums[:, 0, :].reshape(pairs * halves, head_dim), axis=1)[:heads_here]
     grad_head_gate = lax.dynamic_update_slice_in_dim(
         jnp.zeros((head_count,), F32), own_gate_grad, me * heads_here, 0
@@ -1107,8 +1099,8 @@
         list(zip(*backs)), projected, stats_all, cosine, sine, head_gains, part,
         lambda value: fsdp_share(value, narrow, 4),
     )
-    grad_projected_low, grad_gate_up_weight, text_part, out_part = lax.optimization_barrier(
-        (grad_projected_low, grad_gate_up_weight, text_part, out_part)
+    grad_projected_low, grad_gate_up_weight, came_out_z = lax.optimization_barrier(
+        (grad_projected_low, grad_gate_up_weight, came_out_z)
     )
     everyone = ("z", "core", "fsdp")
     grad_text_weight = lax.ppermute(
@@ -1118,16 +1110,54 @@
             ((z * 2 + c) * narrow + f, f * wide + c * deep + z)
             for z in range(deep) for c in range(2) for f in range(narrow)
         ],
-    ).astype(F32)
-    grad_out_weight = z_sum(by_z(out_part), deep)
+    )
+    grad_out_weight = jnp.sum(came_out_z.astype(F32), axis=0)
     grad_normed = lax.psum_scatter(
         times_transposed(grad_projected_low, own_qkv).astype(BF16), "fsdp", scatter_dimension=0, tiled=True
-    ).astype(F32)
+    )
 
     qkv_grad = outer_sum(normed_all, grad_projected_low).astype(BF16).reshape(deep, 2, model_width // wide, 3 * part_pad)
     own_grad, other_grad = by_core(qkv_grad[:, 0], qkv_grad[:, 1])
-    own_grad = own_grad.astype(F32) + core_swap(other_grad).astype(F32)
-    own_grad = z_sum(own_grad.astype(BF16), deep)
+    own_grad = (own_grad.astype(F32) + core_swap(other_grad).astype(F32)).astype(BF16)
+    own_grad, grad_text_columns = lax.optimization_barrier((own_grad, grad_text_columns))
+    own_pieces = z_pieces(own_grad, deep)
+    grad_text_slice = times_transposed(grad_text_columns, text_weight).astype(BF16)
+    came_text = exchange(
+            grad_text_slice.reshape(image_count, narrow, caption_local, text_cols)
+            .transpose(1, 0, 2, 3)
+            .reshape(narrow, text_local, text_cols),
+            "fsdp",
+        )
+
+    def placed_columns(value):
+        return lax.dynamic_update_slice_in_dim(
+            jnp.zeros((model_width,), F32), narrowed(value, 1), me * part, 0
+        )
+
+    group = lax.axis_index("z") * 2 + lax.axis_index("core")
+    later_modulation = jnp.concatenate([grad_gate_attend, grad_scale_feed, grad_gate_feed], axis=1)
+    summed = jnp.concatenate(
+        [
+            grad_gain_one,
+            placed_columns(head_sums[0]),
+            placed_columns(head_sums[2]),
+            placed_columns(own_gain_four),
+            grad_gain_five,
+            grad_gain_six,
+            placed_columns(head_sums[1]),
+            placed_columns(head_sums[3]),
+            grad_head_gate,
+        ]
+    )
+    kept = jnp.concatenate(
+        [later_modulation.reshape(-1), jnp.where(me == 0, cond_low.astype(F32), 0.0).reshape(-1)]
+    )
+    summed, kept = finish(summed, kept, narrow, wide, 5)
+    summed, kept, came_text, grad_text_weight, *own_pieces = lax.optimization_barrier(
+        (summed, kept, came_text, grad_text_weight, *own_pieces)
+    )
+    grad_text_weight = grad_text_weight.astype(F32)
+    own_grad = added(own_pieces)
     grad_qkv_weight = (
         exchange(narrowed(own_grad.astype(BF16), 3).reshape(narrow, -1, 3 * part), "fsdp")
         .reshape(narrow, -1, 3, part)
@@ -1135,6 +1165,29 @@
         .reshape(-1, 3 * model_width)
         .astype(F32)
     )
+
+    grad_text_normed = (
+        came_text
+        .transpose(1, 0, 2)
+        .reshape(text_local, caption_width)
+        .astype(F32)
+    )
+    text_state_unit = text_in * text_inverse
+    grad_text_gain = jnp.sum(grad_text_normed * text_state_unit, axis=0)
+    grad_text = (
+        norm_pull(grad_text_normed * text_gain, text_state_unit, text_inverse)
+        .astype(BF16)
+        .reshape(image_count, caption_local, caption_width)
+    )
+
+    every_image = wide * image_count
+    ada_rows = cond_rows // wide
+    slots = kept[:, : later_modulation.size].reshape(every_image, later_modulation.shape[1])
+    cond_slots = kept[:, later_modulation.size :].reshape(every_image, cond_low.shape[1])
+    own_cond = lax.dynamic_slice_in_dim(cond_slots, (group * narrow + me) * ada_rows, ada_rows, 1)
+    ada_later = exact_outer(own_cond, slots)
+    grad_normed, ada_later, own_cond = lax.optimization_barrier((grad_normed, ada_later, own_cond))
+    grad_normed = grad_normed.astype(F32)
 
     token_unit = token_in * token_inverse
     scale_attend = 1.0 + per_token(0)
@@ -1144,49 +1197,18 @@
     grad_tokens = (
         grad_hidden + norm_pull(grad_normed_y * norm_gains[0], token_unit, token_inverse)
     ).astype(BF16)
-
-    def placed_columns(value):
-        return lax.dynamic_update_slice_in_dim(
-            jnp.zeros((model_width,), F32), narrowed(value, 1), me * part, 0
-        )
-
-    grad_modulation = jnp.concatenate(
-        [grad_scale_attend, grad_gate_attend, grad_scale_feed, grad_gate_feed], axis=1
-    )
-    group = lax.axis_index("z") * 2 + lax.axis_index("core")
-    summed = jnp.concatenate(
-        [
-            grad_gain_zero,
-            grad_gain_one,
-            placed_columns(head_sums[0]),
-            placed_columns(head_sums[2]),
-            placed_columns(own_gain_four),
-            grad_gain_five,
-            grad_gain_six,
-            placed_columns(head_sums[1]),
-            placed_columns(head_sums[3]),
-            grad_text_gain,
-            grad_head_gate,
-        ]
-    )
-    kept = jnp.concatenate(
-        [grad_modulation.reshape(-1), jnp.where(me == 0, cond_low.astype(F32), 0.0).reshape(-1)]
-    )
-    summed, kept = finish(summed, kept, narrow, wide, 5)
-    gain_count = norm_gains.size
+    last_sums, first_slots = finish(
+        jnp.concatenate([grad_gain_zero, grad_text_gain]), grad_scale_attend.reshape(-1), narrow, wide, 6
+    )
+    grad_text_gain = last_sums[model_width:]
+    first_slots = first_slots.reshape(every_image, model_width)
+    grad_ada_weight = jnp.concatenate([exact_outer(own_cond, first_slots), ada_later], axis=1)
+    grad_ada_bias = jnp.concatenate([jnp.sum(first_slots, axis=0), jnp.sum(slots, axis=0)])
+    gain_count = norm_gains.size - model_width
     shift_end = gain_count + norm_shifts.size
-    text_end = shift_end + text_gain.size
-    grad_gains = summed[:gain_count].reshape(norm_gains.shape)
+    grad_gains = jnp.concatenate([last_sums[:model_width], summed[:gain_count]]).reshape(norm_gains.shape)
     grad_shifts = summed[gain_count:shift_end].reshape(norm_shifts.shape)
-    grad_text_gain = summed[shift_end:text_end]
-    grad_head_gate = summed[text_end:]
-    every_image = wide * image_count
-    slots = kept[:, : grad_modulation.size].reshape(every_image, grad_modulation.shape[1])
-    cond_slots = kept[:, grad_modulation.size :].reshape(every_image, cond_low.shape[1])
-    grad_ada_bias = jnp.sum(slots, axis=0)
-    ada_rows = cond_rows // wide
-    own_cond = lax.dynamic_slice_in_dim(cond_slots, (group * narrow + me) * ada_rows, ada_rows, 1)
-    grad_ada_weight = exact_outer(own_cond, slots)
+    grad_head_gate = summed[shift_end:]
     return (
         result[None],
         grad_tokens[None],

time: 1150 us -> 1150 us (level)
  waiting for transfers between devices: 117 us -> 75.8 us
  local copies, waits for them, and re-layouts: 99.5 us -> 121 us
  Pallas kernels: 467 us -> 483 us
  other arithmetic: 112 us -> 126 us
  starting transfers between devices: 85.7 us -> 73.2 us
    ppermute x12 -> x6, waiting for transfers between devices: 48.8 us -> 0.02 us  [z_pieces(): lax.ppermute(lax.dynamic_index_in_dim(blocks, me ^ step, 0, keepdims=Fals...]
    ppermute x12 -> x6, starting transfers between devices: 34.6 us -> 8.78 us  [z_pieces(): lax.ppermute(lax.dynamic_index_in_dim(blocks, me ^ step, 0, keepdims=Fals...]
    pallas_call x1 -> x2, Pallas kernels: 52 us -> 69 us  [finish(): pl.pallas_call(functools.partial(finish_kernel, narrow, wide, sum_rows),...]
    ppermute x3, waiting for transfers between devices: 3.13 us -> 19 us  [to_all(): lax.ppermute(block, 'fsdp', [(i, i ^ step) for i in range(narrow)])]
    all_to_all x10 -> x12, waiting for transfers between devices: 52.3 us -> 43.2 us  [exchange(): return lax.all_to_all(blocks, axis, 0, 0, tiled=True)]
    all_to_all x10 -> x12, starting transfers between devices: 44.7 us -> 52.4 us  [exchange(): return lax.all_to_all(blocks, axis, 0, 0, tiled=True)]
    unnamed x276 -> x232, local copies, waits for them, and re-layouts: 20.7 us -> 28.4 us
  transfers between devices with their start and end apart: 40 -> 36, of which waited for: 13 -> 10; matrix products, arithmetic and copies ran while one was open for 33% -> 35% of each run, Pallas kernels for 36% -> 41%
where the time goes in v4:
time: 1150 us; the launch traced here: 1140 us
  Pallas kernels  483 us (42%)
  matrix products  239 us (21%)
  other arithmetic  126 us (11%)
  local copies, waits for them, and re-layouts  121 us (11%)
  waiting for transfers between devices  75.8 us (7%)
  starting transfers between devices  73.2 us (6%)
  between operations  18.8 us (2%)
    pallas_call x3, Pallas kernels, self_back(): pl.pallas_call(functools.partial(self_back_kernel, head_dim, FIRST_PATCHE...  137 us
    pallas_call x3, Pallas kernels, attend(): pl.pallas_call(functools.partial(attend_kernel, head_dim, FIRST_PATCHES,...  91.8 us
    dot_general x9, matrix products, outer_sum(): lax.dot_general(left, right, (((0,), (0,)), ((), ())), preferred_element_...  83.1 us
    dot_general x11, matrix products, low_product(): return jnp.dot(left, right, preferred_element_type=F32)  77.3 us
    dot_general x5, matrix products, times_transposed(): lax.dot_general(left, right, (((1,), (1,)), ((), ())), preferred_element_...  74.8 us
    pallas_call x2, Pallas kernels, finish(): pl.pallas_call(functools.partial(finish_kernel, narrow, wide, sum_rows),...  69 us
    pallas_call x5, Pallas kernels, fsdp_share(): pl.pallas_call(functools.partial(fsdp_share_kernel, narrow), in_specs=[pl...  63.7 us
    all_to_all x12, starting transfers between devices, exchange(): return lax.all_to_all(blocks, axis, 0, 0, tiled=True)  52.4 us
  transfers between devices with their start and end apart: 36, of which 10 were waited for; matrix products, arithmetic and copies ran while one was open for 35% of the time, Pallas kernels for 41%

profile of v4, /device:TPU:0, one launch (start us, length us, event | category | flops | bytes accessed | tf_op | source)
XLA Modules:
  0.0 1137.1 jit_solution(1256473165603293814)
XLA Ops:
  40.9 26.8 %shard_map.263 = f32[4,96,128]{2,1,0:T(8,128)} custom-call(f32[96,128]{1,0:T(8,128)} %reshape.628.x_ref), custom_call_target="tpu_custom_call" | custom-call | bytes 393216 | tf_op jit(solution)/shard_map/pallas_call | solution.py:648
  75.9 10.6 negate_select_fusion
  150.5 13.6 %fusion.157.projected_ref.refs_6_.refs_9_ = f32[2624,1152]{1,0:T(8,128)} fusion(bf16[2624,1536]{1,0:T(8,128)(2,1)S(1)} %fusion.3, bf16[1536,1152]{1,0:T(8,128)(2,1)S(1)} %bitcast.241), kind=kOutput, calls=%fused_computation.374 | convolution fusion | flops 9286189056 | bytes 23691264 | tf_op jit(solution)/shard_map/dot_general | solution.py:28
  164.0 9.4 shard_map.264.x_ref
  173.4 16.2 %shard_map.265.stats_ref.refs_7_.refs_10_ = f32[4,8,2624]{2,1,0:T(8,128)} custom-call(f32[8,2624]{1,0:T(8,128)} %shard_map.264.x_ref), custom_call_target="tpu_custom_call" | custom-call | bytes 671744 | tf_op jit(solution)/shard_map/pallas_call | solution.py:648
  189.6 15.5 %shard_map.266.q_ref.k_ref.v_ref = bf16[2624,1152]{1,0:T(8,128)(2,1)} custom-call(f32[2624,1152]{1,0:T(8,128)} %fusion.157.projected_ref.refs_6_.refs_9_, f32[4,8,2624]{2,1,0:T(8,128)} %shard_map.265.stats_ref.refs_7_.refs_10_, f32[2624,128]{1,0:T(8,128)} %get-tuple-element.230.cos_ref.refs_8_.refs_12_, ...), custom_call_target="tpu_custom_call" | custom-call | flops 120913920 | bytes 18137088 | tf_op jit(solution)/shard_map/pallas_call | solution.py:183
  221.8 31.0 %shard_map.271 = (bf16[2624,128]{1,0:T(8,128)(2,1)}, f32[2624,128]{1,0:T(8,128)}, f32[2624,128]{1,0:T(8,128)}, f32[8,2624]{1,0:T(8,128)}) custom-call(f32[3,1,2]{2,1,0:T(1,128)} %reshape.682.gate_ref, bf16[2624,1152]{1,0:T(8,128)(2,1)} %shard_map.266.q_ref.k_ref.v_ref, bf16[2624,1152]{1,0:T(8,128)(2,1)} %shard_map.266.q_ref.k_ref.v_ref, ...), custom_call_target="tpu_custom_call" | custom-call | flops 4213178368 | bytes 6717440 | tf_op jit(solution)/shard_map/pallas_call | solution.py:379
  256.5 30.4 %shard_map.270 = (bf16[2624,128]{1,0:T(8,128)(2,1)}, f32[2624,128]{1,0:T(8,128)}, f32[2624,128]{1,0:T(8,128)}, f32[8,2624]{1,0:T(8,128)}) custom-call(f32[3,1,2]{2,1,0:T(1,128)} %reshape.682.gate_ref, bf16[2624,1152]{1,0:T(8,128)(2,1)} %shard_map.266.q_ref.k_ref.v_ref, bf16[2624,1152]{1,0:T(8,128)(2,1)} %shard_map.266.q_ref.k_ref.v_ref, ...), custom_call_target="tpu_custom_call" | custom-call | flops 4213178368 | bytes 6717440 | tf_op jit(solution)/shard_map/pallas_call | solution.py:379
  291.2 30.4 %shard_map.269 = (bf16[2624,128]{1,0:T(8,128)(2,1)}, f32[2624,128]{1,0:T(8,128)}, f32[2624,128]{1,0:T(8,128)}, f32[8,2624]{1,0:T(8,128)}) custom-call(f32[3,1,2]{2,1,0:T(1,128)} %reshape.682.gate_ref, bf16[2624,1152]{1,0:T(8,128)(2,1)} %shard_map.266.q_ref.k_ref.v_ref, bf16[2624,1152]{1,0:T(8,128)(2,1)} %shard_map.266.q_ref.k_ref.v_ref, ...), custom_call_target="tpu_custom_call" | custom-call | flops 4213178368 | bytes 6717440 | tf_op jit(solution)/shard_map/pallas_call | solution.py:379
  326.0 16.1 %all-to-all-done.3 = bf16[4,656,128]{2,1,0:T(8,128)(2,1)} async-done(((bf16[4,656,128]{2,1,0:T(8,128)(2,1)}), bf16[4,656,128]{2,1,0:T(8,128)(2,1)}, u32[]{:S(2)}, u32[]{:S(2)}) %all-to-all-start.3) | async-done | bytes 671776 | tf_op jit(solution)/shard_map/all_to_all | solution.py:738
  366.6 26.5 %fusion.158.gate_ref.up_ref = f32[656,8192]{1,0:T(8,128)} fusion(bf16[656,1536]{1,0:T(8,128)(2,1)} %copy-done.29, bf16[1536,8192]{1,0:T(8,128)(2,1)} %all-gather.8.cloned.1.call-done), kind=kOutput, calls=%fused_computation.375 | convolution fusion | flops 16508780544 | bytes 48676864 | tf_op jit(solution)/shard_map/dot_general | solution.py:28
  393.1 23.1 %shard_map.272 = (bf16[656,4096]{1,0:T(8,128)(2,1)}, bf16[656,4096]{1,0:T(8,128)(2,1)}) custom-call(s32[1]{0:T(128)} %bitcast.29.core_ref, f32[656,8192]{1,0:T(8,128)} %fusion.158.gate_ref.up_ref, f32[656,8192]{1,0:T(8,128)} %fusion.158.gate_ref.up_ref), custom_call_target="tpu_custom_call" | custom-call | flops 16121856 | bytes 32243712 | tf_op jit(solution)/shard_map/pallas_call | solution.py:602
  419.7 13.1 %multiply_reduce_fusion.14 = (f32[656]{0:T(1024)S(1)}, f32[656,1536]{1,0:T(8,128)S(1)}) fusion(bf16[656,4096]{1,0:T(8,128)(2,1)} %get-tuple-element.92, bf16[4096,1536]{1,0:T(8,128)(2,1)} %all-gather.10.cloned.1.call-done), kind=kOutput, calls=%fused_computation.67 | convolution fusion | flops 8256404992 | bytes 21989952 | tf_op jit(solution)/shard_map/dot_general | solution.py:28
  449.3 20.8 %fusion.6 = (bf16[656,4096]{1,0:T(8,128)(2,1)}, bf16[656,4096]{1,0:T(8,128)(2,1)}) fusion(f32[656,8192]{1,0:T(8,128)} %fusion.158.gate_ref.up_ref, bf16[656,1536]{1,0:T(8,128)(2,1)S(1)} %get-tuple-element.213, bf16[4096,1536]{1,0:T(8,128)(2,1)} %all-gather.10.cloned.1.call-done), kind=kOutput, calls=%fused_computation.13 | convolution fusion | flops 8289320960 | bytes 46841856 | tf_op jit(solution)/shard_map/dot_general | solution.py:32
  470.2 17.2 %convolution_convert_fusion = bf16[768,8192]{1,0:T(8,128)(2,1)} fusion(bf16[656,4096]{1,0:T(8,128)(2,1)} %get-tuple-element.208, bf16[656,4096]{1,0:T(8,128)(2,1)} %get-tuple-element.207, bf16[656,1536]{1,0:T(8,128)(2,1)} %fusion.29), kind=kOutput, calls=%fused_computation.7 | convolution fusion | flops 8282177536 | bytes 24338432 | tf_op jit(solution)/shard_map/dot_general | solution.py:36
  487.6 10.1 add_convert_fusion.1
  498.5 28.6 %multiply_reduce_fusion.9 = (f32[1536]{0:T(1024)}, f32[656]{0:T(1024)S(1)}, f32[1536]{0:T(1024)}, f32[1536]{0:T(1024)}, f32[656,1536]{1,0:T(8,128)}) fusion(f32[656,1536]{1,0:T(8,128)} %copy-done.5, f32[656]{0:T(1024)S(1)} %copy-done.83, f32[1536]{0:T(1024)S(1)} %copy-done.64, f32[656]{0:T(1024)S(1)} %get-tuple-element.245, f32[1536]{0:T(1024)S(1)} %copy-done.66, ...), kind=kOutput, calls=%fused_computation.59 | convolution fusion | flops 16547399680 | bytes 44022016 | tf_op jit(solution)/shard_map/dot_general | solution.py:32
  558.6 18.3 %add_convert_fusion = bf16[768,8192]{1,0:T(8,128)(2,1)} fusion(bf16[768,8192]{1,0:T(8,128)(2,1)} %collective-permute-done.1, bf16[656,4096]{1,0:T(8,128)(2,1)} %get-tuple-element.208, bf16[656,4096]{1,0:T(8,128)(2,1)} %get-tuple-element.207, bf16[656,1536]{1,0:T(8,128)(2,1)} %fusion.29), kind=kOutput, calls=%fused_computation | convolution fusion | flops 8294760448 | bytes 36921344 | tf_op jit(solution)/shard_map/dot_general | solution.py:36
  576.9 10.9 all-to-all-done.6
  595.0 13.3 %shard_map.275 = (bf16[2624,128]{1,0:T(8,128)(2,1)}, bf16[512,128]{1,0:T(8,128)(2,1)}, bf16[512,128]{1,0:T(8,128)(2,1)}, f32[8,128]{1,0:T(8,128)}) custom-call(f32[3,1,2]{2,1,0:T(1,128)} %reshape.682.gate_ref, bf16[2624,1152]{1,0:T(8,128)(2,1)} %shard_map.266.q_ref.k_ref.v_ref, bf16[512,768]{1,0:T(8,128)(2,1)} %pad_maximum_fusion.8.tk_ref.tv_ref, ...), custom_call_target="tpu_custom_call" | custom-call | flops 1719664640 | bytes 4030464 | tf_op jit(solution)/shard_map/pallas_call | solution.py:495
  608.3 13.3 %shard_map.274 = (bf16[2624,128]{1,0:T(8,128)(2,1)}, bf16[512,128]{1,0:T(8,128)(2,1)}, bf16[512,128]{1,0:T(8,128)(2,1)}, f32[8,128]{1,0:T(8,128)}) custom-call(f32[3,1,2]{2,1,0:T(1,128)} %reshape.682.gate_ref, bf16[2624,1152]{1,0:T(8,128)(2,1)} %shard_map.266.q_ref.k_ref.v_ref, bf16[512,768]{1,0:T(8,128)(2,1)} %pad_maximum_fusion.8.tk_ref.tv_ref, ...), custom_call_target="tpu_custom_call" | custom-call | flops 1719664640 | bytes 4030464 | tf_op jit(solution)/shard_map/pallas_call | solution.py:495
  621.7 13.4 %shard_map.273 = (bf16[2624,128]{1,0:T(8,128)(2,1)}, bf16[512,128]{1,0:T(8,128)(2,1)}, bf16[512,128]{1,0:T(8,128)(2,1)}, f32[8,128]{1,0:T(8,128)}) custom-call(f32[3,1,2]{2,1,0:T(1,128)} %reshape.682.gate_ref, bf16[2624,1152]{1,0:T(8,128)(2,1)} %shard_map.266.q_ref.k_ref.v_ref, bf16[512,768]{1,0:T(8,128)(2,1)} %pad_maximum_fusion.8.tk_ref.tv_ref, ...), custom_call_target="tpu_custom_call" | custom-call | flops 1719664640 | bytes 4030464 | tf_op jit(solution)/shard_map/pallas_call | solution.py:495
  654.1 45.6 %shard_map.277 = (bf16[2624,128]{1,0:T(8,128)(2,1)}, bf16[2624,128]{1,0:T(8,128)(2,1)}, bf16[2624,128]{1,0:T(8,128)(2,1)}) custom-call(bf16[2624,1152]{1,0:T(8,128)(2,1)} %shard_map.266.q_ref.k_ref.v_ref, bf16[2624,1152]{1,0:T(8,128)(2,1)} %shard_map.266.q_ref.k_ref.v_ref, bf16[2624,1152]{1,0:T(8,128)(2,1)} %shard_map.266.q_ref.k_ref.v_ref, ...), custom_call_target="tpu_custom_call" | custom-call | flops 8813281280 | bytes 10076160 | tf_op jit(solution)/shard_map/pallas_call | solution.py:562
  699.7 19.0 %collective-permute-done.6 = bf16[512,768]{1,0:T(8,128)(2,1)} collective-permute-done((bf16[512,768]{1,0:T(8,128)(2,1)}, bf16[512,768]{1,0:T(8,128)(2,1)}, u32[]{:S(2)}, u32[]{:S(2)}) %collective-permute-start.6) | collective-permute-done | bytes 786464 | tf_op jit(solution)/shard_map/ppermute | solution.py:780
  746.4 45.5 %shard_map.278 = (bf16[2624,128]{1,0:T(8,128)(2,1)}, bf16[2624,128]{1,0:T(8,128)(2,1)}, bf16[2624,128]{1,0:T(8,128)(2,1)}) custom-call(bf16[2624,1152]{1,0:T(8,128)(2,1)} %shard_map.266.q_ref.k_ref.v_ref, bf16[2624,1152]{1,0:T(8,128)(2,1)} %shard_map.266.q_ref.k_ref.v_ref, bf16[2624,1152]{1,0:T(8,128)(2,1)} %shard_map.266.q_ref.k_ref.v_ref, ...), custom_call_target="tpu_custom_call" | custom-call | flops 8813281280 | bytes 10076160 | tf_op jit(solution)/shard_map/pallas_call | solution.py:562
  799.3 45.6 %shard_map.279 = (bf16[2624,128]{1,0:T(8,128)(2,1)}, bf16[2624,128]{1,0:T(8,128)(2,1)}, bf16[2624,128]{1,0:T(8,128)(2,1)}) custom-call(bf16[2624,1152]{1,0:T(8,128)(2,1)} %shard_map.266.q_ref.k_ref.v_ref, bf16[2624,1152]{1,0:T(8,128)(2,1)} %shard_map.266.q_ref.k_ref.v_ref, bf16[2624,1152]{1,0:T(8,128)(2,1)} %shard_map.266.q_ref.k_ref.v_ref, ...), custom_call_target="tpu_custom_call" | custom-call | flops 8813281280 | bytes 10076160 | tf_op jit(solution)/shard_map/pallas_call | solution.py:562
  852.1 16.3 %shard_map.280 = (f32[8,2624]{1,0:T(8,128)}, f32[8,384]{1,0:T(8,128)}) custom-call(bf16[2624,128]{1,0:T(8,128)(2,1)} %get-tuple-element.115.refs_0_, bf16[2624,128]{1,0:T(8,128)(2,1)} %get-tuple-element.122.refs_1_, bf16[2624,128]{1,0:T(8,128)(2,1)} %get-tuple-element.128.refs_2_, bf16[2624,128]{1,0:T(8,128)(2,1)} %get-tuple-element.129.refs_3_, ...), custom_call_target="tpu_custom_call" | custom-call | flops 120913920 | bytes 15114240 | tf_op jit(solution)/shard_map/pallas_call | solution.py:269
  880.3 15.6 %shard_map.282 = bf16[2624,1152]{1,0:T(8,128)(2,1)} custom-call(bf16[2624,128]{1,0:T(8,128)(2,1)} %get-tuple-element.115.refs_0_, bf16[2624,128]{1,0:T(8,128)(2,1)} %get-tuple-element.122.refs_1_, bf16[2624,128]{1,0:T(8,128)(2,1)} %get-tuple-element.128.refs_2_, bf16[2624,128]{1,0:T(8,128)(2,1)} %get-tuple-element.129.refs_3_, ...), custom_call_target="tpu_custom_call" | custom-call | flops 120913920 | bytes 21159936 | tf_op jit(solution)/shard_map/pallas_call | solution.py:282
  899.4 15.4 %convolution_convert_fusion.1 = bf16[2624,1536]{1,0:T(8,128)(2,1)} fusion(bf16[2624,1152]{1,0:T(8,128)(2,1)} %shard_map.282, bf16[1536,1152]{1,0:T(8,128)(2,1)S(1)} %bitcast.242), kind=kOutput, calls=%fused_computation.9 | convolution fusion | flops 9290219520 | bytes 17645568 | tf_op jit(solution)/shard_map/dot_general | solution.py:32
  916.9 15.4 %convolution_convert_fusion.3 = bf16[1536,1152]{1,0:T(8,128)(2,1)S(1)} fusion(bf16[2624,1536]{1,0:T(8,128)(2,1)} %copy-done.20, bf16[2624,1152]{1,0:T(8,128)(2,1)} %shard_map.282), kind=kOutput, calls=%fused_computation.21 | convolution fusion | flops 9287958528 | bytes 17645568 | tf_op jit(solution)/shard_map/dot_general | solution.py:36
  995.3 51.3 %shard_map.283 = f32[4,224,128]{2,1,0:T(8,128)} custom-call(f32[4,56,128]{2,1,0:T(8,128)} %pad_maximum_fusion.12.x_ref), custom_call_target="tpu_custom_call" | custom-call | tf_op jit(solution)/shard_map/pallas_call | solution.py:719
  1088.8 17.7 %shard_map.284 = f32[4,80,128]{2,1,0:T(8,128)} custom-call(f32[4,24,128]{2,1,0:T(8,128)} %pad_maximum_fusion.13.x_ref), custom_call_target="tpu_custom_call" | custom-call | tf_op jit(solution)/shard_map/pallas_call | solution.py:719
  (506 shorter events, 422.1 us)
Async XLA Ops:
  7.2 122.6 %all-gather.12.cloned.1.call-start = ((), (), s32[]{:S(2)}) async-start(), calls=%async_computation.23 | async-start | bytes 10076160 | tf_op jit(solution)/shard_map/all_gather | solution.py:885
  7.9 337.0 %all-gather.6.cloned.1.call-start = ((), (), s32[]{:S(2)}) async-start(), calls=%async_computation.16 | async-start | bytes 5308416 | tf_op jit(solution)/shard_map/all_gather | solution.py:813
  10.2 356.5 %all-gather.8.cloned.1.call-start = ((), (), s32[]{:S(2)}) async-start(), calls=%async_computation.17 | async-start | bytes 28311552 | tf_op jit(solution)/shard_map/all_gather | solution.py:813
  25.0 61.4 %all-to-all-start.1 = ((bf16[4,192,1152]{2,1,0:T(8,128)(2,1)}), bf16[4,192,1152]{2,1,0:T(8,128)(2,1)}, u32[]{:S(2)}, u32[]{:S(2)}) async-start(bf16[4,192,1152]{2,1,0:T(8,128)(2,1)} %reshape.635), calls=%async_computation.1 | async-start | bytes 3538944 | tf_op jit(solution)/shard_map/all_to_all | solution.py:738
  30.3 389.4 %all-gather.10.cloned.1.call-start = ((), (), s32[]{:S(2)}) async-start(), calls=%async_computation.18 | async-start | bytes 14155776 | tf_op jit(solution)/shard_map/all_gather | solution.py:813
  86.4 29.6 %all-to-all-start = ((bf16[4,128,1024]{2,1,0:T(8,128)(2,1)}), bf16[4,128,1024]{2,1,0:T(8,128)(2,1)S(1)}, u32[]{:S(2)}, u32[]{:S(2)}) async-start(bf16[4,128,1024]{2,1,0:T(8,128)(2,1)} %fusion.50), calls=%async_computation | async-start | bytes 2097152 | tf_op jit(solution)/shard_map/all_to_all | solution.py:738
  129.8 75.3 %all-to-all-start.2 = ((bf16[4,512,768]{2,1,0:T(8,128)(2,1)}), bf16[4,512,768]{2,1,0:T(8,128)(2,1)}, u32[]{:S(2)}, u32[]{:S(2)}) async-start(bf16[4,512,768]{2,1,0:T(8,128)(2,1)} %pad_maximum_fusion.2), calls=%async_computation.2 | async-start | bytes 6291456 | tf_op jit(solution)/shard_map/all_to_all | solution.py:738
  252.9 34.0 %all-to-all-start.5 = ((bf16[4,656,128]{2,1,0:T(8,128)(2,1)}), bf16[4,656,128]{2,1,0:T(8,128)(2,1)S(1)}, u32[]{:S(2)}, u32[]{:S(2)}) async-start(bf16[4,656,128]{2,1,0:T(8,128)(2,1)} %bitcast.268), calls=%async_computation.5 | async-start | bytes 1343488 | tf_op jit(solution)/shard_map/all_to_all | solution.py:738
  286.9 34.8 %all-to-all-start.4 = ((bf16[4,656,128]{2,1,0:T(8,128)(2,1)}), bf16[4,656,128]{2,1,0:T(8,128)(2,1)S(1)}, u32[]{:S(2)}, u32[]{:S(2)}) async-start(bf16[4,656,128]{2,1,0:T(8,128)(2,1)} %bitcast.267), calls=%async_computation.4 | async-start | bytes 1343488 | tf_op jit(solution)/shard_map/all_to_all | solution.py:738
  321.6 20.5 %all-to-all-start.3 = ((bf16[4,656,128]{2,1,0:T(8,128)(2,1)}), bf16[4,656,128]{2,1,0:T(8,128)(2,1)}, u32[]{:S(2)}, u32[]{:S(2)}) async-start(bf16[4,656,128]{2,1,0:T(8,128)(2,1)} %bitcast.266), calls=%async_computation.3 | async-start | bytes 1343488 | tf_op jit(solution)/shard_map/all_to_all | solution.py:738
  325.9 263.5 %reduce-scatter.5.cloned.1.call-start = ((), (), s32[]{:S(2)}) async-start(), calls=%async_computation.19 | async-start | bytes 7864320 | tf_op jit(solution)/shard_map/reduce_scatter | solution.py:761
  449.1 38.5 %collective-permute-start.3 = (bf16[2048,1536]{1,0:T(8,128)(2,1)}, bf16[2048,1536]{1,0:T(8,128)(2,1)}, u32[]{:S(2)}, u32[]{:S(2)}) collective-permute-start(bf16[2048,1536]{1,0:T(8,128)(2,1)} %convolution_convert_fusion.2), channel_id=1, source_target_pairs={{0,4},{4,0},{1,5},{5,1},{2,6},{6,2},{3,7},{7,3},{8,12},{12,8},{9,1... | collective-permute-start | bytes 18874376 | tf_op jit(solution)/shard_map/ppermute | solution.py:742
  487.3 71.3 %collective-permute-start.1 = (bf16[768,8192]{1,0:T(8,128)(2,1)}, bf16[768,8192]{1,0:T(8,128)(2,1)}, u32[]{:S(2)}, u32[]{:S(2)}) collective-permute-start(bf16[768,8192]{1,0:T(8,128)(2,1)} %convolution_convert_fusion), channel_id=1, source_target_pairs={{0,4},{4,0},{1,5},{5,1},{2,6},{6,2},{3,7},{7,3},{8,12},{12,8},{9,1... | collective-permute-start | bytes 37748744 | tf_op jit(solution)/shard_map/ppermute | solution.py:742
  548.9 38.9 %all-to-all-start.6 = ((bf16[4,656,384]{2,1,0:T(8,128)(2,1)}), bf16[4,656,384]{2,1,0:T(8,128)(2,1)S(1)}, u32[]{:S(2)}, u32[]{:S(2)}) async-start(bf16[4,656,384]{2,1,0:T(8,128)(2,1)} %bitcast.236), calls=%async_computation.6 | async-start | bytes 4030464 | tf_op jit(solution)/shard_map/all_to_all | solution.py:738
  552.5 239.3 %reduce-scatter.9.cloned.1.call-start = ((), (), s32[]{:S(2)}) async-start(), calls=%async_computation.21 | async-start | bytes 2949120 | tf_op jit(solution)/shard_map/reduce_scatter | solution.py:761
  589.4 202.4 %reduce-scatter.7.cloned.1.call-start = ((), (), s32[]{:S(2)}) async-start(), calls=%async_computation.20 | async-start | bytes 15728640 | tf_op jit(solution)/shard_map/reduce_scatter | solution.py:761
  590.2 128.6 %all-to-all-start.7 = ((bf16[4,128,1536]{2,1,0:T(8,128)(2,1)}), bf16[4,128,1536]{2,1,0:T(8,128)(2,1)}, u32[]{:S(2)}, u32[]{:S(2)}) async-start(bf16[4,128,1536]{2,1,0:T(8,128)(2,1)} %bitcast.257), calls=%async_computation.8 | async-start | bytes 3145728 | tf_op jit(solution)/shard_map/all_to_all | solution.py:738
  648.0 51.7 %collective-permute-start.4 = (bf16[512,768]{1,0:T(8,128)(2,1)}, bf16[512,768]{1,0:T(8,128)(2,1)}, u32[]{:S(2)}, u32[]{:S(2)}) collective-permute-start(bf16[512,768]{1,0:T(8,128)(2,1)} %get-tuple-element.225), channel_id=1, source_target_pairs={{0,1},{1,0},{2,3},{3,2},{4,5},{5,4},{6,7},{7,6},{8,9},{9,8},{10,11... | collective-permute-start | bytes 2359304 | tf_op jit(solution)/shard_map/ppermute | solution.py:780
  649.1 50.7 %collective-permute-start.5 = (bf16[512,768]{1,0:T(8,128)(2,1)}, bf16[512,768]{1,0:T(8,128)(2,1)}, u32[]{:S(2)}, u32[]{:S(2)}) collective-permute-start(bf16[512,768]{1,0:T(8,128)(2,1)} %get-tuple-element.225), channel_id=1, source_target_pairs={{0,2},{1,3},{2,0},{3,1},{4,6},{5,7},{6,4},{7,5},{8,10},{9,11},{10,... | collective-permute-start | bytes 2359304 | tf_op jit(solution)/shard_map/ppermute | solution.py:780
  650.0 68.8 %collective-permute-start.6 = (bf16[512,768]{1,0:T(8,128)(2,1)}, bf16[512,768]{1,0:T(8,128)(2,1)}, u32[]{:S(2)}, u32[]{:S(2)}) collective-permute-start(bf16[512,768]{1,0:T(8,128)(2,1)} %get-tuple-element.225), channel_id=1, source_target_pairs={{0,3},{1,2},{2,1},{3,0},{4,7},{5,6},{6,5},{7,4},{8,11},{9,10},{10,... | collective-permute-start | bytes 2359304 | tf_op jit(solution)/shard_map/ppermute | solution.py:780
  740.9 111.1 %all-to-all-start.8 = ((bf16[4,128,3072]{2,1,0:T(8,128)(2,1)}), bf16[4,128,3072]{2,1,0:T(8,128)(2,1)S(1)}, u32[]{:S(2)}, u32[]{:S(2)}) async-start(bf16[4,128,3072]{2,1,0:T(8,128)(2,1)} %bitcast.246), calls=%async_computation.11 | async-start | bytes 6291456 | tf_op jit(solution)/shard_map/all_to_all | solution.py:738
  794.9 101.0 %collective-permute-start.10 = (bf16[48,8192]{1,0:T(8,128)(2,1)}, bf16[48,8192]{1,0:T(8,128)(2,1)}, u32[]{:S(2)}, u32[]{:S(2)}) collective-permute-start(bf16[48,8192]{1,0:T(8,128)(2,1)} %get-tuple-element.218), channel_id=1, source_target_pairs={{0,24},{8,16},{16,8},{24,0},{1,25},{9,17},{17,9},{25,1},{2,26},{10... | collective-permute-start | bytes 2359304 | tf_op jit(solution)/shard_map/ppermute | solution.py:767
  798.7 97.2 %collective-permute-start.9 = (bf16[48,8192]{1,0:T(8,128)(2,1)}, bf16[48,8192]{1,0:T(8,128)(2,1)}, u32[]{:S(2)}, u32[]{:S(2)}) collective-permute-start(bf16[48,8192]{1,0:T(8,128)(2,1)} %get-tuple-element.219), channel_id=1, source_target_pairs={{0,16},{8,24},{16,0},{24,8},{1,17},{9,25},{17,1},{25,9},{2,18},{10... | collective-permute-start | bytes 2359304 | tf_op jit(solution)/shard_map/ppermute | solution.py:767
  798.7 97.2 %collective-permute-start.8 = (bf16[48,8192]{1,0:T(8,128)(2,1)}, bf16[48,8192]{1,0:T(8,128)(2,1)}, u32[]{:S(2)}, u32[]{:S(2)}) collective-permute-start(bf16[48,8192]{1,0:T(8,128)(2,1)} %get-tuple-element.217), channel_id=1, source_target_pairs={{0,8},{8,0},{16,24},{24,16},{1,9},{9,1},{17,25},{25,17},{2,10},{10... | collective-permute-start | bytes 2359304 | tf_op jit(solution)/shard_map/ppermute | solution.py:767
  876.0 23.4 %all-to-all-start.9 = ((bf16[4,48,1536]{2,1,0:T(8,128)(2,1)}), bf16[4,48,1536]{2,1,0:T(8,128)(2,1)}, u32[]{:S(2)}, u32[]{:S(2)}) async-start(bf16[4,48,1536]{2,1,0:T(8,128)(2,1)} %bitcast.269), calls=%async_computation.12 | async-start | bytes 1179648 | tf_op jit(solution)/shard_map/all_to_all | solution.py:738
  880.2 202.7 %reduce-scatter.11.cloned.1.call-start = ((), (), s32[]{:S(2)}) async-start(), calls=%async_computation.22 | async-start | bytes 10076160 | tf_op jit(solution)/shard_map/reduce_scatter | solution.py:1115
  933.7 40.9 %collective-permute-start.11 = (bf16[4,192,1152]{2,1,0:T(8,128)(2,1)}, bf16[4,192,1152]{2,1,0:T(8,128)(2,1)}, u32[]{:S(2)}, u32[]{:S(2)}) collective-permute-start(bf16[4,192,1152]{2,1,0:T(8,128)(2,1)} %fusion.40), channel_id=1, source_target_pairs={{0,4},{4,0},{1,5},{5,1},{2,6},{6,2},{3,7},{7,3},{8,12},{12,8},{9,1... | collective-permute-start | bytes 5308424 | tf_op jit(solution)/shard_map/ppermute | solution.py:742
  950.2 100.3 %collective-permute-start.12 = (bf16[128,3072]{1,0:T(8,128)(2,1)}, bf16[128,3072]{1,0:T(8,128)(2,1)}, u32[]{:S(2)}, u32[]{:S(2)}) collective-permute-start(bf16[128,3072]{1,0:T(8,128)(2,1)} %reduce_sum.383), channel_id=1, source_target_pairs={{0,0},{1,8},{2,16},{3,24},{4,4},{5,12},{6,20},{7,28},{8,1},{9,9},{... | collective-permute-start | bytes 2359304 | tf_op jit(solution)/shard_map/ppermute | solution.py:1106
  985.4 65.2 %all-to-all-start.10 = ((bf16[4,128,1024]{2,1,0:T(8,128)(2,1)}), bf16[4,128,1024]{2,1,0:T(8,128)(2,1)S(1)}, u32[]{:S(2)}, u32[]{:S(2)}) async-start(bf16[4,128,1024]{2,1,0:T(8,128)(2,1)} %bitcast.239), calls=%async_computation.14 | async-start | bytes 2097152 | tf_op jit(solution)/shard_map/all_to_all | solution.py:738
  990.2 60.3 %collective-permute-start.13 = (bf16[192,1152]{1,0:T(8,128)(2,1)}, bf16[192,1152]{1,0:T(8,128)(2,1)S(1)}, u32[]{:S(2)}, u32[]{:S(2)}) collective-permute-start(bf16[192,1152]{1,0:T(8,128)(2,1)} %get-tuple-element.223), channel_id=1, source_target_pairs={{0,8},{8,0},{16,24},{24,16},{1,9},{9,1},{17,25},{25,17},{2,10},{10... | collective-permute-start | bytes 1327112 | tf_op jit(solution)/shard_map/ppermute | solution.py:767
  991.4 59.1 %collective-permute-start.14 = (bf16[192,1152]{1,0:T(8,128)(2,1)}, bf16[192,1152]{1,0:T(8,128)(2,1)S(1)}, u32[]{:S(2)}, u32[]{:S(2)}) collective-permute-start(bf16[192,1152]{1,0:T(8,128)(2,1)} %get-tuple-element.222), channel_id=1, source_target_pairs={{0,16},{8,24},{16,0},{24,8},{1,17},{9,25},{17,1},{25,9},{2,18},{10... | collective-permute-start | bytes 1327112 | tf_op jit(solution)/shard_map/ppermute | solution.py:767
  994.0 56.5 %collective-permute-start.15 = (bf16[192,1152]{1,0:T(8,128)(2,1)}, bf16[192,1152]{1,0:T(8,128)(2,1)S(1)}, u32[]{:S(2)}, u32[]{:S(2)}) collective-permute-start(bf16[192,1152]{1,0:T(8,128)(2,1)} %get-tuple-element.221), channel_id=1, source_target_pairs={{0,24},{8,16},{16,8},{24,0},{1,25},{9,17},{17,9},{25,1},{2,26},{10... | collective-permute-start | bytes 1327112 | tf_op jit(solution)/shard_map/ppermute | solution.py:767
  (116 other events, 2137.4 us)
Sparse Core Ops, SparseCore 0:
  9.9 119.8 all-gather.11
  131.7 63.9 all-gather.5
  197.6 147.6 all-gather.7
  347.6 72.1 all-gather.9
  497.9 91.4 reduce-scatter.4
  592.3 36.6 reduce-scatter.8
  632.1 155.1 reduce-scatter.6
  915.0 130.5 reduce-scatter.10

commit v5 on v4

--- a/solution.py
+++ b/solution.py
@@ -656,7 +656,25 @@
     )(value)
 
 
-def finish_kernel(narrow, wide, sum_rows, x_ref, out_ref, first_ref, second_ref, sends, recvs):
+def place_rows(items, x_ref, chunk, base):
+    rows = [(ref, row) for ref in items for row in range(ref.shape[0])]
+    at = 0
+    while at < len(rows):
+        ref, row = rows[at]
+        off = at % chunk
+        take = min(ref.shape[0] - row, chunk - off)
+        x_ref[at // chunk, base + off : base + off + take, :] = ref[row : row + take, :]
+        at += take
+    while at < x_ref.shape[0] * chunk:
+        off = at % chunk
+        x_ref[at // chunk, base + off : base + chunk, :] = jnp.zeros((chunk - off, 128), F32)
+        at += chunk - off
+
+
+def finish_kernel(narrow, wide, sum_rows, sum_count, *refs):
+    items, (out_ref, x_ref, first_ref, second_ref, sends, recvs) = refs[:-6], refs[-6:]
+    place_rows(items[:sum_count], x_ref, sum_rows, 0)
+    place_rows(items[sum_count:], x_ref, x_ref.shape[1] - sum_rows, sum_rows)
     me = lax.axis_index("fsdp")
     group = lax.axis_index("z") * 2 + lax.axis_index("core")
     rows = x_ref.shape[1]
@@ -707,31 +725,29 @@
 
 
 def finish(summed, kept, narrow, wide, collective_id):
-    sum_rows = round_up(-(-summed.size // (128 * narrow)), 8)
-    kept_rows = round_up(-(-kept.size // (128 * narrow)), 8)
-
-    def chunked(value, rows):
-        return jnp.pad(value, (0, narrow * rows * 128 - value.size)).reshape(narrow, rows, 128)
-
-    joined = jnp.concatenate([chunked(summed, sum_rows), chunked(kept, kept_rows)], axis=1)
+    sum_total = sum(item.shape[0] for item in summed)
+    kept_total = sum(item.shape[0] for item in kept)
+    sum_rows = round_up(-(-sum_total // narrow), 8)
+    kept_rows = round_up(-(-kept_total // narrow), 8)
     rows = sum_rows + kept_rows
     count = 2 * narrow + wide
     out = pl.pallas_call(
-        functools.partial(finish_kernel, narrow, wide, sum_rows),
-        in_specs=[pl.BlockSpec(memory_space=pltpu.VMEM)],
+        functools.partial(finish_kernel, narrow, wide, sum_rows, len(summed)),
+        in_specs=[pl.BlockSpec(memory_space=pltpu.VMEM)] * (len(summed) + len(kept)),
         out_specs=pl.BlockSpec(memory_space=pltpu.VMEM),
         out_shape=jax.ShapeDtypeStruct((narrow, sum_rows + wide * kept_rows, 128), F32),
         scratch_shapes=[
+            pltpu.VMEM((narrow, rows, 128), F32),
             pltpu.VMEM((narrow, rows, 128), F32),
             pltpu.VMEM((wide, rows, 128), F32),
             pltpu.SemaphoreType.DMA((count,)),
             pltpu.SemaphoreType.DMA((count,)),
         ],
         compiler_params=pltpu.CompilerParams(collective_id=collective_id, has_side_effects=True),
-    )(joined)
-    total = out[:, :sum_rows, :].reshape(-1)[: summed.size]
-    groups = out[:, sum_rows:, :].reshape(narrow, wide, kept_rows * 128).transpose(1, 0, 2)
-    return total, groups.reshape(wide, -1)[:, : kept.size]
+    )(*summed, *kept)
+    total = out[:, :sum_rows, :].reshape(narrow * sum_rows, 128)[:sum_total]
+    groups = out[:, sum_rows:, :].reshape(narrow, wide, kept_rows, 128).transpose(1, 0, 2, 3)
+    return total, groups.reshape(wide, narrow * kept_rows, 128)[:, :kept_total]
 
 
 def exchange(blocks, axis):
@@ -878,7 +894,7 @@
         )
 
     def per_image(value):
-        return jnp.stack([jnp.sum(member[i] * value, axis=0) for i in range(image_count)])
+        return [jnp.sum(member[i] * value, axis=0).reshape(-1, 128) for i in range(image_count)]
 
     token_in = tokens[0].astype(F32)
     token_inverse = inverse_rms(token_in)
@@ -1099,9 +1115,6 @@
         list(zip(*backs)), projected, stats_all, cosine, sine, head_gains, part,
         lambda value: fsdp_share(value, narrow, 4),
     )
-    grad_projected_low, grad_gate_up_weight, came_out_z = lax.optimization_barrier(
-        (grad_projected_low, grad_gate_up_weight, came_out_z)
-    )
     everyone = ("z", "core", "fsdp")
     grad_text_weight = lax.ppermute(
         text_part,
@@ -1111,52 +1124,59 @@
             for z in range(deep) for c in range(2) for f in range(narrow)
         ],
     )
+    grad_projected_low, grad_gate_up_weight, came_out_z, grad_text_weight = lax.optimization_barrier(
+        (grad_projected_low, grad_gate_up_weight, came_out_z, grad_text_weight)
+    )
+    grad_text_weight = grad_text_weight.astype(F32)
     grad_out_weight = jnp.sum(came_out_z.astype(F32), axis=0)
     grad_normed = lax.psum_scatter(
         times_transposed(grad_projected_low, own_qkv).astype(BF16), "fsdp", scatter_dimension=0, tiled=True
     )
 
-    qkv_grad = outer_sum(normed_all, grad_projected_low).astype(BF16).reshape(deep, 2, model_width // wide, 3 * part_pad)
+    def lane_rows(value):
+        return value.reshape(-1, 128)
+
+    group = lax.axis_index("z") * 2 + lax.axis_index("core")
+    columns_here = jnp.stack(
+        [narrowed(value, 1) for value in (head_sums[0], head_sums[2], own_gain_four, head_sums[1], head_sums[3])]
+    )
+    here = (jnp.arange(narrow, dtype=jnp.int32) == me)[None, :, None]
+    placed = lane_rows(jnp.where(here, columns_here[:, None, :], 0.0))
+    cond_rows_here = lane_rows(jnp.where(me == 0, cond_low.astype(F32), 0.0))
+    gate_row = jnp.pad(grad_head_gate, (0, 128 - head_count)).reshape(1, 128)
+    ready = [lane_rows(grad_gain_one), lane_rows(grad_gain_five), lane_rows(grad_gain_six), placed, gate_row]
+    summed, kept = finish(
+        ready, [*grad_gate_attend, *grad_scale_feed, *grad_gate_feed, cond_rows_here], narrow, wide, 5
+    )
+    projected_again, summed, kept = lax.optimization_barrier((grad_projected_low, summed, kept))
+    qkv_grad = outer_sum(normed_all, projected_again).astype(BF16).reshape(deep, 2, model_width // wide, 3 * part_pad)
     own_grad, other_grad = by_core(qkv_grad[:, 0], qkv_grad[:, 1])
     own_grad = (own_grad.astype(F32) + core_swap(other_grad).astype(F32)).astype(BF16)
     own_grad, grad_text_columns = lax.optimization_barrier((own_grad, grad_text_columns))
     own_pieces = z_pieces(own_grad, deep)
     grad_text_slice = times_transposed(grad_text_columns, text_weight).astype(BF16)
     came_text = exchange(
-            grad_text_slice.reshape(image_count, narrow, caption_local, text_cols)
-            .transpose(1, 0, 2, 3)
-            .reshape(narrow, text_local, text_cols),
-            "fsdp",
-        )
-
-    def placed_columns(value):
-        return lax.dynamic_update_slice_in_dim(
-            jnp.zeros((model_width,), F32), narrowed(value, 1), me * part, 0
-        )
-
-    group = lax.axis_index("z") * 2 + lax.axis_index("core")
-    later_modulation = jnp.concatenate([grad_gate_attend, grad_scale_feed, grad_gate_feed], axis=1)
-    summed = jnp.concatenate(
-        [
-            grad_gain_one,
-            placed_columns(head_sums[0]),
-            placed_columns(head_sums[2]),
-            placed_columns(own_gain_four),
-            grad_gain_five,
-            grad_gain_six,
-            placed_columns(head_sums[1]),
-            placed_columns(head_sums[3]),
-            grad_head_gate,
-        ]
-    )
-    kept = jnp.concatenate(
-        [later_modulation.reshape(-1), jnp.where(me == 0, cond_low.astype(F32), 0.0).reshape(-1)]
-    )
-    summed, kept = finish(summed, kept, narrow, wide, 5)
-    summed, kept, came_text, grad_text_weight, *own_pieces = lax.optimization_barrier(
-        (summed, kept, came_text, grad_text_weight, *own_pieces)
-    )
-    grad_text_weight = grad_text_weight.astype(F32)
+        grad_text_slice.reshape(image_count, narrow, caption_local, text_cols)
+        .transpose(1, 0, 2, 3)
+        .reshape(narrow, text_local, text_cols),
+        "fsdp",
+    )
+
+    grad_text_normed = (
+        came_text
+        .transpose(1, 0, 2)
+        .reshape(text_local, caption_width)
+        .astype(F32)
+    )
+    text_state_unit = text_in * text_inverse
+    grad_text_gain = jnp.sum(grad_text_normed * text_state_unit, axis=0)
+    grad_text = (
+        norm_pull(grad_text_normed * text_gain, text_state_unit, text_inverse)
+        .astype(BF16)
+        .reshape(image_count, caption_local, caption_width)
+    )
+
+    grad_text, grad_text_gain, *own_pieces = lax.optimization_barrier((grad_text, grad_text_gain, *own_pieces))
     own_grad = added(own_pieces)
     grad_qkv_weight = (
         exchange(narrowed(own_grad.astype(BF16), 3).reshape(narrow, -1, 3 * part), "fsdp")
@@ -1166,27 +1186,24 @@
         .astype(F32)
     )
 
-    grad_text_normed = (
-        came_text
-        .transpose(1, 0, 2)
-        .reshape(text_local, caption_width)
-        .astype(F32)
-    )
-    text_state_unit = text_in * text_inverse
-    grad_text_gain = jnp.sum(grad_text_normed * text_state_unit, axis=0)
-    grad_text = (
-        norm_pull(grad_text_normed * text_gain, text_state_unit, text_inverse)
-        .astype(BF16)
-        .reshape(image_count, caption_local, caption_width)
-    )
-
     every_image = wide * image_count
     ada_rows = cond_rows // wide
-    slots = kept[:, : later_modulation.size].reshape(every_image, later_modulation.shape[1])
-    cond_slots = kept[:, later_modulation.size :].reshape(every_image, cond_low.shape[1])
+    lanes_of_row = model_width // 128
+
+    def image_rows(value, width):
+        return value.reshape(every_image, width)
+
+    per_part = image_count * lanes_of_row
+    slots = jnp.concatenate(
+        [image_rows(kept[:, i * per_part : (i + 1) * per_part], model_width) for i in range(3)], axis=1
+    )
+    cond_slots = image_rows(kept[:, 3 * per_part :], cond_low.shape[1])
     own_cond = lax.dynamic_slice_in_dim(cond_slots, (group * narrow + me) * ada_rows, ada_rows, 1)
     ada_later = exact_outer(own_cond, slots)
-    grad_normed, ada_later, own_cond = lax.optimization_barrier((grad_normed, ada_later, own_cond))
+    later_bias = jnp.sum(slots, axis=0)
+    grad_normed, ada_later, own_cond, later_bias = lax.optimization_barrier(
+        (grad_normed, ada_later, own_cond, later_bias)
+    )
     grad_normed = grad_normed.astype(F32)
 
     token_unit = token_in * token_inverse
@@ -1198,17 +1215,19 @@
         grad_hidden + norm_pull(grad_normed_y * norm_gains[0], token_unit, token_inverse)
     ).astype(BF16)
     last_sums, first_slots = finish(
-        jnp.concatenate([grad_gain_zero, grad_text_gain]), grad_scale_attend.reshape(-1), narrow, wide, 6
-    )
-    grad_text_gain = last_sums[model_width:]
-    first_slots = first_slots.reshape(every_image, model_width)
+        [lane_rows(grad_gain_zero), lane_rows(grad_text_gain)], grad_scale_attend, narrow, wide, 6
+    )
+    grad_text_gain = last_sums[lanes_of_row:].reshape(-1)
+    first_slots = image_rows(first_slots, model_width)
     grad_ada_weight = jnp.concatenate([exact_outer(own_cond, first_slots), ada_later], axis=1)
-    grad_ada_bias = jnp.concatenate([jnp.sum(first_slots, axis=0), jnp.sum(slots, axis=0)])
-    gain_count = norm_gains.size - model_width
-    shift_end = gain_count + norm_shifts.size
-    grad_gains = jnp.concatenate([last_sums[:model_width], summed[:gain_count]]).reshape(norm_gains.shape)
-    grad_shifts = summed[gain_count:shift_end].reshape(norm_shifts.shape)
-    grad_head_gate = summed[shift_end:]
+    grad_ada_bias = jnp.concatenate([jnp.sum(first_slots, axis=0), later_bias])
+    first, two, three, four = (summed[i * lanes_of_row : (i + 1) * lanes_of_row] for i in (0, 3, 4, 5))
+    five, six = (summed[i * lanes_of_row : (i + 1) * lanes_of_row] for i in (1, 2))
+    grad_gains = jnp.concatenate(
+        [last_sums[:lanes_of_row], first, two, three, four, five, six]
+    ).reshape(norm_gains.shape)
+    grad_shifts = summed[6 * lanes_of_row : 8 * lanes_of_row].reshape(norm_shifts.shape)
+    grad_head_gate = summed[8 * lanes_of_row, :head_count]
     return (
         result[None],
         grad_tokens[None],

time: 1150 us -> 1170 us (1.017)
  waiting for transfers between devices: 75.8 us -> 102 us
    ppermute x6, waiting for transfers between devices: 0.02 us -> 18.3 us  [z_pieces(): lax.ppermute(lax.dynamic_index_in_dim(blocks, me ^ step, 0, keepdims=Fals...]
    unnamed x232 -> x206, local copies, waits for them, and re-layouts: 28.4 us -> 21.8 us
  transfers between devices with their start and end apart: 36 -> 36, of which waited for: 10 -> 14; matrix products, arithmetic and copies ran while one was open for 35% -> 34% of each run, Pallas kernels for 41% -> 40%
where the time goes in v5:
time: 1170 us; the launch traced here: 1160 us
  Pallas kernels  493 us (42%)
  matrix products  240 us (21%)
  other arithmetic  117 us (10%)
  local copies, waits for them, and re-layouts  114 us (10%)
  waiting for transfers between devices  102 us (9%)
  starting transfers between devices  74.3 us (6%)
  between operations  18.5 us (2%)
    pallas_call x3, Pallas kernels, self_back(): pl.pallas_call(functools.partial(self_back_kernel, head_dim, FIRST_PATCHE...  137 us
    pallas_call x3, Pallas kernels, attend(): pl.pallas_call(functools.partial(attend_kernel, head_dim, FIRST_PATCHES,...  91.8 us
    dot_general x9, matrix products, outer_sum(): lax.dot_general(left, right, (((0,), (0,)), ((), ())), preferred_element_...  84.1 us
    pallas_call x2, Pallas kernels, finish(): pl.pallas_call(functools.partial(finish_kernel, narrow, wide, sum_rows, l...  78.4 us
    dot_general x11, matrix products, low_product(): return jnp.dot(left, right, preferred_element_type=F32)  77.1 us
    dot_general x5, matrix products, times_transposed(): lax.dot_general(left, right, (((1,), (1,)), ((), ())), preferred_element_...  74.7 us
    pallas_call x5, Pallas kernels, fsdp_share(): pl.pallas_call(functools.partial(fsdp_share_kernel, narrow), in_specs=[pl...  64.8 us
    all_to_all x12, waiting for transfers between devices, exchange(): return lax.all_to_all(blocks, axis, 0, 0, tiled=True)  52.2 us
  transfers between devices with their start and end apart: 36, of which 14 were waited for; matrix products, arithmetic and copies ran while one was open for 34% of the time, Pallas kernels for 40%

profile of v5, /device:TPU:0, one launch (start us, length us, event | category | flops | bytes accessed | tf_op | source)
XLA Modules:
  0.0 1158.8 jit_solution(10972050596710445231)
XLA Ops:
  40.4 27.4 %shard_map.263 = f32[4,96,128]{2,1,0:T(8,128)} custom-call(f32[96,128]{1,0:T(8,128)} %reshape.657.x_ref), custom_call_target="tpu_custom_call" | custom-call | bytes 393216 | tf_op jit(solution)/shard_map/pallas_call | solution.py:648
  75.8 10.6 negate_select_fusion
  150.3 13.6 %fusion.160.projected_ref.refs_6_.refs_9_ = f32[2624,1152]{1,0:T(8,128)} fusion(bf16[2624,1536]{1,0:T(8,128)(2,1)S(1)} %fusion.3, bf16[1536,1152]{1,0:T(8,128)(2,1)S(1)} %bitcast.254), kind=kOutput, calls=%fused_computation.364 | convolution fusion | flops 9286189056 | bytes 23691264 | tf_op jit(solution)/shard_map/dot_general | solution.py:28
  173.3 16.2 %shard_map.265.stats_ref.refs_7_.refs_10_ = f32[4,8,2624]{2,1,0:T(8,128)} custom-call(f32[8,2624]{1,0:T(8,128)} %shard_map.264.x_ref), custom_call_target="tpu_custom_call" | custom-call | bytes 671744 | tf_op jit(solution)/shard_map/pallas_call | solution.py:648
  189.5 15.5 %shard_map.266.q_ref.k_ref.v_ref = bf16[2624,1152]{1,0:T(8,128)(2,1)} custom-call(f32[2624,1152]{1,0:T(8,128)} %fusion.160.projected_ref.refs_6_.refs_9_, f32[4,8,2624]{2,1,0:T(8,128)} %shard_map.265.stats_ref.refs_7_.refs_10_, f32[2624,128]{1,0:T(8,128)} %get-tuple-element.238.cos_ref.refs_8_.refs_12_, ...), custom_call_target="tpu_custom_call" | custom-call | flops 120913920 | bytes 18137088 | tf_op jit(solution)/shard_map/pallas_call | solution.py:183
  221.7 31.0 %shard_map.271 = (bf16[2624,128]{1,0:T(8,128)(2,1)}, f32[2624,128]{1,0:T(8,128)}, f32[2624,128]{1,0:T(8,128)}, f32[8,2624]{1,0:T(8,128)}) custom-call(f32[3,1,2]{2,1,0:T(1,128)} %reshape.723.gate_ref, bf16[2624,1152]{1,0:T(8,128)(2,1)} %shard_map.266.q_ref.k_ref.v_ref, bf16[2624,1152]{1,0:T(8,128)(2,1)} %shard_map.266.q_ref.k_ref.v_ref, ...), custom_call_target="tpu_custom_call" | custom-call | flops 4213178368 | bytes 6717440 | tf_op jit(solution)/shard_map/pallas_call | solution.py:379
  256.4 30.4 %shard_map.270 = (bf16[2624,128]{1,0:T(8,128)(2,1)}, f32[2624,128]{1,0:T(8,128)}, f32[2624,128]{1,0:T(8,128)}, f32[8,2624]{1,0:T(8,128)}) custom-call(f32[3,1,2]{2,1,0:T(1,128)} %reshape.723.gate_ref, bf16[2624,1152]{1,0:T(8,128)(2,1)} %shard_map.266.q_ref.k_ref.v_ref, bf16[2624,1152]{1,0:T(8,128)(2,1)} %shard_map.266.q_ref.k_ref.v_ref, ...), custom_call_target="tpu_custom_call" | custom-call | flops 4213178368 | bytes 6717440 | tf_op jit(solution)/shard_map/pallas_call | solution.py:379
  291.1 30.4 %shard_map.269 = (bf16[2624,128]{1,0:T(8,128)(2,1)}, f32[2624,128]{1,0:T(8,128)}, f32[2624,128]{1,0:T(8,128)}, f32[8,2624]{1,0:T(8,128)}) custom-call(f32[3,1,2]{2,1,0:T(1,128)} %reshape.723.gate_ref, bf16[2624,1152]{1,0:T(8,128)(2,1)} %shard_map.266.q_ref.k_ref.v_ref, bf16[2624,1152]{1,0:T(8,128)(2,1)} %shard_map.266.q_ref.k_ref.v_ref, ...), custom_call_target="tpu_custom_call" | custom-call | flops 4213178368 | bytes 6717440 | tf_op jit(solution)/shard_map/pallas_call | solution.py:379
  325.8 16.1 %all-to-all-done.3 = bf16[4,656,128]{2,1,0:T(8,128)(2,1)} async-done(((bf16[4,656,128]{2,1,0:T(8,128)(2,1)}), bf16[4,656,128]{2,1,0:T(8,128)(2,1)}, u32[]{:S(2)}, u32[]{:S(2)}) %all-to-all-start.3) | async-done | bytes 671776 | tf_op jit(solution)/shard_map/all_to_all | solution.py:754
  366.6 26.2 %fusion.161.gate_ref.up_ref = f32[656,8192]{1,0:T(8,128)} fusion(bf16[656,1536]{1,0:T(8,128)(2,1)} %copy-done.27, bf16[1536,8192]{1,0:T(8,128)(2,1)} %all-gather.8.cloned.1.call-done), kind=kOutput, calls=%fused_computation.365 | convolution fusion | flops 16508780544 | bytes 48676864 | tf_op jit(solution)/shard_map/dot_general | solution.py:28
  392.8 23.1 %shard_map.272 = (bf16[656,4096]{1,0:T(8,128)(2,1)}, bf16[656,4096]{1,0:T(8,128)(2,1)}) custom-call(s32[1]{0:T(128)} %bitcast.29.core_ref, f32[656,8192]{1,0:T(8,128)} %fusion.161.gate_ref.up_ref, f32[656,8192]{1,0:T(8,128)} %fusion.161.gate_ref.up_ref), custom_call_target="tpu_custom_call" | custom-call | flops 16121856 | bytes 32243712 | tf_op jit(solution)/shard_map/pallas_call | solution.py:602
  419.6 13.1 %multiply_reduce_fusion.14 = (f32[656]{0:T(1024)S(1)}, f32[656,1536]{1,0:T(8,128)S(1)}) fusion(bf16[656,4096]{1,0:T(8,128)(2,1)} %get-tuple-element.95, bf16[4096,1536]{1,0:T(8,128)(2,1)} %all-gather.10.cloned.1.call-done), kind=kOutput, calls=%fused_computation.67 | convolution fusion | flops 8256404992 | bytes 21989952 | tf_op jit(solution)/shard_map/dot_general | solution.py:28
  448.3 20.7 %fusion.6 = (bf16[656,4096]{1,0:T(8,128)(2,1)}, bf16[656,4096]{1,0:T(8,128)(2,1)}) fusion(f32[656,8192]{1,0:T(8,128)} %fusion.161.gate_ref.up_ref, bf16[656,1536]{1,0:T(8,128)(2,1)S(1)} %get-tuple-element.216, bf16[4096,1536]{1,0:T(8,128)(2,1)} %all-gather.10.cloned.1.call-done), kind=kOutput, calls=%fused_computation.13 | convolution fusion | flops 8289320960 | bytes 46841856 | tf_op jit(solution)/shard_map/dot_general | solution.py:32
  469.0 17.2 %convolution_convert_fusion = bf16[768,8192]{1,0:T(8,128)(2,1)} fusion(bf16[656,4096]{1,0:T(8,128)(2,1)} %get-tuple-element.210, bf16[656,4096]{1,0:T(8,128)(2,1)} %get-tuple-element.209, bf16[656,1536]{1,0:T(8,128)(2,1)} %fusion.29), kind=kOutput, calls=%fused_computation.7 | convolution fusion | flops 8282177536 | bytes 24338432 | tf_op jit(solution)/shard_map/dot_general | solution.py:36
  486.4 10.3 add_convert_fusion.1
  497.5 28.6 %multiply_reduce_fusion.9 = (f32[1536]{0:T(1024)}, f32[656]{0:T(1024)S(1)}, f32[1536]{0:T(1024)}, f32[1536]{0:T(1024)}, f32[656,1536]{1,0:T(8,128)}) fusion(f32[656,1536]{1,0:T(8,128)} %copy-done.2, f32[656]{0:T(1024)S(1)} %copy-done.76, f32[1536]{0:T(1024)S(1)} %copy-done.62, f32[656]{0:T(1024)S(1)} %get-tuple-element.255, f32[1536]{0:T(1024)S(1)} %copy-done.64, ...), kind=kOutput, calls=%fused_computation.59 | convolution fusion | flops 16547399680 | bytes 44022016 | tf_op jit(solution)/shard_map/dot_general | solution.py:32
  558.9 18.4 %add_convert_fusion = bf16[768,8192]{1,0:T(8,128)(2,1)} fusion(bf16[768,8192]{1,0:T(8,128)(2,1)} %collective-permute-done.1, bf16[656,4096]{1,0:T(8,128)(2,1)} %get-tuple-element.210, bf16[656,4096]{1,0:T(8,128)(2,1)} %get-tuple-element.209, bf16[656,1536]{1,0:T(8,128)(2,1)} %fusion.29), kind=kOutput, calls=%fused_computation | convolution fusion | flops 8294760448 | bytes 36921344 | tf_op jit(solution)/shard_map/dot_general | solution.py:36
  577.4 9.5 all-to-all-done.6
  593.1 13.3 %shard_map.275 = (bf16[2624,128]{1,0:T(8,128)(2,1)}, bf16[512,128]{1,0:T(8,128)(2,1)}, bf16[512,128]{1,0:T(8,128)(2,1)}, f32[8,128]{1,0:T(8,128)}) custom-call(f32[3,1,2]{2,1,0:T(1,128)} %reshape.723.gate_ref, bf16[2624,1152]{1,0:T(8,128)(2,1)} %shard_map.266.q_ref.k_ref.v_ref, bf16[512,768]{1,0:T(8,128)(2,1)} %pad_maximum_fusion.8.tk_ref.tv_ref, ...), custom_call_target="tpu_custom_call" | custom-call | flops 1719664640 | bytes 4030464 | tf_op jit(solution)/shard_map/pallas_call | solution.py:495
  606.5 13.3 %shard_map.274 = (bf16[2624,128]{1,0:T(8,128)(2,1)}, bf16[512,128]{1,0:T(8,128)(2,1)}, bf16[512,128]{1,0:T(8,128)(2,1)}, f32[8,128]{1,0:T(8,128)}) custom-call(f32[3,1,2]{2,1,0:T(1,128)} %reshape.723.gate_ref, bf16[2624,1152]{1,0:T(8,128)(2,1)} %shard_map.266.q_ref.k_ref.v_ref, bf16[512,768]{1,0:T(8,128)(2,1)} %pad_maximum_fusion.8.tk_ref.tv_ref, ...), custom_call_target="tpu_custom_call" | custom-call | flops 1719664640 | bytes 4030464 | tf_op jit(solution)/shard_map/pallas_call | solution.py:495
  619.9 13.4 %shard_map.273 = (bf16[2624,128]{1,0:T(8,128)(2,1)}, bf16[512,128]{1,0:T(8,128)(2,1)}, bf16[512,128]{1,0:T(8,128)(2,1)}, f32[8,128]{1,0:T(8,128)}) custom-call(f32[3,1,2]{2,1,0:T(1,128)} %reshape.723.gate_ref, bf16[2624,1152]{1,0:T(8,128)(2,1)} %shard_map.266.q_ref.k_ref.v_ref, bf16[512,768]{1,0:T(8,128)(2,1)} %pad_maximum_fusion.8.tk_ref.tv_ref, ...), custom_call_target="tpu_custom_call" | custom-call | flops 1719664640 | bytes 4030464 | tf_op jit(solution)/shard_map/pallas_call | solution.py:495
  652.1 45.9 %shard_map.277 = (bf16[2624,128]{1,0:T(8,128)(2,1)}, bf16[2624,128]{1,0:T(8,128)(2,1)}, bf16[2624,128]{1,0:T(8,128)(2,1)}) custom-call(bf16[2624,1152]{1,0:T(8,128)(2,1)} %shard_map.266.q_ref.k_ref.v_ref, bf16[2624,1152]{1,0:T(8,128)(2,1)} %shard_map.266.q_ref.k_ref.v_ref, bf16[2624,1152]{1,0:T(8,128)(2,1)} %shard_map.266.q_ref.k_ref.v_ref, ...), custom_call_target="tpu_custom_call" | custom-call | flops 8813281280 | bytes 10076160 | tf_op jit(solution)/shard_map/pallas_call | solution.py:562
  698.0 18.8 %collective-permute-done.6 = bf16[512,768]{1,0:T(8,128)(2,1)} collective-permute-done((bf16[512,768]{1,0:T(8,128)(2,1)}, bf16[512,768]{1,0:T(8,128)(2,1)}, u32[]{:S(2)}, u32[]{:S(2)}) %collective-permute-start.6) | collective-permute-done | bytes 786464 | tf_op jit(solution)/shard_map/ppermute | solution.py:796
  744.2 45.4 %shard_map.278 = (bf16[2624,128]{1,0:T(8,128)(2,1)}, bf16[2624,128]{1,0:T(8,128)(2,1)}, bf16[2624,128]{1,0:T(8,128)(2,1)}) custom-call(bf16[2624,1152]{1,0:T(8,128)(2,1)} %shard_map.266.q_ref.k_ref.v_ref, bf16[2624,1152]{1,0:T(8,128)(2,1)} %shard_map.266.q_ref.k_ref.v_ref, bf16[2624,1152]{1,0:T(8,128)(2,1)} %shard_map.266.q_ref.k_ref.v_ref, ...), custom_call_target="tpu_custom_call" | custom-call | flops 8813281280 | bytes 10076160 | tf_op jit(solution)/shard_map/pallas_call | solution.py:562
  797.1 45.6 %shard_map.279 = (bf16[2624,128]{1,0:T(8,128)(2,1)}, bf16[2624,128]{1,0:T(8,128)(2,1)}, bf16[2624,128]{1,0:T(8,128)(2,1)}) custom-call(bf16[2624,1152]{1,0:T(8,128)(2,1)} %shard_map.266.q_ref.k_ref.v_ref, bf16[2624,1152]{1,0:T(8,128)(2,1)} %shard_map.266.q_ref.k_ref.v_ref, bf16[2624,1152]{1,0:T(8,128)(2,1)} %shard_map.266.q_ref.k_ref.v_ref, ...), custom_call_target="tpu_custom_call" | custom-call | flops 8813281280 | bytes 10076160 | tf_op jit(solution)/shard_map/pallas_call | solution.py:562
  849.9 15.2 %shard_map.280 = (f32[8,2624]{1,0:T(8,128)}, f32[8,384]{1,0:T(8,128)}) custom-call(bf16[2624,128]{1,0:T(8,128)(2,1)} %get-tuple-element.118.refs_0_, bf16[2624,128]{1,0:T(8,128)(2,1)} %get-tuple-element.125.refs_1_, bf16[2624,128]{1,0:T(8,128)(2,1)} %get-tuple-element.131.refs_2_, bf16[2624,128]{1,0:T(8,128)(2,1)} %get-tuple-element.132.refs_3_, ...), custom_call_target="tpu_custom_call" | custom-call | flops 120913920 | bytes 15114240 | tf_op jit(solution)/shard_map/pallas_call | solution.py:269
  886.6 15.4 %shard_map.282 = bf16[2624,1152]{1,0:T(8,128)(2,1)} custom-call(bf16[2624,128]{1,0:T(8,128)(2,1)} %get-tuple-element.118.refs_0_, bf16[2624,128]{1,0:T(8,128)(2,1)} %get-tuple-element.125.refs_1_, bf16[2624,128]{1,0:T(8,128)(2,1)} %get-tuple-element.131.refs_2_, bf16[2624,128]{1,0:T(8,128)(2,1)} %get-tuple-element.132.refs_3_, ...), custom_call_target="tpu_custom_call" | custom-call | flops 120913920 | bytes 21159936 | tf_op jit(solution)/shard_map/pallas_call | solution.py:282
  913.4 15.5 %convolution_convert_fusion.1 = bf16[2624,1536]{1,0:T(8,128)(2,1)} fusion(bf16[2624,1152]{1,0:T(8,128)(2,1)} %shard_map.282, bf16[1536,1152]{1,0:T(8,128)(2,1)S(1)} %bitcast.255), kind=kOutput, calls=%fused_computation.9 | convolution fusion | flops 9290219520 | bytes 17645568 | tf_op jit(solution)/shard_map/dot_general | solution.py:32
  931.9 54.5 %shard_map.283 = f32[4,224,128]{2,1,0:T(8,128)} custom-call(f32[12,128]{1,0:T(8,128)} %bitcast.297, f32[12,128]{1,0:T(8,128)} %bitcast.302, f32[12,128]{1,0:T(8,128)} %bitcast.292, f32[60,128]{1,0:T(8,128)} %select_n.423.refs_3_, f32[1,128]{1,0:T(1,128)} %pad_bitcast_fusion.refs_4_, f32[12,128]{1,0:T(8,128)} %bitcast.294, f32[12,128]{1,0:T(8,128)} %bitcast.293, ...), custom_call_target="tpu_custom_call" | custom-call | tf_op jit(solution)/shard_map/pallas_call | solution.py:734
  989.8 15.8 %convolution_convert_fusion.3 = bf16[1536,1152]{1,0:T(8,128)(2,1)S(1)} fusion(bf16[2624,1536]{1,0:T(8,128)(2,1)} %copy-done.18, bf16[2624,1152]{1,0:T(8,128)(2,1)} %shard_map.282), kind=kOutput, calls=%fused_computation.21 | convolution fusion | flops 9287958528 | bytes 17645568 | tf_op jit(solution)/shard_map/dot_general | solution.py:36
  1070.7 13.4 %collective-permute-done.14 = bf16[192,1152]{1,0:T(8,128)(2,1)} collective-permute-done((bf16[192,1152]{1,0:T(8,128)(2,1)}, bf16[192,1152]{1,0:T(8,128)(2,1)}, u32[]{:S(2)}, u32[]{:S(2)}) %collective-permute-start.14) | collective-permute-done | bytes 442400 | tf_op jit(solution)/shard_map/ppermute | solution.py:783
  1108.3 23.8 %shard_map.284 = f32[4,80,128]{2,1,0:T(8,128)} custom-call(f32[12,128]{1,0:T(8,128)} %bitcast.289, f32[32,128]{1,0:T(8,128)} %bitcast.288, f32[12,128]{1,0:T(8,128)} %bitcast.291, f32[12,128]{1,0:T(8,128)} %bitcast.290), custom_call_target="tpu_custom_call" | custom-call | tf_op jit(solution)/shard_map/pallas_call | solution.py:734
  (461 shorter events, 432.4 us)
Async XLA Ops:
  7.2 122.6 %all-gather.12.cloned.1.call-start = ((), (), s32[]{:S(2)}) async-start(), calls=%async_computation.23 | async-start | bytes 10076160 | tf_op jit(solution)/shard_map/all_gather | solution.py:901
  7.9 336.9 %all-gather.6.cloned.1.call-start = ((), (), s32[]{:S(2)}) async-start(), calls=%async_computation.16 | async-start | bytes 5308416 | tf_op jit(solution)/shard_map/all_gather | solution.py:829
  10.2 356.4 %all-gather.8.cloned.1.call-start = ((), (), s32[]{:S(2)}) async-start(), calls=%async_computation.17 | async-start | bytes 28311552 | tf_op jit(solution)/shard_map/all_gather | solution.py:829
  25.0 61.4 %all-to-all-start.1 = ((bf16[4,192,1152]{2,1,0:T(8,128)(2,1)}), bf16[4,192,1152]{2,1,0:T(8,128)(2,1)}, u32[]{:S(2)}, u32[]{:S(2)}) async-start(bf16[4,192,1152]{2,1,0:T(8,128)(2,1)} %reshape.664), calls=%async_computation.1 | async-start | bytes 3538944 | tf_op jit(solution)/shard_map/all_to_all | solution.py:754
  30.3 389.3 %all-gather.10.cloned.1.call-start = ((), (), s32[]{:S(2)}) async-start(), calls=%async_computation.18 | async-start | bytes 14155776 | tf_op jit(solution)/shard_map/all_gather | solution.py:829
  86.4 29.5 %all-to-all-start = ((bf16[4,128,1024]{2,1,0:T(8,128)(2,1)}), bf16[4,128,1024]{2,1,0:T(8,128)(2,1)S(1)}, u32[]{:S(2)}, u32[]{:S(2)}) async-start(bf16[4,128,1024]{2,1,0:T(8,128)(2,1)} %fusion.54), calls=%async_computation | async-start | bytes 2097152 | tf_op jit(solution)/shard_map/all_to_all | solution.py:754
  129.8 75.2 %all-to-all-start.2 = ((bf16[4,512,768]{2,1,0:T(8,128)(2,1)}), bf16[4,512,768]{2,1,0:T(8,128)(2,1)}, u32[]{:S(2)}, u32[]{:S(2)}) async-start(bf16[4,512,768]{2,1,0:T(8,128)(2,1)} %pad_maximum_fusion.2), calls=%async_computation.2 | async-start | bytes 6291456 | tf_op jit(solution)/shard_map/all_to_all | solution.py:754
  252.8 34.0 %all-to-all-start.5 = ((bf16[4,656,128]{2,1,0:T(8,128)(2,1)}), bf16[4,656,128]{2,1,0:T(8,128)(2,1)S(1)}, u32[]{:S(2)}, u32[]{:S(2)}) async-start(bf16[4,656,128]{2,1,0:T(8,128)(2,1)} %bitcast.282), calls=%async_computation.5 | async-start | bytes 1343488 | tf_op jit(solution)/shard_map/all_to_all | solution.py:754
  286.8 34.8 %all-to-all-start.4 = ((bf16[4,656,128]{2,1,0:T(8,128)(2,1)}), bf16[4,656,128]{2,1,0:T(8,128)(2,1)S(1)}, u32[]{:S(2)}, u32[]{:S(2)}) async-start(bf16[4,656,128]{2,1,0:T(8,128)(2,1)} %bitcast.281), calls=%async_computation.4 | async-start | bytes 1343488 | tf_op jit(solution)/shard_map/all_to_all | solution.py:754
  321.5 20.4 %all-to-all-start.3 = ((bf16[4,656,128]{2,1,0:T(8,128)(2,1)}), bf16[4,656,128]{2,1,0:T(8,128)(2,1)}, u32[]{:S(2)}, u32[]{:S(2)}) async-start(bf16[4,656,128]{2,1,0:T(8,128)(2,1)} %bitcast.280), calls=%async_computation.3 | async-start | bytes 1343488 | tf_op jit(solution)/shard_map/all_to_all | solution.py:754
  325.7 261.8 %reduce-scatter.5.cloned.1.call-start = ((), (), s32[]{:S(2)}) async-start(), calls=%async_computation.19 | async-start | bytes 7864320 | tf_op jit(solution)/shard_map/reduce_scatter | solution.py:777
  448.0 38.4 %collective-permute-start.3 = (bf16[2048,1536]{1,0:T(8,128)(2,1)}, bf16[2048,1536]{1,0:T(8,128)(2,1)}, u32[]{:S(2)}, u32[]{:S(2)}) collective-permute-start(bf16[2048,1536]{1,0:T(8,128)(2,1)} %convolution_convert_fusion.2), channel_id=1, source_target_pairs={{0,4},{4,0},{1,5},{5,1},{2,6},{6,2},{3,7},{7,3},{8,12},{12,8},{9,1... | collective-permute-start | bytes 18874376 | tf_op jit(solution)/shard_map/ppermute | solution.py:758
  486.2 72.8 %collective-permute-start.1 = (bf16[768,8192]{1,0:T(8,128)(2,1)}, bf16[768,8192]{1,0:T(8,128)(2,1)}, u32[]{:S(2)}, u32[]{:S(2)}) collective-permute-start(bf16[768,8192]{1,0:T(8,128)(2,1)} %convolution_convert_fusion), channel_id=1, source_target_pairs={{0,4},{4,0},{1,5},{5,1},{2,6},{6,2},{3,7},{7,3},{8,12},{12,8},{9,1... | collective-permute-start | bytes 37748744 | tf_op jit(solution)/shard_map/ppermute | solution.py:758
  549.1 37.8 %all-to-all-start.6 = ((bf16[4,656,384]{2,1,0:T(8,128)(2,1)}), bf16[4,656,384]{2,1,0:T(8,128)(2,1)S(1)}, u32[]{:S(2)}, u32[]{:S(2)}) async-start(bf16[4,656,384]{2,1,0:T(8,128)(2,1)} %bitcast.249), calls=%async_computation.6 | async-start | bytes 4030464 | tf_op jit(solution)/shard_map/all_to_all | solution.py:754
  552.7 237.0 %reduce-scatter.9.cloned.1.call-start = ((), (), s32[]{:S(2)}) async-start(), calls=%async_computation.21 | async-start | bytes 2949120 | tf_op jit(solution)/shard_map/reduce_scatter | solution.py:777
  587.5 202.1 %reduce-scatter.7.cloned.1.call-start = ((), (), s32[]{:S(2)}) async-start(), calls=%async_computation.20 | async-start | bytes 15728640 | tf_op jit(solution)/shard_map/reduce_scatter | solution.py:777
  588.3 128.5 %all-to-all-start.7 = ((bf16[4,128,1536]{2,1,0:T(8,128)(2,1)}), bf16[4,128,1536]{2,1,0:T(8,128)(2,1)}, u32[]{:S(2)}, u32[]{:S(2)}) async-start(bf16[4,128,1536]{2,1,0:T(8,128)(2,1)} %bitcast.269), calls=%async_computation.8 | async-start | bytes 3145728 | tf_op jit(solution)/shard_map/all_to_all | solution.py:754
  646.0 52.0 %collective-permute-start.4 = (bf16[512,768]{1,0:T(8,128)(2,1)}, bf16[512,768]{1,0:T(8,128)(2,1)}, u32[]{:S(2)}, u32[]{:S(2)}) collective-permute-start(bf16[512,768]{1,0:T(8,128)(2,1)} %get-tuple-element.228), channel_id=1, source_target_pairs={{0,1},{1,0},{2,3},{3,2},{4,5},{5,4},{6,7},{7,6},{8,9},{9,8},{10,11... | collective-permute-start | bytes 2359304 | tf_op jit(solution)/shard_map/ppermute | solution.py:796
  647.4 50.5 %collective-permute-start.5 = (bf16[512,768]{1,0:T(8,128)(2,1)}, bf16[512,768]{1,0:T(8,128)(2,1)}, u32[]{:S(2)}, u32[]{:S(2)}) collective-permute-start(bf16[512,768]{1,0:T(8,128)(2,1)} %get-tuple-element.228), channel_id=1, source_target_pairs={{0,2},{1,3},{2,0},{3,1},{4,6},{5,7},{6,4},{7,5},{8,10},{9,11},{10,... | collective-permute-start | bytes 2359304 | tf_op jit(solution)/shard_map/ppermute | solution.py:796
  648.1 68.6 %collective-permute-start.6 = (bf16[512,768]{1,0:T(8,128)(2,1)}, bf16[512,768]{1,0:T(8,128)(2,1)}, u32[]{:S(2)}, u32[]{:S(2)}) collective-permute-start(bf16[512,768]{1,0:T(8,128)(2,1)} %get-tuple-element.228), channel_id=1, source_target_pairs={{0,3},{1,2},{2,1},{3,0},{4,7},{5,6},{6,5},{7,4},{8,11},{9,10},{10,... | collective-permute-start | bytes 2359304 | tf_op jit(solution)/shard_map/ppermute | solution.py:796
  739.0 110.9 %all-to-all-start.8 = ((bf16[4,128,3072]{2,1,0:T(8,128)(2,1)}), bf16[4,128,3072]{2,1,0:T(8,128)(2,1)S(1)}, u32[]{:S(2)}, u32[]{:S(2)}) async-start(bf16[4,128,3072]{2,1,0:T(8,128)(2,1)} %bitcast.259), calls=%async_computation.11 | async-start | bytes 6291456 | tf_op jit(solution)/shard_map/all_to_all | solution.py:754
  792.7 109.3 %collective-permute-start.10 = (bf16[48,8192]{1,0:T(8,128)(2,1)}, bf16[48,8192]{1,0:T(8,128)(2,1)}, u32[]{:S(2)}, u32[]{:S(2)}) collective-permute-start(bf16[48,8192]{1,0:T(8,128)(2,1)} %get-tuple-element.221), channel_id=1, source_target_pairs={{0,24},{8,16},{16,8},{24,0},{1,25},{9,17},{17,9},{25,1},{2,26},{10... | collective-permute-start | bytes 2359304 | tf_op jit(solution)/shard_map/ppermute | solution.py:783
  796.5 110.4 %collective-permute-start.9 = (bf16[48,8192]{1,0:T(8,128)(2,1)}, bf16[48,8192]{1,0:T(8,128)(2,1)}, u32[]{:S(2)}, u32[]{:S(2)}) collective-permute-start(bf16[48,8192]{1,0:T(8,128)(2,1)} %get-tuple-element.222), channel_id=1, source_target_pairs={{0,16},{8,24},{16,0},{24,8},{1,17},{9,25},{17,1},{25,9},{2,18},{10... | collective-permute-start | bytes 2359304 | tf_op jit(solution)/shard_map/ppermute | solution.py:783
  796.5 110.4 %collective-permute-start.8 = (bf16[48,8192]{1,0:T(8,128)(2,1)}, bf16[48,8192]{1,0:T(8,128)(2,1)}, u32[]{:S(2)}, u32[]{:S(2)}) collective-permute-start(bf16[48,8192]{1,0:T(8,128)(2,1)} %get-tuple-element.220), channel_id=1, source_target_pairs={{0,8},{8,0},{16,24},{24,16},{1,9},{9,1},{17,25},{25,17},{2,10},{10... | collective-permute-start | bytes 2359304 | tf_op jit(solution)/shard_map/ppermute | solution.py:783
  872.9 40.5 %all-to-all-start.9 = ((bf16[4,48,1536]{2,1,0:T(8,128)(2,1)}), bf16[4,48,1536]{2,1,0:T(8,128)(2,1)}, u32[]{:S(2)}, u32[]{:S(2)}) async-start(bf16[4,48,1536]{2,1,0:T(8,128)(2,1)} %bitcast.283), calls=%async_computation.12 | async-start | bytes 1179648 | tf_op jit(solution)/shard_map/all_to_all | solution.py:754
  877.1 226.1 %reduce-scatter.11.cloned.1.call-start = ((), (), s32[]{:S(2)}) async-start(), calls=%async_computation.22 | async-start | bytes 10076160 | tf_op jit(solution)/shard_map/reduce_scatter | solution.py:1132
  879.1 31.2 %collective-permute-start.11 = (bf16[128,3072]{1,0:T(8,128)(2,1)}, bf16[128,3072]{1,0:T(8,128)(2,1)}, u32[]{:S(2)}, u32[]{:S(2)}) collective-permute-start(bf16[128,3072]{1,0:T(8,128)(2,1)} %reduce_sum.372), channel_id=1, source_target_pairs={{0,0},{1,8},{2,16},{3,24},{4,4},{5,12},{6,20},{7,28},{8,1},{9,9},{... | collective-permute-start | bytes 2359304 | tf_op jit(solution)/shard_map/ppermute | solution.py:1119
  1007.0 22.0 %collective-permute-start.12 = (bf16[4,192,1152]{2,1,0:T(8,128)(2,1)}, bf16[4,192,1152]{2,1,0:T(8,128)(2,1)}, u32[]{:S(2)}, u32[]{:S(2)}) collective-permute-start(bf16[4,192,1152]{2,1,0:T(8,128)(2,1)} %fusion.44), channel_id=1, source_target_pairs={{0,4},{4,0},{1,5},{5,1},{2,6},{6,2},{3,7},{7,3},{8,12},{12,8},{9,1... | collective-permute-start | bytes 5308424 | tf_op jit(solution)/shard_map/ppermute | solution.py:758
  1040.1 18.1 %all-to-all-start.10 = ((bf16[4,128,1024]{2,1,0:T(8,128)(2,1)}), bf16[4,128,1024]{2,1,0:T(8,128)(2,1)S(1)}, u32[]{:S(2)}, u32[]{:S(2)}) async-start(bf16[4,128,1024]{2,1,0:T(8,128)(2,1)} %bitcast.253), calls=%async_computation.14 | async-start | bytes 2097152 | tf_op jit(solution)/shard_map/all_to_all | solution.py:754
  1048.5 22.2 %collective-permute-start.13 = (bf16[192,1152]{1,0:T(8,128)(2,1)}, bf16[192,1152]{1,0:T(8,128)(2,1)}, u32[]{:S(2)}, u32[]{:S(2)}) collective-permute-start(bf16[192,1152]{1,0:T(8,128)(2,1)} %get-tuple-element.226), channel_id=1, source_target_pairs={{0,8},{8,0},{16,24},{24,16},{1,9},{9,1},{17,25},{25,17},{2,10},{10... | collective-permute-start | bytes 1327112 | tf_op jit(solution)/shard_map/ppermute | solution.py:783
  1050.6 33.5 %collective-permute-start.14 = (bf16[192,1152]{1,0:T(8,128)(2,1)}, bf16[192,1152]{1,0:T(8,128)(2,1)}, u32[]{:S(2)}, u32[]{:S(2)}) collective-permute-start(bf16[192,1152]{1,0:T(8,128)(2,1)} %get-tuple-element.225), channel_id=1, source_target_pairs={{0,16},{8,24},{16,0},{24,8},{1,17},{9,25},{17,1},{25,9},{2,18},{10... | collective-permute-start | bytes 1327112 | tf_op jit(solution)/shard_map/ppermute | solution.py:783
  1053.8 30.3 %collective-permute-start.15 = (bf16[192,1152]{1,0:T(8,128)(2,1)}, bf16[192,1152]{1,0:T(8,128)(2,1)}, u32[]{:S(2)}, u32[]{:S(2)}) collective-permute-start(bf16[192,1152]{1,0:T(8,128)(2,1)} %get-tuple-element.224), channel_id=1, source_target_pairs={{0,24},{8,16},{16,8},{24,0},{1,25},{9,17},{17,9},{25,1},{2,26},{10... | collective-permute-start | bytes 1327112 | tf_op jit(solution)/shard_map/ppermute | solution.py:783
  (106 other events, 2136.7 us)
Sparse Core Ops, SparseCore 0:
  9.9 119.8 all-gather.11
  131.7 63.8 all-gather.5
  197.5 147.6 all-gather.7
  347.4 72.1 all-gather.9
  496.9 90.5 reduce-scatter.4
  590.4 36.8 reduce-scatter.8
  630.4 155.1 reduce-scatter.6
  929.0 117.1 reduce-scatter.10

commit v6 on v5

--- a/solution.py
+++ b/solution.py
@@ -1094,7 +1094,7 @@
     text_both = (outer_sum(own_text, grad_text_columns) + came_text.astype(F32)).astype(BF16)
     grad_heads, text_both, first = lax.optimization_barrier((grad_heads, text_both, backs[0][0]))
     backs[0] = (first, *backs[0][1:])
-    came_text_z = exchange(by_z(text_both), "z")
+    text_part = lax.psum_scatter(text_both, "z", scatter_dimension=0, tiled=True)
     backs.append(self_pair(1))
     if pairs > 2:
         grad_heads, gate_up_part, out_part, second = lax.optimization_barrier(
@@ -1103,9 +1103,8 @@
         backs[1] = (second, *backs[1][1:])
         backs += [self_pair(pair) for pair in range(2, pairs)]
     grad_gate_up_weight = added(z_pieces(by_z(gate_up_part), deep))
-    last, came_text_z = lax.optimization_barrier((backs[-1][0], came_text_z))
+    last, text_part = lax.optimization_barrier((backs[-1][0], text_part))
     backs[-1] = (last, *backs[-1][1:])
-    text_part = jnp.sum(came_text_z.astype(F32), axis=0).astype(BF16)
     came_out_z = exchange(by_z(out_part), "z")
     own_gate_grad = jnp.sum(gate_sums[:, 0, :].reshape(pairs * halves, head_dim), axis=1)[:heads_here]
     grad_head_gate = lax.dynamic_update_slice_in_dim(
@@ -1124,11 +1123,7 @@
             for z in range(deep) for c in range(2) for f in range(narrow)
         ],
     )
-    grad_projected_low, grad_gate_up_weight, came_out_z, grad_text_weight = lax.optimization_barrier(
-        (grad_projected_low, grad_gate_up_weight, came_out_z, grad_text_weight)
-    )
-    grad_text_weight = grad_text_weight.astype(F32)
-    grad_out_weight = jnp.sum(came_out_z.astype(F32), axis=0)
+    grad_projected_low, grad_gate_up_weight = lax.optimization_barrier((grad_projected_low, grad_gate_up_weight))
     grad_normed = lax.psum_scatter(
         times_transposed(grad_projected_low, own_qkv).astype(BF16), "fsdp", scatter_dimension=0, tiled=True
     )
@@ -1145,11 +1140,12 @@
     cond_rows_here = lane_rows(jnp.where(me == 0, cond_low.astype(F32), 0.0))
     gate_row = jnp.pad(grad_head_gate, (0, 128 - head_count)).reshape(1, 128)
     ready = [lane_rows(grad_gain_one), lane_rows(grad_gain_five), lane_rows(grad_gain_six), placed, gate_row]
-    summed, kept = finish(
-        ready, [*grad_gate_attend, *grad_scale_feed, *grad_gate_feed, cond_rows_here], narrow, wide, 5
-    )
-    projected_again, summed, kept = lax.optimization_barrier((grad_projected_low, summed, kept))
-    qkv_grad = outer_sum(normed_all, projected_again).astype(BF16).reshape(deep, 2, model_width // wide, 3 * part_pad)
+    later = [*grad_gate_attend, *grad_scale_feed, *grad_gate_feed, cond_rows_here]
+    ready = lax.optimization_barrier(tuple(ready))
+    qkv_grad = outer_sum(normed_all, grad_projected_low).astype(BF16).reshape(deep, 2, model_width // wide, 3 * part_pad)
+    qkv_grad, came_out_z, grad_text_weight = lax.optimization_barrier((qkv_grad, came_out_z, grad_text_weight))
+    grad_text_weight = grad_text_weight.astype(F32)
+    grad_out_weight = jnp.sum(came_out_z.astype(F32), axis=0)
     own_grad, other_grad = by_core(qkv_grad[:, 0], qkv_grad[:, 1])
     own_grad = (own_grad.astype(F32) + core_swap(other_grad).astype(F32)).astype(BF16)
     own_grad, grad_text_columns = lax.optimization_barrier((own_grad, grad_text_columns))
@@ -1186,24 +1182,6 @@
         .astype(F32)
     )
 
-    every_image = wide * image_count
-    ada_rows = cond_rows // wide
-    lanes_of_row = model_width // 128
-
-    def image_rows(value, width):
-        return value.reshape(every_image, width)
-
-    per_part = image_count * lanes_of_row
-    slots = jnp.concatenate(
-        [image_rows(kept[:, i * per_part : (i + 1) * per_part], model_width) for i in range(3)], axis=1
-    )
-    cond_slots = image_rows(kept[:, 3 * per_part :], cond_low.shape[1])
-    own_cond = lax.dynamic_slice_in_dim(cond_slots, (group * narrow + me) * ada_rows, ada_rows, 1)
-    ada_later = exact_outer(own_cond, slots)
-    later_bias = jnp.sum(slots, axis=0)
-    grad_normed, ada_later, own_cond, later_bias = lax.optimization_barrier(
-        (grad_normed, ada_later, own_cond, later_bias)
-    )
     grad_normed = grad_normed.astype(F32)
 
     token_unit = token_in * token_inverse
@@ -1214,20 +1192,28 @@
     grad_tokens = (
         grad_hidden + norm_pull(grad_normed_y * norm_gains[0], token_unit, token_inverse)
     ).astype(BF16)
-    last_sums, first_slots = finish(
-        [lane_rows(grad_gain_zero), lane_rows(grad_text_gain)], grad_scale_attend, narrow, wide, 6
-    )
-    grad_text_gain = last_sums[lanes_of_row:].reshape(-1)
-    first_slots = image_rows(first_slots, model_width)
-    grad_ada_weight = jnp.concatenate([exact_outer(own_cond, first_slots), ada_later], axis=1)
-    grad_ada_bias = jnp.concatenate([jnp.sum(first_slots, axis=0), later_bias])
-    first, two, three, four = (summed[i * lanes_of_row : (i + 1) * lanes_of_row] for i in (0, 3, 4, 5))
-    five, six = (summed[i * lanes_of_row : (i + 1) * lanes_of_row] for i in (1, 2))
-    grad_gains = jnp.concatenate(
-        [last_sums[:lanes_of_row], first, two, three, four, five, six]
-    ).reshape(norm_gains.shape)
-    grad_shifts = summed[6 * lanes_of_row : 8 * lanes_of_row].reshape(norm_shifts.shape)
-    grad_head_gate = summed[8 * lanes_of_row, :head_count]
+    lanes_of_row = model_width // 128
+    summed, kept = finish(
+        [lane_rows(grad_gain_zero), *ready, lane_rows(grad_text_gain)], [*grad_scale_attend, *later], narrow, wide, 5
+    )
+    every_image = wide * image_count
+    per_part = image_count * lanes_of_row
+    slots = jnp.concatenate(
+        [kept[:, i * per_part : (i + 1) * per_part].reshape(every_image, model_width) for i in range(4)], axis=1
+    )
+    cond_slots = kept[:, 4 * per_part :].reshape(every_image, cond_low.shape[1])
+    ada_rows = cond_rows // wide
+    own_cond = lax.dynamic_slice_in_dim(cond_slots, (group * narrow + me) * ada_rows, ada_rows, 1)
+    grad_ada_weight = exact_outer(own_cond, slots)
+    grad_ada_bias = jnp.sum(slots, axis=0)
+
+    def rows_of(first, count):
+        return summed[first * lanes_of_row : (first + count) * lanes_of_row]
+
+    grad_gains = jnp.concatenate([rows_of(0, 2), rows_of(4, 3), rows_of(2, 2)]).reshape(norm_gains.shape)
+    grad_shifts = rows_of(7, 2).reshape(norm_shifts.shape)
+    grad_head_gate = summed[9 * lanes_of_row, :head_count]
+    grad_text_gain = summed[9 * lanes_of_row + 1 :].reshape(-1)
     return (
         result[None],
         grad_tokens[None],

time: 1170 us -> 1180 us (level)
  waiting for transfers between devices: 102 us -> 151 us
  Pallas kernels: 493 us -> 449 us
  starting transfers between devices: 74.3 us -> 104 us
  local copies, waits for them, and re-layouts: 114 us -> 93.3 us
    reduce_scatter x0 -> x1, waiting for transfers between devices: none -> 55.9 us  [shards(): lax.psum_scatter(text_both, 'z', scatter_dimension=0, tiled=True)]
    pallas_call x2 -> x1, Pallas kernels: 78.4 us -> 31.5 us  [finish(): pl.pallas_call(functools.partial(finish_kernel, narrow, wide, sum_rows, l...]
    all_to_all x12 -> x11, starting transfers between devices: 52.1 us -> 83.4 us  [exchange(): return lax.all_to_all(blocks, axis, 0, 0, tiled=True)]
    ppermute x6, waiting for transfers between devices: 18.3 us -> 3.26 us  [z_pieces(): lax.ppermute(lax.dynamic_index_in_dim(blocks, me ^ step, 0, keepdims=Fals...]
    all_to_all x12 -> x11, waiting for transfers between devices: 52.2 us -> 60.2 us  [exchange(): return lax.all_to_all(blocks, axis, 0, 0, tiled=True)]
  transfers between devices with their start and end apart: 36 -> 36, of which waited for: 14 -> 13; matrix products, arithmetic and copies ran while one was open for 34% -> 31% of each run, Pallas kernels for 40% -> 36%
where the time goes in v6:
time: 1180 us; the launch traced here: 1170 us
  Pallas kernels  449 us (38%)
  matrix products  239 us (20%)
  waiting for transfers between devices  151 us (13%)
  other arithmetic  112 us (9%)
  starting transfers between devices  104 us (9%)
  local copies, waits for them, and re-layouts  93.3 us (8%)
  between operations  18.4 us (2%)
    pallas_call x3, Pallas kernels, self_back(): pl.pallas_call(functools.partial(self_back_kernel, head_dim, FIRST_PATCHE...  138 us
    pallas_call x3, Pallas kernels, attend(): pl.pallas_call(functools.partial(attend_kernel, head_dim, FIRST_PATCHES,...  91.9 us
    dot_general x9, matrix products, outer_sum(): lax.dot_general(left, right, (((0,), (0,)), ((), ())), preferred_element_...  83.8 us
    all_to_all x11, starting transfers between devices, exchange(): return lax.all_to_all(blocks, axis, 0, 0, tiled=True)  83.4 us
    dot_general x11, matrix products, low_product(): return jnp.dot(left, right, preferred_element_type=F32)  76.8 us
    dot_general x5, matrix products, times_transposed(): lax.dot_general(left, right, (((1,), (1,)), ((), ())), preferred_element_...  75.1 us
    pallas_call x5, Pallas kernels, fsdp_share(): pl.pallas_call(functools.partial(fsdp_share_kernel, narrow), in_specs=[pl...  66.3 us
    all_to_all x11, waiting for transfers between devices, exchange(): return lax.all_to_all(blocks, axis, 0, 0, tiled=True)  60.2 us
  transfers between devices with their start and end apart: 36, of which 13 were waited for; matrix products, arithmetic and copies ran while one was open for 31% of the time, Pallas kernels for 36%

profile of v6, /device:TPU:0, one launch (start us, length us, event | category | flops | bytes accessed | tf_op | source)
XLA Modules:
  0.0 1167.2 jit_solution(16550730113543988753)
XLA Ops:
  40.4 27.4 %shard_map.263 = f32[4,96,128]{2,1,0:T(8,128)} custom-call(f32[96,128]{1,0:T(8,128)} %reshape.645.x_ref), custom_call_target="tpu_custom_call" | custom-call | bytes 393216 | tf_op jit(solution)/shard_map/pallas_call | solution.py:648
  75.9 10.5 negate_select_fusion
  150.0 13.6 %fusion.162.projected_ref.refs_6_.refs_9_ = f32[2624,1152]{1,0:T(8,128)} fusion(bf16[2624,1536]{1,0:T(8,128)(2,1)S(1)} %fusion.3, bf16[1536,1152]{1,0:T(8,128)(2,1)S(1)} %bitcast.236), kind=kOutput, calls=%fused_computation.362 | convolution fusion | flops 9286189056 | bytes 23691264 | tf_op jit(solution)/shard_map/dot_general | solution.py:28
  173.0 16.3 %shard_map.265.stats_ref.refs_7_.refs_10_ = f32[4,8,2624]{2,1,0:T(8,128)} custom-call(f32[8,2624]{1,0:T(8,128)} %shard_map.264.x_ref), custom_call_target="tpu_custom_call" | custom-call | bytes 671744 | tf_op jit(solution)/shard_map/pallas_call | solution.py:648
  189.3 15.5 %shard_map.266.q_ref.k_ref.v_ref = bf16[2624,1152]{1,0:T(8,128)(2,1)} custom-call(f32[2624,1152]{1,0:T(8,128)} %fusion.162.projected_ref.refs_6_.refs_9_, f32[4,8,2624]{2,1,0:T(8,128)} %shard_map.265.stats_ref.refs_7_.refs_10_, f32[2624,128]{1,0:T(8,128)} %get-tuple-element.238.cos_ref.refs_8_.refs_12_, ...), custom_call_target="tpu_custom_call" | custom-call | flops 120913920 | bytes 18137088 | tf_op jit(solution)/shard_map/pallas_call | solution.py:183
  221.5 31.1 %shard_map.271 = (bf16[2624,128]{1,0:T(8,128)(2,1)}, f32[2624,128]{1,0:T(8,128)}, f32[2624,128]{1,0:T(8,128)}, f32[8,2624]{1,0:T(8,128)}) custom-call(f32[3,1,2]{2,1,0:T(1,128)} %reshape.707.gate_ref, bf16[2624,1152]{1,0:T(8,128)(2,1)} %shard_map.266.q_ref.k_ref.v_ref, bf16[2624,1152]{1,0:T(8,128)(2,1)} %shard_map.266.q_ref.k_ref.v_ref, ...), custom_call_target="tpu_custom_call" | custom-call | flops 4213178368 | bytes 6717440 | tf_op jit(solution)/shard_map/pallas_call | solution.py:379
  256.2 30.4 %shard_map.270 = (bf16[2624,128]{1,0:T(8,128)(2,1)}, f32[2624,128]{1,0:T(8,128)}, f32[2624,128]{1,0:T(8,128)}, f32[8,2624]{1,0:T(8,128)}) custom-call(f32[3,1,2]{2,1,0:T(1,128)} %reshape.707.gate_ref, bf16[2624,1152]{1,0:T(8,128)(2,1)} %shard_map.266.q_ref.k_ref.v_ref, bf16[2624,1152]{1,0:T(8,128)(2,1)} %shard_map.266.q_ref.k_ref.v_ref, ...), custom_call_target="tpu_custom_call" | custom-call | flops 4213178368 | bytes 6717440 | tf_op jit(solution)/shard_map/pallas_call | solution.py:379
  291.3 30.4 %shard_map.269 = (bf16[2624,128]{1,0:T(8,128)(2,1)}, f32[2624,128]{1,0:T(8,128)}, f32[2624,128]{1,0:T(8,128)}, f32[8,2624]{1,0:T(8,128)}) custom-call(f32[3,1,2]{2,1,0:T(1,128)} %reshape.707.gate_ref, bf16[2624,1152]{1,0:T(8,128)(2,1)} %shard_map.266.q_ref.k_ref.v_ref, bf16[2624,1152]{1,0:T(8,128)(2,1)} %shard_map.266.q_ref.k_ref.v_ref, ...), custom_call_target="tpu_custom_call" | custom-call | flops 4213178368 | bytes 6717440 | tf_op jit(solution)/shard_map/pallas_call | solution.py:379
  326.0 16.0 %all-to-all-done.3 = bf16[4,656,128]{2,1,0:T(8,128)(2,1)} async-done(((bf16[4,656,128]{2,1,0:T(8,128)(2,1)}), bf16[4,656,128]{2,1,0:T(8,128)(2,1)}, u32[]{:S(2)}, u32[]{:S(2)}) %all-to-all-start.3) | async-done | bytes 671776 | tf_op jit(solution)/shard_map/all_to_all | solution.py:754
  366.2 26.2 %fusion.163.gate_ref.up_ref = f32[656,8192]{1,0:T(8,128)} fusion(bf16[656,1536]{1,0:T(8,128)(2,1)} %copy-done.27, bf16[1536,8192]{1,0:T(8,128)(2,1)} %all-gather.8.cloned.1.call-done), kind=kOutput, calls=%fused_computation.363 | convolution fusion | flops 16508780544 | bytes 48676864 | tf_op jit(solution)/shard_map/dot_general | solution.py:28
  392.4 23.2 %shard_map.272 = (bf16[656,4096]{1,0:T(8,128)(2,1)}, bf16[656,4096]{1,0:T(8,128)(2,1)}) custom-call(s32[1]{0:T(128)} %bitcast.29.core_ref, f32[656,8192]{1,0:T(8,128)} %fusion.163.gate_ref.up_ref, f32[656,8192]{1,0:T(8,128)} %fusion.163.gate_ref.up_ref), custom_call_target="tpu_custom_call" | custom-call | flops 16121856 | bytes 32243712 | tf_op jit(solution)/shard_map/pallas_call | solution.py:602
  419.4 13.1 %multiply_reduce_fusion.14 = (f32[656]{0:T(1024)S(1)}, f32[656,1536]{1,0:T(8,128)S(1)}) fusion(bf16[656,4096]{1,0:T(8,128)(2,1)} %get-tuple-element.94, bf16[4096,1536]{1,0:T(8,128)(2,1)} %all-gather.10.cloned.1.call-done), kind=kOutput, calls=%fused_computation.67 | convolution fusion | flops 8256404992 | bytes 21989952 | tf_op jit(solution)/shard_map/dot_general | solution.py:28
  448.3 20.8 %fusion.6 = (bf16[656,4096]{1,0:T(8,128)(2,1)}, bf16[656,4096]{1,0:T(8,128)(2,1)}) fusion(f32[656,8192]{1,0:T(8,128)} %fusion.163.gate_ref.up_ref, bf16[656,1536]{1,0:T(8,128)(2,1)S(1)} %get-tuple-element.214, bf16[4096,1536]{1,0:T(8,128)(2,1)} %all-gather.10.cloned.1.call-done), kind=kOutput, calls=%fused_computation.13 | convolution fusion | flops 8289320960 | bytes 46841856 | tf_op jit(solution)/shard_map/dot_general | solution.py:32
  469.1 17.2 %convolution_convert_fusion = bf16[768,8192]{1,0:T(8,128)(2,1)} fusion(bf16[656,4096]{1,0:T(8,128)(2,1)} %get-tuple-element.208, bf16[656,4096]{1,0:T(8,128)(2,1)} %get-tuple-element.207, bf16[656,1536]{1,0:T(8,128)(2,1)} %fusion.29), kind=kOutput, calls=%fused_computation.7 | convolution fusion | flops 8282177536 | bytes 24338432 | tf_op jit(solution)/shard_map/dot_general | solution.py:36
  497.4 28.6 %multiply_reduce_fusion.9 = (f32[1536]{0:T(1024)}, f32[656]{0:T(1024)S(1)}, f32[1536]{0:T(1024)}, f32[1536]{0:T(1024)}, f32[656,1536]{1,0:T(8,128)}) fusion(f32[656,1536]{1,0:T(8,128)} %copy-done.2, f32[656]{0:T(1024)S(1)} %copy-done.75, f32[1536]{0:T(1024)S(1)} %copy-done.62, f32[656]{0:T(1024)S(1)} %get-tuple-element.255, f32[1536]{0:T(1024)S(1)} %copy-done.64, ...), kind=kOutput, calls=%fused_computation.59 | convolution fusion | flops 16547399680 | bytes 44022016 | tf_op jit(solution)/shard_map/dot_general | solution.py:32
  558.9 18.4 %add_convert_fusion = bf16[768,8192]{1,0:T(8,128)(2,1)} fusion(bf16[768,8192]{1,0:T(8,128)(2,1)} %collective-permute-done.1, bf16[656,4096]{1,0:T(8,128)(2,1)} %get-tuple-element.208, bf16[656,4096]{1,0:T(8,128)(2,1)} %get-tuple-element.207, bf16[656,1536]{1,0:T(8,128)(2,1)} %fusion.29), kind=kOutput, calls=%fused_computation | convolution fusion | flops 8294760448 | bytes 36921344 | tf_op jit(solution)/shard_map/dot_general | solution.py:36
  592.7 13.7 %shard_map.275 = (bf16[2624,128]{1,0:T(8,128)(2,1)}, bf16[512,128]{1,0:T(8,128)(2,1)}, bf16[512,128]{1,0:T(8,128)(2,1)}, f32[8,128]{1,0:T(8,128)}) custom-call(f32[3,1,2]{2,1,0:T(1,128)} %reshape.707.gate_ref, bf16[2624,1152]{1,0:T(8,128)(2,1)} %shard_map.266.q_ref.k_ref.v_ref, bf16[512,768]{1,0:T(8,128)(2,1)} %pad_maximum_fusion.8.tk_ref.tv_ref, ...), custom_call_target="tpu_custom_call" | custom-call | flops 1719664640 | bytes 4030464 | tf_op jit(solution)/shard_map/pallas_call | solution.py:495
  606.4 13.4 %shard_map.274 = (bf16[2624,128]{1,0:T(8,128)(2,1)}, bf16[512,128]{1,0:T(8,128)(2,1)}, bf16[512,128]{1,0:T(8,128)(2,1)}, f32[8,128]{1,0:T(8,128)}) custom-call(f32[3,1,2]{2,1,0:T(1,128)} %reshape.707.gate_ref, bf16[2624,1152]{1,0:T(8,128)(2,1)} %shard_map.266.q_ref.k_ref.v_ref, bf16[512,768]{1,0:T(8,128)(2,1)} %pad_maximum_fusion.8.tk_ref.tv_ref, ...), custom_call_target="tpu_custom_call" | custom-call | flops 1719664640 | bytes 4030464 | tf_op jit(solution)/shard_map/pallas_call | solution.py:495
  619.8 13.4 %shard_map.273 = (bf16[2624,128]{1,0:T(8,128)(2,1)}, bf16[512,128]{1,0:T(8,128)(2,1)}, bf16[512,128]{1,0:T(8,128)(2,1)}, f32[8,128]{1,0:T(8,128)}) custom-call(f32[3,1,2]{2,1,0:T(1,128)} %reshape.707.gate_ref, bf16[2624,1152]{1,0:T(8,128)(2,1)} %shard_map.266.q_ref.k_ref.v_ref, bf16[512,768]{1,0:T(8,128)(2,1)} %pad_maximum_fusion.8.tk_ref.tv_ref, ...), custom_call_target="tpu_custom_call" | custom-call | flops 1719664640 | bytes 4030464 | tf_op jit(solution)/shard_map/pallas_call | solution.py:495
  652.9 45.6 %shard_map.277 = (bf16[2624,128]{1,0:T(8,128)(2,1)}, bf16[2624,128]{1,0:T(8,128)(2,1)}, bf16[2624,128]{1,0:T(8,128)(2,1)}) custom-call(bf16[2624,1152]{1,0:T(8,128)(2,1)} %shard_map.266.q_ref.k_ref.v_ref, bf16[2624,1152]{1,0:T(8,128)(2,1)} %shard_map.266.q_ref.k_ref.v_ref, bf16[2624,1152]{1,0:T(8,128)(2,1)} %shard_map.266.q_ref.k_ref.v_ref, ...), custom_call_target="tpu_custom_call" | custom-call | flops 8813281280 | bytes 10076160 | tf_op jit(solution)/shard_map/pallas_call | solution.py:562
  698.5 19.1 %collective-permute-done.6 = bf16[512,768]{1,0:T(8,128)(2,1)} collective-permute-done((bf16[512,768]{1,0:T(8,128)(2,1)}, bf16[512,768]{1,0:T(8,128)(2,1)}, u32[]{:S(2)}, u32[]{:S(2)}) %collective-permute-start.6) | collective-permute-done | bytes 786464 | tf_op jit(solution)/shard_map/ppermute | solution.py:796
  739.7 45.7 %shard_map.278 = (bf16[2624,128]{1,0:T(8,128)(2,1)}, bf16[2624,128]{1,0:T(8,128)(2,1)}, bf16[2624,128]{1,0:T(8,128)(2,1)}) custom-call(bf16[2624,1152]{1,0:T(8,128)(2,1)} %shard_map.266.q_ref.k_ref.v_ref, bf16[2624,1152]{1,0:T(8,128)(2,1)} %shard_map.266.q_ref.k_ref.v_ref, bf16[2624,1152]{1,0:T(8,128)(2,1)} %shard_map.266.q_ref.k_ref.v_ref, ...), custom_call_target="tpu_custom_call" | custom-call | flops 8813281280 | bytes 10076160 | tf_op jit(solution)/shard_map/pallas_call | solution.py:562
  792.8 46.4 %shard_map.279 = (bf16[2624,128]{1,0:T(8,128)(2,1)}, bf16[2624,128]{1,0:T(8,128)(2,1)}, bf16[2624,128]{1,0:T(8,128)(2,1)}) custom-call(bf16[2624,1152]{1,0:T(8,128)(2,1)} %shard_map.266.q_ref.k_ref.v_ref, bf16[2624,1152]{1,0:T(8,128)(2,1)} %shard_map.266.q_ref.k_ref.v_ref, bf16[2624,1152]{1,0:T(8,128)(2,1)} %shard_map.266.q_ref.k_ref.v_ref, ...), custom_call_target="tpu_custom_call" | custom-call | flops 8813281280 | bytes 10076160 | tf_op jit(solution)/shard_map/pallas_call | solution.py:562
  839.2 55.9 %reduce-scatter.12.cloned.1.call-done = bf16[128,3072]{1,0:T(8,128)(2,1)} async-done(((bf16[512,3072]{1,0:T(8,128)(2,1)}), bf16[128,3072]{1,0:T(8,128)(2,1)}) %reduce-scatter.12.cloned.1.call-update) | async-done | bytes 786448 | tf_op jit(solution)/shard_map/reduce_scatter | solution.py:1097
  895.1 15.2 %shard_map.280 = (f32[8,2624]{1,0:T(8,128)}, f32[8,384]{1,0:T(8,128)}) custom-call(bf16[2624,128]{1,0:T(8,128)(2,1)} %get-tuple-element.117.refs_0_, bf16[2624,128]{1,0:T(8,128)(2,1)} %get-tuple-element.124.refs_1_, bf16[2624,128]{1,0:T(8,128)(2,1)} %get-tuple-element.130.refs_2_, bf16[2624,128]{1,0:T(8,128)(2,1)} %get-tuple-element.131.refs_3_, ...), custom_call_target="tpu_custom_call" | custom-call | flops 120913920 | bytes 15114240 | tf_op jit(solution)/shard_map/pallas_call | solution.py:269
  919.2 15.6 %shard_map.282 = bf16[2624,1152]{1,0:T(8,128)(2,1)} custom-call(bf16[2624,128]{1,0:T(8,128)(2,1)} %get-tuple-element.117.refs_0_, bf16[2624,128]{1,0:T(8,128)(2,1)} %get-tuple-element.124.refs_1_, bf16[2624,128]{1,0:T(8,128)(2,1)} %get-tuple-element.130.refs_2_, bf16[2624,128]{1,0:T(8,128)(2,1)} %get-tuple-element.131.refs_3_, ...), custom_call_target="tpu_custom_call" | custom-call | flops 120913920 | bytes 21159936 | tf_op jit(solution)/shard_map/pallas_call | solution.py:282
  938.3 15.4 %convolution_convert_fusion.1 = bf16[2624,1536]{1,0:T(8,128)(2,1)} fusion(bf16[2624,1152]{1,0:T(8,128)(2,1)} %shard_map.282, bf16[1536,1152]{1,0:T(8,128)(2,1)S(1)} %bitcast.237), kind=kOutput, calls=%fused_computation.9 | convolution fusion | flops 9290219520 | bytes 17645568 | tf_op jit(solution)/shard_map/dot_general | solution.py:32
  953.8 13.2 %all-to-all-start.8 = ((bf16[4,48,1536]{2,1,0:T(8,128)(2,1)}), bf16[4,48,1536]{2,1,0:T(8,128)(2,1)}, u32[]{:S(2)}, u32[]{:S(2)}) async-start(bf16[4,48,1536]{2,1,0:T(8,128)(2,1)} %bitcast.55), calls=%async_computation.13 | async-start | bytes 1179648 | tf_op jit(solution)/shard_map/all_to_all | solution.py:754
  974.4 15.6 %convolution_convert_fusion.3 = bf16[1536,1152]{1,0:T(8,128)(2,1)S(1)} fusion(bf16[2624,1536]{1,0:T(8,128)(2,1)} %copy-done.18, bf16[2624,1152]{1,0:T(8,128)(2,1)} %shard_map.282), kind=kOutput, calls=%fused_computation.21 | convolution fusion | flops 9287958528 | bytes 17645568 | tf_op jit(solution)/shard_map/dot_general | solution.py:36
  1019.0 31.4 %all-to-all-start.9 = ((bf16[4,128,1024]{2,1,0:T(8,128)(2,1)}), bf16[4,128,1024]{2,1,0:T(8,128)(2,1)S(1)}, u32[]{:S(2)}, u32[]{:S(2)}) async-start(bf16[4,128,1024]{2,1,0:T(8,128)(2,1)} %bitcast.234), calls=%async_computation.14 | async-start | bytes 2097152 | tf_op jit(solution)/shard_map/all_to_all | solution.py:754
  1059.2 14.2 %all-to-all-done.9 = bf16[4,128,1024]{2,1,0:T(8,128)(2,1)S(1)} async-done(((bf16[4,128,1024]{2,1,0:T(8,128)(2,1)}), bf16[4,128,1024]{2,1,0:T(8,128)(2,1)S(1)}, u32[]{:S(2)}, u32[]{:S(2)}) %all-to-all-start.9) | async-done | bytes 1048608 | tf_op jit(solution)/shard_map/all_to_all | solution.py:754
  1113.3 31.5 %shard_map.283 = f32[4,296,128]{2,1,0:T(8,128)} custom-call(f32[12,128]{1,0:T(8,128)} %bitcast.277, f32[12,128]{1,0:T(8,128)} %bitcast.276, f32[12,128]{1,0:T(8,128)} %bitcast.284, f32[12,128]{1,0:T(8,128)} %bitcast.271, f32[60,128]{1,0:T(8,128)} %select_n.427.refs_4_, f32[1,128]{1,0:T(1,128)} %pad_bitcast_fusion.refs_5_, f32[32,128]{1,0:T(8,128)} %bitcast.270, ...), custom_call_target="tpu_custom_call" | custom-call | tf_op jit(solution)/shard_map/pallas_call | solution.py:734
  (438 shorter events, 404.8 us)
Async XLA Ops:
  7.2 122.6 %all-gather.12.cloned.1.call-start = ((), (), s32[]{:S(2)}) async-start(), calls=%async_computation.24 | async-start | bytes 10076160 | tf_op jit(solution)/shard_map/all_gather | solution.py:901
  7.9 336.9 %all-gather.6.cloned.1.call-start = ((), (), s32[]{:S(2)}) async-start(), calls=%async_computation.16 | async-start | bytes 5308416 | tf_op jit(solution)/shard_map/all_gather | solution.py:829
  10.2 356.0 %all-gather.8.cloned.1.call-start = ((), (), s32[]{:S(2)}) async-start(), calls=%async_computation.17 | async-start | bytes 28311552 | tf_op jit(solution)/shard_map/all_gather | solution.py:829
  25.0 61.4 %all-to-all-start.1 = ((bf16[4,192,1152]{2,1,0:T(8,128)(2,1)}), bf16[4,192,1152]{2,1,0:T(8,128)(2,1)}, u32[]{:S(2)}, u32[]{:S(2)}) async-start(bf16[4,192,1152]{2,1,0:T(8,128)(2,1)} %reshape.652), calls=%async_computation.1 | async-start | bytes 3538944 | tf_op jit(solution)/shard_map/all_to_all | solution.py:754
  30.3 389.1 %all-gather.10.cloned.1.call-start = ((), (), s32[]{:S(2)}) async-start(), calls=%async_computation.18 | async-start | bytes 14155776 | tf_op jit(solution)/shard_map/all_gather | solution.py:829
  86.5 29.5 %all-to-all-start = ((bf16[4,128,1024]{2,1,0:T(8,128)(2,1)}), bf16[4,128,1024]{2,1,0:T(8,128)(2,1)S(1)}, u32[]{:S(2)}, u32[]{:S(2)}) async-start(bf16[4,128,1024]{2,1,0:T(8,128)(2,1)} %fusion.53), calls=%async_computation | async-start | bytes 2097152 | tf_op jit(solution)/shard_map/all_to_all | solution.py:754
  107.1 16.9 %collective-permute-start = (bf16[4,192,1152]{2,1,0:T(8,128)(2,1)}, bf16[4,192,1152]{2,1,0:T(8,128)(2,1)}, u32[]{:S(2)}, u32[]{:S(2)}) collective-permute-start(bf16[4,192,1152]{2,1,0:T(8,128)(2,1)} %all-to-all-done.1), channel_id=1, source_target_pairs={{0,4},{4,0},{1,5},{5,1},{2,6},{6,2},{3,7},{7,3},{8,12},{12,8},{9,1... | collective-permute-start | bytes 5308424 | tf_op jit(solution)/shard_map/ppermute | solution.py:758
  129.8 75.0 %all-to-all-start.2 = ((bf16[4,512,768]{2,1,0:T(8,128)(2,1)}), bf16[4,512,768]{2,1,0:T(8,128)(2,1)}, u32[]{:S(2)}, u32[]{:S(2)}) async-start(bf16[4,512,768]{2,1,0:T(8,128)(2,1)} %pad_maximum_fusion.2), calls=%async_computation.2 | async-start | bytes 6291456 | tf_op jit(solution)/shard_map/all_to_all | solution.py:754
  252.7 34.0 %all-to-all-start.5 = ((bf16[4,656,128]{2,1,0:T(8,128)(2,1)}), bf16[4,656,128]{2,1,0:T(8,128)(2,1)S(1)}, u32[]{:S(2)}, u32[]{:S(2)}) async-start(bf16[4,656,128]{2,1,0:T(8,128)(2,1)} %bitcast.264), calls=%async_computation.5 | async-start | bytes 1343488 | tf_op jit(solution)/shard_map/all_to_all | solution.py:754
  286.6 35.0 %all-to-all-start.4 = ((bf16[4,656,128]{2,1,0:T(8,128)(2,1)}), bf16[4,656,128]{2,1,0:T(8,128)(2,1)S(1)}, u32[]{:S(2)}, u32[]{:S(2)}) async-start(bf16[4,656,128]{2,1,0:T(8,128)(2,1)} %bitcast.263), calls=%async_computation.4 | async-start | bytes 1343488 | tf_op jit(solution)/shard_map/all_to_all | solution.py:754
  321.6 20.3 %all-to-all-start.3 = ((bf16[4,656,128]{2,1,0:T(8,128)(2,1)}), bf16[4,656,128]{2,1,0:T(8,128)(2,1)}, u32[]{:S(2)}, u32[]{:S(2)}) async-start(bf16[4,656,128]{2,1,0:T(8,128)(2,1)} %bitcast.262), calls=%async_computation.3 | async-start | bytes 1343488 | tf_op jit(solution)/shard_map/all_to_all | solution.py:754
  325.9 261.4 %reduce-scatter.6.cloned.1.call-start = ((), (), s32[]{:S(2)}) async-start(), calls=%async_computation.19 | async-start | bytes 7864320 | tf_op jit(solution)/shard_map/reduce_scatter | solution.py:777
  448.0 38.5 %collective-permute-start.3 = (bf16[2048,1536]{1,0:T(8,128)(2,1)}, bf16[2048,1536]{1,0:T(8,128)(2,1)}, u32[]{:S(2)}, u32[]{:S(2)}) collective-permute-start(bf16[2048,1536]{1,0:T(8,128)(2,1)} %convolution_convert_fusion.2), channel_id=1, source_target_pairs={{0,4},{4,0},{1,5},{5,1},{2,6},{6,2},{3,7},{7,3},{8,12},{12,8},{9,1... | collective-permute-start | bytes 18874376 | tf_op jit(solution)/shard_map/ppermute | solution.py:758
  486.3 72.5 %collective-permute-start.1 = (bf16[768,8192]{1,0:T(8,128)(2,1)}, bf16[768,8192]{1,0:T(8,128)(2,1)}, u32[]{:S(2)}, u32[]{:S(2)}) collective-permute-start(bf16[768,8192]{1,0:T(8,128)(2,1)} %convolution_convert_fusion), channel_id=1, source_target_pairs={{0,4},{4,0},{1,5},{5,1},{2,6},{6,2},{3,7},{7,3},{8,12},{12,8},{9,1... | collective-permute-start | bytes 37748744 | tf_op jit(solution)/shard_map/ppermute | solution.py:758
  549.0 37.8 %all-to-all-start.6 = ((bf16[4,656,384]{2,1,0:T(8,128)(2,1)}), bf16[4,656,384]{2,1,0:T(8,128)(2,1)S(1)}, u32[]{:S(2)}, u32[]{:S(2)}) async-start(bf16[4,656,384]{2,1,0:T(8,128)(2,1)} %bitcast.231), calls=%async_computation.6 | async-start | bytes 4030464 | tf_op jit(solution)/shard_map/all_to_all | solution.py:754
  552.6 232.8 %reduce-scatter.10.cloned.1.call-start = ((), (), s32[]{:S(2)}) async-start(), calls=%async_computation.21 | async-start | bytes 2949120 | tf_op jit(solution)/shard_map/reduce_scatter | solution.py:777
  587.3 198.1 %reduce-scatter.8.cloned.1.call-start = ((), (), s32[]{:S(2)}) async-start(), calls=%async_computation.20 | async-start | bytes 15728640 | tf_op jit(solution)/shard_map/reduce_scatter | solution.py:777
  588.1 129.5 %all-to-all-start.7 = ((bf16[4,128,1536]{2,1,0:T(8,128)(2,1)}), bf16[4,128,1536]{2,1,0:T(8,128)(2,1)}, u32[]{:S(2)}, u32[]{:S(2)}) async-start(bf16[4,128,1536]{2,1,0:T(8,128)(2,1)} %bitcast.253), calls=%async_computation.8 | async-start | bytes 3145728 | tf_op jit(solution)/shard_map/all_to_all | solution.py:754
  592.7 302.4 %reduce-scatter.12.cloned.1.call-start = ((), (), s32[]{:S(2)}) async-start(), calls=%async_computation.22 | async-start | bytes 3932160 | tf_op jit(solution)/shard_map/reduce_scatter | solution.py:1097
  646.8 51.7 %collective-permute-start.4 = (bf16[512,768]{1,0:T(8,128)(2,1)}, bf16[512,768]{1,0:T(8,128)(2,1)}, u32[]{:S(2)}, u32[]{:S(2)}) collective-permute-start(bf16[512,768]{1,0:T(8,128)(2,1)} %get-tuple-element.226), channel_id=1, source_target_pairs={{0,1},{1,0},{2,3},{3,2},{4,5},{5,4},{6,7},{7,6},{8,9},{9,8},{10,11... | collective-permute-start | bytes 2359304 | tf_op jit(solution)/shard_map/ppermute | solution.py:796
  648.3 50.2 %collective-permute-start.5 = (bf16[512,768]{1,0:T(8,128)(2,1)}, bf16[512,768]{1,0:T(8,128)(2,1)}, u32[]{:S(2)}, u32[]{:S(2)}) collective-permute-start(bf16[512,768]{1,0:T(8,128)(2,1)} %get-tuple-element.226), channel_id=1, source_target_pairs={{0,2},{1,3},{2,0},{3,1},{4,6},{5,7},{6,4},{7,5},{8,10},{9,11},{10,... | collective-permute-start | bytes 2359304 | tf_op jit(solution)/shard_map/ppermute | solution.py:796
  648.8 68.8 %collective-permute-start.6 = (bf16[512,768]{1,0:T(8,128)(2,1)}, bf16[512,768]{1,0:T(8,128)(2,1)}, u32[]{:S(2)}, u32[]{:S(2)}) collective-permute-start(bf16[512,768]{1,0:T(8,128)(2,1)} %get-tuple-element.226), channel_id=1, source_target_pairs={{0,3},{1,2},{2,1},{3,0},{4,7},{5,6},{6,5},{7,4},{8,11},{9,10},{10,... | collective-permute-start | bytes 2359304 | tf_op jit(solution)/shard_map/ppermute | solution.py:796
  739.6 368.5 %reduce-scatter.14.cloned.1.call-start = ((), (), s32[]{:S(2)}) async-start(), calls=%async_computation.23 | async-start | bytes 10076160 | tf_op jit(solution)/shard_map/reduce_scatter | solution.py:1127
  788.5 146.4 %collective-permute-start.10 = (bf16[48,8192]{1,0:T(8,128)(2,1)}, bf16[48,8192]{1,0:T(8,128)(2,1)}, u32[]{:S(2)}, u32[]{:S(2)}) collective-permute-start(bf16[48,8192]{1,0:T(8,128)(2,1)} %get-tuple-element.219), channel_id=1, source_target_pairs={{0,24},{8,16},{16,8},{24,0},{1,25},{9,17},{17,9},{25,1},{2,26},{10... | collective-permute-start | bytes 2359304 | tf_op jit(solution)/shard_map/ppermute | solution.py:783
  792.3 142.5 %collective-permute-start.9 = (bf16[48,8192]{1,0:T(8,128)(2,1)}, bf16[48,8192]{1,0:T(8,128)(2,1)}, u32[]{:S(2)}, u32[]{:S(2)}) collective-permute-start(bf16[48,8192]{1,0:T(8,128)(2,1)} %get-tuple-element.220), channel_id=1, source_target_pairs={{0,16},{8,24},{16,0},{24,8},{1,17},{9,25},{17,1},{25,9},{2,18},{10... | collective-permute-start | bytes 2359304 | tf_op jit(solution)/shard_map/ppermute | solution.py:783
  792.3 142.6 %collective-permute-start.8 = (bf16[48,8192]{1,0:T(8,128)(2,1)}, bf16[48,8192]{1,0:T(8,128)(2,1)}, u32[]{:S(2)}, u32[]{:S(2)}) collective-permute-start(bf16[48,8192]{1,0:T(8,128)(2,1)} %get-tuple-element.218), channel_id=1, source_target_pairs={{0,8},{8,0},{16,24},{24,16},{1,9},{9,1},{17,25},{25,17},{2,10},{10... | collective-permute-start | bytes 2359304 | tf_op jit(solution)/shard_map/ppermute | solution.py:783
  953.8 46.8 %all-to-all-start.8 = ((bf16[4,48,1536]{2,1,0:T(8,128)(2,1)}), bf16[4,48,1536]{2,1,0:T(8,128)(2,1)}, u32[]{:S(2)}, u32[]{:S(2)}) async-start(bf16[4,48,1536]{2,1,0:T(8,128)(2,1)} %bitcast.55), calls=%async_computation.13 | async-start | bytes 1179648 | tf_op jit(solution)/shard_map/all_to_all | solution.py:754
  967.0 23.1 %collective-permute-start.11 = (bf16[128,3072]{1,0:T(8,128)(2,1)}, bf16[128,3072]{1,0:T(8,128)(2,1)}, u32[]{:S(2)}, u32[]{:S(2)}) collective-permute-start(bf16[128,3072]{1,0:T(8,128)(2,1)} %reduce-scatter.12.cloned.1.call-done), channel_id=1, source_target_pairs={{0,0},{1,8},{2,16},{3,24},{4,4},{5,12},{6,20},{7,28},{8,1},{9,9},{... | collective-permute-start | bytes 2359304 | tf_op jit(solution)/shard_map/ppermute | solution.py:1118
  1019.0 54.4 %all-to-all-start.9 = ((bf16[4,128,1024]{2,1,0:T(8,128)(2,1)}), bf16[4,128,1024]{2,1,0:T(8,128)(2,1)S(1)}, u32[]{:S(2)}, u32[]{:S(2)}) async-start(bf16[4,128,1024]{2,1,0:T(8,128)(2,1)} %bitcast.234), calls=%async_computation.14 | async-start | bytes 2097152 | tf_op jit(solution)/shard_map/all_to_all | solution.py:754
  1054.8 31.2 %collective-permute-start.13 = (bf16[192,1152]{1,0:T(8,128)(2,1)}, bf16[192,1152]{1,0:T(8,128)(2,1)}, u32[]{:S(2)}, u32[]{:S(2)}) collective-permute-start(bf16[192,1152]{1,0:T(8,128)(2,1)} %get-tuple-element.224), channel_id=1, source_target_pairs={{0,8},{8,0},{16,24},{24,16},{1,9},{9,1},{17,25},{25,17},{2,10},{10... | collective-permute-start | bytes 1327112 | tf_op jit(solution)/shard_map/ppermute | solution.py:783
  1055.4 33.8 %collective-permute-start.14 = (bf16[192,1152]{1,0:T(8,128)(2,1)}, bf16[192,1152]{1,0:T(8,128)(2,1)}, u32[]{:S(2)}, u32[]{:S(2)}) collective-permute-start(bf16[192,1152]{1,0:T(8,128)(2,1)} %get-tuple-element.223), channel_id=1, source_target_pairs={{0,16},{8,24},{16,0},{24,8},{1,17},{9,25},{17,1},{25,9},{2,18},{10... | collective-permute-start | bytes 1327112 | tf_op jit(solution)/shard_map/ppermute | solution.py:783
  1058.9 30.3 %collective-permute-start.15 = (bf16[192,1152]{1,0:T(8,128)(2,1)}, bf16[192,1152]{1,0:T(8,128)(2,1)}, u32[]{:S(2)}, u32[]{:S(2)}) collective-permute-start(bf16[192,1152]{1,0:T(8,128)(2,1)} %get-tuple-element.222), channel_id=1, source_target_pairs={{0,24},{8,16},{16,8},{24,0},{1,25},{9,17},{17,9},{25,1},{2,26},{10... | collective-permute-start | bytes 1327112 | tf_op jit(solution)/shard_map/ppermute | solution.py:783
  (100 other events, 2030.1 us)
Sparse Core Ops, SparseCore 0:
  9.9 119.8 all-gather.11
  131.7 63.6 all-gather.5
  197.3 147.6 all-gather.7
  347.3 72.1 all-gather.9
  496.8 90.4 reduce-scatter.5
  590.2 36.7 reduce-scatter.9
  630.1 155.1 reduce-scatter.7
  787.6 107.4 reduce-scatter.11
  953.9 134.5 reduce-scatter.13

commit v7 on v6

--- a/solution.py
+++ b/solution.py
@@ -1018,13 +1018,9 @@
     grad_gate_feed = per_image(grad_result * down_normed * (1.0 - gate_feed * gate_feed))
     grad_down_low = norm_pull(grad_down_y * norm_gains[6], down_unit, down_inverse).astype(BF16)
     grad_activated = times_transposed(grad_down_low, full_down)
-    grad_gate_up_low = jnp.concatenate(
-        [
-            (grad_activated * up_half * sigmoid * (1.0 + gate_half * (1.0 - sigmoid))).astype(BF16),
-            (grad_activated * gate_half * sigmoid).astype(BF16),
-        ],
-        axis=1,
-    )
+    grad_gate_low = (grad_activated * up_half * sigmoid * (1.0 + gate_half * (1.0 - sigmoid))).astype(BF16)
+    grad_up_low = (grad_activated * gate_half * sigmoid).astype(BF16)
+    grad_gate_up_low = jnp.concatenate([grad_gate_low, grad_up_low], axis=1)
     grad_normed_feed = times_transposed(grad_gate_up_low, full_gate_up)
     grad_feed_y = grad_normed_feed * scale_feed
     grad_gain_five = jnp.sum(grad_feed_y * hidden_unit, axis=0)
@@ -1043,15 +1039,18 @@
         return value.reshape(deep, -1, value.shape[1])
 
     down_both = chip_sum(*down_columns, grad_down_low)
-    gate_up_both = chip_sum(*device_columns(normed_feed_low, deep, narrow), grad_gate_up_low)
+    feed_columns = device_columns(normed_feed_low, deep, narrow)
+    gate_both = chip_sum(*feed_columns, grad_gate_low)
+    up_both = chip_sum(*feed_columns, grad_up_low)
     out_both = chip_sum(*device_columns(mixed_low, deep, narrow), grad_branch_low)
     down_part = fsdp_sum(down_both)
-    grad_heads, gate_up_both, out_both, down_part = lax.optimization_barrier(
-        (grad_heads, gate_up_both, out_both, down_part)
-    )
+    grad_heads, gate_both, up_both, out_both, down_part = lax.optimization_barrier(
+        (grad_heads, gate_both, up_both, out_both, down_part)
+    )
+    gate_part = fsdp_sum(gate_both)
+    out_part = fsdp_sum(out_both)
+    up_part = fsdp_sum(up_both)
     came_downs = exchange(by_z(down_part), "z")
-    gate_up_part = fsdp_sum(gate_up_both)
-    out_part = fsdp_sum(out_both)
     crossed = [
         cross_back(
             pair, own_gates, packed, text_packed, row, grad_heads, cross_outs[pair], stats[pair],
@@ -1081,7 +1080,10 @@
 
     came_texts = to_all(grad_text_own, narrow)
     backs = [self_pair(0)]
-    first, came_downs, *came_texts = lax.optimization_barrier((backs[0][0], came_downs, *came_texts))
+    first, came_downs, gate_part, *came_texts = lax.optimization_barrier(
+        (backs[0][0], came_downs, gate_part, *came_texts)
+    )
+    gate_pieces = z_pieces(by_z(gate_part), deep)
     grad_down_weight = jnp.sum(came_downs.astype(F32), axis=0)
     backs[0] = (first, *backs[0][1:])
     grad_text_all = in_order(grad_text_own, came_texts)
@@ -1094,17 +1096,27 @@
     text_both = (outer_sum(own_text, grad_text_columns) + came_text.astype(F32)).astype(BF16)
     grad_heads, text_both, first = lax.optimization_barrier((grad_heads, text_both, backs[0][0]))
     backs[0] = (first, *backs[0][1:])
-    text_part = lax.psum_scatter(text_both, "z", scatter_dimension=0, tiled=True)
+    came_text_z = exchange(by_z(text_both), "z")
     backs.append(self_pair(1))
     if pairs > 2:
-        grad_heads, gate_up_part, out_part, second = lax.optimization_barrier(
-            (grad_heads, gate_up_part, out_part, backs[1][0])
+        grad_heads, up_part, out_part, second = lax.optimization_barrier(
+            (grad_heads, up_part, out_part, backs[1][0])
         )
         backs[1] = (second, *backs[1][1:])
         backs += [self_pair(pair) for pair in range(2, pairs)]
-    grad_gate_up_weight = added(z_pieces(by_z(gate_up_part), deep))
-    last, text_part = lax.optimization_barrier((backs[-1][0], text_part))
+    up_pieces = z_pieces(by_z(up_part), deep)
+    last, came_text_z = lax.optimization_barrier((backs[-1][0], came_text_z))
     backs[-1] = (last, *backs[-1][1:])
+    text_part = jnp.sum(came_text_z.astype(F32), axis=0).astype(BF16)
+    last, grad_text_columns = lax.optimization_barrier((backs[-1][0], grad_text_columns))
+    backs[-1] = (last, *backs[-1][1:])
+    grad_text_slice = times_transposed(grad_text_columns, text_weight).astype(BF16)
+    came_text = exchange(
+        grad_text_slice.reshape(image_count, narrow, caption_local, text_cols)
+        .transpose(1, 0, 2, 3)
+        .reshape(narrow, text_local, text_cols),
+        "fsdp",
+    )
     came_out_z = exchange(by_z(out_part), "z")
     own_gate_grad = jnp.sum(gate_sums[:, 0, :].reshape(pairs * halves, head_dim), axis=1)[:heads_here]
     grad_head_gate = lax.dynamic_update_slice_in_dim(
@@ -1123,7 +1135,10 @@
             for z in range(deep) for c in range(2) for f in range(narrow)
         ],
     )
-    grad_projected_low, grad_gate_up_weight = lax.optimization_barrier((grad_projected_low, grad_gate_up_weight))
+    grad_projected_low, came_text, *pieces = lax.optimization_barrier(
+        (grad_projected_low, came_text, *gate_pieces, *up_pieces)
+    )
+    grad_gate_up_weight = jnp.concatenate([added(pieces[:deep]), added(pieces[deep:])], axis=1)
     grad_normed = lax.psum_scatter(
         times_transposed(grad_projected_low, own_qkv).astype(BF16), "fsdp", scatter_dimension=0, tiled=True
     )
@@ -1148,16 +1163,7 @@
     grad_out_weight = jnp.sum(came_out_z.astype(F32), axis=0)
     own_grad, other_grad = by_core(qkv_grad[:, 0], qkv_grad[:, 1])
     own_grad = (own_grad.astype(F32) + core_swap(other_grad).astype(F32)).astype(BF16)
-    own_grad, grad_text_columns = lax.optimization_barrier((own_grad, grad_text_columns))
     own_pieces = z_pieces(own_grad, deep)
-    grad_text_slice = times_transposed(grad_text_columns, text_weight).astype(BF16)
-    came_text = exchange(
-        grad_text_slice.reshape(image_count, narrow, caption_local, text_cols)
-        .transpose(1, 0, 2, 3)
-        .reshape(narrow, text_local, text_cols),
-        "fsdp",
-    )
-
     grad_text_normed = (
         came_text
         .transpose(1, 0, 2)
@@ -1173,15 +1179,6 @@
     )
 
     grad_text, grad_text_gain, *own_pieces = lax.optimization_barrier((grad_text, grad_text_gain, *own_pieces))
-    own_grad = added(own_pieces)
-    grad_qkv_weight = (
-        exchange(narrowed(own_grad.astype(BF16), 3).reshape(narrow, -1, 3 * part), "fsdp")
-        .reshape(narrow, -1, 3, part)
-        .transpose(1, 2, 0, 3)
-        .reshape(-1, 3 * model_width)
-        .astype(F32)
-    )
-
     grad_normed = grad_normed.astype(F32)
 
     token_unit = token_in * token_inverse
@@ -1195,6 +1192,15 @@
     lanes_of_row = model_width // 128
     summed, kept = finish(
         [lane_rows(grad_gain_zero), *ready, lane_rows(grad_text_gain)], [*grad_scale_attend, *later], narrow, wide, 5
+    )
+    summed, kept, *own_pieces = lax.optimization_barrier((summed, kept, *own_pieces))
+    own_grad = added(own_pieces)
+    grad_qkv_weight = (
+        exchange(narrowed(own_grad.astype(BF16), 3).reshape(narrow, -1, 3 * part), "fsdp")
+        .reshape(narrow, -1, 3, part)
+        .transpose(1, 2, 0, 3)
+        .reshape(-1, 3 * model_width)
+        .astype(F32)
     )
     every_image = wide * image_count
     per_part = image_count * lanes_of_row

time: 1180 us -> 1110 us (0.941)
  waiting for transfers between devices: 151 us -> 88.7 us
    reduce_scatter x1 -> x0, waiting for transfers between devices: 55.9 us -> none  [shards(): lax.psum_scatter(text_both, 'z', scatter_dimension=0, tiled=True)]
    ppermute x6 -> x9, starting transfers between devices: 8.77 us -> 39 us  [z_pieces(): lax.ppermute(lax.dynamic_index_in_dim(blocks, me ^ step, 0, keepdims=Fals...]
    all_to_all x11 -> x12, starting transfers between devices: 83.4 us -> 53.9 us  [exchange(): return lax.all_to_all(blocks, axis, 0, 0, tiled=True)]
    all_to_all x11 -> x12, waiting for transfers between devices: 60.2 us -> 30.8 us  [exchange(): return lax.all_to_all(blocks, axis, 0, 0, tiled=True)]
    ppermute x6 -> x9, waiting for transfers between devices: 3.26 us -> 24.5 us  [z_pieces(): lax.ppermute(lax.dynamic_index_in_dim(blocks, me ^ step, 0, keepdims=Fals...]
    ppermute x3, waiting for transfers between devices: 19.1 us -> 5.07 us  [to_all(): lax.ppermute(block, 'fsdp', [(i, i ^ step) for i in range(narrow)])]
    dot_general x9 -> x11, matrix products: 83.8 us -> 88.4 us  [outer_sum(): lax.dot_general(left, right, (((0,), (0,)), ((), ())), preferred_element_...]
  transfers between devices with their start and end apart: 36 -> 41, of which waited for: 13 -> 13; matrix products, arithmetic and copies ran while one was open for 31% -> 34% of each run, Pallas kernels for 36% -> 38%
where the time goes in v7:
time: 1110 us; the launch traced here: 1100 us
  Pallas kernels  444 us (40%)
  matrix products  244 us (22%)
  other arithmetic  110 us (10%)
  starting transfers between devices  99.7 us (9%)
  local copies, waits for them, and re-layouts  99.3 us (9%)
  waiting for transfers between devices  88.7 us (8%)
  between operations  18.5 us (2%)
    pallas_call x3, Pallas kernels, self_back(): pl.pallas_call(functools.partial(self_back_kernel, head_dim, FIRST_PATCHE...  137 us
    pallas_call x3, Pallas kernels, attend(): pl.pallas_call(functools.partial(attend_kernel, head_dim, FIRST_PATCHES,...  91.9 us
    dot_general x11, matrix products, outer_sum(): lax.dot_general(left, right, (((0,), (0,)), ((), ())), preferred_element_...  88.4 us
    dot_general x11, matrix products, low_product(): return jnp.dot(left, right, preferred_element_type=F32)  77.1 us
    dot_general x5, matrix products, times_transposed(): lax.dot_general(left, right, (((1,), (1,)), ((), ())), preferred_element_...  75.2 us
    pallas_call x5, Pallas kernels, fsdp_share(): pl.pallas_call(functools.partial(fsdp_share_kernel, narrow), in_specs=[pl...  65.7 us
    all_to_all x12, starting transfers between devices, exchange(): return lax.all_to_all(blocks, axis, 0, 0, tiled=True)  53.9 us
    pallas_call x3, Pallas kernels, cross_back(): pl.pallas_call(functools.partial(cross_back_kernel, head_dim, FIRST_PATCH...  40.3 us
  transfers between devices with their start and end apart: 41, of which 13 were waited for; matrix products, arithmetic and copies ran while one was open for 34% of the time, Pallas kernels for 38%

profile of v7, /device:TPU:0, one launch (start us, length us, event | category | flops | bytes accessed | tf_op | source)
XLA Modules:
  0.0 1104.0 jit_solution(16953142571399467093)
XLA Ops:
  40.4 27.4 %shard_map.263 = f32[4,96,128]{2,1,0:T(8,128)} custom-call(f32[96,128]{1,0:T(8,128)} %reshape.649.x_ref), custom_call_target="tpu_custom_call" | custom-call | bytes 393216 | tf_op jit(solution)/shard_map/pallas_call | solution.py:648
  75.8 10.5 negate_select_fusion
  150.1 13.6 %fusion.168.projected_ref.refs_6_.refs_9_ = f32[2624,1152]{1,0:T(8,128)} fusion(bf16[2624,1536]{1,0:T(8,128)(2,1)S(1)} %fusion.3, bf16[1536,1152]{1,0:T(8,128)(2,1)S(1)} %bitcast.250), kind=kOutput, calls=%fused_computation.372 | convolution fusion | flops 9286189056 | bytes 23691264 | tf_op jit(solution)/shard_map/dot_general | solution.py:28
  163.7 9.4 shard_map.264.x_ref
  173.1 16.2 %shard_map.265.stats_ref.refs_7_.refs_10_ = f32[4,8,2624]{2,1,0:T(8,128)} custom-call(f32[8,2624]{1,0:T(8,128)} %shard_map.264.x_ref), custom_call_target="tpu_custom_call" | custom-call | bytes 671744 | tf_op jit(solution)/shard_map/pallas_call | solution.py:648
  189.3 15.5 %shard_map.266.q_ref.k_ref.v_ref = bf16[2624,1152]{1,0:T(8,128)(2,1)} custom-call(f32[2624,1152]{1,0:T(8,128)} %fusion.168.projected_ref.refs_6_.refs_9_, f32[4,8,2624]{2,1,0:T(8,128)} %shard_map.265.stats_ref.refs_7_.refs_10_, f32[2624,128]{1,0:T(8,128)} %get-tuple-element.275.cos_ref.refs_8_.refs_12_, ...), custom_call_target="tpu_custom_call" | custom-call | flops 120913920 | bytes 18137088 | tf_op jit(solution)/shard_map/pallas_call | solution.py:183
  221.5 31.1 %shard_map.271 = (bf16[2624,128]{1,0:T(8,128)(2,1)}, f32[2624,128]{1,0:T(8,128)}, f32[2624,128]{1,0:T(8,128)}, f32[8,2624]{1,0:T(8,128)}) custom-call(f32[3,1,2]{2,1,0:T(1,128)} %reshape.712.gate_ref, bf16[2624,1152]{1,0:T(8,128)(2,1)} %shard_map.266.q_ref.k_ref.v_ref, bf16[2624,1152]{1,0:T(8,128)(2,1)} %shard_map.266.q_ref.k_ref.v_ref, ...), custom_call_target="tpu_custom_call" | custom-call | flops 4213178368 | bytes 6717440 | tf_op jit(solution)/shard_map/pallas_call | solution.py:379
  256.2 30.4 %shard_map.270 = (bf16[2624,128]{1,0:T(8,128)(2,1)}, f32[2624,128]{1,0:T(8,128)}, f32[2624,128]{1,0:T(8,128)}, f32[8,2624]{1,0:T(8,128)}) custom-call(f32[3,1,2]{2,1,0:T(1,128)} %reshape.712.gate_ref, bf16[2624,1152]{1,0:T(8,128)(2,1)} %shard_map.266.q_ref.k_ref.v_ref, bf16[2624,1152]{1,0:T(8,128)(2,1)} %shard_map.266.q_ref.k_ref.v_ref, ...), custom_call_target="tpu_custom_call" | custom-call | flops 4213178368 | bytes 6717440 | tf_op jit(solution)/shard_map/pallas_call | solution.py:379
  291.2 30.4 %shard_map.269 = (bf16[2624,128]{1,0:T(8,128)(2,1)}, f32[2624,128]{1,0:T(8,128)}, f32[2624,128]{1,0:T(8,128)}, f32[8,2624]{1,0:T(8,128)}) custom-call(f32[3,1,2]{2,1,0:T(1,128)} %reshape.712.gate_ref, bf16[2624,1152]{1,0:T(8,128)(2,1)} %shard_map.266.q_ref.k_ref.v_ref, bf16[2624,1152]{1,0:T(8,128)(2,1)} %shard_map.266.q_ref.k_ref.v_ref, ...), custom_call_target="tpu_custom_call" | custom-call | flops 4213178368 | bytes 6717440 | tf_op jit(solution)/shard_map/pallas_call | solution.py:379
  325.9 16.0 %all-to-all-done.3 = bf16[4,656,128]{2,1,0:T(8,128)(2,1)} async-done(((bf16[4,656,128]{2,1,0:T(8,128)(2,1)}), bf16[4,656,128]{2,1,0:T(8,128)(2,1)}, u32[]{:S(2)}, u32[]{:S(2)}) %all-to-all-start.3) | async-done | bytes 671776 | tf_op jit(solution)/shard_map/all_to_all | solution.py:754
  366.3 26.4 %fusion.169.gate_ref.up_ref = f32[656,8192]{1,0:T(8,128)} fusion(bf16[656,1536]{1,0:T(8,128)(2,1)} %copy-done.30, bf16[1536,8192]{1,0:T(8,128)(2,1)} %all-gather.8.cloned.1.call-done), kind=kOutput, calls=%fused_computation.373 | convolution fusion | flops 16508780544 | bytes 48676864 | tf_op jit(solution)/shard_map/dot_general | solution.py:28
  392.7 23.0 %shard_map.272 = (bf16[656,4096]{1,0:T(8,128)(2,1)}, bf16[656,4096]{1,0:T(8,128)(2,1)}) custom-call(s32[1]{0:T(128)} %bitcast.29.core_ref, f32[656,8192]{1,0:T(8,128)} %fusion.169.gate_ref.up_ref, f32[656,8192]{1,0:T(8,128)} %fusion.169.gate_ref.up_ref), custom_call_target="tpu_custom_call" | custom-call | flops 16121856 | bytes 32243712 | tf_op jit(solution)/shard_map/pallas_call | solution.py:602
  419.4 13.1 %multiply_reduce_fusion.14 = (f32[656]{0:T(1024)S(1)}, f32[656,1536]{1,0:T(8,128)S(1)}) fusion(bf16[656,4096]{1,0:T(8,128)(2,1)} %get-tuple-element.110, bf16[4096,1536]{1,0:T(8,128)(2,1)} %all-gather.10.cloned.1.call-done), kind=kOutput, calls=%fused_computation.72 | convolution fusion | flops 8256404992 | bytes 21989952 | tf_op jit(solution)/shard_map/dot_general | solution.py:28
  448.2 19.6 %fusion.6 = (bf16[656,4096]{1,0:T(8,128)(2,1)}, bf16[656,4096]{1,0:T(8,128)(2,1)S(1)}) fusion(f32[656,8192]{1,0:T(8,128)} %fusion.169.gate_ref.up_ref, bf16[656,1536]{1,0:T(8,128)(2,1)} %copy-done.26, bf16[4096,1536]{1,0:T(8,128)(2,1)} %all-gather.10.cloned.1.call-done), kind=kOutput, calls=%fused_computation.13 | convolution fusion | flops 8289320960 | bytes 46841856 | tf_op jit(solution)/shard_map/dot_general | solution.py:32
  467.8 11.5 %convolution_convert_fusion.4 = bf16[768,4096]{1,0:T(8,128)(2,1)} fusion(bf16[656,4096]{1,0:T(8,128)(2,1)} %get-tuple-element.239, bf16[656,1536]{1,0:T(8,128)(2,1)S(1)} %copy-done.25), kind=kOutput, calls=%fused_computation.26 | convolution fusion | flops 4130340864 | bytes 12673024 | tf_op jit(solution)/shard_map/dot_general | solution.py:36
  496.8 28.7 %multiply_reduce_fusion.9 = (f32[1536]{0:T(1024)}, f32[656]{0:T(1024)S(1)}, f32[1536]{0:T(1024)}, f32[1536]{0:T(1024)}, f32[656,1536]{1,0:T(8,128)}) fusion(f32[656,1536]{1,0:T(8,128)} %copy-done.2, f32[656]{0:T(1024)S(1)} %copy-done.90, f32[1536]{0:T(1024)S(1)} %copy-done.74, f32[656]{0:T(1024)S(1)} %get-tuple-element.294, f32[1536]{0:T(1024)S(1)} %copy-done.76, ...), kind=kOutput, calls=%fused_computation.64 | convolution fusion | flops 16547399680 | bytes 44022016 | tf_op jit(solution)/shard_map/dot_general | solution.py:32
  558.5 10.9 add_convert_fusion.2
  569.4 10.7 add_convert_fusion.1
  593.1 13.3 %shard_map.275 = (bf16[2624,128]{1,0:T(8,128)(2,1)}, bf16[512,128]{1,0:T(8,128)(2,1)}, bf16[512,128]{1,0:T(8,128)(2,1)}, f32[8,128]{1,0:T(8,128)}) custom-call(f32[3,1,2]{2,1,0:T(1,128)} %reshape.712.gate_ref, bf16[2624,1152]{1,0:T(8,128)(2,1)} %shard_map.266.q_ref.k_ref.v_ref, bf16[512,768]{1,0:T(8,128)(2,1)} %pad_maximum_fusion.3.tk_ref.tv_ref, ...), custom_call_target="tpu_custom_call" | custom-call | flops 1719664640 | bytes 4030464 | tf_op jit(solution)/shard_map/pallas_call | solution.py:495
  606.4 13.6 %shard_map.274 = (bf16[2624,128]{1,0:T(8,128)(2,1)}, bf16[512,128]{1,0:T(8,128)(2,1)}, bf16[512,128]{1,0:T(8,128)(2,1)}, f32[8,128]{1,0:T(8,128)}) custom-call(f32[3,1,2]{2,1,0:T(1,128)} %reshape.712.gate_ref, bf16[2624,1152]{1,0:T(8,128)(2,1)} %shard_map.266.q_ref.k_ref.v_ref, bf16[512,768]{1,0:T(8,128)(2,1)} %pad_maximum_fusion.3.tk_ref.tv_ref, ...), custom_call_target="tpu_custom_call" | custom-call | flops 1719664640 | bytes 4030464 | tf_op jit(solution)/shard_map/pallas_call | solution.py:495
  620.1 13.4 %shard_map.273 = (bf16[2624,128]{1,0:T(8,128)(2,1)}, bf16[512,128]{1,0:T(8,128)(2,1)}, bf16[512,128]{1,0:T(8,128)(2,1)}, f32[8,128]{1,0:T(8,128)}) custom-call(f32[3,1,2]{2,1,0:T(1,128)} %reshape.712.gate_ref, bf16[2624,1152]{1,0:T(8,128)(2,1)} %shard_map.266.q_ref.k_ref.v_ref, bf16[512,768]{1,0:T(8,128)(2,1)} %pad_maximum_fusion.3.tk_ref.tv_ref, ...), custom_call_target="tpu_custom_call" | custom-call | flops 1719664640 | bytes 4030464 | tf_op jit(solution)/shard_map/pallas_call | solution.py:495
  652.5 45.6 %shard_map.277 = (bf16[2624,128]{1,0:T(8,128)(2,1)}, bf16[2624,128]{1,0:T(8,128)(2,1)}, bf16[2624,128]{1,0:T(8,128)(2,1)}) custom-call(bf16[2624,1152]{1,0:T(8,128)(2,1)} %shard_map.266.q_ref.k_ref.v_ref, bf16[2624,1152]{1,0:T(8,128)(2,1)} %shard_map.266.q_ref.k_ref.v_ref, bf16[2624,1152]{1,0:T(8,128)(2,1)} %shard_map.266.q_ref.k_ref.v_ref, ...), custom_call_target="tpu_custom_call" | custom-call | flops 8813281280 | bytes 10076160 | tf_op jit(solution)/shard_map/pallas_call | solution.py:562
  738.0 45.4 %shard_map.278 = (bf16[2624,128]{1,0:T(8,128)(2,1)}, bf16[2624,128]{1,0:T(8,128)(2,1)}, bf16[2624,128]{1,0:T(8,128)(2,1)}) custom-call(bf16[2624,1152]{1,0:T(8,128)(2,1)} %shard_map.266.q_ref.k_ref.v_ref, bf16[2624,1152]{1,0:T(8,128)(2,1)} %shard_map.266.q_ref.k_ref.v_ref, bf16[2624,1152]{1,0:T(8,128)(2,1)} %shard_map.266.q_ref.k_ref.v_ref, ...), custom_call_target="tpu_custom_call" | custom-call | flops 8813281280 | bytes 10076160 | tf_op jit(solution)/shard_map/pallas_call | solution.py:562
  783.5 9.8 reduce-scatter.10.cloned.1.call-done
  793.3 45.6 %shard_map.279 = (bf16[2624,128]{1,0:T(8,128)(2,1)}, bf16[2624,128]{1,0:T(8,128)(2,1)}, bf16[2624,128]{1,0:T(8,128)(2,1)}) custom-call(bf16[2624,1152]{1,0:T(8,128)(2,1)} %shard_map.266.q_ref.k_ref.v_ref, bf16[2624,1152]{1,0:T(8,128)(2,1)} %shard_map.266.q_ref.k_ref.v_ref, bf16[2624,1152]{1,0:T(8,128)(2,1)} %shard_map.266.q_ref.k_ref.v_ref, ...), custom_call_target="tpu_custom_call" | custom-call | flops 8813281280 | bytes 10076160 | tf_op jit(solution)/shard_map/pallas_call | solution.py:562
  858.4 15.6 %shard_map.280 = (f32[8,2624]{1,0:T(8,128)}, f32[8,384]{1,0:T(8,128)}) custom-call(bf16[2624,128]{1,0:T(8,128)(2,1)} %get-tuple-element.134.refs_0_, bf16[2624,128]{1,0:T(8,128)(2,1)} %get-tuple-element.141.refs_1_, bf16[2624,128]{1,0:T(8,128)(2,1)} %get-tuple-element.148.refs_2_, bf16[2624,128]{1,0:T(8,128)(2,1)} %get-tuple-element.149.refs_3_, ...), custom_call_target="tpu_custom_call" | custom-call | flops 120913920 | bytes 15114240 | tf_op jit(solution)/shard_map/pallas_call | solution.py:269
  882.5 15.4 %shard_map.282 = bf16[2624,1152]{1,0:T(8,128)(2,1)} custom-call(bf16[2624,128]{1,0:T(8,128)(2,1)} %get-tuple-element.134.refs_0_, bf16[2624,128]{1,0:T(8,128)(2,1)} %get-tuple-element.141.refs_1_, bf16[2624,128]{1,0:T(8,128)(2,1)} %get-tuple-element.148.refs_2_, bf16[2624,128]{1,0:T(8,128)(2,1)} %get-tuple-element.149.refs_3_, ...), custom_call_target="tpu_custom_call" | custom-call | flops 120913920 | bytes 21159936 | tf_op jit(solution)/shard_map/pallas_call | solution.py:282
  898.0 16.2 %convolution_convert_fusion = bf16[2624,1536]{1,0:T(8,128)(2,1)} fusion(bf16[2624,1152]{1,0:T(8,128)(2,1)} %shard_map.282, bf16[1536,1152]{1,0:T(8,128)(2,1)} %bitcast.249), kind=kOutput, calls=%fused_computation.9 | convolution fusion | flops 9290219520 | bytes 17645568 | tf_op jit(solution)/shard_map/dot_general | solution.py:32
  928.5 16.6 %convolution_convert_fusion.2 = bf16[1536,1152]{1,0:T(8,128)(2,1)} fusion(bf16[2624,1536]{1,0:T(8,128)(2,1)} %copy-done.21, bf16[2624,1152]{1,0:T(8,128)(2,1)} %shard_map.282), kind=kOutput, calls=%fused_computation.24 | convolution fusion | flops 9287958528 | bytes 17645568 | tf_op jit(solution)/shard_map/dot_general | solution.py:36
  966.5 27.8 %collective-permute-start.17 = (bf16[192,1152]{1,0:T(8,128)(2,1)S(1)}, bf16[192,1152]{1,0:T(8,128)(2,1)S(1)}, u32[]{:S(2)}, u32[]{:S(2)}) collective-permute-start(bf16[192,1152]{1,0:T(8,128)(2,1)S(1)} %get-tuple-element.253), channel_id=1, source_target_pairs={{0,8},{8,0},{16,24},{24,16},{1,9},{9,1},{17,25},{25,17},{2,10},{10... | collective-permute-start | bytes 1327112 | tf_op jit(solution)/shard_map/ppermute | solution.py:783
  1005.2 21.1 %collective-permute-done.18 = bf16[192,1152]{1,0:T(8,128)(2,1)S(1)} collective-permute-done((bf16[192,1152]{1,0:T(8,128)(2,1)S(1)}, bf16[192,1152]{1,0:T(8,128)(2,1)S(1)}, u32[]{:S(2)}, u32[]{:S(2)}) %collective-permute-start.18) | collective-permute-done | bytes 442400 | tf_op jit(solution)/shard_map/ppermute | solution.py:783
  1037.9 28.1 %shard_map.283 = f32[4,296,128]{2,1,0:T(8,128)} custom-call(f32[12,128]{1,0:T(8,128)} %bitcast.287, f32[12,128]{1,0:T(8,128)} %bitcast.286, f32[12,128]{1,0:T(8,128)} %bitcast.294, f32[12,128]{1,0:T(8,128)} %bitcast.281, f32[60,128]{1,0:T(8,128)} %select_n.431.refs_4_, f32[1,128]{1,0:T(1,128)} %pad_bitcast_fusion.refs_5_, f32[32,128]{1,0:T(8,128)} %bitcast.280, ...), custom_call_target="tpu_custom_call" | custom-call | tf_op jit(solution)/shard_map/pallas_call | solution.py:734
  (500 shorter events, 413.4 us)
Async XLA Ops:
  7.2 122.6 %all-gather.12.cloned.1.call-start = ((), (), s32[]{:S(2)}) async-start(), calls=%async_computation.25 | async-start | bytes 10076160 | tf_op jit(solution)/shard_map/all_gather | solution.py:901
  7.9 336.8 %all-gather.6.cloned.1.call-start = ((), (), s32[]{:S(2)}) async-start(), calls=%async_computation.17 | async-start | bytes 5308416 | tf_op jit(solution)/shard_map/all_gather | solution.py:829
  10.2 356.1 %all-gather.8.cloned.1.call-start = ((), (), s32[]{:S(2)}) async-start(), calls=%async_computation.18 | async-start | bytes 28311552 | tf_op jit(solution)/shard_map/all_gather | solution.py:829
  25.0 61.3 %all-to-all-start.1 = ((bf16[4,192,1152]{2,1,0:T(8,128)(2,1)}), bf16[4,192,1152]{2,1,0:T(8,128)(2,1)}, u32[]{:S(2)}, u32[]{:S(2)}) async-start(bf16[4,192,1152]{2,1,0:T(8,128)(2,1)} %reshape.656), calls=%async_computation.1 | async-start | bytes 3538944 | tf_op jit(solution)/shard_map/all_to_all | solution.py:754
  30.3 389.1 %all-gather.10.cloned.1.call-start = ((), (), s32[]{:S(2)}) async-start(), calls=%async_computation.19 | async-start | bytes 14155776 | tf_op jit(solution)/shard_map/all_gather | solution.py:829
  129.8 75.0 %all-to-all-start.2 = ((bf16[4,512,768]{2,1,0:T(8,128)(2,1)}), bf16[4,512,768]{2,1,0:T(8,128)(2,1)}, u32[]{:S(2)}, u32[]{:S(2)}) async-start(bf16[4,512,768]{2,1,0:T(8,128)(2,1)} %pad_maximum_fusion.1), calls=%async_computation.2 | async-start | bytes 6291456 | tf_op jit(solution)/shard_map/all_to_all | solution.py:754
  252.6 34.0 %all-to-all-start.5 = ((bf16[4,656,128]{2,1,0:T(8,128)(2,1)}), bf16[4,656,128]{2,1,0:T(8,128)(2,1)S(1)}, u32[]{:S(2)}, u32[]{:S(2)}) async-start(bf16[4,656,128]{2,1,0:T(8,128)(2,1)} %bitcast.276), calls=%async_computation.5 | async-start | bytes 1343488 | tf_op jit(solution)/shard_map/all_to_all | solution.py:754
  286.6 35.0 %all-to-all-start.4 = ((bf16[4,656,128]{2,1,0:T(8,128)(2,1)}), bf16[4,656,128]{2,1,0:T(8,128)(2,1)S(1)}, u32[]{:S(2)}, u32[]{:S(2)}) async-start(bf16[4,656,128]{2,1,0:T(8,128)(2,1)} %bitcast.275), calls=%async_computation.4 | async-start | bytes 1343488 | tf_op jit(solution)/shard_map/all_to_all | solution.py:754
  325.8 260.9 %reduce-scatter.6.cloned.1.call-start = ((), (), s32[]{:S(2)}) async-start(), calls=%async_computation.20 | async-start | bytes 7864320 | tf_op jit(solution)/shard_map/reduce_scatter | solution.py:777
  448.0 38.9 %collective-permute-start.4 = (bf16[2048,1536]{1,0:T(8,128)(2,1)}, bf16[2048,1536]{1,0:T(8,128)(2,1)}, u32[]{:S(2)}, u32[]{:S(2)}) collective-permute-start(bf16[2048,1536]{1,0:T(8,128)(2,1)} %convolution_convert_fusion.1), channel_id=1, source_target_pairs={{0,4},{4,0},{1,5},{5,1},{2,6},{6,2},{3,7},{7,3},{8,12},{12,8},{9,1... | collective-permute-start | bytes 18874376 | tf_op jit(solution)/shard_map/ppermute | solution.py:758
  479.3 79.2 %collective-permute-start.1 = (bf16[768,4096]{1,0:T(8,128)(2,1)}, bf16[768,4096]{1,0:T(8,128)(2,1)}, u32[]{:S(2)}, u32[]{:S(2)}) collective-permute-start(bf16[768,4096]{1,0:T(8,128)(2,1)} %convolution_convert_fusion.4), channel_id=1, source_target_pairs={{0,4},{4,0},{1,5},{5,1},{2,6},{6,2},{3,7},{7,3},{8,12},{12,8},{9,1... | collective-permute-start | bytes 18874376 | tf_op jit(solution)/shard_map/ppermute | solution.py:758
  486.6 82.8 %collective-permute-start.2 = (bf16[768,4096]{1,0:T(8,128)(2,1)}, bf16[768,4096]{1,0:T(8,128)(2,1)}, u32[]{:S(2)}, u32[]{:S(2)}) collective-permute-start(bf16[768,4096]{1,0:T(8,128)(2,1)} %convolution_convert_fusion.3), channel_id=1, source_target_pairs={{0,4},{4,0},{1,5},{5,1},{2,6},{6,2},{3,7},{7,3},{8,12},{12,8},{9,1... | collective-permute-start | bytes 18874376 | tf_op jit(solution)/shard_map/ppermute | solution.py:758
  548.7 37.6 %all-to-all-start.6 = ((bf16[4,656,384]{2,1,0:T(8,128)(2,1)}), bf16[4,656,384]{2,1,0:T(8,128)(2,1)S(1)}, u32[]{:S(2)}, u32[]{:S(2)}) async-start(bf16[4,656,384]{2,1,0:T(8,128)(2,1)} %bitcast.244), calls=%async_computation.6 | async-start | bytes 4030464 | tf_op jit(solution)/shard_map/all_to_all | solution.py:754
  552.3 151.0 %reduce-scatter.8.cloned.1.call-start = ((), (), s32[]{:S(2)}) async-start(), calls=%async_computation.21 | async-start | bytes 7864320 | tf_op jit(solution)/shard_map/reduce_scatter | solution.py:777
  586.7 196.8 %reduce-scatter.12.cloned.1.call-start = ((), (), s32[]{:S(2)}) async-start(), calls=%async_computation.23 | async-start | bytes 2949120 | tf_op jit(solution)/shard_map/reduce_scatter | solution.py:777
  587.5 205.8 %reduce-scatter.10.cloned.1.call-start = ((), (), s32[]{:S(2)}) async-start(), calls=%async_computation.22 | async-start | bytes 7864320 | tf_op jit(solution)/shard_map/reduce_scatter | solution.py:777
  588.3 114.9 %all-to-all-start.7 = ((bf16[4,128,1536]{2,1,0:T(8,128)(2,1)}), bf16[4,128,1536]{2,1,0:T(8,128)(2,1)}, u32[]{:S(2)}, u32[]{:S(2)}) async-start(bf16[4,128,1536]{2,1,0:T(8,128)(2,1)} %bitcast.40), calls=%async_computation.8 | async-start | bytes 3145728 | tf_op jit(solution)/shard_map/all_to_all | solution.py:754
  646.4 51.8 %collective-permute-start.5 = (bf16[512,768]{1,0:T(8,128)(2,1)}, bf16[512,768]{1,0:T(8,128)(2,1)}, u32[]{:S(2)}, u32[]{:S(2)}) collective-permute-start(bf16[512,768]{1,0:T(8,128)(2,1)} %get-tuple-element.263), channel_id=1, source_target_pairs={{0,1},{1,0},{2,3},{3,2},{4,5},{5,4},{6,7},{7,6},{8,9},{9,8},{10,11... | collective-permute-start | bytes 2359304 | tf_op jit(solution)/shard_map/ppermute | solution.py:796
  647.8 50.4 %collective-permute-start.6 = (bf16[512,768]{1,0:T(8,128)(2,1)}, bf16[512,768]{1,0:T(8,128)(2,1)}, u32[]{:S(2)}, u32[]{:S(2)}) collective-permute-start(bf16[512,768]{1,0:T(8,128)(2,1)} %get-tuple-element.263), channel_id=1, source_target_pairs={{0,2},{1,3},{2,0},{3,1},{4,6},{5,7},{6,4},{7,5},{8,10},{9,11},{10,... | collective-permute-start | bytes 2359304 | tf_op jit(solution)/shard_map/ppermute | solution.py:796
  648.2 55.0 %collective-permute-start.7 = (bf16[512,768]{1,0:T(8,128)(2,1)}, bf16[512,768]{1,0:T(8,128)(2,1)}, u32[]{:S(2)}, u32[]{:S(2)}) collective-permute-start(bf16[512,768]{1,0:T(8,128)(2,1)} %get-tuple-element.263), channel_id=1, source_target_pairs={{0,3},{1,2},{2,1},{3,0},{4,7},{5,6},{6,5},{7,4},{8,11},{9,10},{10,... | collective-permute-start | bytes 2359304 | tf_op jit(solution)/shard_map/ppermute | solution.py:796
  725.3 113.6 %all-to-all-start.8 = ((bf16[4,128,3072]{2,1,0:T(8,128)(2,1)}), bf16[4,128,3072]{2,1,0:T(8,128)(2,1)S(1)}, u32[]{:S(2)}, u32[]{:S(2)}) async-start(bf16[4,128,3072]{2,1,0:T(8,128)(2,1)} %bitcast.254), calls=%async_computation.12 | async-start | bytes 6291456 | tf_op jit(solution)/shard_map/all_to_all | solution.py:754
  733.7 124.3 %collective-permute-start.9 = (bf16[48,4096]{1,0:T(8,128)(2,1)}, bf16[48,4096]{1,0:T(8,128)(2,1)S(1)}, u32[]{:S(2)}, u32[]{:S(2)}) collective-permute-start(bf16[48,4096]{1,0:T(8,128)(2,1)} %get-tuple-element.261), channel_id=1, source_target_pairs={{0,8},{8,0},{16,24},{24,16},{1,9},{9,1},{17,25},{25,17},{2,10},{10... | collective-permute-start | bytes 1179656 | tf_op jit(solution)/shard_map/ppermute | solution.py:783
  735.7 162.3 %collective-permute-start.10 = (bf16[48,4096]{1,0:T(8,128)(2,1)}, bf16[48,4096]{1,0:T(8,128)(2,1)}, u32[]{:S(2)}, u32[]{:S(2)}) collective-permute-start(bf16[48,4096]{1,0:T(8,128)(2,1)} %get-tuple-element.260), channel_id=1, source_target_pairs={{0,16},{8,24},{16,0},{24,8},{1,17},{9,25},{17,1},{25,9},{2,18},{10... | collective-permute-start | bytes 1179656 | tf_op jit(solution)/shard_map/ppermute | solution.py:783
  738.0 159.9 %collective-permute-start.11 = (bf16[48,4096]{1,0:T(8,128)(2,1)}, bf16[48,4096]{1,0:T(8,128)(2,1)}, u32[]{:S(2)}, u32[]{:S(2)}) collective-permute-start(bf16[48,4096]{1,0:T(8,128)(2,1)} %get-tuple-element.259), channel_id=1, source_target_pairs={{0,24},{8,16},{16,8},{24,0},{1,25},{9,17},{17,9},{25,1},{2,26},{10... | collective-permute-start | bytes 1179656 | tf_op jit(solution)/shard_map/ppermute | solution.py:783
  847.2 50.8 %all-to-all-start.9 = ((bf16[4,128,1024]{2,1,0:T(8,128)(2,1)}), bf16[4,128,1024]{2,1,0:T(8,128)(2,1)}, u32[]{:S(2)}, u32[]{:S(2)}) async-start(bf16[4,128,1024]{2,1,0:T(8,128)(2,1)} %bitcast.247), calls=%async_computation.13 | async-start | bytes 2097152 | tf_op jit(solution)/shard_map/all_to_all | solution.py:754
  851.5 181.2 %reduce-scatter.14.cloned.1.call-start = ((), (), s32[]{:S(2)}) async-start(), calls=%async_computation.24 | async-start | bytes 10076160 | tf_op jit(solution)/shard_map/reduce_scatter | solution.py:1142
  854.0 43.9 %collective-permute-start.12 = (bf16[48,4096]{1,0:T(8,128)(2,1)}, bf16[48,4096]{1,0:T(8,128)(2,1)}, u32[]{:S(2)}, u32[]{:S(2)}) collective-permute-start(bf16[48,4096]{1,0:T(8,128)(2,1)} %get-tuple-element.257), channel_id=1, source_target_pairs={{0,8},{8,0},{16,24},{24,16},{1,9},{9,1},{17,25},{25,17},{2,10},{10... | collective-permute-start | bytes 1179656 | tf_op jit(solution)/shard_map/ppermute | solution.py:783
  855.5 42.4 %collective-permute-start.13 = (bf16[48,4096]{1,0:T(8,128)(2,1)}, bf16[48,4096]{1,0:T(8,128)(2,1)}, u32[]{:S(2)}, u32[]{:S(2)}) collective-permute-start(bf16[48,4096]{1,0:T(8,128)(2,1)} %get-tuple-element.256), channel_id=1, source_target_pairs={{0,16},{8,24},{16,0},{24,8},{1,17},{9,25},{17,1},{25,9},{2,18},{10... | collective-permute-start | bytes 1179656 | tf_op jit(solution)/shard_map/ppermute | solution.py:783
  857.9 40.0 %collective-permute-start.14 = (bf16[48,4096]{1,0:T(8,128)(2,1)}, bf16[48,4096]{1,0:T(8,128)(2,1)}, u32[]{:S(2)}, u32[]{:S(2)}) collective-permute-start(bf16[48,4096]{1,0:T(8,128)(2,1)} %get-tuple-element.255), channel_id=1, source_target_pairs={{0,24},{8,16},{16,8},{24,0},{1,25},{9,17},{17,9},{25,1},{2,26},{10... | collective-permute-start | bytes 1179656 | tf_op jit(solution)/shard_map/ppermute | solution.py:783
  919.7 37.4 %all-to-all-start.10 = ((bf16[4,48,1536]{2,1,0:T(8,128)(2,1)}), bf16[4,48,1536]{2,1,0:T(8,128)(2,1)}, u32[]{:S(2)}, u32[]{:S(2)}) async-start(bf16[4,48,1536]{2,1,0:T(8,128)(2,1)} %bitcast.277), calls=%async_computation.15 | async-start | bytes 1179648 | tf_op jit(solution)/shard_map/all_to_all | solution.py:754
  966.5 38.7 %collective-permute-start.17 = (bf16[192,1152]{1,0:T(8,128)(2,1)S(1)}, bf16[192,1152]{1,0:T(8,128)(2,1)S(1)}, u32[]{:S(2)}, u32[]{:S(2)}) collective-permute-start(bf16[192,1152]{1,0:T(8,128)(2,1)S(1)} %get-tuple-element.253), channel_id=1, source_target_pairs={{0,8},{8,0},{16,24},{24,16},{1,9},{9,1},{17,25},{25,17},{2,10},{10... | collective-permute-start | bytes 1327112 | tf_op jit(solution)/shard_map/ppermute | solution.py:783
  994.3 32.0 %collective-permute-start.19 = (bf16[192,1152]{1,0:T(8,128)(2,1)S(1)}, bf16[192,1152]{1,0:T(8,128)(2,1)S(1)}, u32[]{:S(2)}, u32[]{:S(2)}) collective-permute-start(bf16[192,1152]{1,0:T(8,128)(2,1)S(1)} %get-tuple-element.251), channel_id=1, source_target_pairs={{0,24},{8,16},{16,8},{24,0},{1,25},{9,17},{17,9},{25,1},{2,26},{10... | collective-permute-start | bytes 1327112 | tf_op jit(solution)/shard_map/ppermute | solution.py:783
  (127 other events, 2783.3 us)
Sparse Core Ops, SparseCore 0:
  9.9 119.8 all-gather.11
  131.7 63.6 all-gather.5
  197.3 147.6 all-gather.7
  347.2 72.1 all-gather.9
  496.3 90.3 reduce-scatter.5
  589.5 79.4 reduce-scatter.7
  672.0 47.9 reduce-scatter.11
  723.1 70.2 reduce-scatter.9
  914.4 118.2 reduce-scatter.13

commit v8 on v7

--- a/solution.py
+++ b/solution.py
@@ -276,7 +276,7 @@
         ],
         out_shape=[jax.ShapeDtypeStruct((8, rows), F32), jax.ShapeDtypeStruct((8, padded), F32)],
         compiler_params=pltpu.CompilerParams(vmem_limit_bytes=VMEM_LIMIT),
-        cost_estimate=pl.CostEstimate(flops=40 * rows * triple, bytes_accessed=5 * rows * triple, transcendentals=0),
+        cost_estimate=pl.CostEstimate(flops=4 * rows * triple, bytes_accessed=rows * triple // 16, transcendentals=0),
     )(*grads[0], *grads[1], projected, stats, cosine, sine, gains)
     totals = share(own)
     out = pl.pallas_call(
@@ -286,7 +286,7 @@
         out_specs=pl.BlockSpec((QBLOCK, triple), lambda i: (i, 0)),
         out_shape=jax.ShapeDtypeStruct((rows, triple), BF16),
         compiler_params=pltpu.CompilerParams(vmem_limit_bytes=VMEM_LIMIT),
-        cost_estimate=pl.CostEstimate(flops=40 * rows * triple, bytes_accessed=7 * rows * triple, transcendentals=0),
+        cost_estimate=pl.CostEstimate(flops=4 * rows * triple, bytes_accessed=rows * triple // 16, transcendentals=0),
     )(*grads[0], *grads[1], *grads[2], projected, stats, totals, cosine, sine, gains)
     return out, sums
 
@@ -797,15 +797,10 @@
     ]
 
 
-def in_order(block, came):
-    me = lax.axis_index("fsdp")
-    narrow = len(came) + 1
-    result = lax.dynamic_update_slice_in_dim(
-        jnp.zeros((narrow,) + block.shape, block.dtype), block[None], me, 0
-    )
-    for step in range(1, narrow):
-        result = lax.dynamic_update_slice_in_dim(result, came[step - 1][None], me ^ step, 0)
-    return result
+def relative(blocks, me, axis):
+    return jnp.concatenate(
+        [lax.dynamic_slice_in_dim(blocks, me ^ step, 1, axis) for step in range(blocks.shape[axis])], axis=axis
+    )
 
 
 def device_columns(value, deep, narrow):
@@ -942,6 +937,9 @@
     own_text_weight = (
         text_weight.reshape(text_cols, 2, narrow, part).transpose(2, 0, 1, 3).reshape(narrow, text_cols, 2 * part)
     )
+    relative_text_weight = (
+        relative(own_text_weight, me, 0).transpose(1, 0, 2).reshape(text_cols, 2 * model_width)
+    )
     text_partial = jnp.stack([low_product(text_slice, own_text_weight[i]).astype(BF16) for i in range(narrow)])
     text_partial, tokens_all = lax.optimization_barrier((text_partial, tokens_all))
     text_projected = widened(jnp.sum(exchange(text_partial, "fsdp").astype(F32), axis=0), 2)
@@ -1080,16 +1078,10 @@
 
     came_texts = to_all(grad_text_own, narrow)
     backs = [self_pair(0)]
-    first, came_downs, gate_part, *came_texts = lax.optimization_barrier(
-        (backs[0][0], came_downs, gate_part, *came_texts)
-    )
-    gate_pieces = z_pieces(by_z(gate_part), deep)
+    first, came_downs, *came_texts = lax.optimization_barrier((backs[0][0], came_downs, *came_texts))
     grad_down_weight = jnp.sum(came_downs.astype(F32), axis=0)
     backs[0] = (first, *backs[0][1:])
-    grad_text_all = in_order(grad_text_own, came_texts)
-    grad_text_columns = (
-        grad_text_all.reshape(narrow, text_total, 2, part).transpose(1, 2, 0, 3).reshape(text_total, 2 * model_width)
-    )
+    grad_text_columns = jnp.concatenate([grad_text_own, *came_texts], axis=1)
     text_half = text_cols // 2
     own_text, other_text = by_core(text_slice[:, :text_half], text_slice[:, text_half:])
     came_text = core_swap(outer_sum(other_text, grad_text_columns).astype(BF16))
@@ -1099,18 +1091,30 @@
     came_text_z = exchange(by_z(text_both), "z")
     backs.append(self_pair(1))
     if pairs > 2:
-        grad_heads, up_part, out_part, second = lax.optimization_barrier(
-            (grad_heads, up_part, out_part, backs[1][0])
+        grad_heads, gate_part, up_part, second = lax.optimization_barrier(
+            (grad_heads, gate_part, up_part, backs[1][0])
         )
         backs[1] = (second, *backs[1][1:])
         backs += [self_pair(pair) for pair in range(2, pairs)]
+    gate_pieces = z_pieces(by_z(gate_part), deep)
+    last, came_text_z, up_part, *gate_pieces = lax.optimization_barrier(
+        (backs[-1][0], came_text_z, up_part, *gate_pieces)
+    )
     up_pieces = z_pieces(by_z(up_part), deep)
-    last, came_text_z = lax.optimization_barrier((backs[-1][0], came_text_z))
     backs[-1] = (last, *backs[-1][1:])
     text_part = jnp.sum(came_text_z.astype(F32), axis=0).astype(BF16)
+    everyone = ("z", "core", "fsdp")
+    grad_text_weight = lax.ppermute(
+        text_part,
+        everyone,
+        [
+            ((z * 2 + c) * narrow + f, f * wide + c * deep + z)
+            for z in range(deep) for c in range(2) for f in range(narrow)
+        ],
+    )
     last, grad_text_columns = lax.optimization_barrier((backs[-1][0], grad_text_columns))
     backs[-1] = (last, *backs[-1][1:])
-    grad_text_slice = times_transposed(grad_text_columns, text_weight).astype(BF16)
+    grad_text_slice = times_transposed(grad_text_columns, relative_text_weight).astype(BF16)
     came_text = exchange(
         grad_text_slice.reshape(image_count, narrow, caption_local, text_cols)
         .transpose(1, 0, 2, 3)
@@ -1126,22 +1130,14 @@
         list(zip(*backs)), projected, stats_all, cosine, sine, head_gains, part,
         lambda value: fsdp_share(value, narrow, 4),
     )
-    everyone = ("z", "core", "fsdp")
-    grad_text_weight = lax.ppermute(
-        text_part,
-        everyone,
-        [
-            ((z * 2 + c) * narrow + f, f * wide + c * deep + z)
-            for z in range(deep) for c in range(2) for f in range(narrow)
-        ],
-    )
-    grad_projected_low, came_text, *pieces = lax.optimization_barrier(
-        (grad_projected_low, came_text, *gate_pieces, *up_pieces)
-    )
-    grad_gate_up_weight = jnp.concatenate([added(pieces[:deep]), added(pieces[deep:])], axis=1)
-    grad_normed = lax.psum_scatter(
-        times_transposed(grad_projected_low, own_qkv).astype(BF16), "fsdp", scatter_dimension=0, tiled=True
-    )
+    grad_projected_low, came_text, *up_pieces = lax.optimization_barrier(
+        (grad_projected_low, came_text, *up_pieces)
+    )
+    grad_gate_up_weight = jnp.concatenate([added(gate_pieces), added(up_pieces)], axis=1)
+    partial_normed, grad_text_weight = lax.optimization_barrier(
+        (times_transposed(grad_projected_low, own_qkv).astype(BF16), grad_text_weight)
+    )
+    grad_normed = lax.psum_scatter(partial_normed, "fsdp", scatter_dimension=0, tiled=True)
 
     def lane_rows(value):
         return value.reshape(-1, 128)
@@ -1158,8 +1154,15 @@
     later = [*grad_gate_attend, *grad_scale_feed, *grad_gate_feed, cond_rows_here]
     ready = lax.optimization_barrier(tuple(ready))
     qkv_grad = outer_sum(normed_all, grad_projected_low).astype(BF16).reshape(deep, 2, model_width // wide, 3 * part_pad)
-    qkv_grad, came_out_z, grad_text_weight = lax.optimization_barrier((qkv_grad, came_out_z, grad_text_weight))
-    grad_text_weight = grad_text_weight.astype(F32)
+    qkv_grad, came_out_z = lax.optimization_barrier((qkv_grad, came_out_z))
+    place = (lax.axis_index("z") * 2 + lax.axis_index("core")) * narrow + me
+    grad_text_weight = (
+        relative(grad_text_weight.reshape(-1, narrow, 2 * part), place // wide, 1)
+        .reshape(-1, narrow, 2, part)
+        .transpose(0, 2, 1, 3)
+        .reshape(-1, 2 * model_width)
+        .astype(F32)
+    )
     grad_out_weight = jnp.sum(came_out_z.astype(F32), axis=0)
     own_grad, other_grad = by_core(qkv_grad[:, 0], qkv_grad[:, 1])
     own_grad = (own_grad.astype(F32) + core_swap(other_grad).astype(F32)).astype(BF16)
@@ -1179,6 +1182,15 @@
     )
 
     grad_text, grad_text_gain, *own_pieces = lax.optimization_barrier((grad_text, grad_text_gain, *own_pieces))
+    own_grad = added(own_pieces)
+    grad_qkv_weight = (
+        exchange(narrowed(own_grad.astype(BF16), 3).reshape(narrow, -1, 3 * part), "fsdp")
+        .reshape(narrow, -1, 3, part)
+        .transpose(1, 2, 0, 3)
+        .reshape(-1, 3 * model_width)
+        .astype(F32)
+    )
+    grad_normed, grad_qkv_weight = lax.optimization_barrier((grad_normed, grad_qkv_weight))
     grad_normed = grad_normed.astype(F32)
 
     token_unit = token_in * token_inverse
@@ -1192,15 +1204,6 @@
     lanes_of_row = model_width // 128
     summed, kept = finish(
         [lane_rows(grad_gain_zero), *ready, lane_rows(grad_text_gain)], [*grad_scale_attend, *later], narrow, wide, 5
-    )
-    summed, kept, *own_pieces = lax.optimization_barrier((summed, kept, *own_pieces))
-    own_grad = added(own_pieces)
-    grad_qkv_weight = (
-        exchange(narrowed(own_grad.astype(BF16), 3).reshape(narrow, -1, 3 * part), "fsdp")
-        .reshape(narrow, -1, 3, part)
-        .transpose(1, 2, 0, 3)
-        .reshape(-1, 3 * model_width)
-        .astype(F32)
     )
     every_image = wide * image_count
     per_part = image_count * lanes_of_row

time: 1110 us -> 1130 us (1.018)
  local copies, waits for them, and re-layouts: 99.3 us -> 127 us
  waiting for transfers between devices: 88.7 us -> 71.6 us
    ppermute x9, starting transfers between devices: 39 us -> 13.3 us  [z_pieces(): lax.ppermute(lax.dynamic_index_in_dim(blocks, me ^ step, 0, keepdims=Fals...]
    unnamed x239 -> x230, local copies, waits for them, and re-layouts: 21.5 us -> 33.6 us
  transfers between devices with their start and end apart: 41 -> 41, of which waited for: 13 -> 11; matrix products, arithmetic and copies ran while one was open for 34% -> 37% of each run, Pallas kernels for 38% -> 37%
where the time goes in v8:
time: 1130 us; the launch traced here: 1120 us
  Pallas kernels  446 us (39%)
  matrix products  246 us (22%)
  local copies, waits for them, and re-layouts  127 us (11%)
  other arithmetic  119 us (11%)
  starting transfers between devices  90.4 us (8%)
  waiting for transfers between devices  71.6 us (6%)
  between operations  18.2 us (2%)
    pallas_call x3, Pallas kernels, self_back(): pl.pallas_call(functools.partial(self_back_kernel, head_dim, FIRST_PATCHE...  137 us
    dot_general x11, matrix products, outer_sum(): lax.dot_general(left, right, (((0,), (0,)), ((), ())), preferred_element_...  92 us
    pallas_call x3, Pallas kernels, attend(): pl.pallas_call(functools.partial(attend_kernel, head_dim, FIRST_PATCHES,...  91.9 us
    dot_general x11, matrix products, low_product(): return jnp.dot(left, right, preferred_element_type=F32)  77 us
    dot_general x5, matrix products, times_transposed(): lax.dot_general(left, right, (((1,), (1,)), ((), ())), preferred_element_...  74.3 us
    pallas_call x5, Pallas kernels, fsdp_share(): pl.pallas_call(functools.partial(fsdp_share_kernel, narrow), in_specs=[pl...  65 us
    all_to_all x12, starting transfers between devices, exchange(): return lax.all_to_all(blocks, axis, 0, 0, tiled=True)  64.6 us
    pallas_call x3, Pallas kernels, cross_back(): pl.pallas_call(functools.partial(cross_back_kernel, head_dim, FIRST_PATCH...  40.1 us
  transfers between devices with their start and end apart: 41, of which 11 were waited for; matrix products, arithmetic and copies ran while one was open for 37% of the time, Pallas kernels for 37%

profile of v8, /device:TPU:0, one launch (start us, length us, event | category | flops | bytes accessed | tf_op | source)
XLA Modules:
  0.0 1119.3 jit_solution(9329086474731998951)
XLA Ops:
  40.4 27.4 %shard_map.263 = f32[4,96,128]{2,1,0:T(8,128)} custom-call(f32[96,128]{1,0:T(8,128)} %reshape.657.x_ref), custom_call_target="tpu_custom_call" | custom-call | bytes 393216 | tf_op jit(solution)/shard_map/pallas_call | solution.py:648
  75.9 10.5 negate_select_fusion
  150.1 13.6 %fusion.165.projected_ref.refs_6_.refs_9_ = f32[2624,1152]{1,0:T(8,128)} fusion(bf16[2624,1536]{1,0:T(8,128)(2,1)S(1)} %fusion.3, bf16[1536,1152]{1,0:T(8,128)(2,1)S(1)} %bitcast.250), kind=kOutput, calls=%fused_computation.384 | convolution fusion | flops 9286189056 | bytes 23691264 | tf_op jit(solution)/shard_map/dot_general | solution.py:28
  163.7 9.4 shard_map.264.x_ref
  173.1 16.2 %shard_map.265.stats_ref.refs_7_.refs_10_ = f32[4,8,2624]{2,1,0:T(8,128)} custom-call(f32[8,2624]{1,0:T(8,128)} %shard_map.264.x_ref), custom_call_target="tpu_custom_call" | custom-call | bytes 671744 | tf_op jit(solution)/shard_map/pallas_call | solution.py:648
  189.3 15.5 %shard_map.266.q_ref.k_ref.v_ref = bf16[2624,1152]{1,0:T(8,128)(2,1)} custom-call(f32[2624,1152]{1,0:T(8,128)} %fusion.165.projected_ref.refs_6_.refs_9_, f32[4,8,2624]{2,1,0:T(8,128)} %shard_map.265.stats_ref.refs_7_.refs_10_, f32[2624,128]{1,0:T(8,128)} %get-tuple-element.277.cos_ref.refs_8_.refs_12_, ...), custom_call_target="tpu_custom_call" | custom-call | flops 120913920 | bytes 18137088 | tf_op jit(solution)/shard_map/pallas_call | solution.py:183
  221.5 31.1 %shard_map.271 = (bf16[2624,128]{1,0:T(8,128)(2,1)}, f32[2624,128]{1,0:T(8,128)}, f32[2624,128]{1,0:T(8,128)}, f32[8,2624]{1,0:T(8,128)}) custom-call(f32[3,1,2]{2,1,0:T(1,128)} %reshape.723.gate_ref, bf16[2624,1152]{1,0:T(8,128)(2,1)} %shard_map.266.q_ref.k_ref.v_ref, bf16[2624,1152]{1,0:T(8,128)(2,1)} %shard_map.266.q_ref.k_ref.v_ref, ...), custom_call_target="tpu_custom_call" | custom-call | flops 4213178368 | bytes 6717440 | tf_op jit(solution)/shard_map/pallas_call | solution.py:379
  256.2 30.4 %shard_map.270 = (bf16[2624,128]{1,0:T(8,128)(2,1)}, f32[2624,128]{1,0:T(8,128)}, f32[2624,128]{1,0:T(8,128)}, f32[8,2624]{1,0:T(8,128)}) custom-call(f32[3,1,2]{2,1,0:T(1,128)} %reshape.723.gate_ref, bf16[2624,1152]{1,0:T(8,128)(2,1)} %shard_map.266.q_ref.k_ref.v_ref, bf16[2624,1152]{1,0:T(8,128)(2,1)} %shard_map.266.q_ref.k_ref.v_ref, ...), custom_call_target="tpu_custom_call" | custom-call | flops 4213178368 | bytes 6717440 | tf_op jit(solution)/shard_map/pallas_call | solution.py:379
  291.1 30.4 %shard_map.269 = (bf16[2624,128]{1,0:T(8,128)(2,1)}, f32[2624,128]{1,0:T(8,128)}, f32[2624,128]{1,0:T(8,128)}, f32[8,2624]{1,0:T(8,128)}) custom-call(f32[3,1,2]{2,1,0:T(1,128)} %reshape.723.gate_ref, bf16[2624,1152]{1,0:T(8,128)(2,1)} %shard_map.266.q_ref.k_ref.v_ref, bf16[2624,1152]{1,0:T(8,128)(2,1)} %shard_map.266.q_ref.k_ref.v_ref, ...), custom_call_target="tpu_custom_call" | custom-call | flops 4213178368 | bytes 6717440 | tf_op jit(solution)/shard_map/pallas_call | solution.py:379
  325.8 16.0 %all-to-all-done.3 = bf16[4,656,128]{2,1,0:T(8,128)(2,1)} async-done(((bf16[4,656,128]{2,1,0:T(8,128)(2,1)}), bf16[4,656,128]{2,1,0:T(8,128)(2,1)}, u32[]{:S(2)}, u32[]{:S(2)}) %all-to-all-start.3) | async-done | bytes 671776 | tf_op jit(solution)/shard_map/all_to_all | solution.py:754
  366.2 26.3 %fusion.166.gate_ref.up_ref = f32[656,8192]{1,0:T(8,128)} fusion(bf16[656,1536]{1,0:T(8,128)(2,1)} %copy-done.36, bf16[1536,8192]{1,0:T(8,128)(2,1)} %all-gather.8.cloned.1.call-done), kind=kOutput, calls=%fused_computation.385 | convolution fusion | flops 16508780544 | bytes 48676864 | tf_op jit(solution)/shard_map/dot_general | solution.py:28
  392.5 22.9 %shard_map.272 = (bf16[656,4096]{1,0:T(8,128)(2,1)}, bf16[656,4096]{1,0:T(8,128)(2,1)}) custom-call(s32[1]{0:T(128)} %bitcast.29.core_ref, f32[656,8192]{1,0:T(8,128)} %fusion.166.gate_ref.up_ref, f32[656,8192]{1,0:T(8,128)} %fusion.166.gate_ref.up_ref), custom_call_target="tpu_custom_call" | custom-call | flops 16121856 | bytes 32243712 | tf_op jit(solution)/shard_map/pallas_call | solution.py:602
  418.9 13.1 %multiply_reduce_fusion.14 = (f32[656]{0:T(1024)S(1)}, f32[656,1536]{1,0:T(8,128)S(1)}) fusion(bf16[656,4096]{1,0:T(8,128)(2,1)} %get-tuple-element.107, bf16[4096,1536]{1,0:T(8,128)(2,1)} %all-gather.10.cloned.1.call-done), kind=kOutput, calls=%fused_computation.73 | convolution fusion | flops 8256404992 | bytes 21989952 | tf_op jit(solution)/shard_map/dot_general | solution.py:28
  447.7 19.5 %fusion.6 = (bf16[656,4096]{1,0:T(8,128)(2,1)}, bf16[656,4096]{1,0:T(8,128)(2,1)S(1)}) fusion(f32[656,8192]{1,0:T(8,128)} %fusion.166.gate_ref.up_ref, bf16[656,1536]{1,0:T(8,128)(2,1)} %copy-done.32, bf16[4096,1536]{1,0:T(8,128)(2,1)} %all-gather.10.cloned.1.call-done), kind=kOutput, calls=%fused_computation.13 | convolution fusion | flops 8289320960 | bytes 46841856 | tf_op jit(solution)/shard_map/dot_general | solution.py:32
  467.2 11.5 %convolution_convert_fusion.4 = bf16[768,4096]{1,0:T(8,128)(2,1)} fusion(bf16[656,4096]{1,0:T(8,128)(2,1)} %get-tuple-element.235, bf16[656,1536]{1,0:T(8,128)(2,1)S(1)} %copy-done.31), kind=kOutput, calls=%fused_computation.26 | convolution fusion | flops 4130340864 | bytes 12673024 | tf_op jit(solution)/shard_map/dot_general | solution.py:36
  496.3 28.7 %multiply_reduce_fusion.9 = (f32[1536]{0:T(1024)}, f32[656]{0:T(1024)S(1)}, f32[1536]{0:T(1024)}, f32[1536]{0:T(1024)}, f32[656,1536]{1,0:T(8,128)}) fusion(f32[656,1536]{1,0:T(8,128)} %copy-done.2, f32[656]{0:T(1024)S(1)} %copy-done.83, f32[1536]{0:T(1024)S(1)} %copy-done.69, f32[656]{0:T(1024)S(1)} %get-tuple-element.296, f32[1536]{0:T(1024)S(1)} %copy-done.71, ...), kind=kOutput, calls=%fused_computation.65 | convolution fusion | flops 16547399680 | bytes 44022016 | tf_op jit(solution)/shard_map/dot_general | solution.py:32
  557.7 10.8 add_convert_fusion.2
  568.5 10.7 add_convert_fusion.1
  592.0 13.3 %shard_map.275 = (bf16[2624,128]{1,0:T(8,128)(2,1)}, bf16[512,128]{1,0:T(8,128)(2,1)}, bf16[512,128]{1,0:T(8,128)(2,1)}, f32[8,128]{1,0:T(8,128)}) custom-call(f32[3,1,2]{2,1,0:T(1,128)} %reshape.723.gate_ref, bf16[2624,1152]{1,0:T(8,128)(2,1)} %shard_map.266.q_ref.k_ref.v_ref, bf16[512,768]{1,0:T(8,128)(2,1)} %pad_maximum_fusion.4.tk_ref.tv_ref, ...), custom_call_target="tpu_custom_call" | custom-call | flops 1719664640 | bytes 4030464 | tf_op jit(solution)/shard_map/pallas_call | solution.py:495
  605.3 13.3 %shard_map.274 = (bf16[2624,128]{1,0:T(8,128)(2,1)}, bf16[512,128]{1,0:T(8,128)(2,1)}, bf16[512,128]{1,0:T(8,128)(2,1)}, f32[8,128]{1,0:T(8,128)}) custom-call(f32[3,1,2]{2,1,0:T(1,128)} %reshape.723.gate_ref, bf16[2624,1152]{1,0:T(8,128)(2,1)} %shard_map.266.q_ref.k_ref.v_ref, bf16[512,768]{1,0:T(8,128)(2,1)} %pad_maximum_fusion.4.tk_ref.tv_ref, ...), custom_call_target="tpu_custom_call" | custom-call | flops 1719664640 | bytes 4030464 | tf_op jit(solution)/shard_map/pallas_call | solution.py:495
  618.7 13.5 %shard_map.273 = (bf16[2624,128]{1,0:T(8,128)(2,1)}, bf16[512,128]{1,0:T(8,128)(2,1)}, bf16[512,128]{1,0:T(8,128)(2,1)}, f32[8,128]{1,0:T(8,128)}) custom-call(f32[3,1,2]{2,1,0:T(1,128)} %reshape.723.gate_ref, bf16[2624,1152]{1,0:T(8,128)(2,1)} %shard_map.266.q_ref.k_ref.v_ref, bf16[512,768]{1,0:T(8,128)(2,1)} %pad_maximum_fusion.4.tk_ref.tv_ref, ...), custom_call_target="tpu_custom_call" | custom-call | flops 1719664640 | bytes 4030464 | tf_op jit(solution)/shard_map/pallas_call | solution.py:495
  653.8 45.6 %shard_map.277 = (bf16[2624,128]{1,0:T(8,128)(2,1)}, bf16[2624,128]{1,0:T(8,128)(2,1)}, bf16[2624,128]{1,0:T(8,128)(2,1)}) custom-call(bf16[2624,1152]{1,0:T(8,128)(2,1)} %shard_map.266.q_ref.k_ref.v_ref, bf16[2624,1152]{1,0:T(8,128)(2,1)} %shard_map.266.q_ref.k_ref.v_ref, bf16[2624,1152]{1,0:T(8,128)(2,1)} %shard_map.266.q_ref.k_ref.v_ref, ...), custom_call_target="tpu_custom_call" | custom-call | flops 8813281280 | bytes 10076160 | tf_op jit(solution)/shard_map/pallas_call | solution.py:562
  744.0 45.4 %shard_map.278 = (bf16[2624,128]{1,0:T(8,128)(2,1)}, bf16[2624,128]{1,0:T(8,128)(2,1)}, bf16[2624,128]{1,0:T(8,128)(2,1)}) custom-call(bf16[2624,1152]{1,0:T(8,128)(2,1)} %shard_map.266.q_ref.k_ref.v_ref, bf16[2624,1152]{1,0:T(8,128)(2,1)} %shard_map.266.q_ref.k_ref.v_ref, bf16[2624,1152]{1,0:T(8,128)(2,1)} %shard_map.266.q_ref.k_ref.v_ref, ...), custom_call_target="tpu_custom_call" | custom-call | flops 8813281280 | bytes 10076160 | tf_op jit(solution)/shard_map/pallas_call | solution.py:562
  796.6 45.6 %shard_map.279 = (bf16[2624,128]{1,0:T(8,128)(2,1)}, bf16[2624,128]{1,0:T(8,128)(2,1)}, bf16[2624,128]{1,0:T(8,128)(2,1)}) custom-call(bf16[2624,1152]{1,0:T(8,128)(2,1)} %shard_map.266.q_ref.k_ref.v_ref, bf16[2624,1152]{1,0:T(8,128)(2,1)} %shard_map.266.q_ref.k_ref.v_ref, bf16[2624,1152]{1,0:T(8,128)(2,1)} %shard_map.266.q_ref.k_ref.v_ref, ...), custom_call_target="tpu_custom_call" | custom-call | flops 8813281280 | bytes 10076160 | tf_op jit(solution)/shard_map/pallas_call | solution.py:562
  861.8 15.2 %shard_map.280 = (f32[8,2624]{1,0:T(8,128)}, f32[8,384]{1,0:T(8,128)}) custom-call(bf16[2624,128]{1,0:T(8,128)(2,1)} %get-tuple-element.130.refs_0_, bf16[2624,128]{1,0:T(8,128)(2,1)} %get-tuple-element.137.refs_1_, bf16[2624,128]{1,0:T(8,128)(2,1)} %get-tuple-element.146.refs_2_, bf16[2624,128]{1,0:T(8,128)(2,1)} %get-tuple-element.147.refs_3_, ...), custom_call_target="tpu_custom_call" | custom-call | flops 12091392 | bytes 188928 | tf_op jit(solution)/shard_map/pallas_call | solution.py:269
  894.5 16.0 %shard_map.282 = bf16[2624,1152]{1,0:T(8,128)(2,1)} custom-call(bf16[2624,128]{1,0:T(8,128)(2,1)} %get-tuple-element.130.refs_0_, bf16[2624,128]{1,0:T(8,128)(2,1)} %get-tuple-element.137.refs_1_, bf16[2624,128]{1,0:T(8,128)(2,1)} %get-tuple-element.146.refs_2_, bf16[2624,128]{1,0:T(8,128)(2,1)} %get-tuple-element.147.refs_3_, ...), custom_call_target="tpu_custom_call" | custom-call | flops 12091392 | bytes 188928 | tf_op jit(solution)/shard_map/pallas_call | solution.py:282
  910.6 15.4 %convolution_convert_fusion = bf16[2624,1536]{1,0:T(8,128)(2,1)} fusion(bf16[2624,1152]{1,0:T(8,128)(2,1)} %shard_map.282, bf16[1536,1152]{1,0:T(8,128)(2,1)S(1)} %bitcast.251), kind=kOutput, calls=%fused_computation.9 | convolution fusion | flops 9290219520 | bytes 17645568 | tf_op jit(solution)/shard_map/dot_general | solution.py:32
  930.0 14.2 %all-to-all-start.10 = ((bf16[4,48,1536]{2,1,0:T(8,128)(2,1)}), bf16[4,48,1536]{2,1,0:T(8,128)(2,1)S(1)}, u32[]{:S(2)}, u32[]{:S(2)}) async-start(bf16[4,48,1536]{2,1,0:T(8,128)(2,1)} %bitcast.278), calls=%async_computation.15 | async-start | bytes 1179648 | tf_op jit(solution)/shard_map/all_to_all | solution.py:754
  947.1 16.4 %convolution_convert_fusion.2 = bf16[1536,1152]{1,0:T(8,128)(2,1)} fusion(bf16[2624,1536]{1,0:T(8,128)(2,1)} %copy-done.20, bf16[2624,1152]{1,0:T(8,128)(2,1)} %shard_map.282), kind=kOutput, calls=%fused_computation.24 | convolution fusion | flops 9287958528 | bytes 17645568 | tf_op jit(solution)/shard_map/dot_general | solution.py:36
  998.4 9.8 collective-permute-done.17
  1008.1 13.5 %collective-permute-done.18 = bf16[192,1152]{1,0:T(8,128)(2,1)} collective-permute-done((bf16[192,1152]{1,0:T(8,128)(2,1)}, bf16[192,1152]{1,0:T(8,128)(2,1)}, u32[]{:S(2)}, u32[]{:S(2)}) %collective-permute-start.18) | collective-permute-done | bytes 442400 | tf_op jit(solution)/shard_map/ppermute | solution.py:783
  1047.9 31.4 %shard_map.283 = f32[4,296,128]{2,1,0:T(8,128)} custom-call(f32[12,128]{1,0:T(8,128)} %bitcast.291, f32[12,128]{1,0:T(8,128)} %bitcast.290, f32[12,128]{1,0:T(8,128)} %bitcast.298, f32[12,128]{1,0:T(8,128)} %bitcast.285, f32[60,128]{1,0:T(8,128)} %select_n.447.refs_4_, f32[1,128]{1,0:T(1,128)} %pad_bitcast_fusion.refs_5_, f32[32,128]{1,0:T(8,128)} %bitcast.284, ...), custom_call_target="tpu_custom_call" | custom-call | tf_op jit(solution)/shard_map/pallas_call | solution.py:734
  (486 shorter events, 448.4 us)
Async XLA Ops:
  7.2 122.6 %all-gather.12.cloned.1.call-start = ((), (), s32[]{:S(2)}) async-start(), calls=%async_computation.25 | async-start | bytes 10076160 | tf_op jit(solution)/shard_map/all_gather | solution.py:896
  7.9 336.8 %all-gather.6.cloned.1.call-start = ((), (), s32[]{:S(2)}) async-start(), calls=%async_computation.17 | async-start | bytes 5308416 | tf_op jit(solution)/shard_map/all_gather | solution.py:824
  10.2 356.0 %all-gather.8.cloned.1.call-start = ((), (), s32[]{:S(2)}) async-start(), calls=%async_computation.18 | async-start | bytes 28311552 | tf_op jit(solution)/shard_map/all_gather | solution.py:824
  25.0 61.4 %all-to-all-start.1 = ((bf16[4,192,1152]{2,1,0:T(8,128)(2,1)}), bf16[4,192,1152]{2,1,0:T(8,128)(2,1)}, u32[]{:S(2)}, u32[]{:S(2)}) async-start(bf16[4,192,1152]{2,1,0:T(8,128)(2,1)} %reshape.664), calls=%async_computation.1 | async-start | bytes 3538944 | tf_op jit(solution)/shard_map/all_to_all | solution.py:754
  30.3 388.6 %all-gather.10.cloned.1.call-start = ((), (), s32[]{:S(2)}) async-start(), calls=%async_computation.19 | async-start | bytes 14155776 | tf_op jit(solution)/shard_map/all_gather | solution.py:824
  129.8 75.0 %all-to-all-start.2 = ((bf16[4,512,768]{2,1,0:T(8,128)(2,1)}), bf16[4,512,768]{2,1,0:T(8,128)(2,1)}, u32[]{:S(2)}, u32[]{:S(2)}) async-start(bf16[4,512,768]{2,1,0:T(8,128)(2,1)} %pad_maximum_fusion.2), calls=%async_computation.2 | async-start | bytes 6291456 | tf_op jit(solution)/shard_map/all_to_all | solution.py:754
  252.6 34.0 %all-to-all-start.5 = ((bf16[4,656,128]{2,1,0:T(8,128)(2,1)}), bf16[4,656,128]{2,1,0:T(8,128)(2,1)S(1)}, u32[]{:S(2)}, u32[]{:S(2)}) async-start(bf16[4,656,128]{2,1,0:T(8,128)(2,1)} %bitcast.277), calls=%async_computation.5 | async-start | bytes 1343488 | tf_op jit(solution)/shard_map/all_to_all | solution.py:754
  286.6 35.0 %all-to-all-start.4 = ((bf16[4,656,128]{2,1,0:T(8,128)(2,1)}), bf16[4,656,128]{2,1,0:T(8,128)(2,1)S(1)}, u32[]{:S(2)}, u32[]{:S(2)}) async-start(bf16[4,656,128]{2,1,0:T(8,128)(2,1)} %bitcast.276), calls=%async_computation.4 | async-start | bytes 1343488 | tf_op jit(solution)/shard_map/all_to_all | solution.py:754
  325.7 260.4 %reduce-scatter.6.cloned.1.call-start = ((), (), s32[]{:S(2)}) async-start(), calls=%async_computation.20 | async-start | bytes 7864320 | tf_op jit(solution)/shard_map/reduce_scatter | solution.py:777
  447.5 38.8 %collective-permute-start.4 = (bf16[2048,1536]{1,0:T(8,128)(2,1)}, bf16[2048,1536]{1,0:T(8,128)(2,1)}, u32[]{:S(2)}, u32[]{:S(2)}) collective-permute-start(bf16[2048,1536]{1,0:T(8,128)(2,1)} %convolution_convert_fusion.1), channel_id=1, source_target_pairs={{0,4},{4,0},{1,5},{5,1},{2,6},{6,2},{3,7},{7,3},{8,12},{12,8},{9,1... | collective-permute-start | bytes 18874376 | tf_op jit(solution)/shard_map/ppermute | solution.py:758
  478.7 79.0 %collective-permute-start.1 = (bf16[768,4096]{1,0:T(8,128)(2,1)}, bf16[768,4096]{1,0:T(8,128)(2,1)}, u32[]{:S(2)}, u32[]{:S(2)}) collective-permute-start(bf16[768,4096]{1,0:T(8,128)(2,1)} %convolution_convert_fusion.4), channel_id=1, source_target_pairs={{0,4},{4,0},{1,5},{5,1},{2,6},{6,2},{3,7},{7,3},{8,12},{12,8},{9,1... | collective-permute-start | bytes 18874376 | tf_op jit(solution)/shard_map/ppermute | solution.py:758
  486.1 82.5 %collective-permute-start.2 = (bf16[768,4096]{1,0:T(8,128)(2,1)}, bf16[768,4096]{1,0:T(8,128)(2,1)}, u32[]{:S(2)}, u32[]{:S(2)}) collective-permute-start(bf16[768,4096]{1,0:T(8,128)(2,1)} %convolution_convert_fusion.3), channel_id=1, source_target_pairs={{0,4},{4,0},{1,5},{5,1},{2,6},{6,2},{3,7},{7,3},{8,12},{12,8},{9,1... | collective-permute-start | bytes 18874376 | tf_op jit(solution)/shard_map/ppermute | solution.py:758
  547.9 37.7 %all-to-all-start.6 = ((bf16[4,656,384]{2,1,0:T(8,128)(2,1)}), bf16[4,656,384]{2,1,0:T(8,128)(2,1)S(1)}, u32[]{:S(2)}, u32[]{:S(2)}) async-start(bf16[4,656,384]{2,1,0:T(8,128)(2,1)} %bitcast.244), calls=%async_computation.6 | async-start | bytes 4030464 | tf_op jit(solution)/shard_map/all_to_all | solution.py:754
  551.5 238.0 %reduce-scatter.8.cloned.1.call-start = ((), (), s32[]{:S(2)}) async-start(), calls=%async_computation.21 | async-start | bytes 7864320 | tf_op jit(solution)/shard_map/reduce_scatter | solution.py:777
  586.2 203.3 %reduce-scatter.10.cloned.1.call-start = ((), (), s32[]{:S(2)}) async-start(), calls=%async_computation.22 | async-start | bytes 7864320 | tf_op jit(solution)/shard_map/reduce_scatter | solution.py:777
  587.0 116.4 %all-to-all-start.7 = ((bf16[4,128,1536]{2,1,0:T(8,128)(2,1)}), bf16[4,128,1536]{2,1,0:T(8,128)(2,1)S(1)}, u32[]{:S(2)}, u32[]{:S(2)}) async-start(bf16[4,128,1536]{2,1,0:T(8,128)(2,1)} %bitcast.270), calls=%async_computation.8 | async-start | bytes 3145728 | tf_op jit(solution)/shard_map/all_to_all | solution.py:754
  645.5 53.9 %collective-permute-start.5 = (bf16[512,768]{1,0:T(8,128)(2,1)}, bf16[512,768]{1,0:T(8,128)(2,1)}, u32[]{:S(2)}, u32[]{:S(2)}) collective-permute-start(bf16[512,768]{1,0:T(8,128)(2,1)} %pad_maximum_fusion.5), channel_id=1, source_target_pairs={{0,1},{1,0},{2,3},{3,2},{4,5},{5,4},{6,7},{7,6},{8,9},{9,8},{10,11... | collective-permute-start | bytes 2359304 | tf_op jit(solution)/shard_map/ppermute | solution.py:796
  647.0 52.4 %collective-permute-start.6 = (bf16[512,768]{1,0:T(8,128)(2,1)}, bf16[512,768]{1,0:T(8,128)(2,1)}, u32[]{:S(2)}, u32[]{:S(2)}) collective-permute-start(bf16[512,768]{1,0:T(8,128)(2,1)} %pad_maximum_fusion.5), channel_id=1, source_target_pairs={{0,2},{1,3},{2,0},{3,1},{4,6},{5,7},{6,4},{7,5},{8,10},{9,11},{10,... | collective-permute-start | bytes 2359304 | tf_op jit(solution)/shard_map/ppermute | solution.py:796
  647.6 55.7 %collective-permute-start.7 = (bf16[512,768]{1,0:T(8,128)(2,1)}, bf16[512,768]{1,0:T(8,128)(2,1)}, u32[]{:S(2)}, u32[]{:S(2)}) collective-permute-start(bf16[512,768]{1,0:T(8,128)(2,1)} %pad_maximum_fusion.5), channel_id=1, source_target_pairs={{0,3},{1,2},{2,1},{3,0},{4,7},{5,6},{6,5},{7,4},{8,11},{9,10},{10,... | collective-permute-start | bytes 2359304 | tf_op jit(solution)/shard_map/ppermute | solution.py:796
  725.1 117.1 %all-to-all-start.8 = ((bf16[4,128,3072]{2,1,0:T(8,128)(2,1)}), bf16[4,128,3072]{2,1,0:T(8,128)(2,1)S(1)}, u32[]{:S(2)}, u32[]{:S(2)}) async-start(bf16[4,128,3072]{2,1,0:T(8,128)(2,1)} %bitcast.252), calls=%async_computation.11 | async-start | bytes 6291456 | tf_op jit(solution)/shard_map/all_to_all | solution.py:754
  729.9 200.1 %reduce-scatter.14.cloned.1.call-start = ((), (), s32[]{:S(2)}) async-start(), calls=%async_computation.24 | async-start | bytes 2949120 | tf_op jit(solution)/shard_map/reduce_scatter | solution.py:777
  792.0 50.2 %collective-permute-start.9 = (bf16[48,4096]{1,0:T(8,128)(2,1)}, bf16[48,4096]{1,0:T(8,128)(2,1)S(1)}, u32[]{:S(2)}, u32[]{:S(2)}) collective-permute-start(bf16[48,4096]{1,0:T(8,128)(2,1)} %get-tuple-element.261), channel_id=1, source_target_pairs={{0,8},{8,0},{16,24},{24,16},{1,9},{9,1},{17,25},{25,17},{2,10},{10... | collective-permute-start | bytes 1179656 | tf_op jit(solution)/shard_map/ppermute | solution.py:783
  794.2 48.0 %collective-permute-start.10 = (bf16[48,4096]{1,0:T(8,128)(2,1)}, bf16[48,4096]{1,0:T(8,128)(2,1)}, u32[]{:S(2)}, u32[]{:S(2)}) collective-permute-start(bf16[48,4096]{1,0:T(8,128)(2,1)} %get-tuple-element.260), channel_id=1, source_target_pairs={{0,16},{8,24},{16,0},{24,8},{1,17},{9,25},{17,1},{25,9},{2,18},{10... | collective-permute-start | bytes 1179656 | tf_op jit(solution)/shard_map/ppermute | solution.py:783
  796.6 45.7 %collective-permute-start.11 = (bf16[48,4096]{1,0:T(8,128)(2,1)}, bf16[48,4096]{1,0:T(8,128)(2,1)}, u32[]{:S(2)}, u32[]{:S(2)}) collective-permute-start(bf16[48,4096]{1,0:T(8,128)(2,1)} %get-tuple-element.259), channel_id=1, source_target_pairs={{0,24},{8,16},{16,8},{24,0},{1,25},{9,17},{17,9},{25,1},{2,26},{10... | collective-permute-start | bytes 1179656 | tf_op jit(solution)/shard_map/ppermute | solution.py:783
  850.6 59.9 %all-to-all-start.9 = ((bf16[4,128,1024]{2,1,0:T(8,128)(2,1)}), bf16[4,128,1024]{2,1,0:T(8,128)(2,1)}, u32[]{:S(2)}, u32[]{:S(2)}) async-start(bf16[4,128,1024]{2,1,0:T(8,128)(2,1)} %bitcast.248), calls=%async_computation.12 | async-start | bytes 2097152 | tf_op jit(solution)/shard_map/all_to_all | solution.py:754
  854.8 187.9 %reduce-scatter.12.cloned.1.call-start = ((), (), s32[]{:S(2)}) async-start(), calls=%async_computation.23 | async-start | bytes 10076160 | tf_op jit(solution)/shard_map/reduce_scatter | solution.py:1140
  857.4 53.1 %collective-permute-start.12 = (bf16[48,4096]{1,0:T(8,128)(2,1)}, bf16[48,4096]{1,0:T(8,128)(2,1)}, u32[]{:S(2)}, u32[]{:S(2)}) collective-permute-start(bf16[48,4096]{1,0:T(8,128)(2,1)} %get-tuple-element.257), channel_id=1, source_target_pairs={{0,8},{8,0},{16,24},{24,16},{1,9},{9,1},{17,25},{25,17},{2,10},{10... | collective-permute-start | bytes 1179656 | tf_op jit(solution)/shard_map/ppermute | solution.py:783
  858.5 52.0 %collective-permute-start.13 = (bf16[48,4096]{1,0:T(8,128)(2,1)}, bf16[48,4096]{1,0:T(8,128)(2,1)}, u32[]{:S(2)}, u32[]{:S(2)}) collective-permute-start(bf16[48,4096]{1,0:T(8,128)(2,1)} %get-tuple-element.256), channel_id=1, source_target_pairs={{0,16},{8,24},{16,0},{24,8},{1,17},{9,25},{17,1},{25,9},{2,18},{10... | collective-permute-start | bytes 1179656 | tf_op jit(solution)/shard_map/ppermute | solution.py:783
  861.8 48.7 %collective-permute-start.14 = (bf16[48,4096]{1,0:T(8,128)(2,1)}, bf16[48,4096]{1,0:T(8,128)(2,1)}, u32[]{:S(2)}, u32[]{:S(2)}) collective-permute-start(bf16[48,4096]{1,0:T(8,128)(2,1)} %get-tuple-element.255), channel_id=1, source_target_pairs={{0,24},{8,16},{16,8},{24,0},{1,25},{9,17},{17,9},{25,1},{2,26},{10... | collective-permute-start | bytes 1179656 | tf_op jit(solution)/shard_map/ppermute | solution.py:783
  887.1 38.9 %collective-permute-start.15 = (bf16[128,3072]{1,0:T(8,128)(2,1)}, bf16[128,3072]{1,0:T(8,128)(2,1)}, u32[]{:S(2)}, u32[]{:S(2)}) collective-permute-start(bf16[128,3072]{1,0:T(8,128)(2,1)} %reduce_sum.363), channel_id=1, source_target_pairs={{0,0},{1,8},{2,16},{3,24},{4,4},{5,12},{6,20},{7,28},{8,1},{9,9},{... | collective-permute-start | bytes 2359304 | tf_op jit(solution)/shard_map/ppermute | solution.py:1107
  930.0 45.8 %all-to-all-start.10 = ((bf16[4,48,1536]{2,1,0:T(8,128)(2,1)}), bf16[4,48,1536]{2,1,0:T(8,128)(2,1)S(1)}, u32[]{:S(2)}, u32[]{:S(2)}) async-start(bf16[4,48,1536]{2,1,0:T(8,128)(2,1)} %bitcast.278), calls=%async_computation.15 | async-start | bytes 1179648 | tf_op jit(solution)/shard_map/all_to_all | solution.py:754
  988.4 33.2 %collective-permute-start.18 = (bf16[192,1152]{1,0:T(8,128)(2,1)}, bf16[192,1152]{1,0:T(8,128)(2,1)}, u32[]{:S(2)}, u32[]{:S(2)}) collective-permute-start(bf16[192,1152]{1,0:T(8,128)(2,1)} %get-tuple-element.252), channel_id=1, source_target_pairs={{0,16},{8,24},{16,0},{24,8},{1,17},{9,25},{17,1},{25,9},{2,18},{10... | collective-permute-start | bytes 1327112 | tf_op jit(solution)/shard_map/ppermute | solution.py:783
  (119 other events, 2214.3 us)
Sparse Core Ops, SparseCore 0:
  9.9 119.8 all-gather.11
  131.7 63.6 all-gather.5
  197.3 147.6 all-gather.7
  346.7 72.1 all-gather.9
  495.7 90.4 reduce-scatter.5
  589.0 78.8 reduce-scatter.7
  670.9 81.5 reduce-scatter.9
  755.6 37.3 reduce-scatter.13
  926.2 97.8 reduce-scatter.11

commit v9 on v8

--- a/solution.py
+++ b/solution.py
@@ -671,8 +671,11 @@
         at += chunk - off
 
 
-def finish_kernel(narrow, wide, sum_rows, sum_count, *refs):
-    items, (out_ref, x_ref, first_ref, second_ref, sends, recvs) = refs[:-6], refs[-6:]
+def finish_kernel(narrow, wide, sum_rows, sum_count, plan, *refs):
+    plans, outs = len(plan), len(plan) + 2
+    scratch = refs[-7:]
+    items, results = refs[: -7 - outs], refs[-7 - outs : -7]
+    out_ref, kept_ref, x_ref, first_ref, second_ref, sends, recvs = scratch
     place_rows(items[:sum_count], x_ref, sum_rows, 0)
     place_rows(items[sum_count:], x_ref, x_ref.shape[1] - sum_rows, sum_rows)
     me = lax.axis_index("fsdp")
@@ -716,27 +719,56 @@
     total = second_ref[0, :sum_rows, :]
     for i in range(1, wide):
         total = total + second_ref[i, :sum_rows, :]
-    out_ref[me, :sum_rows, :] = total
+    out_ref[me] = total
     for i in range(wide):
-        out_ref[me, sum_rows + i * rest : sum_rows + (i + 1) * rest, :] = second_ref[i, sum_rows:, :]
+        kept_ref[me, i] = second_ref[i, sum_rows:, :]
     copies = send_all(places, lambda i: out_ref.at[me], out_ref.at[me], narrow + wide)
+    copies += send_all(places, lambda i: kept_ref.at[me], kept_ref.at[me], 2 * narrow + wide)
     for copy in copies:
         copy.wait()
-
-
-def finish(summed, kept, narrow, wide, collective_id):
+    for result, source_rows in zip(results[:plans], plan):
+        lanes = result.shape[1] // 128
+        for i, source in enumerate(source_rows):
+            result[i // lanes : i // lanes + 1, i % lanes * 128 : (i % lanes + 1) * 128] = out_ref[
+                source // sum_rows, source % sum_rows : source % sum_rows + 1, :
+            ]
+    slots_ref, cond_ref = results[plans:]
+    images = slots_ref.shape[1]
+    width = slots_ref.shape[2] // 128
+    lanes = width // 4
+    targets = [
+        (slots_ref, image, part * lanes + lane)
+        for part in range(4) for image in range(images) for lane in range(lanes)
+    ] + [(cond_ref, image, lane) for image in range(images) for lane in range(cond_ref.shape[2] // 128)]
+
+    def unpack(g, carry):
+        for at, (target, image, lane) in enumerate(targets):
+            row = kept_ref[at // rest, g, at % rest : at % rest + 1, :]
+            target[g, image : image + 1, lane * 128 : (lane + 1) * 128] = row
+        return carry
+
+    lax.fori_loop(0, wide, unpack, 0)
+
+
+def finish(summed, kept, plan, images, narrow, wide, collective_id):
     sum_total = sum(item.shape[0] for item in summed)
     kept_total = sum(item.shape[0] for item in kept)
     sum_rows = round_up(-(-sum_total // narrow), 8)
     kept_rows = round_up(-(-kept_total // narrow), 8)
     rows = sum_rows + kept_rows
-    count = 2 * narrow + wide
-    out = pl.pallas_call(
-        functools.partial(finish_kernel, narrow, wide, sum_rows, len(summed)),
-        in_specs=[pl.BlockSpec(memory_space=pltpu.VMEM)] * (len(summed) + len(kept)),
-        out_specs=pl.BlockSpec(memory_space=pltpu.VMEM),
-        out_shape=jax.ShapeDtypeStruct((narrow, sum_rows + wide * kept_rows, 128), F32),
+    count = 3 * narrow + wide
+    cond_width = kept[-1].shape[0] * 128 // images
+    slot_width = (kept_total - kept[-1].shape[0]) * 128 // images
+    vmem = pl.BlockSpec(memory_space=pltpu.VMEM)
+    shapes = [shape for shape, _ in plan] + [(wide, images, slot_width), (wide, images, cond_width)]
+    return pl.pallas_call(
+        functools.partial(finish_kernel, narrow, wide, sum_rows, len(summed), [source for _, source in plan]),
+        in_specs=[vmem] * (len(summed) + len(kept)),
+        out_specs=[vmem] * len(shapes),
+        out_shape=[jax.ShapeDtypeStruct(shape, F32) for shape in shapes],
         scratch_shapes=[
+            pltpu.VMEM((narrow, sum_rows, 128), F32),
+            pltpu.VMEM((narrow, wide, kept_rows, 128), F32),
             pltpu.VMEM((narrow, rows, 128), F32),
             pltpu.VMEM((narrow, rows, 128), F32),
             pltpu.VMEM((wide, rows, 128), F32),
@@ -745,9 +777,6 @@
         ],
         compiler_params=pltpu.CompilerParams(collective_id=collective_id, has_side_effects=True),
     )(*summed, *kept)
-    total = out[:, :sum_rows, :].reshape(narrow * sum_rows, 128)[:sum_total]
-    groups = out[:, sum_rows:, :].reshape(narrow, wide, kept_rows, 128).transpose(1, 0, 2, 3)
-    return total, groups.reshape(wide, narrow * kept_rows, 128)[:, :kept_total]
 
 
 def exchange(blocks, axis):
@@ -941,7 +970,9 @@
         relative(own_text_weight, me, 0).transpose(1, 0, 2).reshape(text_cols, 2 * model_width)
     )
     text_partial = jnp.stack([low_product(text_slice, own_text_weight[i]).astype(BF16) for i in range(narrow)])
-    text_partial, tokens_all = lax.optimization_barrier((text_partial, tokens_all))
+    text_partial, tokens_all, relative_text_weight = lax.optimization_barrier(
+        (text_partial, tokens_all, relative_text_weight)
+    )
     text_projected = widened(jnp.sum(exchange(text_partial, "fsdp").astype(F32), axis=0), 2)
     text_parts = fsdp_share(column_stats(text_projected, part, part_pad, 1), narrow, 1)
     text_means = text_parts[:, 0, :]
@@ -1097,10 +1128,11 @@
         backs[1] = (second, *backs[1][1:])
         backs += [self_pair(pair) for pair in range(2, pairs)]
     gate_pieces = z_pieces(by_z(gate_part), deep)
-    last, came_text_z, up_part, *gate_pieces = lax.optimization_barrier(
-        (backs[-1][0], came_text_z, up_part, *gate_pieces)
-    )
-    up_pieces = z_pieces(by_z(up_part), deep)
+    last, came_text_z, up_part, out_part, *gate_pieces = lax.optimization_barrier(
+        (backs[-1][0], came_text_z, up_part, out_part, *gate_pieces)
+    )
+    up_width = up_part.shape[1]
+    up_pieces = z_pieces(by_z(jnp.concatenate([up_part, out_part], axis=1)), deep)
     backs[-1] = (last, *backs[-1][1:])
     text_part = jnp.sum(came_text_z.astype(F32), axis=0).astype(BF16)
     everyone = ("z", "core", "fsdp")
@@ -1121,7 +1153,6 @@
         .reshape(narrow, text_local, text_cols),
         "fsdp",
     )
-    came_out_z = exchange(by_z(out_part), "z")
     own_gate_grad = jnp.sum(gate_sums[:, 0, :].reshape(pairs * halves, head_dim), axis=1)[:heads_here]
     grad_head_gate = lax.dynamic_update_slice_in_dim(
         jnp.zeros((head_count,), F32), own_gate_grad, me * heads_here, 0
@@ -1133,7 +1164,10 @@
     grad_projected_low, came_text, *up_pieces = lax.optimization_barrier(
         (grad_projected_low, came_text, *up_pieces)
     )
-    grad_gate_up_weight = jnp.concatenate([added(gate_pieces), added(up_pieces)], axis=1)
+    grad_gate_up_weight = jnp.concatenate(
+        [added(gate_pieces), added([piece[:, :up_width] for piece in up_pieces])], axis=1
+    )
+    grad_out_weight = added([piece[:, up_width:] for piece in up_pieces])
     partial_normed, grad_text_weight = lax.optimization_barrier(
         (times_transposed(grad_projected_low, own_qkv).astype(BF16), grad_text_weight)
     )
@@ -1154,7 +1188,6 @@
     later = [*grad_gate_attend, *grad_scale_feed, *grad_gate_feed, cond_rows_here]
     ready = lax.optimization_barrier(tuple(ready))
     qkv_grad = outer_sum(normed_all, grad_projected_low).astype(BF16).reshape(deep, 2, model_width // wide, 3 * part_pad)
-    qkv_grad, came_out_z = lax.optimization_barrier((qkv_grad, came_out_z))
     place = (lax.axis_index("z") * 2 + lax.axis_index("core")) * narrow + me
     grad_text_weight = (
         relative(grad_text_weight.reshape(-1, narrow, 2 * part), place // wide, 1)
@@ -1163,10 +1196,10 @@
         .reshape(-1, 2 * model_width)
         .astype(F32)
     )
-    grad_out_weight = jnp.sum(came_out_z.astype(F32), axis=0)
     own_grad, other_grad = by_core(qkv_grad[:, 0], qkv_grad[:, 1])
     own_grad = (own_grad.astype(F32) + core_swap(other_grad).astype(F32)).astype(BF16)
     own_pieces = z_pieces(own_grad, deep)
+    came_text, *own_pieces = lax.optimization_barrier((came_text, *own_pieces))
     grad_text_normed = (
         came_text
         .transpose(1, 0, 2)
@@ -1181,7 +1214,6 @@
         .reshape(image_count, caption_local, caption_width)
     )
 
-    grad_text, grad_text_gain, *own_pieces = lax.optimization_barrier((grad_text, grad_text_gain, *own_pieces))
     own_grad = added(own_pieces)
     grad_qkv_weight = (
         exchange(narrowed(own_grad.astype(BF16), 3).reshape(narrow, -1, 3 * part), "fsdp")
@@ -1190,7 +1222,9 @@
         .reshape(-1, 3 * model_width)
         .astype(F32)
     )
-    grad_normed, grad_qkv_weight = lax.optimization_barrier((grad_normed, grad_qkv_weight))
+    grad_normed, grad_qkv_weight, grad_text, grad_text_gain = lax.optimization_barrier(
+        (grad_normed, grad_qkv_weight, grad_text, grad_text_gain)
+    )
     grad_normed = grad_normed.astype(F32)
 
     token_unit = token_in * token_inverse
@@ -1202,27 +1236,30 @@
         grad_hidden + norm_pull(grad_normed_y * norm_gains[0], token_unit, token_inverse)
     ).astype(BF16)
     lanes_of_row = model_width // 128
-    summed, kept = finish(
-        [lane_rows(grad_gain_zero), *ready, lane_rows(grad_text_gain)], [*grad_scale_attend, *later], narrow, wide, 5
-    )
-    every_image = wide * image_count
-    per_part = image_count * lanes_of_row
-    slots = jnp.concatenate(
-        [kept[:, i * per_part : (i + 1) * per_part].reshape(every_image, model_width) for i in range(4)], axis=1
-    )
-    cond_slots = kept[:, 4 * per_part :].reshape(every_image, cond_low.shape[1])
+    def row_range(first, count):
+        return list(range(first * lanes_of_row, (first + count) * lanes_of_row))
+
+    gate_at = 9 * lanes_of_row
+    text_rows = caption_width // 128
+    grad_gains, grad_shifts, gate_row, grad_text_gain, slots, cond_slots = finish(
+        [lane_rows(grad_gain_zero), *ready, lane_rows(grad_text_gain)],
+        [*grad_scale_attend, *later],
+        [
+            (norm_gains.shape, row_range(0, 2) + row_range(4, 3) + row_range(2, 2)),
+            (norm_shifts.shape, row_range(7, 2)),
+            ((1, 128), [gate_at]),
+            ((text_rows, 128), list(range(gate_at + 1, gate_at + 1 + text_rows))),
+        ],
+        image_count, narrow, wide, 5,
+    )
+    slots = slots.reshape(wide * image_count, -1)
+    cond_slots = cond_slots.reshape(wide * image_count, -1)
+    grad_head_gate = gate_row[0, :head_count]
+    grad_text_gain = grad_text_gain.reshape(-1)
     ada_rows = cond_rows // wide
     own_cond = lax.dynamic_slice_in_dim(cond_slots, (group * narrow + me) * ada_rows, ada_rows, 1)
     grad_ada_weight = exact_outer(own_cond, slots)
     grad_ada_bias = jnp.sum(slots, axis=0)
-
-    def rows_of(first, count):
-        return summed[first * lanes_of_row : (first + count) * lanes_of_row]
-
-    grad_gains = jnp.concatenate([rows_of(0, 2), rows_of(4, 3), rows_of(2, 2)]).reshape(norm_gains.shape)
-    grad_shifts = rows_of(7, 2).reshape(norm_shifts.shape)
-    grad_head_gate = summed[9 * lanes_of_row, :head_count]
-    grad_text_gain = summed[9 * lanes_of_row + 1 :].reshape(-1)
     return (
         result[None],
         grad_tokens[None],

time: 1130 us -> 1130 us (level)
  local copies, waits for them, and re-layouts: 127 us -> 113 us
    ppermute x9, starting transfers between devices: 13.3 us -> 32.4 us  [z_pieces(): lax.ppermute(lax.dynamic_index_in_dim(blocks, me ^ step, 0, keepdims=Fals...]
    all_to_all x12 -> x11, starting transfers between devices: 64.6 us -> 47.5 us  [exchange(): return lax.all_to_all(blocks, axis, 0, 0, tiled=True)]
    all_to_all x12 -> x11, waiting for transfers between devices: 32.1 us -> 28.3 us  [exchange(): return lax.all_to_all(blocks, axis, 0, 0, tiled=True)]
    unnamed x230 -> x220, local copies, waits for them, and re-layouts: 33.6 us -> 31.9 us
  transfers between devices with their start and end apart: 41 -> 40, of which waited for: 11 -> 9; matrix products, arithmetic and copies ran while one was open for 37% -> 37% of each run, Pallas kernels for 37% -> 37%
where the time goes in v9:
time: 1130 us; the launch traced here: 1120 us
  Pallas kernels  451 us (40%)
  matrix products  248 us (22%)
  other arithmetic  121 us (11%)
  local copies, waits for them, and re-layouts  113 us (10%)
  starting transfers between devices  92 us (8%)
  waiting for transfers between devices  74.3 us (7%)
  between operations  18.3 us (2%)
    pallas_call x3, Pallas kernels, self_back(): pl.pallas_call(functools.partial(self_back_kernel, head_dim, FIRST_PATCHE...  137 us
    pallas_call x3, Pallas kernels, attend(): pl.pallas_call(functools.partial(attend_kernel, head_dim, FIRST_PATCHES,...  98.9 us
    dot_general x11, matrix products, outer_sum(): lax.dot_general(left, right, (((0,), (0,)), ((), ())), preferred_element_...  93.8 us
    dot_general x11, matrix products, low_product(): return jnp.dot(left, right, preferred_element_type=F32)  77.4 us
    dot_general x5, matrix products, times_transposed(): lax.dot_general(left, right, (((1,), (1,)), ((), ())), preferred_element_...  74.5 us
    pallas_call x5, Pallas kernels, fsdp_share(): pl.pallas_call(functools.partial(fsdp_share_kernel, narrow), in_specs=[pl...  60.5 us
    all_to_all x11, starting transfers between devices, exchange(): return lax.all_to_all(blocks, axis, 0, 0, tiled=True)  47.5 us
    pallas_call x3, Pallas kernels, cross_back(): pl.pallas_call(functools.partial(cross_back_kernel, head_dim, FIRST_PATCH...  40.3 us
  transfers between devices with their start and end apart: 40, of which 9 were waited for; matrix products, arithmetic and copies ran while one was open for 37% of the time, Pallas kernels for 37%

profile of v9, /device:TPU:0, one launch (start us, length us, event | category | flops | bytes accessed | tf_op | source)
XLA Modules:
  0.0 1118.8 jit_solution(6760211350504720250)
XLA Ops:
  40.3 27.4 %shard_map.263 = f32[4,96,128]{2,1,0:T(8,128)} custom-call(f32[96,128]{1,0:T(8,128)} %reshape.630.x_ref), custom_call_target="tpu_custom_call" | custom-call | bytes 393216 | tf_op jit(solution)/shard_map/pallas_call | solution.py:648
  101.0 10.5 negate_select_fusion
  161.6 13.6 %fusion.164.projected_ref.refs_6_.refs_9_ = f32[2624,1152]{1,0:T(8,128)} fusion(bf16[2624,1536]{1,0:T(8,128)(2,1)S(1)} %fusion.3, bf16[1536,1152]{1,0:T(8,128)(2,1)S(1)} %bitcast.250), kind=kOutput, calls=%fused_computation.378 | convolution fusion | flops 9286189056 | bytes 23691264 | tf_op jit(solution)/shard_map/dot_general | solution.py:28
  184.5 11.6 %shard_map.265.stats_ref.refs_7_.refs_10_ = f32[4,8,2624]{2,1,0:T(8,128)} custom-call(f32[8,2624]{1,0:T(8,128)} %shard_map.264.x_ref), custom_call_target="tpu_custom_call" | custom-call | bytes 671744 | tf_op jit(solution)/shard_map/pallas_call | solution.py:648
  196.1 16.0 %shard_map.266.q_ref.k_ref.v_ref = bf16[2624,1152]{1,0:T(8,128)(2,1)} custom-call(f32[2624,1152]{1,0:T(8,128)} %fusion.164.projected_ref.refs_6_.refs_9_, f32[4,8,2624]{2,1,0:T(8,128)} %shard_map.265.stats_ref.refs_7_.refs_10_, f32[2624,128]{1,0:T(8,128)} %get-tuple-element.284.cos_ref.refs_8_.refs_12_, ...), custom_call_target="tpu_custom_call" | custom-call | flops 120913920 | bytes 18137088 | tf_op jit(solution)/shard_map/pallas_call | solution.py:183
  228.0 38.2 %shard_map.271 = (bf16[2624,128]{1,0:T(8,128)(2,1)}, f32[2624,128]{1,0:T(8,128)}, f32[2624,128]{1,0:T(8,128)}, f32[8,2624]{1,0:T(8,128)}) custom-call(f32[3,1,2]{2,1,0:T(1,128)} %reshape.687.gate_ref, bf16[2624,1152]{1,0:T(8,128)(2,1)} %shard_map.266.q_ref.k_ref.v_ref, bf16[2624,1152]{1,0:T(8,128)(2,1)} %shard_map.266.q_ref.k_ref.v_ref, ...), custom_call_target="tpu_custom_call" | custom-call | flops 4213178368 | bytes 6717440 | tf_op jit(solution)/shard_map/pallas_call | solution.py:379
  269.7 30.4 %shard_map.270 = (bf16[2624,128]{1,0:T(8,128)(2,1)}, f32[2624,128]{1,0:T(8,128)}, f32[2624,128]{1,0:T(8,128)}, f32[8,2624]{1,0:T(8,128)}) custom-call(f32[3,1,2]{2,1,0:T(1,128)} %reshape.687.gate_ref, bf16[2624,1152]{1,0:T(8,128)(2,1)} %shard_map.266.q_ref.k_ref.v_ref, bf16[2624,1152]{1,0:T(8,128)(2,1)} %shard_map.266.q_ref.k_ref.v_ref, ...), custom_call_target="tpu_custom_call" | custom-call | flops 4213178368 | bytes 6717440 | tf_op jit(solution)/shard_map/pallas_call | solution.py:379
  304.5 30.4 %shard_map.269 = (bf16[2624,128]{1,0:T(8,128)(2,1)}, f32[2624,128]{1,0:T(8,128)}, f32[2624,128]{1,0:T(8,128)}, f32[8,2624]{1,0:T(8,128)}) custom-call(f32[3,1,2]{2,1,0:T(1,128)} %reshape.687.gate_ref, bf16[2624,1152]{1,0:T(8,128)(2,1)} %shard_map.266.q_ref.k_ref.v_ref, bf16[2624,1152]{1,0:T(8,128)(2,1)} %shard_map.266.q_ref.k_ref.v_ref, ...), custom_call_target="tpu_custom_call" | custom-call | flops 4213178368 | bytes 6717440 | tf_op jit(solution)/shard_map/pallas_call | solution.py:379
  339.3 17.1 %all-to-all-done.3 = bf16[4,656,128]{2,1,0:T(8,128)(2,1)} async-done(((bf16[4,656,128]{2,1,0:T(8,128)(2,1)}), bf16[4,656,128]{2,1,0:T(8,128)(2,1)}, u32[]{:S(2)}, u32[]{:S(2)}) %all-to-all-start.3) | async-done | bytes 671776 | tf_op jit(solution)/shard_map/all_to_all | solution.py:783
  381.0 26.4 %fusion.165.gate_ref.up_ref = f32[656,8192]{1,0:T(8,128)} fusion(bf16[656,1536]{1,0:T(8,128)(2,1)} %copy-done.32, bf16[1536,8192]{1,0:T(8,128)(2,1)} %all-gather.8.cloned.1.call-done), kind=kOutput, calls=%fused_computation.379 | convolution fusion | flops 16508780544 | bytes 48676864 | tf_op jit(solution)/shard_map/dot_general | solution.py:28
  407.4 22.7 %shard_map.272 = (bf16[656,4096]{1,0:T(8,128)(2,1)}, bf16[656,4096]{1,0:T(8,128)(2,1)}) custom-call(s32[1]{0:T(128)} %bitcast.32.core_ref, f32[656,8192]{1,0:T(8,128)} %fusion.165.gate_ref.up_ref, f32[656,8192]{1,0:T(8,128)} %fusion.165.gate_ref.up_ref), custom_call_target="tpu_custom_call" | custom-call | flops 16121856 | bytes 32243712 | tf_op jit(solution)/shard_map/pallas_call | solution.py:602
  430.1 13.1 %multiply_reduce_fusion.14 = (f32[656]{0:T(1024)S(1)}, f32[656,1536]{1,0:T(8,128)S(1)}) fusion(bf16[656,4096]{1,0:T(8,128)(2,1)} %get-tuple-element.114, bf16[4096,1536]{1,0:T(8,128)(2,1)} %all-gather.10.cloned.1.call-done), kind=kOutput, calls=%fused_computation.73 | convolution fusion | flops 8256404992 | bytes 21989952 | tf_op jit(solution)/shard_map/dot_general | solution.py:28
  458.6 19.5 %fusion.6 = (bf16[656,4096]{1,0:T(8,128)(2,1)}, bf16[656,4096]{1,0:T(8,128)(2,1)S(1)}) fusion(f32[656,8192]{1,0:T(8,128)} %fusion.165.gate_ref.up_ref, bf16[656,1536]{1,0:T(8,128)(2,1)} %copy-done.28, bf16[4096,1536]{1,0:T(8,128)(2,1)} %all-gather.10.cloned.1.call-done), kind=kOutput, calls=%fused_computation.13 | convolution fusion | flops 8289320960 | bytes 46841856 | tf_op jit(solution)/shard_map/dot_general | solution.py:32
  478.1 11.5 %convolution_convert_fusion.4 = bf16[768,4096]{1,0:T(8,128)(2,1)} fusion(bf16[656,4096]{1,0:T(8,128)(2,1)} %get-tuple-element.249, bf16[656,1536]{1,0:T(8,128)(2,1)S(1)} %copy-done.27), kind=kOutput, calls=%fused_computation.26 | convolution fusion | flops 4130340864 | bytes 12673024 | tf_op jit(solution)/shard_map/dot_general | solution.py:36
  497.2 9.4 add_convert_fusion
  507.4 28.7 %multiply_reduce_fusion.9 = (f32[1536]{0:T(1024)}, f32[656]{0:T(1024)S(1)}, f32[1536]{0:T(1024)}, f32[1536]{0:T(1024)}, f32[656,1536]{1,0:T(8,128)}) fusion(f32[656,1536]{1,0:T(8,128)} %copy-done.2, f32[656]{0:T(1024)S(1)} %copy-done.78, f32[1536]{0:T(1024)S(1)} %copy-done.65, f32[656]{0:T(1024)S(1)} %get-tuple-element.303, f32[1536]{0:T(1024)S(1)} %copy-done.67, ...), kind=kOutput, calls=%fused_computation.65 | convolution fusion | flops 16547399680 | bytes 44022016 | tf_op jit(solution)/shard_map/dot_general | solution.py:32
  568.9 10.8 add_convert_fusion.2
  579.7 10.8 add_convert_fusion.1
  602.8 13.5 %shard_map.275 = (bf16[2624,128]{1,0:T(8,128)(2,1)}, bf16[512,128]{1,0:T(8,128)(2,1)}, bf16[512,128]{1,0:T(8,128)(2,1)}, f32[8,128]{1,0:T(8,128)}) custom-call(f32[3,1,2]{2,1,0:T(1,128)} %reshape.687.gate_ref, bf16[2624,1152]{1,0:T(8,128)(2,1)} %shard_map.266.q_ref.k_ref.v_ref, bf16[512,768]{1,0:T(8,128)(2,1)} %pad_maximum_fusion.5.tk_ref.tv_ref, ...), custom_call_target="tpu_custom_call" | custom-call | flops 1719664640 | bytes 4030464 | tf_op jit(solution)/shard_map/pallas_call | solution.py:495
  616.3 13.3 %shard_map.274 = (bf16[2624,128]{1,0:T(8,128)(2,1)}, bf16[512,128]{1,0:T(8,128)(2,1)}, bf16[512,128]{1,0:T(8,128)(2,1)}, f32[8,128]{1,0:T(8,128)}) custom-call(f32[3,1,2]{2,1,0:T(1,128)} %reshape.687.gate_ref, bf16[2624,1152]{1,0:T(8,128)(2,1)} %shard_map.266.q_ref.k_ref.v_ref, bf16[512,768]{1,0:T(8,128)(2,1)} %pad_maximum_fusion.5.tk_ref.tv_ref, ...), custom_call_target="tpu_custom_call" | custom-call | flops 1719664640 | bytes 4030464 | tf_op jit(solution)/shard_map/pallas_call | solution.py:495
  629.7 13.5 %shard_map.273 = (bf16[2624,128]{1,0:T(8,128)(2,1)}, bf16[512,128]{1,0:T(8,128)(2,1)}, bf16[512,128]{1,0:T(8,128)(2,1)}, f32[8,128]{1,0:T(8,128)}) custom-call(f32[3,1,2]{2,1,0:T(1,128)} %reshape.687.gate_ref, bf16[2624,1152]{1,0:T(8,128)(2,1)} %shard_map.266.q_ref.k_ref.v_ref, bf16[512,768]{1,0:T(8,128)(2,1)} %pad_maximum_fusion.5.tk_ref.tv_ref, ...), custom_call_target="tpu_custom_call" | custom-call | flops 1719664640 | bytes 4030464 | tf_op jit(solution)/shard_map/pallas_call | solution.py:495
  664.7 45.9 %shard_map.277 = (bf16[2624,128]{1,0:T(8,128)(2,1)}, bf16[2624,128]{1,0:T(8,128)(2,1)}, bf16[2624,128]{1,0:T(8,128)(2,1)}) custom-call(bf16[2624,1152]{1,0:T(8,128)(2,1)} %shard_map.266.q_ref.k_ref.v_ref, bf16[2624,1152]{1,0:T(8,128)(2,1)} %shard_map.266.q_ref.k_ref.v_ref, bf16[2624,1152]{1,0:T(8,128)(2,1)} %shard_map.266.q_ref.k_ref.v_ref, ...), custom_call_target="tpu_custom_call" | custom-call | flops 8813281280 | bytes 10076160 | tf_op jit(solution)/shard_map/pallas_call | solution.py:562
  744.0 45.4 %shard_map.278 = (bf16[2624,128]{1,0:T(8,128)(2,1)}, bf16[2624,128]{1,0:T(8,128)(2,1)}, bf16[2624,128]{1,0:T(8,128)(2,1)}) custom-call(bf16[2624,1152]{1,0:T(8,128)(2,1)} %shard_map.266.q_ref.k_ref.v_ref, bf16[2624,1152]{1,0:T(8,128)(2,1)} %shard_map.266.q_ref.k_ref.v_ref, bf16[2624,1152]{1,0:T(8,128)(2,1)} %shard_map.266.q_ref.k_ref.v_ref, ...), custom_call_target="tpu_custom_call" | custom-call | flops 8813281280 | bytes 10076160 | tf_op jit(solution)/shard_map/pallas_call | solution.py:562
  796.3 45.8 %shard_map.279 = (bf16[2624,128]{1,0:T(8,128)(2,1)}, bf16[2624,128]{1,0:T(8,128)(2,1)}, bf16[2624,128]{1,0:T(8,128)(2,1)}) custom-call(bf16[2624,1152]{1,0:T(8,128)(2,1)} %shard_map.266.q_ref.k_ref.v_ref, bf16[2624,1152]{1,0:T(8,128)(2,1)} %shard_map.266.q_ref.k_ref.v_ref, bf16[2624,1152]{1,0:T(8,128)(2,1)} %shard_map.266.q_ref.k_ref.v_ref, ...), custom_call_target="tpu_custom_call" | custom-call | flops 8813281280 | bytes 10076160 | tf_op jit(solution)/shard_map/pallas_call | solution.py:562
  867.4 15.2 %shard_map.280 = (f32[8,2624]{1,0:T(8,128)}, f32[8,384]{1,0:T(8,128)}) custom-call(bf16[2624,128]{1,0:T(8,128)(2,1)} %get-tuple-element.137.refs_0_, bf16[2624,128]{1,0:T(8,128)(2,1)} %get-tuple-element.144.refs_1_, bf16[2624,128]{1,0:T(8,128)(2,1)} %get-tuple-element.154.refs_2_, bf16[2624,128]{1,0:T(8,128)(2,1)} %get-tuple-element.155.refs_3_, ...), custom_call_target="tpu_custom_call" | custom-call | flops 12091392 | bytes 188928 | tf_op jit(solution)/shard_map/pallas_call | solution.py:269
  900.1 15.7 %shard_map.282 = bf16[2624,1152]{1,0:T(8,128)(2,1)} custom-call(bf16[2624,128]{1,0:T(8,128)(2,1)} %get-tuple-element.137.refs_0_, bf16[2624,128]{1,0:T(8,128)(2,1)} %get-tuple-element.144.refs_1_, bf16[2624,128]{1,0:T(8,128)(2,1)} %get-tuple-element.154.refs_2_, bf16[2624,128]{1,0:T(8,128)(2,1)} %get-tuple-element.155.refs_3_, ...), custom_call_target="tpu_custom_call" | custom-call | flops 12091392 | bytes 188928 | tf_op jit(solution)/shard_map/pallas_call | solution.py:282
  921.5 15.5 %convolution_convert_fusion = bf16[2624,1536]{1,0:T(8,128)(2,1)} fusion(bf16[2624,1152]{1,0:T(8,128)(2,1)} %shard_map.282, bf16[1536,1152]{1,0:T(8,128)(2,1)S(1)} %bitcast.251), kind=kOutput, calls=%fused_computation.9 | convolution fusion | flops 9290219520 | bytes 17645568 | tf_op jit(solution)/shard_map/dot_general | solution.py:32
  944.0 15.4 %convolution_convert_fusion.2 = bf16[1536,1152]{1,0:T(8,128)(2,1)S(1)} fusion(bf16[2624,1536]{1,0:T(8,128)(2,1)} %copy-done.19, bf16[2624,1152]{1,0:T(8,128)(2,1)} %shard_map.282), kind=kOutput, calls=%fused_computation.24 | convolution fusion | flops 9287958528 | bytes 17645568 | tf_op jit(solution)/shard_map/dot_general | solution.py:36
  979.6 16.2 %collective-permute-start.17 = (bf16[192,1152]{1,0:T(8,128)(2,1)S(1)}, bf16[192,1152]{1,0:T(8,128)(2,1)S(1)}, u32[]{:S(2)}, u32[]{:S(2)}) collective-permute-start(bf16[192,1152]{1,0:T(8,128)(2,1)S(1)} %get-tuple-element.271), channel_id=1, source_target_pairs={{0,8},{8,0},{16,24},{24,16},{1,9},{9,1},{17,25},{25,17},{2,10},{10... | collective-permute-start | bytes 1327112 | tf_op jit(solution)/shard_map/ppermute | solution.py:812
  1000.2 9.9 collective-permute-done.17
  1010.1 18.6 %collective-permute-done.18 = bf16[192,1152]{1,0:T(8,128)(2,1)S(1)} collective-permute-done((bf16[192,1152]{1,0:T(8,128)(2,1)S(1)}, bf16[192,1152]{1,0:T(8,128)(2,1)S(1)}, u32[]{:S(2)}, u32[]{:S(2)}) %collective-permute-start.18) | collective-permute-done | bytes 442400 | tf_op jit(solution)/shard_map/ppermute | solution.py:812
  1059.4 32.9 %shard_map.283 = (f32[7,1536]{1,0:T(8,128)}, f32[2,1536]{1,0:T(2,128)}, f32[1,128]{1,0:T(1,128)}, f32[32,128]{1,0:T(8,128)}, f32[8,2,6144]{2,1,0:T(2,128)}, /*index=5*/f32[8,2,1024]{2,1,0:T(2,128)}) custom-call(f32[12,128]{1,0:T(8,128)} %bitcast.282, f32[12,128]{1,0:T(8,128)} %bitcast.281, f32[12,128]{1,0:T(8,128)} %bitcast.290, f32[12,128]{1,0:T(8,128)} %bitcast.276, ...), custom_call_target="tpu_custom_call" | custom-call | tf_op jit(solution)/shard_map/pallas_call | solution.py:764
  (460 shorter events, 435.6 us)
Async XLA Ops:
  7.2 134.7 %all-gather.12.cloned.1.call-start = ((), (), s32[]{:S(2)}) async-start(), calls=%async_computation.24 | async-start | bytes 10076160 | tf_op jit(solution)/shard_map/all_gather | solution.py:925
  7.9 351.4 %all-gather.6.cloned.1.call-start = ((), (), s32[]{:S(2)}) async-start(), calls=%async_computation.16 | async-start | bytes 5308416 | tf_op jit(solution)/shard_map/all_gather | solution.py:853
  10.2 370.9 %all-gather.8.cloned.1.call-start = ((), (), s32[]{:S(2)}) async-start(), calls=%async_computation.17 | async-start | bytes 28311552 | tf_op jit(solution)/shard_map/all_gather | solution.py:853
  25.0 86.5 %all-to-all-start.1 = ((bf16[4,192,1152]{2,1,0:T(8,128)(2,1)}), bf16[4,192,1152]{2,1,0:T(8,128)(2,1)}, u32[]{:S(2)}, u32[]{:S(2)}) async-start(bf16[4,192,1152]{2,1,0:T(8,128)(2,1)} %reshape.639), calls=%async_computation.1 | async-start | bytes 3538944 | tf_op jit(solution)/shard_map/all_to_all | solution.py:783
  30.3 399.8 %all-gather.10.cloned.1.call-start = ((), (), s32[]{:S(2)}) async-start(), calls=%async_computation.18 | async-start | bytes 14155776 | tf_op jit(solution)/shard_map/all_gather | solution.py:853
  141.9 70.2 %all-to-all-start.2 = ((bf16[4,512,768]{2,1,0:T(8,128)(2,1)}), bf16[4,512,768]{2,1,0:T(8,128)(2,1)}, u32[]{:S(2)}, u32[]{:S(2)}) async-start(bf16[4,512,768]{2,1,0:T(8,128)(2,1)} %pad_maximum_fusion.2), calls=%async_computation.2 | async-start | bytes 6291456 | tf_op jit(solution)/shard_map/all_to_all | solution.py:783
  266.2 33.9 %all-to-all-start.5 = ((bf16[4,656,128]{2,1,0:T(8,128)(2,1)}), bf16[4,656,128]{2,1,0:T(8,128)(2,1)S(1)}, u32[]{:S(2)}, u32[]{:S(2)}) async-start(bf16[4,656,128]{2,1,0:T(8,128)(2,1)} %bitcast.273), calls=%async_computation.5 | async-start | bytes 1343488 | tf_op jit(solution)/shard_map/all_to_all | solution.py:783
  300.1 34.8 %all-to-all-start.4 = ((bf16[4,656,128]{2,1,0:T(8,128)(2,1)}), bf16[4,656,128]{2,1,0:T(8,128)(2,1)S(1)}, u32[]{:S(2)}, u32[]{:S(2)}) async-start(bf16[4,656,128]{2,1,0:T(8,128)(2,1)} %bitcast.272), calls=%async_computation.4 | async-start | bytes 1343488 | tf_op jit(solution)/shard_map/all_to_all | solution.py:783
  339.2 258.2 %reduce-scatter.6.cloned.1.call-start = ((), (), s32[]{:S(2)}) async-start(), calls=%async_computation.19 | async-start | bytes 7864320 | tf_op jit(solution)/shard_map/reduce_scatter | solution.py:806
  458.6 38.6 %collective-permute-start.4 = (bf16[2048,1536]{1,0:T(8,128)(2,1)}, bf16[2048,1536]{1,0:T(8,128)(2,1)}, u32[]{:S(2)}, u32[]{:S(2)}) collective-permute-start(bf16[2048,1536]{1,0:T(8,128)(2,1)} %convolution_convert_fusion.1), channel_id=1, source_target_pairs={{0,4},{4,0},{1,5},{5,1},{2,6},{6,2},{3,7},{7,3},{8,12},{12,8},{9,1... | collective-permute-start | bytes 18874376 | tf_op jit(solution)/shard_map/ppermute | solution.py:787
  489.6 79.3 %collective-permute-start.1 = (bf16[768,4096]{1,0:T(8,128)(2,1)}, bf16[768,4096]{1,0:T(8,128)(2,1)}, u32[]{:S(2)}, u32[]{:S(2)}) collective-permute-start(bf16[768,4096]{1,0:T(8,128)(2,1)} %convolution_convert_fusion.4), channel_id=1, source_target_pairs={{0,4},{4,0},{1,5},{5,1},{2,6},{6,2},{3,7},{7,3},{8,12},{12,8},{9,1... | collective-permute-start | bytes 18874376 | tf_op jit(solution)/shard_map/ppermute | solution.py:787
  497.1 82.6 %collective-permute-start.2 = (bf16[768,4096]{1,0:T(8,128)(2,1)}, bf16[768,4096]{1,0:T(8,128)(2,1)}, u32[]{:S(2)}, u32[]{:S(2)}) collective-permute-start(bf16[768,4096]{1,0:T(8,128)(2,1)} %convolution_convert_fusion.3), channel_id=1, source_target_pairs={{0,4},{4,0},{1,5},{5,1},{2,6},{6,2},{3,7},{7,3},{8,12},{12,8},{9,1... | collective-permute-start | bytes 18874376 | tf_op jit(solution)/shard_map/ppermute | solution.py:787
  559.0 37.7 %all-to-all-start.6 = ((bf16[4,656,384]{2,1,0:T(8,128)(2,1)}), bf16[4,656,384]{2,1,0:T(8,128)(2,1)S(1)}, u32[]{:S(2)}, u32[]{:S(2)}) async-start(bf16[4,656,384]{2,1,0:T(8,128)(2,1)} %bitcast.244), calls=%async_computation.6 | async-start | bytes 4030464 | tf_op jit(solution)/shard_map/all_to_all | solution.py:783
  562.7 226.8 %reduce-scatter.8.cloned.1.call-start = ((), (), s32[]{:S(2)}) async-start(), calls=%async_computation.20 | async-start | bytes 7864320 | tf_op jit(solution)/shard_map/reduce_scatter | solution.py:806
  597.4 192.1 %reduce-scatter.10.cloned.1.call-start = ((), (), s32[]{:S(2)}) async-start(), calls=%async_computation.21 | async-start | bytes 7864320 | tf_op jit(solution)/shard_map/reduce_scatter | solution.py:806
  598.1 116.1 %all-to-all-start.7 = ((bf16[4,128,1536]{2,1,0:T(8,128)(2,1)}), bf16[4,128,1536]{2,1,0:T(8,128)(2,1)S(1)}, u32[]{:S(2)}, u32[]{:S(2)}) async-start(bf16[4,128,1536]{2,1,0:T(8,128)(2,1)} %bitcast.267), calls=%async_computation.8 | async-start | bytes 3145728 | tf_op jit(solution)/shard_map/all_to_all | solution.py:783
  602.8 239.4 %reduce-scatter.12.cloned.1.call-start = ((), (), s32[]{:S(2)}) async-start(), calls=%async_computation.22 | async-start | bytes 2949120 | tf_op jit(solution)/shard_map/reduce_scatter | solution.py:806
  656.4 54.2 %collective-permute-start.5 = (bf16[512,768]{1,0:T(8,128)(2,1)}, bf16[512,768]{1,0:T(8,128)(2,1)}, u32[]{:S(2)}, u32[]{:S(2)}) collective-permute-start(bf16[512,768]{1,0:T(8,128)(2,1)} %pad_maximum_fusion.6), channel_id=1, source_target_pairs={{0,1},{1,0},{2,3},{3,2},{4,5},{5,4},{6,7},{7,6},{8,9},{9,8},{10,11... | collective-permute-start | bytes 2359304 | tf_op jit(solution)/shard_map/ppermute | solution.py:825
  657.8 52.8 %collective-permute-start.6 = (bf16[512,768]{1,0:T(8,128)(2,1)}, bf16[512,768]{1,0:T(8,128)(2,1)}, u32[]{:S(2)}, u32[]{:S(2)}) collective-permute-start(bf16[512,768]{1,0:T(8,128)(2,1)} %pad_maximum_fusion.6), channel_id=1, source_target_pairs={{0,2},{1,3},{2,0},{3,1},{4,6},{5,7},{6,4},{7,5},{8,10},{9,11},{10,... | collective-permute-start | bytes 2359304 | tf_op jit(solution)/shard_map/ppermute | solution.py:825
  658.4 55.9 %collective-permute-start.7 = (bf16[512,768]{1,0:T(8,128)(2,1)}, bf16[512,768]{1,0:T(8,128)(2,1)}, u32[]{:S(2)}, u32[]{:S(2)}) collective-permute-start(bf16[512,768]{1,0:T(8,128)(2,1)} %pad_maximum_fusion.6), channel_id=1, source_target_pairs={{0,3},{1,2},{2,1},{3,0},{4,7},{5,6},{6,5},{7,4},{8,11},{9,10},{10,... | collective-permute-start | bytes 2359304 | tf_op jit(solution)/shard_map/ppermute | solution.py:825
  739.1 103.0 %all-to-all-start.8 = ((bf16[4,128,3072]{2,1,0:T(8,128)(2,1)}), bf16[4,128,3072]{2,1,0:T(8,128)(2,1)S(1)}, u32[]{:S(2)}, u32[]{:S(2)}) async-start(bf16[4,128,3072]{2,1,0:T(8,128)(2,1)} %bitcast.252), calls=%async_computation.11 | async-start | bytes 6291456 | tf_op jit(solution)/shard_map/all_to_all | solution.py:783
  791.9 50.2 %collective-permute-start.9 = (bf16[48,4096]{1,0:T(8,128)(2,1)}, bf16[48,4096]{1,0:T(8,128)(2,1)S(1)}, u32[]{:S(2)}, u32[]{:S(2)}) collective-permute-start(bf16[48,4096]{1,0:T(8,128)(2,1)} %get-tuple-element.275), channel_id=1, source_target_pairs={{0,8},{8,0},{16,24},{24,16},{1,9},{9,1},{17,25},{25,17},{2,10},{10... | collective-permute-start | bytes 1179656 | tf_op jit(solution)/shard_map/ppermute | solution.py:812
  794.0 48.2 %collective-permute-start.10 = (bf16[48,4096]{1,0:T(8,128)(2,1)}, bf16[48,4096]{1,0:T(8,128)(2,1)}, u32[]{:S(2)}, u32[]{:S(2)}) collective-permute-start(bf16[48,4096]{1,0:T(8,128)(2,1)} %get-tuple-element.274), channel_id=1, source_target_pairs={{0,16},{8,24},{16,0},{24,8},{1,17},{9,25},{17,1},{25,9},{2,18},{10... | collective-permute-start | bytes 1179656 | tf_op jit(solution)/shard_map/ppermute | solution.py:812
  796.3 45.9 %collective-permute-start.11 = (bf16[48,4096]{1,0:T(8,128)(2,1)}, bf16[48,4096]{1,0:T(8,128)(2,1)}, u32[]{:S(2)}, u32[]{:S(2)}) collective-permute-start(bf16[48,4096]{1,0:T(8,128)(2,1)} %get-tuple-element.273), channel_id=1, source_target_pairs={{0,24},{8,16},{16,8},{24,0},{1,25},{9,17},{17,9},{25,1},{2,26},{10... | collective-permute-start | bytes 1179656 | tf_op jit(solution)/shard_map/ppermute | solution.py:812
  850.5 71.0 %all-to-all-start.9 = ((bf16[4,128,1024]{2,1,0:T(8,128)(2,1)}), bf16[4,128,1024]{2,1,0:T(8,128)(2,1)}, u32[]{:S(2)}, u32[]{:S(2)}) async-start(bf16[4,128,1024]{2,1,0:T(8,128)(2,1)} %bitcast.248), calls=%async_computation.13 | async-start | bytes 2097152 | tf_op jit(solution)/shard_map/all_to_all | solution.py:783
  854.8 199.5 %reduce-scatter.14.cloned.1.call-start = ((), (), s32[]{:S(2)}) async-start(), calls=%async_computation.23 | async-start | bytes 10076160 | tf_op jit(solution)/shard_map/reduce_scatter | solution.py:1174
  858.0 57.8 %collective-permute-start.12 = (bf16[48,5632]{1,0:T(8,128)(2,1)}, bf16[48,5632]{1,0:T(8,128)(2,1)}, u32[]{:S(2)}, u32[]{:S(2)}) collective-permute-start(bf16[48,5632]{1,0:T(8,128)(2,1)} %get-tuple-element.266), channel_id=1, source_target_pairs={{0,8},{8,0},{16,24},{24,16},{1,9},{9,1},{17,25},{25,17},{2,10},{10... | collective-permute-start | bytes 1622024 | tf_op jit(solution)/shard_map/ppermute | solution.py:812
  865.0 56.5 %collective-permute-start.13 = (bf16[48,5632]{1,0:T(8,128)(2,1)}, bf16[48,5632]{1,0:T(8,128)(2,1)}, u32[]{:S(2)}, u32[]{:S(2)}) collective-permute-start(bf16[48,5632]{1,0:T(8,128)(2,1)} %get-tuple-element.265), channel_id=1, source_target_pairs={{0,16},{8,24},{16,0},{24,8},{1,17},{9,25},{17,1},{25,9},{2,18},{10... | collective-permute-start | bytes 1622024 | tf_op jit(solution)/shard_map/ppermute | solution.py:812
  865.0 56.5 %collective-permute-start.14 = (bf16[48,5632]{1,0:T(8,128)(2,1)}, bf16[48,5632]{1,0:T(8,128)(2,1)}, u32[]{:S(2)}, u32[]{:S(2)}) collective-permute-start(bf16[48,5632]{1,0:T(8,128)(2,1)} %get-tuple-element.264), channel_id=1, source_target_pairs={{0,24},{8,16},{16,8},{24,0},{1,25},{9,17},{17,9},{25,1},{2,26},{10... | collective-permute-start | bytes 1622024 | tf_op jit(solution)/shard_map/ppermute | solution.py:812
  892.7 44.4 %collective-permute-start.15 = (bf16[128,3072]{1,0:T(8,128)(2,1)}, bf16[128,3072]{1,0:T(8,128)(2,1)}, u32[]{:S(2)}, u32[]{:S(2)}) collective-permute-start(bf16[128,3072]{1,0:T(8,128)(2,1)} %reduce_sum.354), channel_id=1, source_target_pairs={{0,0},{1,8},{2,16},{3,24},{4,4},{5,12},{6,20},{7,28},{8,1},{9,9},{... | collective-permute-start | bytes 2359304 | tf_op jit(solution)/shard_map/ppermute | solution.py:1139
  995.8 32.9 %collective-permute-start.18 = (bf16[192,1152]{1,0:T(8,128)(2,1)S(1)}, bf16[192,1152]{1,0:T(8,128)(2,1)S(1)}, u32[]{:S(2)}, u32[]{:S(2)}) collective-permute-start(bf16[192,1152]{1,0:T(8,128)(2,1)S(1)} %get-tuple-element.270), channel_id=1, source_target_pairs={{0,16},{8,24},{16,0},{24,8},{1,17},{9,25},{17,1},{25,9},{2,18},{10... | collective-permute-start | bytes 1327112 | tf_op jit(solution)/shard_map/ppermute | solution.py:812
  995.8 32.9 %collective-permute-start.19 = (bf16[192,1152]{1,0:T(8,128)(2,1)S(1)}, bf16[192,1152]{1,0:T(8,128)(2,1)S(1)}, u32[]{:S(2)}, u32[]{:S(2)}) collective-permute-start(bf16[192,1152]{1,0:T(8,128)(2,1)S(1)} %get-tuple-element.269), channel_id=1, source_target_pairs={{0,24},{8,16},{16,8},{24,0},{1,25},{9,17},{17,9},{25,1},{2,26},{10... | collective-permute-start | bytes 1327112 | tf_op jit(solution)/shard_map/ppermute | solution.py:812
  (113 other events, 2078.2 us)
Sparse Core Ops, SparseCore 0:
  9.9 108.9 all-gather.11
  120.7 64.5 all-gather.5
  187.2 139.7 all-gather.7
  328.7 79.2 all-gather.9
  506.8 90.4 reduce-scatter.5
  600.2 79.3 reduce-scatter.7
  682.5 80.8 reduce-scatter.9
  766.5 37.3 reduce-scatter.11
  937.3 99.9 reduce-scatter.13

commit v10 on v9

--- a/solution.py
+++ b/solution.py
@@ -966,13 +966,8 @@
     own_text_weight = (
         text_weight.reshape(text_cols, 2, narrow, part).transpose(2, 0, 1, 3).reshape(narrow, text_cols, 2 * part)
     )
-    relative_text_weight = (
-        relative(own_text_weight, me, 0).transpose(1, 0, 2).reshape(text_cols, 2 * model_width)
-    )
     text_partial = jnp.stack([low_product(text_slice, own_text_weight[i]).astype(BF16) for i in range(narrow)])
-    text_partial, tokens_all, relative_text_weight = lax.optimization_barrier(
-        (text_partial, tokens_all, relative_text_weight)
-    )
+    text_partial, tokens_all = lax.optimization_barrier((text_partial, tokens_all))
     text_projected = widened(jnp.sum(exchange(text_partial, "fsdp").astype(F32), axis=0), 2)
     text_parts = fsdp_share(column_stats(text_projected, part, part_pad, 1), narrow, 1)
     text_means = text_parts[:, 0, :]
@@ -1144,15 +1139,6 @@
             for z in range(deep) for c in range(2) for f in range(narrow)
         ],
     )
-    last, grad_text_columns = lax.optimization_barrier((backs[-1][0], grad_text_columns))
-    backs[-1] = (last, *backs[-1][1:])
-    grad_text_slice = times_transposed(grad_text_columns, relative_text_weight).astype(BF16)
-    came_text = exchange(
-        grad_text_slice.reshape(image_count, narrow, caption_local, text_cols)
-        .transpose(1, 0, 2, 3)
-        .reshape(narrow, text_local, text_cols),
-        "fsdp",
-    )
     own_gate_grad = jnp.sum(gate_sums[:, 0, :].reshape(pairs * halves, head_dim), axis=1)[:heads_here]
     grad_head_gate = lax.dynamic_update_slice_in_dim(
         jnp.zeros((head_count,), F32), own_gate_grad, me * heads_here, 0
@@ -1161,9 +1147,7 @@
         list(zip(*backs)), projected, stats_all, cosine, sine, head_gains, part,
         lambda value: fsdp_share(value, narrow, 4),
     )
-    grad_projected_low, came_text, *up_pieces = lax.optimization_barrier(
-        (grad_projected_low, came_text, *up_pieces)
-    )
+    grad_projected_low, *up_pieces = lax.optimization_barrier((grad_projected_low, *up_pieces))
     grad_gate_up_weight = jnp.concatenate(
         [added(gate_pieces), added([piece[:, :up_width] for piece in up_pieces])], axis=1
     )
@@ -1188,6 +1172,23 @@
     later = [*grad_gate_attend, *grad_scale_feed, *grad_gate_feed, cond_rows_here]
     ready = lax.optimization_barrier(tuple(ready))
     qkv_grad = outer_sum(normed_all, grad_projected_low).astype(BF16).reshape(deep, 2, model_width // wide, 3 * part_pad)
+    own_grad, other_grad = by_core(qkv_grad[:, 0], qkv_grad[:, 1])
+    own_grad = (own_grad.astype(F32) + core_swap(other_grad).astype(F32)).astype(BF16)
+    own_pieces = z_pieces(own_grad, deep)
+    own_pieces[0], grad_text_columns, grad_text_weight = lax.optimization_barrier(
+        (own_pieces[0], grad_text_columns, grad_text_weight)
+    )
+    ordered = relative(grad_text_columns.reshape(text_total, narrow, 2 * part), me, 1)
+    grad_text_ordered = (
+        ordered.reshape(text_total, narrow, 2, part).transpose(0, 2, 1, 3).reshape(text_total, 2 * model_width)
+    )
+    grad_text_slice = times_transposed(grad_text_ordered, text_weight).astype(BF16)
+    came_text = exchange(
+        grad_text_slice.reshape(image_count, narrow, caption_local, text_cols)
+        .transpose(1, 0, 2, 3)
+        .reshape(narrow, text_local, text_cols),
+        "fsdp",
+    )
     place = (lax.axis_index("z") * 2 + lax.axis_index("core")) * narrow + me
     grad_text_weight = (
         relative(grad_text_weight.reshape(-1, narrow, 2 * part), place // wide, 1)
@@ -1196,10 +1197,6 @@
         .reshape(-1, 2 * model_width)
         .astype(F32)
     )
-    own_grad, other_grad = by_core(qkv_grad[:, 0], qkv_grad[:, 1])
-    own_grad = (own_grad.astype(F32) + core_swap(other_grad).astype(F32)).astype(BF16)
-    own_pieces = z_pieces(own_grad, deep)
-    came_text, *own_pieces = lax.optimization_barrier((came_text, *own_pieces))
     grad_text_normed = (
         came_text
         .transpose(1, 0, 2)
@@ -1214,16 +1211,17 @@
         .reshape(image_count, caption_local, caption_width)
     )
 
+    grad_text, grad_text_gain, grad_text_weight, *own_pieces = lax.optimization_barrier(
+        (grad_text, grad_text_gain, grad_text_weight, *own_pieces)
+    )
     own_grad = added(own_pieces)
+    own_exchanged = exchange(narrowed(own_grad.astype(BF16), 3).reshape(narrow, -1, 3 * part), "fsdp")
+    grad_normed, own_exchanged = lax.optimization_barrier((grad_normed, own_exchanged))
     grad_qkv_weight = (
-        exchange(narrowed(own_grad.astype(BF16), 3).reshape(narrow, -1, 3 * part), "fsdp")
-        .reshape(narrow, -1, 3, part)
+        own_exchanged.reshape(narrow, -1, 3, part)
         .transpose(1, 2, 0, 3)
         .reshape(-1, 3 * model_width)
         .astype(F32)
-    )
-    grad_normed, grad_qkv_weight, grad_text, grad_text_gain = lax.optimization_barrier(
-        (grad_normed, grad_qkv_weight, grad_text, grad_text_gain)
     )
     grad_normed = grad_normed.astype(F32)
 

time: 1130 us -> 1110 us (0.982)
    ppermute x9, waiting for transfers between devices: 34.2 us -> 17 us  [z_pieces(): lax.ppermute(lax.dynamic_index_in_dim(blocks, me ^ step, 0, keepdims=Fals...]
    all_to_all x11, starting transfers between devices: 47.5 us -> 62.6 us  [exchange(): return lax.all_to_all(blocks, axis, 0, 0, tiled=True)]
    ppermute x9, starting transfers between devices: 32.4 us -> 18.2 us  [z_pieces(): lax.ppermute(lax.dynamic_index_in_dim(blocks, me ^ step, 0, keepdims=Fals...]
    all_to_all x11, waiting for transfers between devices: 28.3 us -> 40.8 us  [exchange(): return lax.all_to_all(blocks, axis, 0, 0, tiled=True)]
    unnamed x220 -> x234, local copies, waits for them, and re-layouts: 31.9 us -> 34.8 us
  transfers between devices with their start and end apart: 40 -> 40, of which waited for: 9 -> 12; matrix products, arithmetic and copies ran while one was open for 37% -> 36% of each run, Pallas kernels for 37% -> 38%
where the time goes in v10:
time: 1110 us; the launch traced here: 1090 us
  Pallas kernels  445 us (40%)
  matrix products  244 us (22%)
  other arithmetic  112 us (10%)
  local copies, waits for them, and re-layouts  108 us (10%)
  starting transfers between devices  93.1 us (8%)
  waiting for transfers between devices  74.4 us (7%)
  between operations  18.3 us (2%)
    pallas_call x3, Pallas kernels, self_back(): pl.pallas_call(functools.partial(self_back_kernel, head_dim, FIRST_PATCHE...  137 us
    dot_general x11, matrix products, outer_sum(): lax.dot_general(left, right, (((0,), (0,)), ((), ())), preferred_element_...  93.7 us
    pallas_call x3, Pallas kernels, attend(): pl.pallas_call(functools.partial(attend_kernel, head_dim, FIRST_PATCHES,...  91.8 us
    dot_general x11, matrix products, low_product(): return jnp.dot(left, right, preferred_element_type=F32)  77.2 us
    dot_general x5, matrix products, times_transposed(): lax.dot_general(left, right, (((1,), (1,)), ((), ())), preferred_element_...  70.7 us
    pallas_call x5, Pallas kernels, fsdp_share(): pl.pallas_call(functools.partial(fsdp_share_kernel, narrow), in_specs=[pl...  63.6 us
    all_to_all x11, starting transfers between devices, exchange(): return lax.all_to_all(blocks, axis, 0, 0, tiled=True)  62.6 us
    all_to_all x11, waiting for transfers between devices, exchange(): return lax.all_to_all(blocks, axis, 0, 0, tiled=True)  40.8 us
  transfers between devices with their start and end apart: 40, of which 12 were waited for; matrix products, arithmetic and copies ran while one was open for 36% of the time, Pallas kernels for 38%

profile of v10, /device:TPU:0, one launch (start us, length us, event | category | flops | bytes accessed | tf_op | source)
XLA Modules:
  0.0 1095.0 jit_solution(7384240288037852110)
XLA Ops:
  40.4 27.4 %shard_map.263 = f32[4,96,128]{2,1,0:T(8,128)} custom-call(f32[96,128]{1,0:T(8,128)} %reshape.634.x_ref), custom_call_target="tpu_custom_call" | custom-call | bytes 393216 | tf_op jit(solution)/shard_map/pallas_call | solution.py:648
  75.8 10.5 negate_select_fusion
  150.4 13.6 %fusion.164.projected_ref.refs_6_.refs_9_ = f32[2624,1152]{1,0:T(8,128)} fusion(bf16[2624,1536]{1,0:T(8,128)(2,1)S(1)} %fusion.3, bf16[1536,1152]{1,0:T(8,128)(2,1)S(1)} %bitcast.251), kind=kOutput, calls=%fused_computation.378 | convolution fusion | flops 9286189056 | bytes 23691264 | tf_op jit(solution)/shard_map/dot_general | solution.py:28
  164.1 9.4 shard_map.264.x_ref
  173.4 16.1 %shard_map.265.stats_ref.refs_7_.refs_10_ = f32[4,8,2624]{2,1,0:T(8,128)} custom-call(f32[8,2624]{1,0:T(8,128)} %shard_map.264.x_ref), custom_call_target="tpu_custom_call" | custom-call | bytes 671744 | tf_op jit(solution)/shard_map/pallas_call | solution.py:648
  189.5 15.5 %shard_map.266.q_ref.k_ref.v_ref = bf16[2624,1152]{1,0:T(8,128)(2,1)} custom-call(f32[2624,1152]{1,0:T(8,128)} %fusion.164.projected_ref.refs_6_.refs_9_, f32[4,8,2624]{2,1,0:T(8,128)} %shard_map.265.stats_ref.refs_7_.refs_10_, f32[2624,128]{1,0:T(8,128)} %get-tuple-element.282.cos_ref.refs_8_.refs_12_, ...), custom_call_target="tpu_custom_call" | custom-call | flops 120913920 | bytes 18137088 | tf_op jit(solution)/shard_map/pallas_call | solution.py:183
  221.8 31.0 %shard_map.271 = (bf16[2624,128]{1,0:T(8,128)(2,1)}, f32[2624,128]{1,0:T(8,128)}, f32[2624,128]{1,0:T(8,128)}, f32[8,2624]{1,0:T(8,128)}) custom-call(f32[3,1,2]{2,1,0:T(1,128)} %reshape.692.gate_ref, bf16[2624,1152]{1,0:T(8,128)(2,1)} %shard_map.266.q_ref.k_ref.v_ref, bf16[2624,1152]{1,0:T(8,128)(2,1)} %shard_map.266.q_ref.k_ref.v_ref, ...), custom_call_target="tpu_custom_call" | custom-call | flops 4213178368 | bytes 6717440 | tf_op jit(solution)/shard_map/pallas_call | solution.py:379
  256.4 30.4 %shard_map.270 = (bf16[2624,128]{1,0:T(8,128)(2,1)}, f32[2624,128]{1,0:T(8,128)}, f32[2624,128]{1,0:T(8,128)}, f32[8,2624]{1,0:T(8,128)}) custom-call(f32[3,1,2]{2,1,0:T(1,128)} %reshape.692.gate_ref, bf16[2624,1152]{1,0:T(8,128)(2,1)} %shard_map.266.q_ref.k_ref.v_ref, bf16[2624,1152]{1,0:T(8,128)(2,1)} %shard_map.266.q_ref.k_ref.v_ref, ...), custom_call_target="tpu_custom_call" | custom-call | flops 4213178368 | bytes 6717440 | tf_op jit(solution)/shard_map/pallas_call | solution.py:379
  291.2 30.4 %shard_map.269 = (bf16[2624,128]{1,0:T(8,128)(2,1)}, f32[2624,128]{1,0:T(8,128)}, f32[2624,128]{1,0:T(8,128)}, f32[8,2624]{1,0:T(8,128)}) custom-call(f32[3,1,2]{2,1,0:T(1,128)} %reshape.692.gate_ref, bf16[2624,1152]{1,0:T(8,128)(2,1)} %shard_map.266.q_ref.k_ref.v_ref, bf16[2624,1152]{1,0:T(8,128)(2,1)} %shard_map.266.q_ref.k_ref.v_ref, ...), custom_call_target="tpu_custom_call" | custom-call | flops 4213178368 | bytes 6717440 | tf_op jit(solution)/shard_map/pallas_call | solution.py:379
  325.9 16.1 %all-to-all-done.3 = bf16[4,656,128]{2,1,0:T(8,128)(2,1)} async-done(((bf16[4,656,128]{2,1,0:T(8,128)(2,1)}), bf16[4,656,128]{2,1,0:T(8,128)(2,1)}, u32[]{:S(2)}, u32[]{:S(2)}) %all-to-all-start.3) | async-done | bytes 671776 | tf_op jit(solution)/shard_map/all_to_all | solution.py:783
  366.7 26.2 %fusion.165.gate_ref.up_ref = f32[656,8192]{1,0:T(8,128)} fusion(bf16[656,1536]{1,0:T(8,128)(2,1)} %copy-done.34, bf16[1536,8192]{1,0:T(8,128)(2,1)} %all-gather.8.cloned.1.call-done), kind=kOutput, calls=%fused_computation.379 | convolution fusion | flops 16508780544 | bytes 48676864 | tf_op jit(solution)/shard_map/dot_general | solution.py:28
  392.9 22.9 %shard_map.272 = (bf16[656,4096]{1,0:T(8,128)(2,1)}, bf16[656,4096]{1,0:T(8,128)(2,1)}) custom-call(s32[1]{0:T(128)} %bitcast.29.core_ref, f32[656,8192]{1,0:T(8,128)} %fusion.165.gate_ref.up_ref, f32[656,8192]{1,0:T(8,128)} %fusion.165.gate_ref.up_ref), custom_call_target="tpu_custom_call" | custom-call | flops 16121856 | bytes 32243712 | tf_op jit(solution)/shard_map/pallas_call | solution.py:602
  419.1 13.1 %multiply_reduce_fusion.14 = (f32[656]{0:T(1024)S(1)}, f32[656,1536]{1,0:T(8,128)S(1)}) fusion(bf16[656,4096]{1,0:T(8,128)(2,1)} %get-tuple-element.113, bf16[4096,1536]{1,0:T(8,128)(2,1)} %all-gather.10.cloned.1.call-done), kind=kOutput, calls=%fused_computation.72 | convolution fusion | flops 8256404992 | bytes 21989952 | tf_op jit(solution)/shard_map/dot_general | solution.py:28
  447.7 19.5 %fusion.6 = (bf16[656,4096]{1,0:T(8,128)(2,1)}, bf16[656,4096]{1,0:T(8,128)(2,1)S(1)}) fusion(f32[656,8192]{1,0:T(8,128)} %fusion.165.gate_ref.up_ref, bf16[656,1536]{1,0:T(8,128)(2,1)} %copy-done.30, bf16[4096,1536]{1,0:T(8,128)(2,1)} %all-gather.10.cloned.1.call-done), kind=kOutput, calls=%fused_computation.13 | convolution fusion | flops 8289320960 | bytes 46841856 | tf_op jit(solution)/shard_map/dot_general | solution.py:32
  467.2 11.5 %convolution_convert_fusion.4 = bf16[768,4096]{1,0:T(8,128)(2,1)} fusion(bf16[656,4096]{1,0:T(8,128)(2,1)} %get-tuple-element.247, bf16[656,1536]{1,0:T(8,128)(2,1)S(1)} %copy-done.29), kind=kOutput, calls=%fused_computation.26 | convolution fusion | flops 4130340864 | bytes 12673024 | tf_op jit(solution)/shard_map/dot_general | solution.py:36
  486.3 9.4 add_convert_fusion
  496.5 28.7 %multiply_reduce_fusion.9 = (f32[1536]{0:T(1024)}, f32[656]{0:T(1024)S(1)}, f32[1536]{0:T(1024)}, f32[1536]{0:T(1024)}, f32[656,1536]{1,0:T(8,128)}) fusion(f32[656,1536]{1,0:T(8,128)} %copy-done.2, f32[656]{0:T(1024)S(1)} %copy-done.82, f32[1536]{0:T(1024)S(1)} %copy-done.69, f32[656]{0:T(1024)S(1)} %get-tuple-element.301, f32[1536]{0:T(1024)S(1)} %copy-done.71, ...), kind=kOutput, calls=%fused_computation.64 | convolution fusion | flops 16547399680 | bytes 44022016 | tf_op jit(solution)/shard_map/dot_general | solution.py:32
  557.8 10.8 add_convert_fusion.2
  568.6 10.8 add_convert_fusion.1
  591.9 13.5 %shard_map.275 = (bf16[2624,128]{1,0:T(8,128)(2,1)}, bf16[512,128]{1,0:T(8,128)(2,1)}, bf16[512,128]{1,0:T(8,128)(2,1)}, f32[8,128]{1,0:T(8,128)}) custom-call(f32[3,1,2]{2,1,0:T(1,128)} %reshape.692.gate_ref, bf16[2624,1152]{1,0:T(8,128)(2,1)} %shard_map.266.q_ref.k_ref.v_ref, bf16[512,768]{1,0:T(8,128)(2,1)} %pad_maximum_fusion.5.tk_ref.tv_ref, ...), custom_call_target="tpu_custom_call" | custom-call | flops 1719664640 | bytes 4030464 | tf_op jit(solution)/shard_map/pallas_call | solution.py:495
  605.4 13.3 %shard_map.274 = (bf16[2624,128]{1,0:T(8,128)(2,1)}, bf16[512,128]{1,0:T(8,128)(2,1)}, bf16[512,128]{1,0:T(8,128)(2,1)}, f32[8,128]{1,0:T(8,128)}) custom-call(f32[3,1,2]{2,1,0:T(1,128)} %reshape.692.gate_ref, bf16[2624,1152]{1,0:T(8,128)(2,1)} %shard_map.266.q_ref.k_ref.v_ref, bf16[512,768]{1,0:T(8,128)(2,1)} %pad_maximum_fusion.5.tk_ref.tv_ref, ...), custom_call_target="tpu_custom_call" | custom-call | flops 1719664640 | bytes 4030464 | tf_op jit(solution)/shard_map/pallas_call | solution.py:495
  618.7 13.5 %shard_map.273 = (bf16[2624,128]{1,0:T(8,128)(2,1)}, bf16[512,128]{1,0:T(8,128)(2,1)}, bf16[512,128]{1,0:T(8,128)(2,1)}, f32[8,128]{1,0:T(8,128)}) custom-call(f32[3,1,2]{2,1,0:T(1,128)} %reshape.692.gate_ref, bf16[2624,1152]{1,0:T(8,128)(2,1)} %shard_map.266.q_ref.k_ref.v_ref, bf16[512,768]{1,0:T(8,128)(2,1)} %pad_maximum_fusion.5.tk_ref.tv_ref, ...), custom_call_target="tpu_custom_call" | custom-call | flops 1719664640 | bytes 4030464 | tf_op jit(solution)/shard_map/pallas_call | solution.py:495
  653.7 45.8 %shard_map.277 = (bf16[2624,128]{1,0:T(8,128)(2,1)}, bf16[2624,128]{1,0:T(8,128)(2,1)}, bf16[2624,128]{1,0:T(8,128)(2,1)}) custom-call(bf16[2624,1152]{1,0:T(8,128)(2,1)} %shard_map.266.q_ref.k_ref.v_ref, bf16[2624,1152]{1,0:T(8,128)(2,1)} %shard_map.266.q_ref.k_ref.v_ref, bf16[2624,1152]{1,0:T(8,128)(2,1)} %shard_map.266.q_ref.k_ref.v_ref, ...), custom_call_target="tpu_custom_call" | custom-call | flops 8813281280 | bytes 10076160 | tf_op jit(solution)/shard_map/pallas_call | solution.py:562
  732.8 45.6 %shard_map.278 = (bf16[2624,128]{1,0:T(8,128)(2,1)}, bf16[2624,128]{1,0:T(8,128)(2,1)}, bf16[2624,128]{1,0:T(8,128)(2,1)}) custom-call(bf16[2624,1152]{1,0:T(8,128)(2,1)} %shard_map.266.q_ref.k_ref.v_ref, bf16[2624,1152]{1,0:T(8,128)(2,1)} %shard_map.266.q_ref.k_ref.v_ref, bf16[2624,1152]{1,0:T(8,128)(2,1)} %shard_map.266.q_ref.k_ref.v_ref, ...), custom_call_target="tpu_custom_call" | custom-call | flops 8813281280 | bytes 10076160 | tf_op jit(solution)/shard_map/pallas_call | solution.py:562
  785.3 45.6 %shard_map.279 = (bf16[2624,128]{1,0:T(8,128)(2,1)}, bf16[2624,128]{1,0:T(8,128)(2,1)}, bf16[2624,128]{1,0:T(8,128)(2,1)}) custom-call(bf16[2624,1152]{1,0:T(8,128)(2,1)} %shard_map.266.q_ref.k_ref.v_ref, bf16[2624,1152]{1,0:T(8,128)(2,1)} %shard_map.266.q_ref.k_ref.v_ref, bf16[2624,1152]{1,0:T(8,128)(2,1)} %shard_map.266.q_ref.k_ref.v_ref, ...), custom_call_target="tpu_custom_call" | custom-call | flops 8813281280 | bytes 10076160 | tf_op jit(solution)/shard_map/pallas_call | solution.py:562
  843.7 15.7 %shard_map.280 = (f32[8,2624]{1,0:T(8,128)}, f32[8,384]{1,0:T(8,128)}) custom-call(bf16[2624,128]{1,0:T(8,128)(2,1)} %get-tuple-element.136.refs_0_, bf16[2624,128]{1,0:T(8,128)(2,1)} %get-tuple-element.143.refs_1_, bf16[2624,128]{1,0:T(8,128)(2,1)} %get-tuple-element.152.refs_2_, bf16[2624,128]{1,0:T(8,128)(2,1)} %get-tuple-element.153.refs_3_, ...), custom_call_target="tpu_custom_call" | custom-call | flops 12091392 | bytes 188928 | tf_op jit(solution)/shard_map/pallas_call | solution.py:269
  875.6 15.5 %shard_map.282 = bf16[2624,1152]{1,0:T(8,128)(2,1)} custom-call(bf16[2624,128]{1,0:T(8,128)(2,1)} %get-tuple-element.136.refs_0_, bf16[2624,128]{1,0:T(8,128)(2,1)} %get-tuple-element.143.refs_1_, bf16[2624,128]{1,0:T(8,128)(2,1)} %get-tuple-element.152.refs_2_, bf16[2624,128]{1,0:T(8,128)(2,1)} %get-tuple-element.153.refs_3_, ...), custom_call_target="tpu_custom_call" | custom-call | flops 12091392 | bytes 188928 | tf_op jit(solution)/shard_map/pallas_call | solution.py:282
  897.9 15.5 %convolution_convert_fusion = bf16[2624,1536]{1,0:T(8,128)(2,1)} fusion(bf16[2624,1152]{1,0:T(8,128)(2,1)} %shard_map.282, bf16[1536,1152]{1,0:T(8,128)(2,1)S(1)} %bitcast.252), kind=kOutput, calls=%fused_computation.9 | convolution fusion | flops 9290219520 | bytes 17645568 | tf_op jit(solution)/shard_map/dot_general | solution.py:32
  918.1 15.4 %convolution_convert_fusion.2 = bf16[1536,1152]{1,0:T(8,128)(2,1)S(1)} fusion(bf16[2624,1536]{1,0:T(8,128)(2,1)} %copy-done.18, bf16[2624,1152]{1,0:T(8,128)(2,1)} %shard_map.282), kind=kOutput, calls=%fused_computation.24 | convolution fusion | flops 9287958528 | bytes 17645568 | tf_op jit(solution)/shard_map/dot_general | solution.py:36
  952.3 19.1 %all-to-all-start.9 = ((bf16[4,128,1024]{2,1,0:T(8,128)(2,1)}), bf16[4,128,1024]{2,1,0:T(8,128)(2,1)S(1)}, u32[]{:S(2)}, u32[]{:S(2)}) async-start(bf16[4,128,1024]{2,1,0:T(8,128)(2,1)} %bitcast.63), calls=%async_computation.14 | async-start | bytes 2097152 | tf_op jit(solution)/shard_map/all_to_all | solution.py:783
  1003.4 10.2 collective-permute-done.18
  1031.7 31.0 %shard_map.283 = (f32[7,1536]{1,0:T(8,128)}, f32[2,1536]{1,0:T(2,128)}, f32[1,128]{1,0:T(1,128)}, f32[32,128]{1,0:T(8,128)}, f32[8,2,6144]{2,1,0:T(2,128)}, /*index=5*/f32[8,2,1024]{2,1,0:T(2,128)}) custom-call(f32[12,128]{1,0:T(8,128)} %bitcast.284, f32[12,128]{1,0:T(8,128)} %bitcast.283, f32[12,128]{1,0:T(8,128)} %bitcast.292, f32[12,128]{1,0:T(8,128)} %bitcast.278, ...), custom_call_target="tpu_custom_call" | custom-call | tf_op jit(solution)/shard_map/pallas_call | solution.py:764
  (476 shorter events, 423.7 us)
Async XLA Ops:
  7.2 122.6 %all-gather.12.cloned.1.call-start = ((), (), s32[]{:S(2)}) async-start(), calls=%async_computation.24 | async-start | bytes 10076160 | tf_op jit(solution)/shard_map/all_gather | solution.py:925
  7.9 337.0 %all-gather.6.cloned.1.call-start = ((), (), s32[]{:S(2)}) async-start(), calls=%async_computation.16 | async-start | bytes 5308416 | tf_op jit(solution)/shard_map/all_gather | solution.py:853
  10.2 356.5 %all-gather.8.cloned.1.call-start = ((), (), s32[]{:S(2)}) async-start(), calls=%async_computation.17 | async-start | bytes 28311552 | tf_op jit(solution)/shard_map/all_gather | solution.py:853
  25.0 61.3 %all-to-all-start.1 = ((bf16[4,192,1152]{2,1,0:T(8,128)(2,1)}), bf16[4,192,1152]{2,1,0:T(8,128)(2,1)}, u32[]{:S(2)}, u32[]{:S(2)}) async-start(bf16[4,192,1152]{2,1,0:T(8,128)(2,1)} %reshape.641), calls=%async_computation.1 | async-start | bytes 3538944 | tf_op jit(solution)/shard_map/all_to_all | solution.py:783
  30.3 388.8 %all-gather.10.cloned.1.call-start = ((), (), s32[]{:S(2)}) async-start(), calls=%async_computation.18 | async-start | bytes 14155776 | tf_op jit(solution)/shard_map/all_gather | solution.py:853
  129.8 75.3 %all-to-all-start.2 = ((bf16[4,512,768]{2,1,0:T(8,128)(2,1)}), bf16[4,512,768]{2,1,0:T(8,128)(2,1)}, u32[]{:S(2)}, u32[]{:S(2)}) async-start(bf16[4,512,768]{2,1,0:T(8,128)(2,1)} %pad_maximum_fusion.1), calls=%async_computation.2 | async-start | bytes 6291456 | tf_op jit(solution)/shard_map/all_to_all | solution.py:783
  252.8 34.0 %all-to-all-start.5 = ((bf16[4,656,128]{2,1,0:T(8,128)(2,1)}), bf16[4,656,128]{2,1,0:T(8,128)(2,1)S(1)}, u32[]{:S(2)}, u32[]{:S(2)}) async-start(bf16[4,656,128]{2,1,0:T(8,128)(2,1)} %bitcast.275), calls=%async_computation.5 | async-start | bytes 1343488 | tf_op jit(solution)/shard_map/all_to_all | solution.py:783
  286.8 34.8 %all-to-all-start.4 = ((bf16[4,656,128]{2,1,0:T(8,128)(2,1)}), bf16[4,656,128]{2,1,0:T(8,128)(2,1)S(1)}, u32[]{:S(2)}, u32[]{:S(2)}) async-start(bf16[4,656,128]{2,1,0:T(8,128)(2,1)} %bitcast.274), calls=%async_computation.4 | async-start | bytes 1343488 | tf_op jit(solution)/shard_map/all_to_all | solution.py:783
  325.8 260.7 %reduce-scatter.6.cloned.1.call-start = ((), (), s32[]{:S(2)}) async-start(), calls=%async_computation.19 | async-start | bytes 7864320 | tf_op jit(solution)/shard_map/reduce_scatter | solution.py:806
  447.4 38.9 %collective-permute-start.4 = (bf16[2048,1536]{1,0:T(8,128)(2,1)}, bf16[2048,1536]{1,0:T(8,128)(2,1)}, u32[]{:S(2)}, u32[]{:S(2)}) collective-permute-start(bf16[2048,1536]{1,0:T(8,128)(2,1)} %convolution_convert_fusion.1), channel_id=1, source_target_pairs={{0,4},{4,0},{1,5},{5,1},{2,6},{6,2},{3,7},{7,3},{8,12},{12,8},{9,1... | collective-permute-start | bytes 18874376 | tf_op jit(solution)/shard_map/ppermute | solution.py:787
  478.7 79.1 %collective-permute-start.1 = (bf16[768,4096]{1,0:T(8,128)(2,1)}, bf16[768,4096]{1,0:T(8,128)(2,1)}, u32[]{:S(2)}, u32[]{:S(2)}) collective-permute-start(bf16[768,4096]{1,0:T(8,128)(2,1)} %convolution_convert_fusion.4), channel_id=1, source_target_pairs={{0,4},{4,0},{1,5},{5,1},{2,6},{6,2},{3,7},{7,3},{8,12},{12,8},{9,1... | collective-permute-start | bytes 18874376 | tf_op jit(solution)/shard_map/ppermute | solution.py:787
  486.0 82.6 %collective-permute-start.2 = (bf16[768,4096]{1,0:T(8,128)(2,1)}, bf16[768,4096]{1,0:T(8,128)(2,1)}, u32[]{:S(2)}, u32[]{:S(2)}) collective-permute-start(bf16[768,4096]{1,0:T(8,128)(2,1)} %convolution_convert_fusion.3), channel_id=1, source_target_pairs={{0,4},{4,0},{1,5},{5,1},{2,6},{6,2},{3,7},{7,3},{8,12},{12,8},{9,1... | collective-permute-start | bytes 18874376 | tf_op jit(solution)/shard_map/ppermute | solution.py:787
  548.0 37.9 %all-to-all-start.6 = ((bf16[4,656,384]{2,1,0:T(8,128)(2,1)}), bf16[4,656,384]{2,1,0:T(8,128)(2,1)S(1)}, u32[]{:S(2)}, u32[]{:S(2)}) async-start(bf16[4,656,384]{2,1,0:T(8,128)(2,1)} %bitcast.245), calls=%async_computation.6 | async-start | bytes 4030464 | tf_op jit(solution)/shard_map/all_to_all | solution.py:783
  551.6 226.8 %reduce-scatter.8.cloned.1.call-start = ((), (), s32[]{:S(2)}) async-start(), calls=%async_computation.20 | async-start | bytes 7864320 | tf_op jit(solution)/shard_map/reduce_scatter | solution.py:806
  586.5 191.9 %reduce-scatter.10.cloned.1.call-start = ((), (), s32[]{:S(2)}) async-start(), calls=%async_computation.21 | async-start | bytes 7864320 | tf_op jit(solution)/shard_map/reduce_scatter | solution.py:806
  587.3 116.0 %all-to-all-start.7 = ((bf16[4,128,1536]{2,1,0:T(8,128)(2,1)}), bf16[4,128,1536]{2,1,0:T(8,128)(2,1)S(1)}, u32[]{:S(2)}, u32[]{:S(2)}) async-start(bf16[4,128,1536]{2,1,0:T(8,128)(2,1)} %bitcast.269), calls=%async_computation.8 | async-start | bytes 3145728 | tf_op jit(solution)/shard_map/all_to_all | solution.py:783
  591.9 239.1 %reduce-scatter.12.cloned.1.call-start = ((), (), s32[]{:S(2)}) async-start(), calls=%async_computation.22 | async-start | bytes 2949120 | tf_op jit(solution)/shard_map/reduce_scatter | solution.py:806
  645.4 54.2 %collective-permute-start.5 = (bf16[512,768]{1,0:T(8,128)(2,1)}, bf16[512,768]{1,0:T(8,128)(2,1)}, u32[]{:S(2)}, u32[]{:S(2)}) collective-permute-start(bf16[512,768]{1,0:T(8,128)(2,1)} %pad_maximum_fusion.6), channel_id=1, source_target_pairs={{0,1},{1,0},{2,3},{3,2},{4,5},{5,4},{6,7},{7,6},{8,9},{9,8},{10,11... | collective-permute-start | bytes 2359304 | tf_op jit(solution)/shard_map/ppermute | solution.py:825
  646.8 52.7 %collective-permute-start.6 = (bf16[512,768]{1,0:T(8,128)(2,1)}, bf16[512,768]{1,0:T(8,128)(2,1)}, u32[]{:S(2)}, u32[]{:S(2)}) collective-permute-start(bf16[512,768]{1,0:T(8,128)(2,1)} %pad_maximum_fusion.6), channel_id=1, source_target_pairs={{0,2},{1,3},{2,0},{3,1},{4,6},{5,7},{6,4},{7,5},{8,10},{9,11},{10,... | collective-permute-start | bytes 2359304 | tf_op jit(solution)/shard_map/ppermute | solution.py:825
  647.4 55.9 %collective-permute-start.7 = (bf16[512,768]{1,0:T(8,128)(2,1)}, bf16[512,768]{1,0:T(8,128)(2,1)}, u32[]{:S(2)}, u32[]{:S(2)}) collective-permute-start(bf16[512,768]{1,0:T(8,128)(2,1)} %pad_maximum_fusion.6), channel_id=1, source_target_pairs={{0,3},{1,2},{2,1},{3,0},{4,7},{5,6},{6,5},{7,4},{8,11},{9,10},{10,... | collective-permute-start | bytes 2359304 | tf_op jit(solution)/shard_map/ppermute | solution.py:825
  728.1 102.8 %all-to-all-start.8 = ((bf16[4,128,3072]{2,1,0:T(8,128)(2,1)}), bf16[4,128,3072]{2,1,0:T(8,128)(2,1)S(1)}, u32[]{:S(2)}, u32[]{:S(2)}) async-start(bf16[4,128,3072]{2,1,0:T(8,128)(2,1)} %bitcast.253), calls=%async_computation.11 | async-start | bytes 6291456 | tf_op jit(solution)/shard_map/all_to_all | solution.py:783
  732.8 293.6 %reduce-scatter.14.cloned.1.call-start = ((), (), s32[]{:S(2)}) async-start(), calls=%async_computation.23 | async-start | bytes 10076160 | tf_op jit(solution)/shard_map/reduce_scatter | solution.py:1158
  780.9 50.0 %collective-permute-start.9 = (bf16[48,4096]{1,0:T(8,128)(2,1)}, bf16[48,4096]{1,0:T(8,128)(2,1)S(1)}, u32[]{:S(2)}, u32[]{:S(2)}) collective-permute-start(bf16[48,4096]{1,0:T(8,128)(2,1)} %get-tuple-element.273), channel_id=1, source_target_pairs={{0,8},{8,0},{16,24},{24,16},{1,9},{9,1},{17,25},{25,17},{2,10},{10... | collective-permute-start | bytes 1179656 | tf_op jit(solution)/shard_map/ppermute | solution.py:812
  783.0 48.0 %collective-permute-start.10 = (bf16[48,4096]{1,0:T(8,128)(2,1)}, bf16[48,4096]{1,0:T(8,128)(2,1)}, u32[]{:S(2)}, u32[]{:S(2)}) collective-permute-start(bf16[48,4096]{1,0:T(8,128)(2,1)} %get-tuple-element.272), channel_id=1, source_target_pairs={{0,16},{8,24},{16,0},{24,8},{1,17},{9,25},{17,1},{25,9},{2,18},{10... | collective-permute-start | bytes 1179656 | tf_op jit(solution)/shard_map/ppermute | solution.py:812
  785.3 45.7 %collective-permute-start.11 = (bf16[48,4096]{1,0:T(8,128)(2,1)}, bf16[48,4096]{1,0:T(8,128)(2,1)}, u32[]{:S(2)}, u32[]{:S(2)}) collective-permute-start(bf16[48,4096]{1,0:T(8,128)(2,1)} %get-tuple-element.271), channel_id=1, source_target_pairs={{0,24},{8,16},{16,8},{24,0},{1,25},{9,17},{17,9},{25,1},{2,26},{10... | collective-permute-start | bytes 1179656 | tf_op jit(solution)/shard_map/ppermute | solution.py:812
  834.3 56.8 %collective-permute-start.12 = (bf16[48,5632]{1,0:T(8,128)(2,1)}, bf16[48,5632]{1,0:T(8,128)(2,1)}, u32[]{:S(2)}, u32[]{:S(2)}) collective-permute-start(bf16[48,5632]{1,0:T(8,128)(2,1)} %get-tuple-element.264), channel_id=1, source_target_pairs={{0,8},{8,0},{16,24},{24,16},{1,9},{9,1},{17,25},{25,17},{2,10},{10... | collective-permute-start | bytes 1622024 | tf_op jit(solution)/shard_map/ppermute | solution.py:812
  841.4 56.5 %collective-permute-start.13 = (bf16[48,5632]{1,0:T(8,128)(2,1)}, bf16[48,5632]{1,0:T(8,128)(2,1)}, u32[]{:S(2)}, u32[]{:S(2)}) collective-permute-start(bf16[48,5632]{1,0:T(8,128)(2,1)} %get-tuple-element.263), channel_id=1, source_target_pairs={{0,16},{8,24},{16,0},{24,8},{1,17},{9,25},{17,1},{25,9},{2,18},{10... | collective-permute-start | bytes 1622024 | tf_op jit(solution)/shard_map/ppermute | solution.py:812
  841.4 56.5 %collective-permute-start.14 = (bf16[48,5632]{1,0:T(8,128)(2,1)}, bf16[48,5632]{1,0:T(8,128)(2,1)}, u32[]{:S(2)}, u32[]{:S(2)}) collective-permute-start(bf16[48,5632]{1,0:T(8,128)(2,1)} %get-tuple-element.262), channel_id=1, source_target_pairs={{0,24},{8,16},{16,8},{24,0},{1,25},{9,17},{17,9},{25,1},{2,26},{10... | collective-permute-start | bytes 1622024 | tf_op jit(solution)/shard_map/ppermute | solution.py:812
  868.2 45.3 %collective-permute-start.15 = (bf16[128,3072]{1,0:T(8,128)(2,1)}, bf16[128,3072]{1,0:T(8,128)(2,1)}, u32[]{:S(2)}, u32[]{:S(2)}) collective-permute-start(bf16[128,3072]{1,0:T(8,128)(2,1)} %reduce_sum.354), channel_id=1, source_target_pairs={{0,0},{1,8},{2,16},{3,24},{4,4},{5,12},{6,20},{7,28},{8,1},{9,9},{... | collective-permute-start | bytes 2359304 | tf_op jit(solution)/shard_map/ppermute | solution.py:1134
  952.3 38.4 %all-to-all-start.9 = ((bf16[4,128,1024]{2,1,0:T(8,128)(2,1)}), bf16[4,128,1024]{2,1,0:T(8,128)(2,1)S(1)}, u32[]{:S(2)}, u32[]{:S(2)}) async-start(bf16[4,128,1024]{2,1,0:T(8,128)(2,1)} %bitcast.63), calls=%async_computation.14 | async-start | bytes 2097152 | tf_op jit(solution)/shard_map/all_to_all | solution.py:783
  980.3 33.2 %collective-permute-start.18 = (bf16[192,1152]{1,0:T(8,128)(2,1)}, bf16[192,1152]{1,0:T(8,128)(2,1)}, u32[]{:S(2)}, u32[]{:S(2)}) collective-permute-start(bf16[192,1152]{1,0:T(8,128)(2,1)} %get-tuple-element.268), channel_id=1, source_target_pairs={{0,16},{8,24},{16,0},{24,8},{1,17},{9,25},{17,1},{25,9},{2,18},{10... | collective-permute-start | bytes 1327112 | tf_op jit(solution)/shard_map/ppermute | solution.py:812
  981.7 31.9 %collective-permute-start.19 = (bf16[192,1152]{1,0:T(8,128)(2,1)}, bf16[192,1152]{1,0:T(8,128)(2,1)}, u32[]{:S(2)}, u32[]{:S(2)}) collective-permute-start(bf16[192,1152]{1,0:T(8,128)(2,1)} %get-tuple-element.267), channel_id=1, source_target_pairs={{0,24},{8,16},{16,8},{24,0},{1,25},{9,17},{17,9},{25,1},{2,26},{10... | collective-permute-start | bytes 1327112 | tf_op jit(solution)/shard_map/ppermute | solution.py:812
  (120 other events, 2290.7 us)
Sparse Core Ops, SparseCore 0:
  9.9 119.8 all-gather.11
  131.7 63.8 all-gather.5
  197.5 147.6 all-gather.7
  346.9 72.1 all-gather.9
  495.9 90.5 reduce-scatter.5
  589.3 79.3 reduce-scatter.7
  671.7 80.7 reduce-scatter.9
  755.5 37.3 reduce-scatter.11
  913.6 108.2 reduce-scatter.13

commit v11 on v10

--- a/solution.py
+++ b/solution.py
@@ -15,6 +15,7 @@
 FIRST_PATCHES = 16 * 12**2
 FIRST_MOST = FIRST_PATCHES + 96
 QBLOCK = 256
+ROW_BLOCK = 384
 BF16 = jnp.bfloat16
 F32 = jnp.float32
 VMEM_LIMIT = 60 * 1024 * 1024
@@ -150,9 +151,9 @@
     rows = projected.shape[0]
     return pl.pallas_call(
         functools.partial(stats_kernel, part, slots),
-        grid=(pl.cdiv(rows, QBLOCK),),
-        in_specs=[pl.BlockSpec((QBLOCK, slots * padded), lambda i: (i, 0))],
-        out_specs=pl.BlockSpec((8, QBLOCK), lambda i: (0, i)),
+        grid=(pl.cdiv(rows, ROW_BLOCK),),
+        in_specs=[pl.BlockSpec((ROW_BLOCK, slots * padded), lambda i: (i, 0))],
+        out_specs=pl.BlockSpec((8, ROW_BLOCK), lambda i: (0, i)),
         out_shape=jax.ShapeDtypeStruct((8, rows), F32),
         compiler_params=pltpu.CompilerParams(vmem_limit_bytes=VMEM_LIMIT),
         cost_estimate=pl.CostEstimate(flops=10 * rows * slots * padded, bytes_accessed=4 * rows * slots * padded, transcendentals=0),
@@ -182,16 +183,16 @@
     narrow = stats.shape[0]
     return pl.pallas_call(
         functools.partial(heads_kernel, part, query_scale),
-        grid=(pl.cdiv(rows, QBLOCK),),
+        grid=(pl.cdiv(rows, ROW_BLOCK),),
         in_specs=[
-            pl.BlockSpec((QBLOCK, triple), lambda i: (i, 0)),
-            pl.BlockSpec((narrow, 8, QBLOCK), lambda i: (0, 0, i)),
-            pl.BlockSpec((QBLOCK, 128), lambda i: (i, 0)),
-            pl.BlockSpec((QBLOCK, 128), lambda i: (i, 0)),
+            pl.BlockSpec((ROW_BLOCK, triple), lambda i: (i, 0)),
+            pl.BlockSpec((narrow, 8, ROW_BLOCK), lambda i: (0, 0, i)),
+            pl.BlockSpec((ROW_BLOCK, 128), lambda i: (i, 0)),
+            pl.BlockSpec((ROW_BLOCK, 128), lambda i: (i, 0)),
             pl.BlockSpec((2, padded), lambda i: (0, 0)),
             pl.BlockSpec((2, padded), lambda i: (0, 0)),
         ],
-        out_specs=pl.BlockSpec((QBLOCK, triple), lambda i: (i, 0)),
+        out_specs=pl.BlockSpec((ROW_BLOCK, triple), lambda i: (i, 0)),
         out_shape=jax.ShapeDtypeStruct((rows, triple), BF16),
         compiler_params=pltpu.CompilerParams(vmem_limit_bytes=VMEM_LIMIT),
         cost_estimate=pl.CostEstimate(flops=40 * rows * triple, bytes_accessed=6 * rows * triple, transcendentals=0),
@@ -262,16 +263,16 @@
     padded = triple // 3
     pairs = padded // 128
     narrow = stats.shape[0]
-    pair_spec = pl.BlockSpec((QBLOCK, 128), lambda i: (i, 0))
-    two_spec = pl.BlockSpec((QBLOCK, 2 * padded), lambda i: (i, 0))
-    stat_spec = pl.BlockSpec((narrow, 8, QBLOCK), lambda i: (0, 0, i))
+    pair_spec = pl.BlockSpec((ROW_BLOCK, 128), lambda i: (i, 0))
+    two_spec = pl.BlockSpec((ROW_BLOCK, 2 * padded), lambda i: (i, 0))
+    stat_spec = pl.BlockSpec((narrow, 8, ROW_BLOCK), lambda i: (0, 0, i))
     gain_spec = pl.BlockSpec((2, padded), lambda i: (0, 0))
     own, sums = pl.pallas_call(
         functools.partial(grad_stats_kernel, rows, part, pairs),
-        grid=(pl.cdiv(rows, QBLOCK),),
+        grid=(pl.cdiv(rows, ROW_BLOCK),),
         in_specs=[pair_spec] * (2 * pairs) + [two_spec, stat_spec, pair_spec, pair_spec, gain_spec],
         out_specs=[
-            pl.BlockSpec((8, QBLOCK), lambda i: (0, i)),
+            pl.BlockSpec((8, ROW_BLOCK), lambda i: (0, i)),
             pl.BlockSpec((8, padded), lambda i: (0, 0)),
         ],
         out_shape=[jax.ShapeDtypeStruct((8, rows), F32), jax.ShapeDtypeStruct((8, padded), F32)],
@@ -281,9 +282,9 @@
     totals = share(own)
     out = pl.pallas_call(
         functools.partial(heads_back_kernel, part, pairs),
-        grid=(pl.cdiv(rows, QBLOCK),),
+        grid=(pl.cdiv(rows, ROW_BLOCK),),
         in_specs=[pair_spec] * (3 * pairs) + [two_spec, stat_spec, stat_spec, pair_spec, pair_spec, gain_spec],
-        out_specs=pl.BlockSpec((QBLOCK, triple), lambda i: (i, 0)),
+        out_specs=pl.BlockSpec((ROW_BLOCK, triple), lambda i: (i, 0)),
         out_shape=jax.ShapeDtypeStruct((rows, triple), BF16),
         compiler_params=pltpu.CompilerParams(vmem_limit_bytes=VMEM_LIMIT),
         cost_estimate=pl.CostEstimate(flops=4 * rows * triple, bytes_accessed=rows * triple // 16, transcendentals=0),

time: 1110 us -> 1100 us (level)
  transfers between devices with their start and end apart: 40 -> 40, of which waited for: 12 -> 12; matrix products, arithmetic and copies ran while one was open for 36% -> 36% of each run, Pallas kernels for 38% -> 37%
where the time goes in v11:
time: 1100 us; the launch traced here: 1090 us
  Pallas kernels  440 us (40%)
  matrix products  244 us (22%)
  other arithmetic  112 us (10%)
  local copies, waits for them, and re-layouts  108 us (10%)
  starting transfers between devices  93.3 us (8%)
  waiting for transfers between devices  77.6 us (7%)
  between operations  18.3 us (2%)
    pallas_call x3, Pallas kernels, self_back(): pl.pallas_call(functools.partial(self_back_kernel, head_dim, FIRST_PATCHE...  137 us
    dot_general x11, matrix products, outer_sum(): lax.dot_general(left, right, (((0,), (0,)), ((), ())), preferred_element_...  93.4 us
    pallas_call x3, Pallas kernels, attend(): pl.pallas_call(functools.partial(attend_kernel, head_dim, FIRST_PATCHES,...  91.6 us
    dot_general x11, matrix products, low_product(): return jnp.dot(left, right, preferred_element_type=F32)  77.3 us
    dot_general x5, matrix products, times_transposed(): lax.dot_general(left, right, (((1,), (1,)), ((), ())), preferred_element_...  70.7 us
    pallas_call x5, Pallas kernels, fsdp_share(): pl.pallas_call(functools.partial(fsdp_share_kernel, narrow), in_specs=[pl...  66.2 us
    all_to_all x11, starting transfers between devices, exchange(): return lax.all_to_all(blocks, axis, 0, 0, tiled=True)  63 us
    all_to_all x11, waiting for transfers between devices, exchange(): return lax.all_to_all(blocks, axis, 0, 0, tiled=True)  40.6 us
  transfers between devices with their start and end apart: 40, of which 12 were waited for; matrix products, arithmetic and copies ran while one was open for 36% of the time, Pallas kernels for 37%

profile of v11, /device:TPU:0, one launch (start us, length us, event | category | flops | bytes accessed | tf_op | source)
XLA Modules:
  0.0 1093.5 jit_solution(3212085114180358263)
XLA Ops:
  40.4 27.4 %shard_map.263 = f32[4,96,128]{2,1,0:T(8,128)} custom-call(f32[96,128]{1,0:T(8,128)} %reshape.634.x_ref), custom_call_target="tpu_custom_call" | custom-call | bytes 393216 | tf_op jit(solution)/shard_map/pallas_call | solution.py:649
  75.8 10.5 negate_select_fusion
  150.2 13.6 %fusion.164.projected_ref.refs_6_.refs_9_ = f32[2624,1152]{1,0:T(8,128)} fusion(bf16[2624,1536]{1,0:T(8,128)(2,1)S(1)} %fusion.3, bf16[1536,1152]{1,0:T(8,128)(2,1)S(1)} %bitcast.251), kind=kOutput, calls=%fused_computation.378 | convolution fusion | flops 9286189056 | bytes 23691264 | tf_op jit(solution)/shard_map/dot_general | solution.py:29
  171.2 18.1 %shard_map.265.stats_ref.refs_7_.refs_10_ = f32[4,8,2624]{2,1,0:T(8,128)} custom-call(f32[8,2624]{1,0:T(8,128)} %shard_map.264.x_ref), custom_call_target="tpu_custom_call" | custom-call | bytes 671744 | tf_op jit(solution)/shard_map/pallas_call | solution.py:649
  189.4 13.3 %shard_map.266.q_ref.k_ref.v_ref = bf16[2624,1152]{1,0:T(8,128)(2,1)} custom-call(f32[2624,1152]{1,0:T(8,128)} %fusion.164.projected_ref.refs_6_.refs_9_, f32[4,8,2624]{2,1,0:T(8,128)} %shard_map.265.stats_ref.refs_7_.refs_10_, f32[2624,128]{1,0:T(8,128)} %get-tuple-element.282.cos_ref.refs_8_.refs_12_, ...), custom_call_target="tpu_custom_call" | custom-call | flops 120913920 | bytes 18137088 | tf_op jit(solution)/shard_map/pallas_call | solution.py:184
  219.3 30.8 %shard_map.271 = (bf16[2624,128]{1,0:T(8,128)(2,1)}, f32[2624,128]{1,0:T(8,128)}, f32[2624,128]{1,0:T(8,128)}, f32[8,2624]{1,0:T(8,128)}) custom-call(f32[3,1,2]{2,1,0:T(1,128)} %reshape.692.gate_ref, bf16[2624,1152]{1,0:T(8,128)(2,1)} %shard_map.266.q_ref.k_ref.v_ref, bf16[2624,1152]{1,0:T(8,128)(2,1)} %shard_map.266.q_ref.k_ref.v_ref, ...), custom_call_target="tpu_custom_call" | custom-call | flops 4213178368 | bytes 6717440 | tf_op jit(solution)/shard_map/pallas_call | solution.py:380
  253.9 30.4 %shard_map.270 = (bf16[2624,128]{1,0:T(8,128)(2,1)}, f32[2624,128]{1,0:T(8,128)}, f32[2624,128]{1,0:T(8,128)}, f32[8,2624]{1,0:T(8,128)}) custom-call(f32[3,1,2]{2,1,0:T(1,128)} %reshape.692.gate_ref, bf16[2624,1152]{1,0:T(8,128)(2,1)} %shard_map.266.q_ref.k_ref.v_ref, bf16[2624,1152]{1,0:T(8,128)(2,1)} %shard_map.266.q_ref.k_ref.v_ref, ...), custom_call_target="tpu_custom_call" | custom-call | flops 4213178368 | bytes 6717440 | tf_op jit(solution)/shard_map/pallas_call | solution.py:380
  288.6 30.4 %shard_map.269 = (bf16[2624,128]{1,0:T(8,128)(2,1)}, f32[2624,128]{1,0:T(8,128)}, f32[2624,128]{1,0:T(8,128)}, f32[8,2624]{1,0:T(8,128)}) custom-call(f32[3,1,2]{2,1,0:T(1,128)} %reshape.692.gate_ref, bf16[2624,1152]{1,0:T(8,128)(2,1)} %shard_map.266.q_ref.k_ref.v_ref, bf16[2624,1152]{1,0:T(8,128)(2,1)} %shard_map.266.q_ref.k_ref.v_ref, ...), custom_call_target="tpu_custom_call" | custom-call | flops 4213178368 | bytes 6717440 | tf_op jit(solution)/shard_map/pallas_call | solution.py:380
  323.4 15.8 %all-to-all-done.3 = bf16[4,656,128]{2,1,0:T(8,128)(2,1)} async-done(((bf16[4,656,128]{2,1,0:T(8,128)(2,1)}), bf16[4,656,128]{2,1,0:T(8,128)(2,1)}, u32[]{:S(2)}, u32[]{:S(2)}) %all-to-all-start.3) | async-done | bytes 671776 | tf_op jit(solution)/shard_map/all_to_all | solution.py:784
  363.6 26.5 %fusion.165.gate_ref.up_ref = f32[656,8192]{1,0:T(8,128)} fusion(bf16[656,1536]{1,0:T(8,128)(2,1)} %copy-done.34, bf16[1536,8192]{1,0:T(8,128)(2,1)} %all-gather.8.cloned.1.call-done), kind=kOutput, calls=%fused_computation.379 | convolution fusion | flops 16508780544 | bytes 48676864 | tf_op jit(solution)/shard_map/dot_general | solution.py:29
  390.1 23.0 %shard_map.272 = (bf16[656,4096]{1,0:T(8,128)(2,1)}, bf16[656,4096]{1,0:T(8,128)(2,1)}) custom-call(s32[1]{0:T(128)} %bitcast.29.core_ref, f32[656,8192]{1,0:T(8,128)} %fusion.165.gate_ref.up_ref, f32[656,8192]{1,0:T(8,128)} %fusion.165.gate_ref.up_ref), custom_call_target="tpu_custom_call" | custom-call | flops 16121856 | bytes 32243712 | tf_op jit(solution)/shard_map/pallas_call | solution.py:603
  417.3 13.1 %multiply_reduce_fusion.14 = (f32[656]{0:T(1024)S(1)}, f32[656,1536]{1,0:T(8,128)S(1)}) fusion(bf16[656,4096]{1,0:T(8,128)(2,1)} %get-tuple-element.113, bf16[4096,1536]{1,0:T(8,128)(2,1)} %all-gather.10.cloned.1.call-done), kind=kOutput, calls=%fused_computation.72 | convolution fusion | flops 8256404992 | bytes 21989952 | tf_op jit(solution)/shard_map/dot_general | solution.py:29
  445.9 19.5 %fusion.6 = (bf16[656,4096]{1,0:T(8,128)(2,1)}, bf16[656,4096]{1,0:T(8,128)(2,1)S(1)}) fusion(f32[656,8192]{1,0:T(8,128)} %fusion.165.gate_ref.up_ref, bf16[656,1536]{1,0:T(8,128)(2,1)} %copy-done.30, bf16[4096,1536]{1,0:T(8,128)(2,1)} %all-gather.10.cloned.1.call-done), kind=kOutput, calls=%fused_computation.13 | convolution fusion | flops 8289320960 | bytes 46841856 | tf_op jit(solution)/shard_map/dot_general | solution.py:33
  465.4 11.5 %convolution_convert_fusion.4 = bf16[768,4096]{1,0:T(8,128)(2,1)} fusion(bf16[656,4096]{1,0:T(8,128)(2,1)} %get-tuple-element.247, bf16[656,1536]{1,0:T(8,128)(2,1)S(1)} %copy-done.29), kind=kOutput, calls=%fused_computation.26 | convolution fusion | flops 4130340864 | bytes 12673024 | tf_op jit(solution)/shard_map/dot_general | solution.py:37
  484.5 9.2 add_convert_fusion
  494.5 28.7 %multiply_reduce_fusion.9 = (f32[1536]{0:T(1024)}, f32[656]{0:T(1024)S(1)}, f32[1536]{0:T(1024)}, f32[1536]{0:T(1024)}, f32[656,1536]{1,0:T(8,128)}) fusion(f32[656,1536]{1,0:T(8,128)} %copy-done.2, f32[656]{0:T(1024)S(1)} %copy-done.82, f32[1536]{0:T(1024)S(1)} %copy-done.69, f32[656]{0:T(1024)S(1)} %get-tuple-element.301, f32[1536]{0:T(1024)S(1)} %copy-done.71, ...), kind=kOutput, calls=%fused_computation.64 | convolution fusion | flops 16547399680 | bytes 44022016 | tf_op jit(solution)/shard_map/dot_general | solution.py:33
  556.1 10.8 add_convert_fusion.2
  566.9 10.8 add_convert_fusion.1
  589.7 13.5 %shard_map.275 = (bf16[2624,128]{1,0:T(8,128)(2,1)}, bf16[512,128]{1,0:T(8,128)(2,1)}, bf16[512,128]{1,0:T(8,128)(2,1)}, f32[8,128]{1,0:T(8,128)}) custom-call(f32[3,1,2]{2,1,0:T(1,128)} %reshape.692.gate_ref, bf16[2624,1152]{1,0:T(8,128)(2,1)} %shard_map.266.q_ref.k_ref.v_ref, bf16[512,768]{1,0:T(8,128)(2,1)} %pad_maximum_fusion.5.tk_ref.tv_ref, ...), custom_call_target="tpu_custom_call" | custom-call | flops 1719664640 | bytes 4030464 | tf_op jit(solution)/shard_map/pallas_call | solution.py:496
  603.2 13.3 %shard_map.274 = (bf16[2624,128]{1,0:T(8,128)(2,1)}, bf16[512,128]{1,0:T(8,128)(2,1)}, bf16[512,128]{1,0:T(8,128)(2,1)}, f32[8,128]{1,0:T(8,128)}) custom-call(f32[3,1,2]{2,1,0:T(1,128)} %reshape.692.gate_ref, bf16[2624,1152]{1,0:T(8,128)(2,1)} %shard_map.266.q_ref.k_ref.v_ref, bf16[512,768]{1,0:T(8,128)(2,1)} %pad_maximum_fusion.5.tk_ref.tv_ref, ...), custom_call_target="tpu_custom_call" | custom-call | flops 1719664640 | bytes 4030464 | tf_op jit(solution)/shard_map/pallas_call | solution.py:496
  616.5 13.5 %shard_map.273 = (bf16[2624,128]{1,0:T(8,128)(2,1)}, bf16[512,128]{1,0:T(8,128)(2,1)}, bf16[512,128]{1,0:T(8,128)(2,1)}, f32[8,128]{1,0:T(8,128)}) custom-call(f32[3,1,2]{2,1,0:T(1,128)} %reshape.692.gate_ref, bf16[2624,1152]{1,0:T(8,128)(2,1)} %shard_map.266.q_ref.k_ref.v_ref, bf16[512,768]{1,0:T(8,128)(2,1)} %pad_maximum_fusion.5.tk_ref.tv_ref, ...), custom_call_target="tpu_custom_call" | custom-call | flops 1719664640 | bytes 4030464 | tf_op jit(solution)/shard_map/pallas_call | solution.py:496
  651.7 45.7 %shard_map.277 = (bf16[2624,128]{1,0:T(8,128)(2,1)}, bf16[2624,128]{1,0:T(8,128)(2,1)}, bf16[2624,128]{1,0:T(8,128)(2,1)}) custom-call(bf16[2624,1152]{1,0:T(8,128)(2,1)} %shard_map.266.q_ref.k_ref.v_ref, bf16[2624,1152]{1,0:T(8,128)(2,1)} %shard_map.266.q_ref.k_ref.v_ref, bf16[2624,1152]{1,0:T(8,128)(2,1)} %shard_map.266.q_ref.k_ref.v_ref, ...), custom_call_target="tpu_custom_call" | custom-call | flops 8813281280 | bytes 10076160 | tf_op jit(solution)/shard_map/pallas_call | solution.py:563
  730.7 45.8 %shard_map.278 = (bf16[2624,128]{1,0:T(8,128)(2,1)}, bf16[2624,128]{1,0:T(8,128)(2,1)}, bf16[2624,128]{1,0:T(8,128)(2,1)}) custom-call(bf16[2624,1152]{1,0:T(8,128)(2,1)} %shard_map.266.q_ref.k_ref.v_ref, bf16[2624,1152]{1,0:T(8,128)(2,1)} %shard_map.266.q_ref.k_ref.v_ref, bf16[2624,1152]{1,0:T(8,128)(2,1)} %shard_map.266.q_ref.k_ref.v_ref, ...), custom_call_target="tpu_custom_call" | custom-call | flops 8813281280 | bytes 10076160 | tf_op jit(solution)/shard_map/pallas_call | solution.py:563
  783.4 45.6 %shard_map.279 = (bf16[2624,128]{1,0:T(8,128)(2,1)}, bf16[2624,128]{1,0:T(8,128)(2,1)}, bf16[2624,128]{1,0:T(8,128)(2,1)}) custom-call(bf16[2624,1152]{1,0:T(8,128)(2,1)} %shard_map.266.q_ref.k_ref.v_ref, bf16[2624,1152]{1,0:T(8,128)(2,1)} %shard_map.266.q_ref.k_ref.v_ref, bf16[2624,1152]{1,0:T(8,128)(2,1)} %shard_map.266.q_ref.k_ref.v_ref, ...), custom_call_target="tpu_custom_call" | custom-call | flops 8813281280 | bytes 10076160 | tf_op jit(solution)/shard_map/pallas_call | solution.py:563
  841.6 13.2 %shard_map.280 = (f32[8,2624]{1,0:T(8,128)}, f32[8,384]{1,0:T(8,128)}) custom-call(bf16[2624,128]{1,0:T(8,128)(2,1)} %get-tuple-element.136.refs_0_, bf16[2624,128]{1,0:T(8,128)(2,1)} %get-tuple-element.143.refs_1_, bf16[2624,128]{1,0:T(8,128)(2,1)} %get-tuple-element.152.refs_2_, bf16[2624,128]{1,0:T(8,128)(2,1)} %get-tuple-element.153.refs_3_, ...), custom_call_target="tpu_custom_call" | custom-call | flops 12091392 | bytes 188928 | tf_op jit(solution)/shard_map/pallas_call | solution.py:270
  871.5 14.4 %shard_map.282 = bf16[2624,1152]{1,0:T(8,128)(2,1)} custom-call(bf16[2624,128]{1,0:T(8,128)(2,1)} %get-tuple-element.136.refs_0_, bf16[2624,128]{1,0:T(8,128)(2,1)} %get-tuple-element.143.refs_1_, bf16[2624,128]{1,0:T(8,128)(2,1)} %get-tuple-element.152.refs_2_, bf16[2624,128]{1,0:T(8,128)(2,1)} %get-tuple-element.153.refs_3_, ...), custom_call_target="tpu_custom_call" | custom-call | flops 12091392 | bytes 188928 | tf_op jit(solution)/shard_map/pallas_call | solution.py:283
  885.9 9.8 collective-permute-done.13
  895.7 15.5 %convolution_convert_fusion = bf16[2624,1536]{1,0:T(8,128)(2,1)} fusion(bf16[2624,1152]{1,0:T(8,128)(2,1)} %shard_map.282, bf16[1536,1152]{1,0:T(8,128)(2,1)S(1)} %bitcast.252), kind=kOutput, calls=%fused_computation.9 | convolution fusion | flops 9290219520 | bytes 17645568 | tf_op jit(solution)/shard_map/dot_general | solution.py:33
  916.0 15.4 %convolution_convert_fusion.2 = bf16[1536,1152]{1,0:T(8,128)(2,1)S(1)} fusion(bf16[2624,1536]{1,0:T(8,128)(2,1)} %copy-done.18, bf16[2624,1152]{1,0:T(8,128)(2,1)} %shard_map.282), kind=kOutput, calls=%fused_computation.24 | convolution fusion | flops 9287958528 | bytes 17645568 | tf_op jit(solution)/shard_map/dot_general | solution.py:37
  949.9 19.5 %all-to-all-start.9 = ((bf16[4,128,1024]{2,1,0:T(8,128)(2,1)}), bf16[4,128,1024]{2,1,0:T(8,128)(2,1)S(1)}, u32[]{:S(2)}, u32[]{:S(2)}) async-start(bf16[4,128,1024]{2,1,0:T(8,128)(2,1)} %bitcast.63), calls=%async_computation.14 | async-start | bytes 2097152 | tf_op jit(solution)/shard_map/all_to_all | solution.py:784
  1001.8 9.7 collective-permute-done.18
  1029.6 31.5 %shard_map.283 = (f32[7,1536]{1,0:T(8,128)}, f32[2,1536]{1,0:T(2,128)}, f32[1,128]{1,0:T(1,128)}, f32[32,128]{1,0:T(8,128)}, f32[8,2,6144]{2,1,0:T(2,128)}, /*index=5*/f32[8,2,1024]{2,1,0:T(2,128)}) custom-call(f32[12,128]{1,0:T(8,128)} %bitcast.284, f32[12,128]{1,0:T(8,128)} %bitcast.283, f32[12,128]{1,0:T(8,128)} %bitcast.292, f32[12,128]{1,0:T(8,128)} %bitcast.278, ...), custom_call_target="tpu_custom_call" | custom-call | tf_op jit(solution)/shard_map/pallas_call | solution.py:765
  (476 shorter events, 425.4 us)
Async XLA Ops:
  7.2 122.6 %all-gather.12.cloned.1.call-start = ((), (), s32[]{:S(2)}) async-start(), calls=%async_computation.24 | async-start | bytes 10076160 | tf_op jit(solution)/shard_map/all_gather | solution.py:926
  7.9 334.1 %all-gather.6.cloned.1.call-start = ((), (), s32[]{:S(2)}) async-start(), calls=%async_computation.16 | async-start | bytes 5308416 | tf_op jit(solution)/shard_map/all_gather | solution.py:854
  10.2 353.4 %all-gather.8.cloned.1.call-start = ((), (), s32[]{:S(2)}) async-start(), calls=%async_computation.17 | async-start | bytes 28311552 | tf_op jit(solution)/shard_map/all_gather | solution.py:854
  25.0 61.3 %all-to-all-start.1 = ((bf16[4,192,1152]{2,1,0:T(8,128)(2,1)}), bf16[4,192,1152]{2,1,0:T(8,128)(2,1)}, u32[]{:S(2)}, u32[]{:S(2)}) async-start(bf16[4,192,1152]{2,1,0:T(8,128)(2,1)} %reshape.641), calls=%async_computation.1 | async-start | bytes 3538944 | tf_op jit(solution)/shard_map/all_to_all | solution.py:784
  30.3 387.0 %all-gather.10.cloned.1.call-start = ((), (), s32[]{:S(2)}) async-start(), calls=%async_computation.18 | async-start | bytes 14155776 | tf_op jit(solution)/shard_map/all_gather | solution.py:854
  129.8 72.8 %all-to-all-start.2 = ((bf16[4,512,768]{2,1,0:T(8,128)(2,1)}), bf16[4,512,768]{2,1,0:T(8,128)(2,1)}, u32[]{:S(2)}, u32[]{:S(2)}) async-start(bf16[4,512,768]{2,1,0:T(8,128)(2,1)} %pad_maximum_fusion.1), calls=%async_computation.2 | async-start | bytes 6291456 | tf_op jit(solution)/shard_map/all_to_all | solution.py:784
  250.1 34.2 %all-to-all-start.5 = ((bf16[4,656,128]{2,1,0:T(8,128)(2,1)}), bf16[4,656,128]{2,1,0:T(8,128)(2,1)S(1)}, u32[]{:S(2)}, u32[]{:S(2)}) async-start(bf16[4,656,128]{2,1,0:T(8,128)(2,1)} %bitcast.275), calls=%async_computation.5 | async-start | bytes 1343488 | tf_op jit(solution)/shard_map/all_to_all | solution.py:784
  284.3 34.8 %all-to-all-start.4 = ((bf16[4,656,128]{2,1,0:T(8,128)(2,1)}), bf16[4,656,128]{2,1,0:T(8,128)(2,1)S(1)}, u32[]{:S(2)}, u32[]{:S(2)}) async-start(bf16[4,656,128]{2,1,0:T(8,128)(2,1)} %bitcast.274), calls=%async_computation.4 | async-start | bytes 1343488 | tf_op jit(solution)/shard_map/all_to_all | solution.py:784
  323.3 261.0 %reduce-scatter.6.cloned.1.call-start = ((), (), s32[]{:S(2)}) async-start(), calls=%async_computation.19 | async-start | bytes 7864320 | tf_op jit(solution)/shard_map/reduce_scatter | solution.py:807
  445.6 38.9 %collective-permute-start.4 = (bf16[2048,1536]{1,0:T(8,128)(2,1)}, bf16[2048,1536]{1,0:T(8,128)(2,1)}, u32[]{:S(2)}, u32[]{:S(2)}) collective-permute-start(bf16[2048,1536]{1,0:T(8,128)(2,1)} %convolution_convert_fusion.1), channel_id=1, source_target_pairs={{0,4},{4,0},{1,5},{5,1},{2,6},{6,2},{3,7},{7,3},{8,12},{12,8},{9,1... | collective-permute-start | bytes 18874376 | tf_op jit(solution)/shard_map/ppermute | solution.py:788
  476.9 79.2 %collective-permute-start.1 = (bf16[768,4096]{1,0:T(8,128)(2,1)}, bf16[768,4096]{1,0:T(8,128)(2,1)}, u32[]{:S(2)}, u32[]{:S(2)}) collective-permute-start(bf16[768,4096]{1,0:T(8,128)(2,1)} %convolution_convert_fusion.4), channel_id=1, source_target_pairs={{0,4},{4,0},{1,5},{5,1},{2,6},{6,2},{3,7},{7,3},{8,12},{12,8},{9,1... | collective-permute-start | bytes 18874376 | tf_op jit(solution)/shard_map/ppermute | solution.py:788
  484.2 82.7 %collective-permute-start.2 = (bf16[768,4096]{1,0:T(8,128)(2,1)}, bf16[768,4096]{1,0:T(8,128)(2,1)}, u32[]{:S(2)}, u32[]{:S(2)}) collective-permute-start(bf16[768,4096]{1,0:T(8,128)(2,1)} %convolution_convert_fusion.3), channel_id=1, source_target_pairs={{0,4},{4,0},{1,5},{5,1},{2,6},{6,2},{3,7},{7,3},{8,12},{12,8},{9,1... | collective-permute-start | bytes 18874376 | tf_op jit(solution)/shard_map/ppermute | solution.py:788
  546.2 37.6 %all-to-all-start.6 = ((bf16[4,656,384]{2,1,0:T(8,128)(2,1)}), bf16[4,656,384]{2,1,0:T(8,128)(2,1)S(1)}, u32[]{:S(2)}, u32[]{:S(2)}) async-start(bf16[4,656,384]{2,1,0:T(8,128)(2,1)} %bitcast.245), calls=%async_computation.6 | async-start | bytes 4030464 | tf_op jit(solution)/shard_map/all_to_all | solution.py:784
  549.8 226.7 %reduce-scatter.8.cloned.1.call-start = ((), (), s32[]{:S(2)}) async-start(), calls=%async_computation.20 | async-start | bytes 7864320 | tf_op jit(solution)/shard_map/reduce_scatter | solution.py:807
  584.3 192.3 %reduce-scatter.10.cloned.1.call-start = ((), (), s32[]{:S(2)}) async-start(), calls=%async_computation.21 | async-start | bytes 7864320 | tf_op jit(solution)/shard_map/reduce_scatter | solution.py:807
  585.1 116.1 %all-to-all-start.7 = ((bf16[4,128,1536]{2,1,0:T(8,128)(2,1)}), bf16[4,128,1536]{2,1,0:T(8,128)(2,1)S(1)}, u32[]{:S(2)}, u32[]{:S(2)}) async-start(bf16[4,128,1536]{2,1,0:T(8,128)(2,1)} %bitcast.269), calls=%async_computation.8 | async-start | bytes 3145728 | tf_op jit(solution)/shard_map/all_to_all | solution.py:784
  589.7 239.3 %reduce-scatter.12.cloned.1.call-start = ((), (), s32[]{:S(2)}) async-start(), calls=%async_computation.22 | async-start | bytes 2949120 | tf_op jit(solution)/shard_map/reduce_scatter | solution.py:807
  643.3 54.0 %collective-permute-start.5 = (bf16[512,768]{1,0:T(8,128)(2,1)}, bf16[512,768]{1,0:T(8,128)(2,1)}, u32[]{:S(2)}, u32[]{:S(2)}) collective-permute-start(bf16[512,768]{1,0:T(8,128)(2,1)} %pad_maximum_fusion.6), channel_id=1, source_target_pairs={{0,1},{1,0},{2,3},{3,2},{4,5},{5,4},{6,7},{7,6},{8,9},{9,8},{10,11... | collective-permute-start | bytes 2359304 | tf_op jit(solution)/shard_map/ppermute | solution.py:826
  644.8 52.5 %collective-permute-start.6 = (bf16[512,768]{1,0:T(8,128)(2,1)}, bf16[512,768]{1,0:T(8,128)(2,1)}, u32[]{:S(2)}, u32[]{:S(2)}) collective-permute-start(bf16[512,768]{1,0:T(8,128)(2,1)} %pad_maximum_fusion.6), channel_id=1, source_target_pairs={{0,2},{1,3},{2,0},{3,1},{4,6},{5,7},{6,4},{7,5},{8,10},{9,11},{10,... | collective-permute-start | bytes 2359304 | tf_op jit(solution)/shard_map/ppermute | solution.py:826
  645.4 55.9 %collective-permute-start.7 = (bf16[512,768]{1,0:T(8,128)(2,1)}, bf16[512,768]{1,0:T(8,128)(2,1)}, u32[]{:S(2)}, u32[]{:S(2)}) collective-permute-start(bf16[512,768]{1,0:T(8,128)(2,1)} %pad_maximum_fusion.6), channel_id=1, source_target_pairs={{0,3},{1,2},{2,1},{3,0},{4,7},{5,6},{6,5},{7,4},{8,11},{9,10},{10,... | collective-permute-start | bytes 2359304 | tf_op jit(solution)/shard_map/ppermute | solution.py:826
  726.0 103.0 %all-to-all-start.8 = ((bf16[4,128,3072]{2,1,0:T(8,128)(2,1)}), bf16[4,128,3072]{2,1,0:T(8,128)(2,1)S(1)}, u32[]{:S(2)}, u32[]{:S(2)}) async-start(bf16[4,128,3072]{2,1,0:T(8,128)(2,1)} %bitcast.253), calls=%async_computation.11 | async-start | bytes 6291456 | tf_op jit(solution)/shard_map/all_to_all | solution.py:784
  730.7 293.6 %reduce-scatter.14.cloned.1.call-start = ((), (), s32[]{:S(2)}) async-start(), calls=%async_computation.23 | async-start | bytes 10076160 | tf_op jit(solution)/shard_map/reduce_scatter | solution.py:1159
  779.1 50.0 %collective-permute-start.9 = (bf16[48,4096]{1,0:T(8,128)(2,1)}, bf16[48,4096]{1,0:T(8,128)(2,1)S(1)}, u32[]{:S(2)}, u32[]{:S(2)}) collective-permute-start(bf16[48,4096]{1,0:T(8,128)(2,1)} %get-tuple-element.273), channel_id=1, source_target_pairs={{0,8},{8,0},{16,24},{24,16},{1,9},{9,1},{17,25},{25,17},{2,10},{10... | collective-permute-start | bytes 1179656 | tf_op jit(solution)/shard_map/ppermute | solution.py:813
  781.1 48.0 %collective-permute-start.10 = (bf16[48,4096]{1,0:T(8,128)(2,1)}, bf16[48,4096]{1,0:T(8,128)(2,1)}, u32[]{:S(2)}, u32[]{:S(2)}) collective-permute-start(bf16[48,4096]{1,0:T(8,128)(2,1)} %get-tuple-element.272), channel_id=1, source_target_pairs={{0,16},{8,24},{16,0},{24,8},{1,17},{9,25},{17,1},{25,9},{2,18},{10... | collective-permute-start | bytes 1179656 | tf_op jit(solution)/shard_map/ppermute | solution.py:813
  783.4 45.6 %collective-permute-start.11 = (bf16[48,4096]{1,0:T(8,128)(2,1)}, bf16[48,4096]{1,0:T(8,128)(2,1)}, u32[]{:S(2)}, u32[]{:S(2)}) collective-permute-start(bf16[48,4096]{1,0:T(8,128)(2,1)} %get-tuple-element.271), channel_id=1, source_target_pairs={{0,24},{8,16},{16,8},{24,0},{1,25},{9,17},{17,9},{25,1},{2,26},{10... | collective-permute-start | bytes 1179656 | tf_op jit(solution)/shard_map/ppermute | solution.py:813
  832.4 53.5 %collective-permute-start.12 = (bf16[48,5632]{1,0:T(8,128)(2,1)}, bf16[48,5632]{1,0:T(8,128)(2,1)}, u32[]{:S(2)}, u32[]{:S(2)}) collective-permute-start(bf16[48,5632]{1,0:T(8,128)(2,1)} %get-tuple-element.264), channel_id=1, source_target_pairs={{0,8},{8,0},{16,24},{24,16},{1,9},{9,1},{17,25},{25,17},{2,10},{10... | collective-permute-start | bytes 1622024 | tf_op jit(solution)/shard_map/ppermute | solution.py:813
  839.2 56.5 %collective-permute-start.13 = (bf16[48,5632]{1,0:T(8,128)(2,1)}, bf16[48,5632]{1,0:T(8,128)(2,1)}, u32[]{:S(2)}, u32[]{:S(2)}) collective-permute-start(bf16[48,5632]{1,0:T(8,128)(2,1)} %get-tuple-element.263), channel_id=1, source_target_pairs={{0,16},{8,24},{16,0},{24,8},{1,17},{9,25},{17,1},{25,9},{2,18},{10... | collective-permute-start | bytes 1622024 | tf_op jit(solution)/shard_map/ppermute | solution.py:813
  839.2 56.5 %collective-permute-start.14 = (bf16[48,5632]{1,0:T(8,128)(2,1)}, bf16[48,5632]{1,0:T(8,128)(2,1)}, u32[]{:S(2)}, u32[]{:S(2)}) collective-permute-start(bf16[48,5632]{1,0:T(8,128)(2,1)} %get-tuple-element.262), channel_id=1, source_target_pairs={{0,24},{8,16},{16,8},{24,0},{1,25},{9,17},{17,9},{25,1},{2,26},{10... | collective-permute-start | bytes 1622024 | tf_op jit(solution)/shard_map/ppermute | solution.py:813
  864.1 47.2 %collective-permute-start.15 = (bf16[128,3072]{1,0:T(8,128)(2,1)}, bf16[128,3072]{1,0:T(8,128)(2,1)}, u32[]{:S(2)}, u32[]{:S(2)}) collective-permute-start(bf16[128,3072]{1,0:T(8,128)(2,1)} %reduce_sum.354), channel_id=1, source_target_pairs={{0,0},{1,8},{2,16},{3,24},{4,4},{5,12},{6,20},{7,28},{8,1},{9,9},{... | collective-permute-start | bytes 2359304 | tf_op jit(solution)/shard_map/ppermute | solution.py:1135
  949.9 39.3 %all-to-all-start.9 = ((bf16[4,128,1024]{2,1,0:T(8,128)(2,1)}), bf16[4,128,1024]{2,1,0:T(8,128)(2,1)S(1)}, u32[]{:S(2)}, u32[]{:S(2)}) async-start(bf16[4,128,1024]{2,1,0:T(8,128)(2,1)} %bitcast.63), calls=%async_computation.14 | async-start | bytes 2097152 | tf_op jit(solution)/shard_map/all_to_all | solution.py:784
  978.2 33.3 %collective-permute-start.18 = (bf16[192,1152]{1,0:T(8,128)(2,1)}, bf16[192,1152]{1,0:T(8,128)(2,1)}, u32[]{:S(2)}, u32[]{:S(2)}) collective-permute-start(bf16[192,1152]{1,0:T(8,128)(2,1)} %get-tuple-element.268), channel_id=1, source_target_pairs={{0,16},{8,24},{16,0},{24,8},{1,17},{9,25},{17,1},{25,9},{2,18},{10... | collective-permute-start | bytes 1327112 | tf_op jit(solution)/shard_map/ppermute | solution.py:813
  980.1 31.4 %collective-permute-start.19 = (bf16[192,1152]{1,0:T(8,128)(2,1)}, bf16[192,1152]{1,0:T(8,128)(2,1)}, u32[]{:S(2)}, u32[]{:S(2)}) collective-permute-start(bf16[192,1152]{1,0:T(8,128)(2,1)} %get-tuple-element.267), channel_id=1, source_target_pairs={{0,24},{8,16},{16,8},{24,0},{1,25},{9,17},{17,9},{25,1},{2,26},{10... | collective-permute-start | bytes 1327112 | tf_op jit(solution)/shard_map/ppermute | solution.py:813
  (120 other events, 2282.8 us)
Sparse Core Ops, SparseCore 0:
  9.9 119.8 all-gather.11
  131.7 63.7 all-gather.5
  197.4 145.9 all-gather.7
  345.1 72.1 all-gather.9
  493.9 90.3 reduce-scatter.5
  587.1 79.1 reduce-scatter.7
  669.2 81.1 reduce-scatter.9
  753.5 37.3 reduce-scatter.11
  911.5 108.8 reduce-scatter.13
